TPU v7x, 512 devices: a whole 4x4x16 slice. The times are simulated.
512 devices in a mesh: ctx: 64 (over z_hi, x, y, core), head: 8 (over z_lo).
Axes of the slice: x: 4, y: 4, z: 16 (z_hi: 2, z_lo: 8; z = z_hi * 8 + z_lo), core: 2. Of those that a mesh axis runs over, the one named last changes fastest.
Arguments:
- queries: bfloat16 [8192, 6144], P('ctx', 'head'), may hold values from -140 to 140
- keys: bfloat16 [8192, 6144], P('ctx', 'head'), may hold values from -5.05 to 5.05
- values: bfloat16 [8192, 6144], P('ctx', 'head'), may hold values from -6 to 6
- plan: int32 [2, 64], replicated, may hold values from 0 to 63, as said below
- w_out: bfloat16 [6144, 6144], P('head', 'ctx'), may hold values from -3.5 to 3.5
Outputs:
- projected: bfloat16 [8192, 6144], P('ctx', 'head')
Inputs may be any that keep to these rules, and one draw needn't show every extreme that they name: plan comes from the circle method over 64 blocks: each row is a pairing, plan[r, plan[r, b]] = b and plan[r, b] != b, and the rounds give each block different partners.
All inputs are finite; a program needn't handle non-finite values.
Results may differ from a plain program's by a relative error of at most 0.017.
Values may be sent and summed in bfloat16 or wider, within the bound.
No kernel may reach another device: no remote copies, remote signals or barrier semaphores. Data moves between devices by JAX's collectives and lax.ppermute only.
A program may use at most 64 MiB of HBM per device.

v0:
```python
import jax
import jax.numpy as jnp
from jax import lax
from jax.sharding import PartitionSpec as P

HEAD_DIM = 128
ROUNDS = 2


def body(queries, keys, values, plan, w_out):
    tok_rows = queries.shape[0]
    inner_width = queries.shape[1]
    head_count = inner_width // HEAD_DIM
    blocks = lax.axis_size("ctx")
    piece_rows = tok_rows // blocks
    score_scale = 1.0 / HEAD_DIM**0.5
    stacked = jnp.concatenate((keys, values), 1).reshape(blocks, piece_rows, 2 * inner_width)
    routed = []
    for turn_index in range(ROUNDS):

        def forward(spread, partner_order=plan[turn_index]):
            chosen = jnp.take(spread, partner_order, axis=0)
            return lax.all_to_all(chosen, "ctx", split_axis=0, concat_axis=0, tiled=True)

        routed.append(
            forward(lax.all_to_all(stacked, "ctx", split_axis=0, concat_axis=0, tiled=True))
        )
    kv_rows = jnp.concatenate(
        [stacked.reshape(tok_rows, 2 * inner_width)]
        + [arrived.reshape(tok_rows, 2 * inner_width) for arrived in routed],
        0,
    )
    key_rows = kv_rows[:, :inner_width].reshape(-1, head_count, HEAD_DIM)
    value_rows = kv_rows[:, inner_width:].reshape(-1, head_count, HEAD_DIM)
    query_rows = queries.reshape(tok_rows, head_count, HEAD_DIM)
    scores = (
        jnp.einsum("qhd,khd->hqk", query_rows, key_rows, preferred_element_type=jnp.float32)
        * score_scale
    )
    row_peak = jnp.max(scores, axis=-1, keepdims=True)
    exponent = jnp.exp(scores - row_peak)
    row_total = jnp.sum(exponent, axis=-1)
    weights = exponent.astype(jnp.bfloat16)
    summed = jnp.einsum("hqk,khd->qhd", weights, value_rows, preferred_element_type=jnp.float32)
    attended = (
        (summed / jnp.transpose(row_total)[:, :, None])
        .astype(jnp.bfloat16)
        .reshape(tok_rows, inner_width)
    )
    partials = jnp.dot(
        attended,
        lax.all_gather(w_out, "ctx", axis=1, tiled=True),
        preferred_element_type=jnp.float32,
    )
    return lax.psum_scatter(partials.astype(jnp.bfloat16), "head", scatter_dimension=1, tiled=True)


def solution(mesh):
    return jax.shard_map(
        body,
        mesh=mesh,
        in_specs=(P("ctx", "head"), P("ctx", "head"), P("ctx", "head"), P(), P("head", "ctx")),
        out_specs=P("ctx", "head"),
        check_vma=False,
    )
```

profile of v0, /device:TPU:6, one launch (start us, length us, event | category | flops | bytes accessed | tf_op | source)
XLA Modules:
  0.0 303.3 jit_solution(18284845962367726207)
XLA Ops:
  6.5 0.0 all-gather.2.cloned.1.call-start
  6.5 0.7 all-gather.2.cloned.1.call-update
  7.3 0.0 copy-start.1
  7.3 0.9 constant_dynamic-update-slice_fusion.1
  8.2 0.9 constant_dynamic-update-slice_fusion
  9.2 0.9 reshape.28
  10.1 21.3 %all-to-all-start = ((bf16[64,2,1536]{2,1,0:T(2,128)(2,1)}), bf16[64,2,1536]{2,1,0:T(2,128)(2,1)S(1)}, u32[]{:S(2)}, u32[]{:S(2)}) async-start(bf16[64,2,1536]{2,1,0:T(2,128)(2,1)} %reshape.28), calls=%async_computation | async-start | bytes 786432 | tf_op jit(solution)/shard_map/all_to_all | solution.py:26
  31.3 0.0 copy-done.1
  31.4 19.0 %all-to-all-done = bf16[64,2,1536]{2,1,0:T(2,128)(2,1)S(1)} async-done(((bf16[64,2,1536]{2,1,0:T(2,128)(2,1)}), bf16[64,2,1536]{2,1,0:T(2,128)(2,1)S(1)}, u32[]{:S(2)}, u32[]{:S(2)}) %all-to-all-start) | async-done | bytes 393248 | tf_op jit(solution)/shard_map/all_to_all | solution.py:26
  50.3 1.4 gather_fusion
  51.7 1.2 broadcast_select_fusion.1
  52.9 5.8 %all-to-all-start.1 = ((bf16[64,2,1536]{2,1,0:T(2,128)(2,1)}), bf16[64,2,1536]{2,1,0:T(2,128)(2,1)S(1)}, u32[]{:S(2)}, u32[]{:S(2)}) async-start(bf16[64,2,1536]{2,1,0:T(2,128)(2,1)} %broadcast_select_fusion.1), calls=%async_computation.1 | async-start | bytes 786432 | tf_op jit(solution)/shard_map/all_to_all | solution.py:23
  58.7 0.0 copy-start
  58.7 1.4 gather_fusion.1
  60.1 1.2 broadcast_select_fusion
  61.3 16.0 %all-to-all-done.1 = bf16[64,2,1536]{2,1,0:T(2,128)(2,1)S(1)} async-done(((bf16[64,2,1536]{2,1,0:T(2,128)(2,1)}), bf16[64,2,1536]{2,1,0:T(2,128)(2,1)S(1)}, u32[]{:S(2)}, u32[]{:S(2)}) %all-to-all-start.1) | async-done | bytes 393248 | tf_op jit(solution)/shard_map/all_to_all | solution.py:23
  77.3 5.6 %all-to-all-start.2 = ((bf16[64,2,1536]{2,1,0:T(2,128)(2,1)}), bf16[64,2,1536]{2,1,0:T(2,128)(2,1)S(1)}, u32[]{:S(2)}, u32[]{:S(2)}) async-start(bf16[64,2,1536]{2,1,0:T(2,128)(2,1)} %broadcast_select_fusion), calls=%async_computation.2 | async-start | bytes 786432 | tf_op jit(solution)/shard_map/all_to_all | solution.py:23
  82.9 0.0 reduce-scatter.2.cloned.1.call-start
  82.9 0.0 copy-done
  82.9 0.2 copy.17
  83.1 0.1 reshape.29
  83.3 32.8 %all-to-all-done.2 = bf16[64,2,1536]{2,1,0:T(2,128)(2,1)S(1)} async-done(((bf16[64,2,1536]{2,1,0:T(2,128)(2,1)}), bf16[64,2,1536]{2,1,0:T(2,128)(2,1)S(1)}, u32[]{:S(2)}, u32[]{:S(2)}) %all-to-all-start.2) | async-done | bytes 393248 | tf_op jit(solution)/shard_map/all_to_all | solution.py:23
  116.0 0.1 reshape.30
  116.2 0.1 pad_maximum_fusion
  116.3 0.1 fusion.7
  116.3 0.3 copy.16
  116.6 0.3 copy.15
  117.0 0.4 fusion.8
  117.3 0.2 fusion.3
  117.5 0.3 fusion.2
  117.9 106.7 %all-gather.2.cloned.1.call-done = bf16[768,6144]{0,1:T(8,128)(2,1)} async-done(((bf16[768,96]{0,1:T(8,128)(2,1)}), bf16[768,6144]{0,1:T(8,128)(2,1)}) %all-gather.2.cloned.1.call-update) | async-done | bytes 9437200 | tf_op jit(solution)/shard_map/all_gather | solution.py:52
  224.6 8.0 %convolution_convert_fusion = bf16[128,6144]{1,0:T(8,128)(2,1)} fusion(bf16[128,768]{0,1:T(8,128)(2,1)S(1)} %bitcast.27, bf16[768,6144]{0,1:T(8,128)(2,1)} %all-gather.2.cloned.1.call-done), kind=kOutput, calls=%fused_computation.2 | convolution fusion | flops 1208745984 | bytes 11206656 | tf_op jit(solution)/shard_map/dot_general | solution.py:50
  232.6 0.0 reduce-scatter.2.cloned.1.call-update
  232.6 63.8 %reduce-scatter.2.cloned.1.call-done = bf16[128,768]{1,0:T(8,128)(2,1)} async-done(((bf16[128,6144]{1,0:T(8,128)(2,1)}), bf16[128,768]{1,0:T(8,128)(2,1)}) %reduce-scatter.2.cloned.1.call-update) | async-done | bytes 196624 | tf_op jit(solution)/shard_map/reduce_scatter | solution.py:55
  (3 shorter events, 0.0 us)
Async XLA Ops:
  6.5 218.0 %all-gather.2.cloned.1.call-start = ((), (), s32[]{:S(2)}) async-start(), calls=%async_computation.4 | async-start | bytes 9584640 | tf_op jit(solution)/shard_map/all_gather | solution.py:52
  7.3 24.1 %copy-start.1 = (s32[2,64]{1,0:T(2,128)S(1)}, s32[2,64]{1,0:T(2,128)}, u32[]{:S(2)}) copy-start(s32[2,64]{1,0:T(2,128)} %param.10) | copy-start | bytes 1540
  10.1 40.3 %all-to-all-start = ((bf16[64,2,1536]{2,1,0:T(2,128)(2,1)}), bf16[64,2,1536]{2,1,0:T(2,128)(2,1)S(1)}, u32[]{:S(2)}, u32[]{:S(2)}) async-start(bf16[64,2,1536]{2,1,0:T(2,128)(2,1)} %reshape.28), calls=%async_computation | async-start | bytes 786432 | tf_op jit(solution)/shard_map/all_to_all | solution.py:26
  52.9 24.4 %all-to-all-start.1 = ((bf16[64,2,1536]{2,1,0:T(2,128)(2,1)}), bf16[64,2,1536]{2,1,0:T(2,128)(2,1)S(1)}, u32[]{:S(2)}, u32[]{:S(2)}) async-start(bf16[64,2,1536]{2,1,0:T(2,128)(2,1)} %broadcast_select_fusion.1), calls=%async_computation.1 | async-start | bytes 786432 | tf_op jit(solution)/shard_map/all_to_all | solution.py:23
  58.7 24.2 %copy-start = (bf16[128,768]{1,0:T(8,128)(2,1)S(1)}, bf16[128,768]{1,0:T(8,128)(2,1)}, u32[]{:S(2)}) copy-start(bf16[128,768]{1,0:T(8,128)(2,1)} %param.7) | copy-start | bytes 589828
  77.3 38.7 %all-to-all-start.2 = ((bf16[64,2,1536]{2,1,0:T(2,128)(2,1)}), bf16[64,2,1536]{2,1,0:T(2,128)(2,1)S(1)}, u32[]{:S(2)}, u32[]{:S(2)}) async-start(bf16[64,2,1536]{2,1,0:T(2,128)(2,1)} %broadcast_select_fusion), calls=%async_computation.2 | async-start | bytes 786432 | tf_op jit(solution)/shard_map/all_to_all | solution.py:23
  82.9 213.6 %reduce-scatter.2.cloned.1.call-start = ((), (), s32[]{:S(2)}) async-start(), calls=%async_computation.5 | async-start | bytes 1769472 | tf_op jit(solution)/shard_map/reduce_scatter | solution.py:55
Sparse Core Ops, SparseCore 0:
  11.8 212.7 all-gather.1
  232.8 63.6 reduce-scatter.1
where the time goes:
time: 304 us; the launch traced here: 303 us
  waiting for transfers between devices  239 us (79%)
  starting transfers between devices  32.7 us (11%)
  between operations  13.5 us (4%)
  matrix products  8.76 us (3%)
  local copies, waits for them, and re-layouts  6.69 us (2%)
    all_gather x1, waiting for transfers between devices, body(): lax.all_gather(w_out, 'ctx', axis=1, tiled=True)  107 us
    reduce_scatter x1, waiting for transfers between devices, body(): lax.psum_scatter(partials.astype(jnp.bfloat16), 'head', scatter_dimension...  63.8 us
    all_to_all x2, waiting for transfers between devices, forward(): lax.all_to_all(chosen, 'ctx', split_axis=0, concat_axis=0, tiled=True)  48.8 us
    all_to_all x1, starting transfers between devices, body(): lax.all_to_all(stacked, 'ctx', split_axis=0, concat_axis=0, tiled=True)  21.3 us
    all_to_all x1, waiting for transfers between devices, body(): lax.all_to_all(stacked, 'ctx', split_axis=0, concat_axis=0, tiled=True)  19 us
    all_to_all x2, starting transfers between devices, forward(): lax.all_to_all(chosen, 'ctx', split_axis=0, concat_axis=0, tiled=True)  11.4 us
    dot_general x1, matrix products, body(): jnp.dot(attended, lax.all_gather(w_out, 'ctx', axis=1, tiled=True), prefe...  8.04 us
  transfers between devices with their start and end apart: 5, of which 5 were waited for; matrix products, arithmetic and copies ran while one was open for 3% of the time, Pallas kernels for 0%

commit v1 on v0

v1 whole, which is shorter than its diff:
```python
import jax
import jax.numpy as jnp
from jax import lax
from jax.experimental import pallas as pl
from jax.experimental.pallas import tpu as pltpu
from jax.sharding import Mesh, PartitionSpec as P

HEAD_DIM = 128
ROUNDS = 2
SIZES = (2, 4, 4, 2, 2, 4)
NAMES = ("zh", "x", "y", "c", "p", "q")
CTX = ("zh", "x", "y", "c")
HEAD = ("p", "q")
PLANE = ("x", "y", "c")
SWAP = ((0, 1), (1, 0))
QUAD = 4
PIECE = 8


def exchange_x_q(flip):
    place = lambda zh, x, q: (zh * QUAD + x) * QUAD + q
    return [
        (place(zh, x, q), place(zh ^ flip, q, x))
        for zh in range(2)
        for x in range(QUAD)
        for q in range(QUAD)
    ]


def project_kernel(order_ref, *refs):
    parts, (w_ref, out_ref, total) = refs[:QUAD], refs[QUAD:]
    step = pl.program_id(0)
    width = w_ref.shape[-1]

    @pl.when(step == 0)
    def _():
        total[...] = jnp.zeros_like(total)

    rows = w_ref[...].reshape(-1, width)
    for at, part in enumerate(parts):

        @pl.when(step == at)
        def _(part=part):
            total[...] += lax.dot_general(
                part[...], rows, (((1,), (1,)), ((), ())), preferred_element_type=jnp.float32
            )

    @pl.when(step == QUAD - 1)
    def _():
        out_ref[...] = total[...].astype(out_ref.dtype)


def project(order, parts, w_all, side, dtype):
    tokens, width = parts[0].shape
    _, chunks, _, columns, _ = w_all.shape
    whole = pl.BlockSpec((tokens, width), lambda k, order: (0, 0))
    return pl.pallas_call(
        project_kernel,
        grid_spec=pltpu.PrefetchScalarGridSpec(
            num_scalar_prefetch=1,
            grid=(QUAD,),
            in_specs=[whole] * QUAD
            + [
                pl.BlockSpec(
                    (None, chunks, None, columns, width),
                    lambda k, order: (order[k], 0, side, 0, 0),
                )
            ],
            out_specs=pl.BlockSpec((tokens, chunks * columns), lambda k, order: (0, 0)),
            scratch_shapes=[pltpu.VMEM((tokens, chunks * columns), jnp.float32)],
        ),
        out_shape=jax.ShapeDtypeStruct((tokens, chunks * columns), dtype),
        compiler_params=pltpu.CompilerParams(
            dimension_semantics=("arbitrary",), vmem_limit_bytes=32 << 20
        ),
        cost_estimate=pl.CostEstimate(
            flops=2 * QUAD * tokens * width * chunks * columns,
            bytes_accessed=2 * QUAD * width * (chunks * columns + tokens),
            transcendentals=0,
        ),
    )(order, *parts, w_all)


def body(queries, keys, values, plan, w_out):
    tokens, width = queries.shape
    heads = width // HEAD_DIM
    half = lax.axis_index("zh")
    quad, member = lax.axis_index("p"), lax.axis_index("q")
    seats = lax.axis_size(PLANE)
    pieces = tokens // PIECE

    own = jnp.stack((keys, values)).reshape(2 * pieces, PIECE, width)
    far = lax.ppermute(own, "zh", SWAP)

    w_rows = w_out.T
    w_near = lax.ppermute(w_rows, ("zh", "x", "q"), exchange_x_q(0))
    w_far = lax.ppermute(w_rows, ("zh", "x", "q"), exchange_x_q(1))
    keeps_near = half == quad
    w_pair = jnp.stack(
        (jnp.where(keeps_near, w_near, w_far), jnp.where(keeps_near, w_far, w_near))
    )
    w_all = lax.all_gather(w_pair, PLANE, axis=0, tiled=False)
    w_all = w_all.reshape(QUAD, seats // QUAD, 2, -1, width)

    both = jnp.stack((own, far), 1)
    spread = lax.all_to_all(both, PLANE, split_axis=0, concat_axis=0, tiled=True)
    spread = spread.reshape(2 * seats, PIECE, width)
    wanted = lax.dynamic_slice_in_dim(plan, half * seats, seats, 1)
    place = (wanted % seats) * 2 + (wanted // seats ^ half)
    chosen = spread.at[place.T].get(mode="promise_in_bounds")
    routed = lax.all_to_all(chosen, PLANE, split_axis=0, concat_axis=0, tiled=True)
    routed = routed.reshape(2, pieces, ROUNDS, PIECE, width).transpose(0, 2, 1, 3, 4)
    routed = routed.reshape(2, ROUNDS * tokens, width)

    key_rows = jnp.concatenate((keys, routed[0])).reshape(-1, heads, HEAD_DIM)
    value_rows = jnp.concatenate((values, routed[1])).reshape(-1, heads, HEAD_DIM)
    query_rows = queries.reshape(tokens, heads, HEAD_DIM)
    scores = jnp.einsum(
        "qhd,khd->hqk", query_rows, key_rows, preferred_element_type=jnp.float32
    ) * (1.0 / HEAD_DIM**0.5)
    exponent = jnp.exp(scores - jnp.max(scores, axis=-1, keepdims=True))
    row_total = jnp.sum(exponent, axis=-1)
    summed = jnp.einsum(
        "hqk,khd->qhd",
        exponent.astype(jnp.bfloat16),
        value_rows,
        preferred_element_type=jnp.float32,
    )
    attended = (summed / row_total.T[:, :, None]).astype(jnp.bfloat16).reshape(tokens, width)

    parts = [attended] + [
        lax.ppermute(attended, "q", [(i, i ^ k) for i in range(QUAD)]) for k in range(1, QUAD)
    ]
    order = member ^ jnp.arange(QUAD, dtype=jnp.int32)
    sent = project(order, parts, w_all, 1, jnp.bfloat16)
    arrived = lax.ppermute(sent, "p", SWAP)
    kept = project(order, parts, w_all, 0, jnp.float32)
    return (kept + arrived.astype(jnp.float32)).astype(jnp.bfloat16)


def solution(mesh):
    fine = Mesh(mesh.devices.reshape(SIZES), NAMES)
    return jax.shard_map(
        body,
        mesh=fine,
        in_specs=(P(CTX, HEAD), P(CTX, HEAD), P(CTX, HEAD), P(), P(HEAD, CTX)),
        out_specs=P(CTX, HEAD),
        check_vma=False,
    )
```

time: 304 us -> 225 us (0.74)
  waiting for transfers between devices: 239 us -> 144 us
  starting transfers between devices: 32.7 us -> 48.3 us
  matrix products: 8.76 us -> 0.65 us
  Pallas kernels: 0 us -> 6.94 us
    ppermute x0 -> x7, waiting for transfers between devices: none -> 113 us  [the longest x1 57.5 us: body(): w_far = lax.ppermute(w_rows, ('zh', 'x', 'q'), exchange_x_q(1))]
    all_gather x1, waiting for transfers between devices: 107 us -> 0.01 us  [body(): w_all = lax.all_gather(w_pair, PLANE, axis=0, tiled=False)]
    reduce_scatter x1 -> x0, waiting for transfers between devices: 63.8 us -> none  [body(): lax.psum_scatter(partials.astype(jnp.bfloat16), 'head', scatter_dimension...]
    all_to_all x3 -> x2, waiting for transfers between devices: 67.7 us -> 30.9 us  [the longest x1 19.2 us: body(): lax.all_to_all(chosen, PLANE, split_axis=0, concat_axis=0, tiled=True)]
    ppermute x0 -> x7, starting transfers between devices: none -> 34.7 us  [the longest x1 13.9 us: body(): w_far = lax.ppermute(w_rows, ('zh', 'x', 'q'), exchange_x_q(1))]
    all_to_all x3 -> x2, starting transfers between devices: 32.6 us -> 13.7 us  [the longest x1 7.48 us: body(): lax.all_to_all(both, PLANE, split_axis=0, concat_axis=0, tiled=True)]
    dot_general x2 -> x1, matrix products: 8.38 us -> 0.34 us  [body(): jnp.einsum('hqk,khd->qhd', exponent.astype(jnp.bfloat16), value_rows, pre...]
    pallas_call x0 -> x2, Pallas kernels: none -> 6.94 us  [project(): pl.pallas_call(project_kernel, grid_spec=pltpu.PrefetchScalarGridSpec(num...]
  transfers between devices with their start and end apart: 5 -> 10, of which waited for: 5 -> 7; matrix products, arithmetic and copies ran while one was open for 3% -> 3% of each run, Pallas kernels for 0% -> 2%
where the time goes in v1:
time: 225 us; the launch traced here: 223 us
  waiting for transfers between devices  144 us (64%)
  starting transfers between devices  48.3 us (21%)
  between operations  13.7 us (6%)
  local copies, waits for them, and re-layouts  7.55 us (3%)
  Pallas kernels  6.94 us (3%)
  other arithmetic  2.77 us (1%)
    ppermute x1, waiting for transfers between devices, body(): w_far = lax.ppermute(w_rows, ('zh', 'x', 'q'), exchange_x_q(1))  57.5 us
    ppermute x1, waiting for transfers between devices, body(): far = lax.ppermute(own, 'zh', SWAP)  25.7 us
    all_to_all x1, waiting for transfers between devices, body(): lax.all_to_all(chosen, PLANE, split_axis=0, concat_axis=0, tiled=True)  19.2 us
    ppermute x1, waiting for transfers between devices, body(): arrived = lax.ppermute(sent, 'p', SWAP)  18.7 us
    ppermute x1, starting transfers between devices, body(): w_far = lax.ppermute(w_rows, ('zh', 'x', 'q'), exchange_x_q(1))  13.9 us
    all_to_all x1, waiting for transfers between devices, body(): lax.all_to_all(both, PLANE, split_axis=0, concat_axis=0, tiled=True)  11.7 us
    ppermute x3, waiting for transfers between devices, body(): lax.ppermute(attended, 'q', [(i, i ^ k) for i in range(QUAD)])  10.8 us
    ppermute x3, starting transfers between devices, body(): lax.ppermute(attended, 'q', [(i, i ^ k) for i in range(QUAD)])  10.1 us
  transfers between devices with their start and end apart: 10, of which 7 were waited for; matrix products, arithmetic and copies ran while one was open for 3% of the time, Pallas kernels for 2%

profile of v1, /device:TPU:6, one launch (start us, length us, event | category | flops | bytes accessed | tf_op | source)
XLA Modules:
  0.0 223.5 jit_solution(12851670653593550560)
XLA Ops:
  6.5 0.0 copy-start.2
  6.5 0.0 all-gather.3.cloned.1.call-start
  6.5 6.6 %collective-permute-start.4 = (bf16[96,768]{1,0:T(8,128)(2,1)}, bf16[96,768]{1,0:T(8,128)(2,1)S(1)}, u32[]{:S(2)}, u32[]{:S(2)}) collective-permute-start(bf16[96,768]{1,0:T(8,128)(2,1)} %bitcast.50), channel_id=1, source_target_pairs={{0,0},{1,64},{2,128},{3,192},{64,1},{65,65},{66,129},{67,193},{128... | collective-permute-start | bytes 442376 | tf_op jit(solution)/shard_map/ppermute | solution.py:96
  13.1 13.9 %collective-permute-start.5 = (bf16[96,768]{1,0:T(8,128)(2,1)}, bf16[96,768]{1,0:T(8,128)(2,1)S(1)}, u32[]{:S(2)}, u32[]{:S(2)}) collective-permute-start(bf16[96,768]{1,0:T(8,128)(2,1)} %bitcast.51), channel_id=1, source_target_pairs={{0,256},{1,320},{2,384},{3,448},{64,257},{65,321},{66,385},{67,449... | collective-permute-start | bytes 442376 | tf_op jit(solution)/shard_map/ppermute | solution.py:97
  27.0 0.0 collective-permute-done.4
  27.0 57.5 %collective-permute-done.5 = bf16[96,768]{1,0:T(8,128)(2,1)S(1)} collective-permute-done((bf16[96,768]{1,0:T(8,128)(2,1)}, bf16[96,768]{1,0:T(8,128)(2,1)S(1)}, u32[]{:S(2)}, u32[]{:S(2)}) %collective-permute-start.5) | collective-permute-done | bytes 147488 | tf_op jit(solution)/shard_map/ppermute | solution.py:97
  84.6 0.8 pad_maximum_fusion.2
  85.3 0.0 all-gather.3.cloned.1.call-update
  85.4 0.0 copy-done.1
  85.4 0.0 copy-done.2
  85.4 2.2 collective-permute-start
  87.6 25.7 %collective-permute-done = bf16[32,8,768]{2,1,0:T(8,128)(2,1)S(1)} collective-permute-done((bf16[32,8,768]{2,1,0:T(8,128)(2,1)S(1)}, bf16[32,8,768]{2,1,0:T(8,128)(2,1)S(1)}, u32[]{:S(2)}, u32[]{:S(2)}) %collective-permute-start) | collective-permute-done | bytes 393248 | tf_op jit(solution)/shard_map/ppermute | solution.py:93
  113.3 1.0 pad_maximum_fusion
  114.3 7.5 %all-to-all-start = ((bf16[32,2,8,768]{3,2,1,0:T(8,128)(2,1)}), bf16[32,2,8,768]{3,2,1,0:T(8,128)(2,1)S(1)}, u32[]{:S(2)}, u32[]{:S(2)}) async-start(bf16[32,2,8,768]{3,2,1,0:T(8,128)(2,1)} %pad_maximum_fusion), calls=%async_computation | async-start | bytes 1572864 | tf_op jit(solution)/shard_map/all_to_all | solution.py:106
  121.8 0.0 copy-done.4
  121.8 0.1 compare_select_fusion
  121.9 0.1 copy.28
  121.9 0.1 reshape.41
  122.1 11.7 %all-to-all-done = bf16[32,2,8,768]{3,2,1,0:T(8,128)(2,1)S(1)} async-done(((bf16[32,2,8,768]{3,2,1,0:T(8,128)(2,1)}), bf16[32,2,8,768]{3,2,1,0:T(8,128)(2,1)S(1)}, u32[]{:S(2)}, u32[]{:S(2)}) %all-to-all-start) | async-done | bytes 786464 | tf_op jit(solution)/shard_map/all_to_all | solution.py:106
  133.8 1.5 gather_fusion
  135.3 6.2 %all-to-all-start.1 = ((bf16[32,2,8,768]{3,2,1,0:T(8,128)(2,1)}), bf16[32,2,8,768]{3,2,1,0:T(8,128)(2,1)S(1)}, u32[]{:S(2)}, u32[]{:S(2)}) async-start(bf16[32,2,8,768]{3,2,1,0:T(8,128)(2,1)} %bitcast.8), calls=%async_computation.1 | async-start | bytes 1572864 | tf_op jit(solution)/shard_map/all_to_all | solution.py:111
  141.4 0.2 copy.31
  141.6 0.2 copy.27
  141.8 0.2 copy.33
  142.0 0.0 copy-done.3
  142.0 0.2 copy.35
  142.1 19.2 %all-to-all-done.1 = bf16[32,2,8,768]{3,2,1,0:T(8,128)(2,1)S(1)} async-done(((bf16[32,2,8,768]{3,2,1,0:T(8,128)(2,1)}), bf16[32,2,8,768]{3,2,1,0:T(8,128)(2,1)S(1)}, u32[]{:S(2)}, u32[]{:S(2)}) %all-to-all-start.1) | async-done | bytes 786464 | tf_op jit(solution)/shard_map/all_to_all | solution.py:111
  161.4 0.1 fusion.17
  161.5 0.5 concatenate.20
  161.9 0.1 copy.34
  162.0 0.5 concatenate.17
  162.5 0.3 copy.30
  162.8 0.3 fusion.18
  163.1 0.2 fusion.3
  163.3 0.3 fusion.2
  163.6 0.1 copy.41.refs_0_
  163.8 1.9 collective-permute-start.1
  165.7 4.3 %collective-permute-start.2 = (bf16[128,768]{1,0:T(8,128)(2,1)S(1)}, bf16[128,768]{1,0:T(8,128)(2,1)S(1)}, u32[]{:S(2)}, u32[]{:S(2)}) collective-permute-start(bf16[128,768]{1,0:T(8,128)(2,1)S(1)} %copy.41.refs_0_), channel_id=1, source_target_pairs={{0,2},{1,3},{2,0},{3,1},{4,6},{5,7},{6,4},{7,5},{8,10},{9,11},{10,... | collective-permute-start | bytes 589832 | tf_op jit(solution)/shard_map/ppermute | solution.py:132
  170.0 3.9 %collective-permute-start.3 = (bf16[128,768]{1,0:T(8,128)(2,1)S(1)}, bf16[128,768]{1,0:T(8,128)(2,1)S(1)}, u32[]{:S(2)}, u32[]{:S(2)}) collective-permute-start(bf16[128,768]{1,0:T(8,128)(2,1)S(1)} %copy.41.refs_0_), channel_id=1, source_target_pairs={{0,3},{1,2},{2,1},{3,0},{4,7},{5,6},{6,5},{7,4},{8,11},{9,10},{10,... | collective-permute-start | bytes 589832 | tf_op jit(solution)/shard_map/ppermute | solution.py:132
  173.9 0.4 collective-permute-done.1.refs_1_
  174.3 10.4 %collective-permute-done.2.refs_2_ = bf16[128,768]{1,0:T(8,128)(2,1)S(1)} collective-permute-done((bf16[128,768]{1,0:T(8,128)(2,1)S(1)}, bf16[128,768]{1,0:T(8,128)(2,1)S(1)}, u32[]{:S(2)}, u32[]{:S(2)}) %collective-permute-start.2) | collective-permute-done | bytes 196640 | tf_op jit(solution)/shard_map/ppermute | solution.py:132
  184.7 0.0 collective-permute-done.3.refs_3_
  184.7 3.7 %copy-done = bf16[64,96,768]{2,1,0:T(8,128)(2,1)S(1)} copy-done((bf16[64,96,768]{2,1,0:T(8,128)(2,1)S(1)}, bf16[64,96,768]{2,1,0:T(8,128)(2,1)}, u32[]{:S(2)}) %copy-start) | copy-done | bytes 9437208
  188.4 3.5 %shard_map.56 = bf16[128,768]{1,0:T(8,128)(2,1)S(1)} custom-call(s32[4]{0:T(128)S(1)} %iota_xor_fusion.order_ref, bf16[128,768]{1,0:T(8,128)(2,1)S(1)} %copy.41.refs_0_, bf16[128,768]{1,0:T(8,128)(2,1)S(1)} %collective-permute-done.1.refs_1_, bf16[128,768]{1,0:T(8,128)(2,1)S(1)} %collective-permute-done.2.refs_2_, ...), custom_call_target="tpu_custom_call" | custom-call | flops 603979776 | bytes 5505024 | tf_op jit(solution)/shard_map/pallas_call | solution.py:57
  191.9 1.9 collective-permute-start.6
  193.8 3.5 %shard_map.55 = f32[128,768]{1,0:T(8,128)S(1)} custom-call(s32[4]{0:T(128)S(1)} %iota_xor_fusion.order_ref, bf16[128,768]{1,0:T(8,128)(2,1)S(1)} %copy.41.refs_0_, bf16[128,768]{1,0:T(8,128)(2,1)S(1)} %collective-permute-done.1.refs_1_, bf16[128,768]{1,0:T(8,128)(2,1)S(1)} %collective-permute-done.2.refs_2_, ...), custom_call_target="tpu_custom_call" | custom-call | flops 603979776 | bytes 5505024 | tf_op jit(solution)/shard_map/pallas_call | solution.py:57
  197.3 18.7 %collective-permute-done.6 = bf16[128,768]{1,0:T(8,128)(2,1)S(1)} collective-permute-done((bf16[128,768]{1,0:T(8,128)(2,1)S(1)}, bf16[128,768]{1,0:T(8,128)(2,1)S(1)}, u32[]{:S(2)}, u32[]{:S(2)}) %collective-permute-start.6) | collective-permute-done | bytes 196640 | tf_op jit(solution)/shard_map/ppermute | solution.py:136
  215.9 0.7 add_convert_fusion
  (11 shorter events, 0.1 us)
Async XLA Ops:
  6.5 78.8 %copy-start.1 = (bf16[128,768]{1,0:T(8,128)(2,1)S(1)}, bf16[128,768]{1,0:T(8,128)(2,1)}, u32[]{:S(2)}) copy-start(bf16[128,768]{1,0:T(8,128)(2,1)} %param.6) | copy-start | bytes 589828
  6.5 78.8 %copy-start.2 = (bf16[128,768]{1,0:T(8,128)(2,1)S(1)}, bf16[128,768]{1,0:T(8,128)(2,1)}, u32[]{:S(2)}) copy-start(bf16[128,768]{1,0:T(8,128)(2,1)} %param.7) | copy-start | bytes 589828
  6.5 178.2 %all-gather.3.cloned.1.call-start = ((), (), s32[]{:S(2)}) async-start(), calls=%async_computation.2 | async-start | bytes 9732096 | tf_op jit(solution)/shard_map/all_gather | solution.py:102
  6.5 20.4 %collective-permute-start.4 = (bf16[96,768]{1,0:T(8,128)(2,1)}, bf16[96,768]{1,0:T(8,128)(2,1)S(1)}, u32[]{:S(2)}, u32[]{:S(2)}) collective-permute-start(bf16[96,768]{1,0:T(8,128)(2,1)} %bitcast.50), channel_id=1, source_target_pairs={{0,0},{1,64},{2,128},{3,192},{64,1},{65,65},{66,129},{67,193},{128... | collective-permute-start | bytes 442376 | tf_op jit(solution)/shard_map/ppermute | solution.py:96
  13.1 71.4 %collective-permute-start.5 = (bf16[96,768]{1,0:T(8,128)(2,1)}, bf16[96,768]{1,0:T(8,128)(2,1)S(1)}, u32[]{:S(2)}, u32[]{:S(2)}) collective-permute-start(bf16[96,768]{1,0:T(8,128)(2,1)} %bitcast.51), channel_id=1, source_target_pairs={{0,256},{1,320},{2,384},{3,448},{64,257},{65,321},{66,385},{67,449... | collective-permute-start | bytes 442376 | tf_op jit(solution)/shard_map/ppermute | solution.py:97
  85.4 27.9 %collective-permute-start = (bf16[32,8,768]{2,1,0:T(8,128)(2,1)S(1)}, bf16[32,8,768]{2,1,0:T(8,128)(2,1)S(1)}, u32[]{:S(2)}, u32[]{:S(2)}) collective-permute-start(bf16[32,8,768]{2,1,0:T(8,128)(2,1)S(1)} %bitcast.40), channel_id=1, source_target_pairs={{0,256},{256,0},{1,257},{257,1},{2,258},{258,2},{3,259},{259,3},{4... | collective-permute-start | bytes 1179656 | tf_op jit(solution)/shard_map/ppermute | solution.py:93
  114.3 7.5 %copy-start.4 = (s32[2,64]{1,0:T(2,128)S(1)}, s32[2,64]{1,0:T(2,128)}, u32[]{:S(2)}) copy-start(s32[2,64]{1,0:T(2,128)} %param.8) | copy-start | bytes 1540
  114.3 19.5 %all-to-all-start = ((bf16[32,2,8,768]{3,2,1,0:T(8,128)(2,1)}), bf16[32,2,8,768]{3,2,1,0:T(8,128)(2,1)S(1)}, u32[]{:S(2)}, u32[]{:S(2)}) async-start(bf16[32,2,8,768]{3,2,1,0:T(8,128)(2,1)} %pad_maximum_fusion), calls=%async_computation | async-start | bytes 1572864 | tf_op jit(solution)/shard_map/all_to_all | solution.py:106
  135.3 6.7 %copy-start.3 = (bf16[128,768]{1,0:T(8,128)(2,1)S(1)}, bf16[128,768]{1,0:T(8,128)(2,1)}, u32[]{:S(2)}) copy-start(bf16[128,768]{1,0:T(8,128)(2,1)} %param.5) | copy-start | bytes 589828
  135.3 26.1 %all-to-all-start.1 = ((bf16[32,2,8,768]{3,2,1,0:T(8,128)(2,1)}), bf16[32,2,8,768]{3,2,1,0:T(8,128)(2,1)S(1)}, u32[]{:S(2)}, u32[]{:S(2)}) async-start(bf16[32,2,8,768]{3,2,1,0:T(8,128)(2,1)} %bitcast.8), calls=%async_computation.1 | async-start | bytes 1572864 | tf_op jit(solution)/shard_map/all_to_all | solution.py:111
  163.8 10.5 %collective-permute-start.1 = (bf16[128,768]{1,0:T(8,128)(2,1)S(1)}, bf16[128,768]{1,0:T(8,128)(2,1)S(1)}, u32[]{:S(2)}, u32[]{:S(2)}) collective-permute-start(bf16[128,768]{1,0:T(8,128)(2,1)S(1)} %copy.41.refs_0_), channel_id=1, source_target_pairs={{0,1},{1,0},{2,3},{3,2},{4,5},{5,4},{6,7},{7,6},{8,9},{9,8},{10,11... | collective-permute-start | bytes 589832 | tf_op jit(solution)/shard_map/ppermute | solution.py:132
  165.7 19.0 %collective-permute-start.2 = (bf16[128,768]{1,0:T(8,128)(2,1)S(1)}, bf16[128,768]{1,0:T(8,128)(2,1)S(1)}, u32[]{:S(2)}, u32[]{:S(2)}) collective-permute-start(bf16[128,768]{1,0:T(8,128)(2,1)S(1)} %copy.41.refs_0_), channel_id=1, source_target_pairs={{0,2},{1,3},{2,0},{3,1},{4,6},{5,7},{6,4},{7,5},{8,10},{9,11},{10,... | collective-permute-start | bytes 589832 | tf_op jit(solution)/shard_map/ppermute | solution.py:132
  170.0 14.7 %collective-permute-start.3 = (bf16[128,768]{1,0:T(8,128)(2,1)S(1)}, bf16[128,768]{1,0:T(8,128)(2,1)S(1)}, u32[]{:S(2)}, u32[]{:S(2)}) collective-permute-start(bf16[128,768]{1,0:T(8,128)(2,1)S(1)} %copy.41.refs_0_), channel_id=1, source_target_pairs={{0,3},{1,2},{2,1},{3,0},{4,7},{5,6},{6,5},{7,4},{8,11},{9,10},{10,... | collective-permute-start | bytes 589832 | tf_op jit(solution)/shard_map/ppermute | solution.py:132
  184.7 3.7 %copy-start = (bf16[64,96,768]{2,1,0:T(8,128)(2,1)S(1)}, bf16[64,96,768]{2,1,0:T(8,128)(2,1)}, u32[]{:S(2)}) copy-start(bf16[64,96,768]{2,1,0:T(8,128)(2,1)} %all-gather.3.cloned.1.call-done) | copy-start | bytes 28311556
  191.9 24.1 %collective-permute-start.6 = (bf16[128,768]{1,0:T(8,128)(2,1)S(1)}, bf16[128,768]{1,0:T(8,128)(2,1)S(1)}, u32[]{:S(2)}, u32[]{:S(2)}) collective-permute-start(bf16[128,768]{1,0:T(8,128)(2,1)S(1)} %shard_map.56), channel_id=1, source_target_pairs={{0,4},{4,0},{1,5},{5,1},{2,6},{6,2},{3,7},{7,3},{8,12},{12,8},{9,1... | collective-permute-start | bytes 589832 | tf_op jit(solution)/shard_map/ppermute | solution.py:136
Sparse Core Ops, SparseCore 0:
  85.5 82.7 all-gather.2

commit v2 on v1

--- a/solution.py
+++ b/solution.py
@@ -71,7 +71,7 @@
         ),
         out_shape=jax.ShapeDtypeStruct((tokens, chunks * columns), dtype),
         compiler_params=pltpu.CompilerParams(
-            dimension_semantics=("arbitrary",), vmem_limit_bytes=32 << 20
+            dimension_semantics=("arbitrary",), vmem_limit_bytes=56 << 20
         ),
         cost_estimate=pl.CostEstimate(
             flops=2 * QUAD * tokens * width * chunks * columns,
@@ -89,9 +89,6 @@
     seats = lax.axis_size(PLANE)
     pieces = tokens // PIECE
 
-    own = jnp.stack((keys, values)).reshape(2 * pieces, PIECE, width)
-    far = lax.ppermute(own, "zh", SWAP)
-
     w_rows = w_out.T
     w_near = lax.ppermute(w_rows, ("zh", "x", "q"), exchange_x_q(0))
     w_far = lax.ppermute(w_rows, ("zh", "x", "q"), exchange_x_q(1))
@@ -99,15 +96,18 @@
     w_pair = jnp.stack(
         (jnp.where(keeps_near, w_near, w_far), jnp.where(keeps_near, w_far, w_near))
     )
+
+    own = jnp.stack((keys, values)).reshape(2 * pieces, PIECE, width)
+    spread = lax.all_to_all(own, PLANE, split_axis=0, concat_axis=0, tiled=True)
+    spread, w_pair = lax.optimization_barrier((spread, w_pair))
+    far = lax.ppermute(spread, "zh", SWAP)
+
     w_all = lax.all_gather(w_pair, PLANE, axis=0, tiled=False)
     w_all = w_all.reshape(QUAD, seats // QUAD, 2, -1, width)
 
-    both = jnp.stack((own, far), 1)
-    spread = lax.all_to_all(both, PLANE, split_axis=0, concat_axis=0, tiled=True)
-    spread = spread.reshape(2 * seats, PIECE, width)
     wanted = lax.dynamic_slice_in_dim(plan, half * seats, seats, 1)
-    place = (wanted % seats) * 2 + (wanted // seats ^ half)
-    chosen = spread.at[place.T].get(mode="promise_in_bounds")
+    place = (wanted // seats ^ half) * seats + wanted % seats
+    chosen = jnp.concatenate((spread, far)).at[place.T].get(mode="promise_in_bounds")
     routed = lax.all_to_all(chosen, PLANE, split_axis=0, concat_axis=0, tiled=True)
     routed = routed.reshape(2, pieces, ROUNDS, PIECE, width).transpose(0, 2, 1, 3, 4)
     routed = routed.reshape(2, ROUNDS * tokens, width)

time: 225 us -> 200 us (0.89)
  waiting for transfers between devices: 144 us -> 101 us
  starting transfers between devices: 48.3 us -> 61.7 us
  Pallas kernels: 6.94 us -> 12.4 us
  local copies, waits for them, and re-layouts: 7.55 us -> 3.87 us
  other arithmetic: 2.77 us -> 5.2 us
    ppermute x1, waiting for transfers between devices: 57.5 us -> 43.5 us  [body(): w_far = lax.ppermute(w_rows, ('zh', 'x', 'q'), exchange_x_q(1))]
    all_to_all x1, waiting for transfers between devices: 11.7 us -> 0.01 us  [body(): spread = lax.all_to_all(own, PLANE, split_axis=0, concat_axis=0, tiled=True)]
    all_to_all x1, waiting for transfers between devices: 19.2 us -> 11.3 us  [body(): lax.all_to_all(chosen, PLANE, split_axis=0, concat_axis=0, tiled=True)]
    ppermute x1, waiting for transfers between devices: 18.7 us -> 12 us  [body(): arrived = lax.ppermute(sent, 'p', SWAP)]
    ppermute x1, waiting for transfers between devices: 25.7 us -> 19.3 us  [body(): far = lax.ppermute(spread, 'zh', SWAP)]
    ppermute x3, starting transfers between devices: 10.1 us -> 15.9 us  [body(): lax.ppermute(attended, 'q', [(i, i ^ k) for i in range(QUAD)])]
    ppermute x1, starting transfers between devices: 1.92 us -> 7.63 us  [body(): arrived = lax.ppermute(sent, 'p', SWAP)]
    pallas_call x2, Pallas kernels: 6.94 us -> 12.4 us  [project(): pl.pallas_call(project_kernel, grid_spec=pltpu.PrefetchScalarGridSpec(num...]
  transfers between devices with their start and end apart: 10 -> 10, of which waited for: 7 -> 6; matrix products, arithmetic and copies ran while one was open for 3% -> 4% of each run, Pallas kernels for 2% -> 3%
where the time goes in v2:
time: 200 us; the launch traced here: 199 us
  waiting for transfers between devices  101 us (50%)
  starting transfers between devices  61.7 us (31%)
  between operations  13.6 us (7%)
  Pallas kernels  12.4 us (6%)
  other arithmetic  5.2 us (3%)
  local copies, waits for them, and re-layouts  3.87 us (2%)
    ppermute x1, waiting for transfers between devices, body(): w_far = lax.ppermute(w_rows, ('zh', 'x', 'q'), exchange_x_q(1))  43.5 us
    ppermute x1, waiting for transfers between devices, body(): far = lax.ppermute(spread, 'zh', SWAP)  19.3 us
    ppermute x3, starting transfers between devices, body(): lax.ppermute(attended, 'q', [(i, i ^ k) for i in range(QUAD)])  15.9 us
    ppermute x1, starting transfers between devices, body(): w_far = lax.ppermute(w_rows, ('zh', 'x', 'q'), exchange_x_q(1))  13.9 us
    pallas_call x2, Pallas kernels, project(): pl.pallas_call(project_kernel, grid_spec=pltpu.PrefetchScalarGridSpec(num...  12.4 us
    ppermute x1, waiting for transfers between devices, body(): arrived = lax.ppermute(sent, 'p', SWAP)  12 us
    ppermute x3, waiting for transfers between devices, body(): lax.ppermute(attended, 'q', [(i, i ^ k) for i in range(QUAD)])  11.6 us
    all_to_all x1, waiting for transfers between devices, body(): lax.all_to_all(chosen, PLANE, split_axis=0, concat_axis=0, tiled=True)  11.3 us
  transfers between devices with their start and end apart: 10, of which 6 were waited for; matrix products, arithmetic and copies ran while one was open for 4% of the time, Pallas kernels for 3%

profile of v2, /device:TPU:6, one launch (start us, length us, event | category | flops | bytes accessed | tf_op | source)
XLA Modules:
  0.0 198.9 jit_solution(7934957100294173019)
XLA Ops:
  6.5 6.4 %collective-permute-start = (bf16[96,768]{1,0:T(8,128)(2,1)}, bf16[96,768]{1,0:T(8,128)(2,1)S(1)}, u32[]{:S(2)}, u32[]{:S(2)}) collective-permute-start(bf16[96,768]{1,0:T(8,128)(2,1)} %bitcast.43), channel_id=1, source_target_pairs={{0,0},{1,64},{2,128},{3,192},{64,1},{65,65},{66,129},{67,193},{128... | collective-permute-start | bytes 442376 | tf_op jit(solution)/shard_map/ppermute | solution.py:93
  13.0 13.9 %collective-permute-start.1 = (bf16[96,768]{1,0:T(8,128)(2,1)}, bf16[96,768]{1,0:T(8,128)(2,1)S(1)}, u32[]{:S(2)}, u32[]{:S(2)}) collective-permute-start(bf16[96,768]{1,0:T(8,128)(2,1)} %bitcast.44), channel_id=1, source_target_pairs={{0,256},{1,320},{2,384},{3,448},{64,257},{65,321},{66,385},{67,449... | collective-permute-start | bytes 442376 | tf_op jit(solution)/shard_map/ppermute | solution.py:94
  26.8 1.8 pad_maximum_fusion.1
  28.6 8.0 %all-to-all-start = ((bf16[32,8,768]{2,1,0:T(8,128)(2,1)}), bf16[32,8,768]{2,1,0:T(8,128)(2,1)S(1)}, u32[]{:S(2)}, u32[]{:S(2)}) async-start(bf16[32,8,768]{2,1,0:T(8,128)(2,1)} %bitcast.3), calls=%async_computation | async-start | bytes 786432 | tf_op jit(solution)/shard_map/all_to_all | solution.py:101
  36.7 0.0 all-gather.3.cloned.1.call-start
  36.7 0.0 collective-permute-done
  36.8 43.5 %collective-permute-done.1 = bf16[96,768]{1,0:T(8,128)(2,1)S(1)} collective-permute-done((bf16[96,768]{1,0:T(8,128)(2,1)}, bf16[96,768]{1,0:T(8,128)(2,1)S(1)}, u32[]{:S(2)}, u32[]{:S(2)}) %collective-permute-start.1) | collective-permute-done | bytes 147488 | tf_op jit(solution)/shard_map/ppermute | solution.py:94
  80.2 0.8 pad_maximum_fusion.2
  81.0 0.0 all-to-all-done
  81.0 0.0 all-gather.3.cloned.1.call-update
  81.0 1.9 collective-permute-start.2
  83.0 0.1 compare_select_fusion
  83.0 0.1 copy.28
  83.1 0.1 reshape.37
  83.3 19.3 %collective-permute-done.2 = bf16[32,8,768]{2,1,0:T(8,128)(2,1)S(1)} collective-permute-done((bf16[32,8,768]{2,1,0:T(8,128)(2,1)S(1)}, bf16[32,8,768]{2,1,0:T(8,128)(2,1)S(1)}, u32[]{:S(2)}, u32[]{:S(2)}) %collective-permute-start.2) | collective-permute-done | bytes 393248 | tf_op jit(solution)/shard_map/ppermute | solution.py:103
  102.5 0.1 pad_maximum_fusion
  102.6 1.5 gather_fusion
  104.1 8.0 %all-to-all-start.1 = ((bf16[32,2,8,768]{3,2,1,0:T(8,128)(2,1)}), bf16[32,2,8,768]{3,2,1,0:T(8,128)(2,1)S(1)}, u32[]{:S(2)}, u32[]{:S(2)}) async-start(bf16[32,2,8,768]{3,2,1,0:T(8,128)(2,1)} %bitcast.8), calls=%async_computation.1 | async-start | bytes 1572864 | tf_op jit(solution)/shard_map/all_to_all | solution.py:111
  112.0 0.0 copy-done.1
  112.1 0.2 copy.31
  112.2 0.2 copy.27
  112.4 0.2 copy.33
  112.6 0.2 copy.35
  112.8 11.3 %all-to-all-done.1 = bf16[32,2,8,768]{3,2,1,0:T(8,128)(2,1)S(1)} async-done(((bf16[32,2,8,768]{3,2,1,0:T(8,128)(2,1)}), bf16[32,2,8,768]{3,2,1,0:T(8,128)(2,1)S(1)}, u32[]{:S(2)}, u32[]{:S(2)}) %all-to-all-start.1) | async-done | bytes 786464 | tf_op jit(solution)/shard_map/all_to_all | solution.py:111
  124.1 0.1 fusion.16
  124.1 0.5 concatenate.24
  124.6 0.1 copy.34
  124.7 0.5 concatenate.21
  125.2 0.3 copy.30
  125.5 0.3 fusion.17
  125.8 0.2 fusion.3
  126.0 0.3 fusion.2
  126.3 0.1 copy.41.refs_0_
  126.5 0.0 copy-start
  126.5 1.9 collective-permute-start.3
  128.4 12.0 %collective-permute-start.4 = (bf16[128,768]{1,0:T(8,128)(2,1)S(1)}, bf16[128,768]{1,0:T(8,128)(2,1)S(1)}, u32[]{:S(2)}, u32[]{:S(2)}) collective-permute-start(bf16[128,768]{1,0:T(8,128)(2,1)S(1)} %copy.41.refs_0_), channel_id=1, source_target_pairs={{0,2},{1,3},{2,0},{3,1},{4,6},{5,7},{6,4},{7,5},{8,10},{9,11},{10,... | collective-permute-start | bytes 589832 | tf_op jit(solution)/shard_map/ppermute | solution.py:132
  140.4 1.9 collective-permute-start.5
  142.4 0.6 iota_xor_fusion.order_ref
  142.9 0.0 collective-permute-done.3.refs_1_
  142.9 11.6 %collective-permute-done.4.refs_2_ = bf16[128,768]{1,0:T(8,128)(2,1)S(1)} collective-permute-done((bf16[128,768]{1,0:T(8,128)(2,1)S(1)}, bf16[128,768]{1,0:T(8,128)(2,1)S(1)}, u32[]{:S(2)}, u32[]{:S(2)}) %collective-permute-start.4) | collective-permute-done | bytes 196640 | tf_op jit(solution)/shard_map/ppermute | solution.py:132
  154.5 0.0 collective-permute-done.5.refs_3_
  154.5 3.8 %all-gather.3.cloned.1.call-done = bf16[64,96,768]{2,1,0:T(8,128)(2,1)} async-done(((bf16[2,96,768]{2,1,0:T(8,128)(2,1)}), bf16[64,96,768]{2,1,0:T(8,128)(2,1)}) %all-gather.3.cloned.1.call-update) | async-done | bytes 9437200 | tf_op jit(solution)/shard_map/all_gather | solution.py:105
  158.4 0.0 copy-done.5
  158.4 6.1 %shard_map.56 = bf16[128,768]{1,0:T(8,128)(2,1)} custom-call(s32[4]{0:T(128)} %iota_xor_fusion.order_ref, bf16[128,768]{1,0:T(8,128)(2,1)} %copy-done, bf16[128,768]{1,0:T(8,128)(2,1)} %copy-done.3, bf16[128,768]{1,0:T(8,128)(2,1)} %copy-done.4, bf16[128,768]{1,0:T(8,128)(2,1)} %copy-done.5, bf16[4,8,2,96,768]{4,3,2,1,0:T(8,128)(2,1)} %bitcast.33), custom_call_target="tpu_custom_call" | custom-call | flops 603979776 | bytes 5505024 | tf_op jit(solution)/shard_map/pallas_call | solution.py:57
  164.5 7.6 %collective-permute-start.6 = (bf16[128,768]{1,0:T(8,128)(2,1)}, bf16[128,768]{1,0:T(8,128)(2,1)S(1)}, u32[]{:S(2)}, u32[]{:S(2)}) collective-permute-start(bf16[128,768]{1,0:T(8,128)(2,1)} %shard_map.56), channel_id=1, source_target_pairs={{0,4},{4,0},{1,5},{5,1},{2,6},{6,2},{3,7},{7,3},{8,12},{12,8},{9,1... | collective-permute-start | bytes 589832 | tf_op jit(solution)/shard_map/ppermute | solution.py:136
  172.1 6.2 %shard_map.55 = f32[128,768]{1,0:T(8,128)} custom-call(s32[4]{0:T(128)} %iota_xor_fusion.order_ref, bf16[128,768]{1,0:T(8,128)(2,1)} %copy-done, bf16[128,768]{1,0:T(8,128)(2,1)} %copy-done.3, bf16[128,768]{1,0:T(8,128)(2,1)} %copy-done.4, bf16[128,768]{1,0:T(8,128)(2,1)} %copy-done.5, bf16[4,8,2,96,768]{4,3,2,1,0:T(8,128)(2,1)} %bitcast.34), custom_call_target="tpu_custom_call" | custom-call | flops 603979776 | bytes 5505024 | tf_op jit(solution)/shard_map/pallas_call | solution.py:57
  178.4 12.0 %collective-permute-done.6 = bf16[128,768]{1,0:T(8,128)(2,1)S(1)} collective-permute-done((bf16[128,768]{1,0:T(8,128)(2,1)}, bf16[128,768]{1,0:T(8,128)(2,1)S(1)}, u32[]{:S(2)}, u32[]{:S(2)}) %collective-permute-start.6) | collective-permute-done | bytes 196640 | tf_op jit(solution)/shard_map/ppermute | solution.py:136
  190.3 1.7 add_convert_fusion
  (17 shorter events, 0.1 us)
Async XLA Ops:
  6.5 30.2 %collective-permute-start = (bf16[96,768]{1,0:T(8,128)(2,1)}, bf16[96,768]{1,0:T(8,128)(2,1)S(1)}, u32[]{:S(2)}, u32[]{:S(2)}) collective-permute-start(bf16[96,768]{1,0:T(8,128)(2,1)} %bitcast.43), channel_id=1, source_target_pairs={{0,0},{1,64},{2,128},{3,192},{64,1},{65,65},{66,129},{67,193},{128... | collective-permute-start | bytes 442376 | tf_op jit(solution)/shard_map/ppermute | solution.py:93
  13.0 67.2 %collective-permute-start.1 = (bf16[96,768]{1,0:T(8,128)(2,1)}, bf16[96,768]{1,0:T(8,128)(2,1)S(1)}, u32[]{:S(2)}, u32[]{:S(2)}) collective-permute-start(bf16[96,768]{1,0:T(8,128)(2,1)} %bitcast.44), channel_id=1, source_target_pairs={{0,256},{1,320},{2,384},{3,448},{64,257},{65,321},{66,385},{67,449... | collective-permute-start | bytes 442376 | tf_op jit(solution)/shard_map/ppermute | solution.py:94
  28.6 54.3 %copy-start.7 = (s32[2,64]{1,0:T(2,128)S(1)}, s32[2,64]{1,0:T(2,128)}, u32[]{:S(2)}) copy-start(s32[2,64]{1,0:T(2,128)} %param.8) | copy-start | bytes 1540
  28.6 52.3 %all-to-all-start = ((bf16[32,8,768]{2,1,0:T(8,128)(2,1)}), bf16[32,8,768]{2,1,0:T(8,128)(2,1)S(1)}, u32[]{:S(2)}, u32[]{:S(2)}) async-start(bf16[32,8,768]{2,1,0:T(8,128)(2,1)} %bitcast.3), calls=%async_computation | async-start | bytes 786432 | tf_op jit(solution)/shard_map/all_to_all | solution.py:101
  36.7 121.7 %all-gather.3.cloned.1.call-start = ((), (), s32[]{:S(2)}) async-start(), calls=%async_computation.2 | async-start | bytes 9732096 | tf_op jit(solution)/shard_map/all_gather | solution.py:105
  81.0 21.5 %collective-permute-start.2 = (bf16[32,8,768]{2,1,0:T(8,128)(2,1)S(1)}, bf16[32,8,768]{2,1,0:T(8,128)(2,1)S(1)}, u32[]{:S(2)}, u32[]{:S(2)}) collective-permute-start(bf16[32,8,768]{2,1,0:T(8,128)(2,1)S(1)} %all-to-all-done), channel_id=1, source_target_pairs={{0,256},{256,0},{1,257},{257,1},{2,258},{258,2},{3,259},{259,3},{4... | collective-permute-start | bytes 1179656 | tf_op jit(solution)/shard_map/ppermute | solution.py:103
  104.1 8.0 %copy-start.1 = (bf16[128,768]{1,0:T(8,128)(2,1)S(1)}, bf16[128,768]{1,0:T(8,128)(2,1)}, u32[]{:S(2)}) copy-start(bf16[128,768]{1,0:T(8,128)(2,1)} %param.6) | copy-start | bytes 589828
  104.1 8.2 %copy-start.2 = (bf16[128,768]{1,0:T(8,128)(2,1)S(1)}, bf16[128,768]{1,0:T(8,128)(2,1)}, u32[]{:S(2)}) copy-start(bf16[128,768]{1,0:T(8,128)(2,1)} %param.7) | copy-start | bytes 589828
  104.1 8.5 %copy-start.6 = (bf16[128,768]{1,0:T(8,128)(2,1)S(1)}, bf16[128,768]{1,0:T(8,128)(2,1)}, u32[]{:S(2)}) copy-start(bf16[128,768]{1,0:T(8,128)(2,1)} %param.5) | copy-start | bytes 589828
  104.1 20.0 %all-to-all-start.1 = ((bf16[32,2,8,768]{3,2,1,0:T(8,128)(2,1)}), bf16[32,2,8,768]{3,2,1,0:T(8,128)(2,1)S(1)}, u32[]{:S(2)}, u32[]{:S(2)}) async-start(bf16[32,2,8,768]{3,2,1,0:T(8,128)(2,1)} %bitcast.8), calls=%async_computation.1 | async-start | bytes 1572864 | tf_op jit(solution)/shard_map/all_to_all | solution.py:111
  126.5 31.9 %copy-start = (bf16[128,768]{1,0:T(8,128)(2,1)}, bf16[128,768]{1,0:T(8,128)(2,1)S(1)}, u32[]{:S(2)}) copy-start(bf16[128,768]{1,0:T(8,128)(2,1)S(1)} %copy.41.refs_0_) | copy-start | bytes 589828
  126.5 16.5 %collective-permute-start.3 = (bf16[128,768]{1,0:T(8,128)(2,1)S(1)}, bf16[128,768]{1,0:T(8,128)(2,1)S(1)}, u32[]{:S(2)}, u32[]{:S(2)}) collective-permute-start(bf16[128,768]{1,0:T(8,128)(2,1)S(1)} %copy.41.refs_0_), channel_id=1, source_target_pairs={{0,1},{1,0},{2,3},{3,2},{4,5},{5,4},{6,7},{7,6},{8,9},{9,8},{10,11... | collective-permute-start | bytes 589832 | tf_op jit(solution)/shard_map/ppermute | solution.py:132
  128.4 26.1 %collective-permute-start.4 = (bf16[128,768]{1,0:T(8,128)(2,1)S(1)}, bf16[128,768]{1,0:T(8,128)(2,1)S(1)}, u32[]{:S(2)}, u32[]{:S(2)}) collective-permute-start(bf16[128,768]{1,0:T(8,128)(2,1)S(1)} %copy.41.refs_0_), channel_id=1, source_target_pairs={{0,2},{1,3},{2,0},{3,1},{4,6},{5,7},{6,4},{7,5},{8,10},{9,11},{10,... | collective-permute-start | bytes 589832 | tf_op jit(solution)/shard_map/ppermute | solution.py:132
  140.4 14.1 %collective-permute-start.5 = (bf16[128,768]{1,0:T(8,128)(2,1)S(1)}, bf16[128,768]{1,0:T(8,128)(2,1)S(1)}, u32[]{:S(2)}, u32[]{:S(2)}) collective-permute-start(bf16[128,768]{1,0:T(8,128)(2,1)S(1)} %copy.41.refs_0_), channel_id=1, source_target_pairs={{0,3},{1,2},{2,1},{3,0},{4,7},{5,6},{6,5},{7,4},{8,11},{9,10},{10,... | collective-permute-start | bytes 589832 | tf_op jit(solution)/shard_map/ppermute | solution.py:132
  142.9 15.4 %copy-start.3 = (bf16[128,768]{1,0:T(8,128)(2,1)}, bf16[128,768]{1,0:T(8,128)(2,1)S(1)}, u32[]{:S(2)}) copy-start(bf16[128,768]{1,0:T(8,128)(2,1)S(1)} %collective-permute-done.3.refs_1_) | copy-start | bytes 589828
  154.5 3.8 %copy-start.4 = (bf16[128,768]{1,0:T(8,128)(2,1)}, bf16[128,768]{1,0:T(8,128)(2,1)S(1)}, u32[]{:S(2)}) copy-start(bf16[128,768]{1,0:T(8,128)(2,1)S(1)} %collective-permute-done.4.refs_2_) | copy-start | bytes 589828
  154.5 3.8 %copy-start.5 = (bf16[128,768]{1,0:T(8,128)(2,1)}, bf16[128,768]{1,0:T(8,128)(2,1)S(1)}, u32[]{:S(2)}) copy-start(bf16[128,768]{1,0:T(8,128)(2,1)S(1)} %collective-permute-done.5.refs_3_) | copy-start | bytes 589828
  164.5 25.8 %collective-permute-start.6 = (bf16[128,768]{1,0:T(8,128)(2,1)}, bf16[128,768]{1,0:T(8,128)(2,1)S(1)}, u32[]{:S(2)}, u32[]{:S(2)}) collective-permute-start(bf16[128,768]{1,0:T(8,128)(2,1)} %shard_map.56), channel_id=1, source_target_pairs={{0,4},{4,0},{1,5},{5,1},{2,6},{6,2},{3,7},{7,3},{8,12},{12,8},{9,1... | collective-permute-start | bytes 589832 | tf_op jit(solution)/shard_map/ppermute | solution.py:136
Sparse Core Ops, SparseCore 0:
  81.1 77.1 all-gather.2

commit v3 on v2

--- a/solution.py
+++ b/solution.py
@@ -1,3 +1,5 @@
+import functools
+
 import jax
 import jax.numpy as jnp
 from jax import lax
@@ -17,68 +19,49 @@
 PIECE = 8
 
 
-def exchange_x_q(flip):
-    place = lambda zh, x, q: (zh * QUAD + x) * QUAD + q
-    return [
-        (place(zh, x, q), place(zh ^ flip, q, x))
-        for zh in range(2)
-        for x in range(QUAD)
-        for q in range(QUAD)
+def project_kernel(order_ref, *refs, side):
+    parts, (w_ref, out_ref, held, arrivals) = refs[:QUAD], refs[QUAD:]
+    width = w_ref.shape[-1]
+    copies = [
+        pltpu.make_async_copy(w_ref.at[order_ref[k], :, side], held.at[k], arrivals.at[k])
+        for k in range(QUAD)
     ]
-
-
-def project_kernel(order_ref, *refs):
-    parts, (w_ref, out_ref, total) = refs[:QUAD], refs[QUAD:]
-    step = pl.program_id(0)
-    width = w_ref.shape[-1]
-
-    @pl.when(step == 0)
-    def _():
-        total[...] = jnp.zeros_like(total)
-
-    rows = w_ref[...].reshape(-1, width)
-    for at, part in enumerate(parts):
-
-        @pl.when(step == at)
-        def _(part=part):
-            total[...] += lax.dot_general(
-                part[...], rows, (((1,), (1,)), ((), ())), preferred_element_type=jnp.float32
-            )
-
-    @pl.when(step == QUAD - 1)
-    def _():
-        out_ref[...] = total[...].astype(out_ref.dtype)
+    for copy in copies:
+        copy.start()
+    total = 0.0
+    for k in range(QUAD):
+        copies[k].wait()
+        total += lax.dot_general(
+            parts[k][...],
+            held[k].reshape(-1, width),
+            (((1,), (1,)), ((), ())),
+            preferred_element_type=jnp.float32,
+        )
+    out_ref[...] = total.astype(out_ref.dtype)
 
 
 def project(order, parts, w_all, side, dtype):
     tokens, width = parts[0].shape
     _, chunks, _, columns, _ = w_all.shape
-    whole = pl.BlockSpec((tokens, width), lambda k, order: (0, 0))
+    in_vmem = pl.BlockSpec(memory_space=pltpu.VMEM)
     return pl.pallas_call(
-        project_kernel,
-        grid_spec=pltpu.PrefetchScalarGridSpec(
-            num_scalar_prefetch=1,
-            grid=(QUAD,),
-            in_specs=[whole] * QUAD
-            + [
-                pl.BlockSpec(
-                    (None, chunks, None, columns, width),
-                    lambda k, order: (order[k], 0, side, 0, 0),
-                )
-            ],
-            out_specs=pl.BlockSpec((tokens, chunks * columns), lambda k, order: (0, 0)),
-            scratch_shapes=[pltpu.VMEM((tokens, chunks * columns), jnp.float32)],
-        ),
+        functools.partial(project_kernel, side=side),
+        in_specs=[pl.BlockSpec(memory_space=pltpu.SMEM)]
+        + [in_vmem] * QUAD
+        + [pl.BlockSpec(memory_space=pltpu.HBM)],
+        out_specs=in_vmem,
         out_shape=jax.ShapeDtypeStruct((tokens, chunks * columns), dtype),
-        compiler_params=pltpu.CompilerParams(
-            dimension_semantics=("arbitrary",), vmem_limit_bytes=56 << 20
-        ),
+        scratch_shapes=[
+            pltpu.VMEM((QUAD, chunks, columns, width), w_all.dtype),
+            pltpu.SemaphoreType.DMA((QUAD,)),
+        ],
+        compiler_params=pltpu.CompilerParams(vmem_limit_bytes=32 << 20),
         cost_estimate=pl.CostEstimate(
             flops=2 * QUAD * tokens * width * chunks * columns,
             bytes_accessed=2 * QUAD * width * (chunks * columns + tokens),
             transcendentals=0,
         ),
-    )(order, *parts, w_all)
+    )(order, *parts, pltpu.with_memory_space_constraint(w_all, pltpu.HBM))
 
 
 def body(queries, keys, values, plan, w_out):
@@ -89,9 +72,12 @@
     seats = lax.axis_size(PLANE)
     pieces = tokens // PIECE
 
-    w_rows = w_out.T
-    w_near = lax.ppermute(w_rows, ("zh", "x", "q"), exchange_x_q(0))
-    w_far = lax.ppermute(w_rows, ("zh", "x", "q"), exchange_x_q(1))
+    w_near = lax.ppermute(
+        w_out.T,
+        ("x", "q"),
+        [(x * QUAD + q, q * QUAD + x) for x in range(QUAD) for q in range(QUAD)],
+    )
+    w_far = lax.ppermute(w_near, "zh", SWAP)
     keeps_near = half == quad
     w_pair = jnp.stack(
         (jnp.where(keeps_near, w_near, w_far), jnp.where(keeps_near, w_far, w_near))

time: 200 us -> 190 us (0.950); the launches traced: 199 us -> 187 us
  Pallas kernels: 12.4 us -> 8.38 us
  starting transfers between devices: 61.7 us -> 58.1 us
  waiting for transfers between devices: 101 us -> 98.3 us
    ppermute x2, waiting for transfers between devices: 43.5 us -> 5.35 us  [the longest x1 5.35 us: body(): lax.ppermute(w_out.T, ('x', 'q'), [(x * QUAD + q, q * QUAD + x) for x in...]
    ppermute x1, waiting for transfers between devices: 19.3 us -> 39.1 us  [body(): far = lax.ppermute(spread, 'zh', SWAP)]
    all_to_all x1, waiting for transfers between devices: 11.3 us -> 18.5 us  [body(): lax.all_to_all(chosen, PLANE, split_axis=0, concat_axis=0, tiled=True)]
    all_to_all x1, waiting for transfers between devices: 0.01 us -> 7.19 us  [body(): spread = lax.all_to_all(own, PLANE, split_axis=0, concat_axis=0, tiled=True)]
    all_to_all x1, starting transfers between devices: 8.03 us -> 14.6 us  [body(): spread = lax.all_to_all(own, PLANE, split_axis=0, concat_axis=0, tiled=True)]
    ppermute x3, starting transfers between devices: 15.9 us -> 10.1 us  [body(): lax.ppermute(attended, 'q', [(i, i ^ k) for i in range(QUAD)])]
    ppermute x1, starting transfers between devices: 7.63 us -> 3.25 us  [body(): arrived = lax.ppermute(sent, 'p', SWAP)]
    pallas_call x2, Pallas kernels: 12.4 us -> 8.38 us  [project(): pl.pallas_call(functools.partial(project_kernel, side=side), in_specs=[pl...]
  transfers between devices with their start and end apart: 10 -> 10, of which waited for: 6 -> 6; matrix products, arithmetic and copies ran while one was open for 4% -> 4% of each run, Pallas kernels for 3% -> 2%
where the time goes in v3:
time: 190 us; the launch traced here: 187 us
  waiting for transfers between devices  98.3 us (52%)
  starting transfers between devices  58.1 us (31%)
  between operations  13.7 us (7%)
  Pallas kernels  8.38 us (4%)
  local copies, waits for them, and re-layouts  3.87 us (2%)
  other arithmetic  3.64 us (2%)
    ppermute x1, waiting for transfers between devices, body(): far = lax.ppermute(spread, 'zh', SWAP)  39.1 us
    all_to_all x1, waiting for transfers between devices, body(): lax.all_to_all(chosen, PLANE, split_axis=0, concat_axis=0, tiled=True)  18.5 us
    ppermute x1, waiting for transfers between devices, body(): arrived = lax.ppermute(sent, 'p', SWAP)  15.7 us
    ppermute x1, starting transfers between devices, body(): w_far = lax.ppermute(w_near, 'zh', SWAP)  15.7 us
    all_to_all x1, starting transfers between devices, body(): spread = lax.all_to_all(own, PLANE, split_axis=0, concat_axis=0, tiled=True)  14.6 us
    ppermute x3, waiting for transfers between devices, body(): lax.ppermute(attended, 'q', [(i, i ^ k) for i in range(QUAD)])  12.4 us
    ppermute x3, starting transfers between devices, body(): lax.ppermute(attended, 'q', [(i, i ^ k) for i in range(QUAD)])  10.1 us
    pallas_call x2, Pallas kernels, project(): pl.pallas_call(functools.partial(project_kernel, side=side), in_specs=[pl...  8.38 us
  transfers between devices with their start and end apart: 10, of which 6 were waited for; matrix products, arithmetic and copies ran while one was open for 4% of the time, Pallas kernels for 2%

profile of v3, /device:TPU:6, one launch (start us, length us, event | category | flops | bytes accessed | tf_op | source)
XLA Modules:
  0.0 186.7 jit_solution(10389206905029305470)
XLA Ops:
  6.5 6.4 %collective-permute-start = (bf16[96,768]{1,0:T(8,128)(2,1)}, bf16[96,768]{1,0:T(8,128)(2,1)S(1)}, u32[]{:S(2)}, u32[]{:S(2)}) collective-permute-start(bf16[96,768]{1,0:T(8,128)(2,1)} %bitcast.43), channel_id=1, source_target_pairs={{0,0},{1,64},{2,128},{3,192},{64,1},{65,65},{66,129},{67,193},{128... | collective-permute-start | bytes 442376 | tf_op jit(solution)/shard_map/ppermute | solution.py:75
  13.0 5.3 %collective-permute-done = bf16[96,768]{1,0:T(8,128)(2,1)S(1)} collective-permute-done((bf16[96,768]{1,0:T(8,128)(2,1)}, bf16[96,768]{1,0:T(8,128)(2,1)S(1)}, u32[]{:S(2)}, u32[]{:S(2)}) %collective-permute-start) | collective-permute-done | bytes 147488 | tf_op jit(solution)/shard_map/ppermute | solution.py:75
  18.3 15.7 %collective-permute-start.1 = (bf16[96,768]{1,0:T(8,128)(2,1)S(1)}, bf16[96,768]{1,0:T(8,128)(2,1)S(1)}, u32[]{:S(2)}, u32[]{:S(2)}) collective-permute-start(bf16[96,768]{1,0:T(8,128)(2,1)S(1)} %collective-permute-done), channel_id=1, source_target_pairs={{0,256},{256,0},{1,257},{257,1},{2,258},{258,2},{3,259},{259,3},{4... | collective-permute-start | bytes 442376 | tf_op jit(solution)/shard_map/ppermute | solution.py:80
  34.0 1.8 pad_maximum_fusion.1
  35.9 0.0 copy-start.3
  35.9 14.6 %all-to-all-start = ((bf16[32,8,768]{2,1,0:T(8,128)(2,1)}), bf16[32,8,768]{2,1,0:T(8,128)(2,1)S(1)}, u32[]{:S(2)}, u32[]{:S(2)}) async-start(bf16[32,8,768]{2,1,0:T(8,128)(2,1)} %bitcast.3), calls=%async_computation | async-start | bytes 786432 | tf_op jit(solution)/shard_map/all_to_all | solution.py:87
  50.5 0.0 all-gather.3.cloned.1.call-start
  50.5 0.0 collective-permute-done.1
  50.6 0.8 pad_maximum_fusion.2
  51.3 7.2 %all-to-all-done = bf16[32,8,768]{2,1,0:T(8,128)(2,1)S(1)} async-done(((bf16[32,8,768]{2,1,0:T(8,128)(2,1)}), bf16[32,8,768]{2,1,0:T(8,128)(2,1)S(1)}, u32[]{:S(2)}, u32[]{:S(2)}) %all-to-all-start) | async-done | bytes 393248 | tf_op jit(solution)/shard_map/all_to_all | solution.py:87
  58.5 0.0 all-gather.3.cloned.1.call-update
  58.6 1.9 %collective-permute-start.2 = (bf16[32,8,768]{2,1,0:T(8,128)(2,1)S(1)}, bf16[32,8,768]{2,1,0:T(8,128)(2,1)S(1)}, u32[]{:S(2)}, u32[]{:S(2)}) collective-permute-start(bf16[32,8,768]{2,1,0:T(8,128)(2,1)S(1)} %all-to-all-done), channel_id=1, source_target_pairs={{0,256},{256,0},{1,257},{257,1},{2,258},{258,2},{3,259},{259,3},{4... | collective-permute-start | bytes 1179656 | tf_op jit(solution)/shard_map/ppermute | solution.py:89
  60.5 0.0 copy-done.3
  60.5 0.1 compare_select_fusion
  60.6 0.1 copy.28
  60.7 0.1 reshape.37
  60.8 39.1 %collective-permute-done.2 = bf16[32,8,768]{2,1,0:T(8,128)(2,1)S(1)} collective-permute-done((bf16[32,8,768]{2,1,0:T(8,128)(2,1)S(1)}, bf16[32,8,768]{2,1,0:T(8,128)(2,1)S(1)}, u32[]{:S(2)}, u32[]{:S(2)}) %collective-permute-start.2) | collective-permute-done | bytes 393248 | tf_op jit(solution)/shard_map/ppermute | solution.py:89
  99.9 0.1 pad_maximum_fusion
  100.0 1.5 gather_fusion
  101.5 6.1 %all-to-all-start.1 = ((bf16[32,2,8,768]{3,2,1,0:T(8,128)(2,1)}), bf16[32,2,8,768]{3,2,1,0:T(8,128)(2,1)S(1)}, u32[]{:S(2)}, u32[]{:S(2)}) async-start(bf16[32,2,8,768]{3,2,1,0:T(8,128)(2,1)} %bitcast.8), calls=%async_computation.1 | async-start | bytes 1572864 | tf_op jit(solution)/shard_map/all_to_all | solution.py:97
  107.5 0.0 copy-done
  107.6 0.2 copy.31
  107.7 0.0 copy-done.1
  107.7 0.2 copy.27
  107.9 0.2 copy.33
  108.1 0.0 copy-done.2
  108.1 0.2 copy.35
  108.2 18.5 %all-to-all-done.1 = bf16[32,2,8,768]{3,2,1,0:T(8,128)(2,1)S(1)} async-done(((bf16[32,2,8,768]{3,2,1,0:T(8,128)(2,1)}), bf16[32,2,8,768]{3,2,1,0:T(8,128)(2,1)S(1)}, u32[]{:S(2)}, u32[]{:S(2)}) %all-to-all-start.1) | async-done | bytes 786464 | tf_op jit(solution)/shard_map/all_to_all | solution.py:97
  126.7 0.1 fusion.16
  126.8 0.5 concatenate.24
  127.3 0.1 copy.34
  127.4 0.5 concatenate.21
  127.9 0.3 copy.30
  128.2 0.3 fusion.17
  128.5 0.2 fusion.3
  128.7 0.3 fusion.2
  129.0 0.1 copy.41.refs_0_
  129.1 3.6 %collective-permute-start.3 = (bf16[128,768]{1,0:T(8,128)(2,1)S(1)}, bf16[128,768]{1,0:T(8,128)(2,1)S(1)}, u32[]{:S(2)}, u32[]{:S(2)}) collective-permute-start(bf16[128,768]{1,0:T(8,128)(2,1)S(1)} %copy.41.refs_0_), channel_id=1, source_target_pairs={{0,1},{1,0},{2,3},{3,2},{4,5},{5,4},{6,7},{7,6},{8,9},{9,8},{10,11... | collective-permute-start | bytes 589832 | tf_op jit(solution)/shard_map/ppermute | solution.py:118
  132.7 2.7 %collective-permute-start.4 = (bf16[128,768]{1,0:T(8,128)(2,1)S(1)}, bf16[128,768]{1,0:T(8,128)(2,1)S(1)}, u32[]{:S(2)}, u32[]{:S(2)}) collective-permute-start(bf16[128,768]{1,0:T(8,128)(2,1)S(1)} %copy.41.refs_0_), channel_id=1, source_target_pairs={{0,2},{1,3},{2,0},{3,1},{4,6},{5,7},{6,4},{7,5},{8,10},{9,11},{10,... | collective-permute-start | bytes 589832 | tf_op jit(solution)/shard_map/ppermute | solution.py:118
  135.5 3.8 %collective-permute-start.5 = (bf16[128,768]{1,0:T(8,128)(2,1)S(1)}, bf16[128,768]{1,0:T(8,128)(2,1)S(1)}, u32[]{:S(2)}, u32[]{:S(2)}) collective-permute-start(bf16[128,768]{1,0:T(8,128)(2,1)S(1)} %copy.41.refs_0_), channel_id=1, source_target_pairs={{0,3},{1,2},{2,1},{3,0},{4,7},{5,6},{6,5},{7,4},{8,11},{9,10},{10,... | collective-permute-start | bytes 589832 | tf_op jit(solution)/shard_map/ppermute | solution.py:118
  139.3 0.0 collective-permute-done.3.refs_1_
  139.3 12.4 %collective-permute-done.4.refs_2_ = bf16[128,768]{1,0:T(8,128)(2,1)S(1)} collective-permute-done((bf16[128,768]{1,0:T(8,128)(2,1)S(1)}, bf16[128,768]{1,0:T(8,128)(2,1)S(1)}, u32[]{:S(2)}, u32[]{:S(2)}) %collective-permute-start.4) | collective-permute-done | bytes 196640 | tf_op jit(solution)/shard_map/ppermute | solution.py:118
  151.7 0.0 collective-permute-done.5.refs_3_
  151.7 4.2 %shard_map.56 = bf16[128,768]{1,0:T(8,128)(2,1)S(1)} custom-call(s32[4]{0:T(128)S(1)} %iota_xor_fusion.order_ref, bf16[128,768]{1,0:T(8,128)(2,1)S(1)} %copy.41.refs_0_, bf16[128,768]{1,0:T(8,128)(2,1)S(1)} %collective-permute-done.3.refs_1_, bf16[128,768]{1,0:T(8,128)(2,1)S(1)} %collective-permute-done.4.refs_2_, ...), custom_call_target="tpu_custom_call" | custom-call | flops 603979776 | bytes 5505024 | tf_op jit(solution)/shard_map/pallas_call | solution.py:47
  155.9 3.2 %collective-permute-start.6 = (bf16[128,768]{1,0:T(8,128)(2,1)S(1)}, bf16[128,768]{1,0:T(8,128)(2,1)S(1)}, u32[]{:S(2)}, u32[]{:S(2)}) collective-permute-start(bf16[128,768]{1,0:T(8,128)(2,1)S(1)} %shard_map.56), channel_id=1, source_target_pairs={{0,4},{4,0},{1,5},{5,1},{2,6},{6,2},{3,7},{7,3},{8,12},{12,8},{9,1... | collective-permute-start | bytes 589832 | tf_op jit(solution)/shard_map/ppermute | solution.py:122
  159.2 4.2 %shard_map.55 = f32[128,768]{1,0:T(8,128)S(1)} custom-call(s32[4]{0:T(128)S(1)} %iota_xor_fusion.order_ref, bf16[128,768]{1,0:T(8,128)(2,1)S(1)} %copy.41.refs_0_, bf16[128,768]{1,0:T(8,128)(2,1)S(1)} %collective-permute-done.3.refs_1_, bf16[128,768]{1,0:T(8,128)(2,1)S(1)} %collective-permute-done.4.refs_2_, ...), custom_call_target="tpu_custom_call" | custom-call | flops 603979776 | bytes 5505024 | tf_op jit(solution)/shard_map/pallas_call | solution.py:47
  163.4 15.7 %collective-permute-done.6 = bf16[128,768]{1,0:T(8,128)(2,1)S(1)} collective-permute-done((bf16[128,768]{1,0:T(8,128)(2,1)S(1)}, bf16[128,768]{1,0:T(8,128)(2,1)S(1)}, u32[]{:S(2)}, u32[]{:S(2)}) %collective-permute-start.6) | collective-permute-done | bytes 196640 | tf_op jit(solution)/shard_map/ppermute | solution.py:122
  179.1 0.7 add_convert_fusion
  (9 shorter events, 0.1 us)
Async XLA Ops:
  6.5 11.8 %collective-permute-start = (bf16[96,768]{1,0:T(8,128)(2,1)}, bf16[96,768]{1,0:T(8,128)(2,1)S(1)}, u32[]{:S(2)}, u32[]{:S(2)}) collective-permute-start(bf16[96,768]{1,0:T(8,128)(2,1)} %bitcast.43), channel_id=1, source_target_pairs={{0,0},{1,64},{2,128},{3,192},{64,1},{65,65},{66,129},{67,193},{128... | collective-permute-start | bytes 442376 | tf_op jit(solution)/shard_map/ppermute | solution.py:75
  18.3 32.2 %collective-permute-start.1 = (bf16[96,768]{1,0:T(8,128)(2,1)S(1)}, bf16[96,768]{1,0:T(8,128)(2,1)S(1)}, u32[]{:S(2)}, u32[]{:S(2)}) collective-permute-start(bf16[96,768]{1,0:T(8,128)(2,1)S(1)} %collective-permute-done), channel_id=1, source_target_pairs={{0,256},{256,0},{1,257},{257,1},{2,258},{258,2},{3,259},{259,3},{4... | collective-permute-start | bytes 442376 | tf_op jit(solution)/shard_map/ppermute | solution.py:80
  35.9 24.6 %copy-start.3 = (s32[2,64]{1,0:T(2,128)S(1)}, s32[2,64]{1,0:T(2,128)}, u32[]{:S(2)}) copy-start(s32[2,64]{1,0:T(2,128)} %param.8) | copy-start | bytes 1540
  35.9 22.7 %all-to-all-start = ((bf16[32,8,768]{2,1,0:T(8,128)(2,1)}), bf16[32,8,768]{2,1,0:T(8,128)(2,1)S(1)}, u32[]{:S(2)}, u32[]{:S(2)}) async-start(bf16[32,8,768]{2,1,0:T(8,128)(2,1)} %bitcast.3), calls=%async_computation | async-start | bytes 786432 | tf_op jit(solution)/shard_map/all_to_all | solution.py:87
  50.5 101.2 %all-gather.3.cloned.1.call-start = ((), (), s32[]{:S(2)}) async-start(), calls=%async_computation.2 | async-start | bytes 9732096 | tf_op jit(solution)/shard_map/all_gather | solution.py:91
  58.6 41.3 %collective-permute-start.2 = (bf16[32,8,768]{2,1,0:T(8,128)(2,1)S(1)}, bf16[32,8,768]{2,1,0:T(8,128)(2,1)S(1)}, u32[]{:S(2)}, u32[]{:S(2)}) collective-permute-start(bf16[32,8,768]{2,1,0:T(8,128)(2,1)S(1)} %all-to-all-done), channel_id=1, source_target_pairs={{0,256},{256,0},{1,257},{257,1},{2,258},{258,2},{3,259},{259,3},{4... | collective-permute-start | bytes 1179656 | tf_op jit(solution)/shard_map/ppermute | solution.py:89
  101.5 6.1 %copy-start = (bf16[128,768]{1,0:T(8,128)(2,1)S(1)}, bf16[128,768]{1,0:T(8,128)(2,1)}, u32[]{:S(2)}) copy-start(bf16[128,768]{1,0:T(8,128)(2,1)} %param.6) | copy-start | bytes 589828
  101.5 6.3 %copy-start.1 = (bf16[128,768]{1,0:T(8,128)(2,1)S(1)}, bf16[128,768]{1,0:T(8,128)(2,1)}, u32[]{:S(2)}) copy-start(bf16[128,768]{1,0:T(8,128)(2,1)} %param.7) | copy-start | bytes 589828
  101.5 6.6 %copy-start.2 = (bf16[128,768]{1,0:T(8,128)(2,1)S(1)}, bf16[128,768]{1,0:T(8,128)(2,1)}, u32[]{:S(2)}) copy-start(bf16[128,768]{1,0:T(8,128)(2,1)} %param.5) | copy-start | bytes 589828
  101.5 25.3 %all-to-all-start.1 = ((bf16[32,2,8,768]{3,2,1,0:T(8,128)(2,1)}), bf16[32,2,8,768]{3,2,1,0:T(8,128)(2,1)S(1)}, u32[]{:S(2)}, u32[]{:S(2)}) async-start(bf16[32,2,8,768]{3,2,1,0:T(8,128)(2,1)} %bitcast.8), calls=%async_computation.1 | async-start | bytes 1572864 | tf_op jit(solution)/shard_map/all_to_all | solution.py:97
  129.1 10.2 %collective-permute-start.3 = (bf16[128,768]{1,0:T(8,128)(2,1)S(1)}, bf16[128,768]{1,0:T(8,128)(2,1)S(1)}, u32[]{:S(2)}, u32[]{:S(2)}) collective-permute-start(bf16[128,768]{1,0:T(8,128)(2,1)S(1)} %copy.41.refs_0_), channel_id=1, source_target_pairs={{0,1},{1,0},{2,3},{3,2},{4,5},{5,4},{6,7},{7,6},{8,9},{9,8},{10,11... | collective-permute-start | bytes 589832 | tf_op jit(solution)/shard_map/ppermute | solution.py:118
  132.7 19.0 %collective-permute-start.4 = (bf16[128,768]{1,0:T(8,128)(2,1)S(1)}, bf16[128,768]{1,0:T(8,128)(2,1)S(1)}, u32[]{:S(2)}, u32[]{:S(2)}) collective-permute-start(bf16[128,768]{1,0:T(8,128)(2,1)S(1)} %copy.41.refs_0_), channel_id=1, source_target_pairs={{0,2},{1,3},{2,0},{3,1},{4,6},{5,7},{6,4},{7,5},{8,10},{9,11},{10,... | collective-permute-start | bytes 589832 | tf_op jit(solution)/shard_map/ppermute | solution.py:118
  135.5 16.3 %collective-permute-start.5 = (bf16[128,768]{1,0:T(8,128)(2,1)S(1)}, bf16[128,768]{1,0:T(8,128)(2,1)S(1)}, u32[]{:S(2)}, u32[]{:S(2)}) collective-permute-start(bf16[128,768]{1,0:T(8,128)(2,1)S(1)} %copy.41.refs_0_), channel_id=1, source_target_pairs={{0,3},{1,2},{2,1},{3,0},{4,7},{5,6},{6,5},{7,4},{8,11},{9,10},{10,... | collective-permute-start | bytes 589832 | tf_op jit(solution)/shard_map/ppermute | solution.py:118
  155.9 23.2 %collective-permute-start.6 = (bf16[128,768]{1,0:T(8,128)(2,1)S(1)}, bf16[128,768]{1,0:T(8,128)(2,1)S(1)}, u32[]{:S(2)}, u32[]{:S(2)}) collective-permute-start(bf16[128,768]{1,0:T(8,128)(2,1)S(1)} %shard_map.56), channel_id=1, source_target_pairs={{0,4},{4,0},{1,5},{5,1},{2,6},{6,2},{3,7},{7,3},{8,12},{12,8},{9,1... | collective-permute-start | bytes 589832 | tf_op jit(solution)/shard_map/ppermute | solution.py:122
Sparse Core Ops, SparseCore 0:
  58.7 69.2 all-gather.2

commit v4 on v3

v4 whole, which is shorter than its diff:
```python
import functools

import jax
import jax.numpy as jnp
from jax import lax
from jax.experimental import pallas as pl
from jax.experimental.pallas import tpu as pltpu
from jax.sharding import Mesh, PartitionSpec as P

HEAD_DIM = 128
ROUNDS = 2
SIZES = (2, 4, 4, 2, 2, 4)
NAMES = ("zh", "x", "y", "c", "p", "q")
CTX = ("zh", "x", "y", "c")
HEAD = ("p", "q")
PLANE = ("x", "y", "c")
SWAP = ((0, 1), (1, 0))
QUAD = 4
HALVES = 2
PIECE = 8


def project_kernel(order_ref, *refs, side):
    parts, (w_ref, out_ref, held, arrivals) = refs[: HALVES * QUAD], refs[HALVES * QUAD :]
    width = w_ref.shape[-1]
    copies = [
        pltpu.make_async_copy(w_ref.at[order_ref[k], :, side], held.at[k], arrivals.at[k])
        for k in range(QUAD)
    ]
    for copy in copies:
        copy.start()
    total = 0.0
    for k in range(QUAD):
        copies[k].wait()
        rows = held[k].reshape(-1, width)
        for half in range(HALVES):
            total += lax.dot_general(
                parts[half * QUAD + k][...],
                rows[:, half * width // HALVES : (half + 1) * width // HALVES],
                (((1,), (1,)), ((), ())),
                preferred_element_type=jnp.float32,
            )
    out_ref[...] = total.astype(out_ref.dtype)


def project(order, parts, w_all, side, dtype):
    tokens = parts[0].shape[0]
    _, chunks, _, columns, width = w_all.shape
    in_vmem = pl.BlockSpec(memory_space=pltpu.VMEM)
    return pl.pallas_call(
        functools.partial(project_kernel, side=side),
        in_specs=[pl.BlockSpec(memory_space=pltpu.SMEM)]
        + [in_vmem] * len(parts)
        + [pl.BlockSpec(memory_space=pltpu.HBM)],
        out_specs=in_vmem,
        out_shape=jax.ShapeDtypeStruct((tokens, chunks * columns), dtype),
        scratch_shapes=[
            pltpu.VMEM((QUAD, chunks, columns, width), w_all.dtype),
            pltpu.SemaphoreType.DMA((QUAD,)),
        ],
        compiler_params=pltpu.CompilerParams(vmem_limit_bytes=32 << 20),
        cost_estimate=pl.CostEstimate(
            flops=2 * QUAD * tokens * width * chunks * columns,
            bytes_accessed=2 * QUAD * width * (chunks * columns + tokens),
            transcendentals=0,
        ),
    )(order, *parts, pltpu.with_memory_space_constraint(w_all, pltpu.HBM))


def attend(query_cols, key_cols, value_cols):
    tokens, width = query_cols.shape
    split = lambda cols: cols.reshape(-1, width // HEAD_DIM, HEAD_DIM)
    scores = jnp.einsum(
        "qhd,khd->hqk", split(query_cols), split(key_cols), preferred_element_type=jnp.float32
    ) * (1.0 / HEAD_DIM**0.5)
    exponent = jnp.exp(scores - jnp.max(scores, axis=-1, keepdims=True))
    row_total = jnp.sum(exponent, axis=-1)
    summed = jnp.einsum(
        "hqk,khd->qhd",
        exponent.astype(jnp.bfloat16),
        split(value_cols),
        preferred_element_type=jnp.float32,
    )
    return (summed / row_total.T[:, :, None]).astype(jnp.bfloat16).reshape(tokens, width)


def body(queries, keys, values, plan, w_out):
    tokens, width = queries.shape
    half = lax.axis_index("zh")
    quad, member = lax.axis_index("p"), lax.axis_index("q")
    seats = lax.axis_size(PLANE)
    pieces = tokens // PIECE
    part = width // HALVES
    cut = lambda cols, h: cols[:, h * part : (h + 1) * part]
    plane_swap = lambda sent: lax.all_to_all(sent, PLANE, split_axis=0, concat_axis=0, tiled=True)

    w_near = lax.ppermute(
        w_out.T,
        ("x", "q"),
        [(x * QUAD + q, q * QUAD + x) for x in range(QUAD) for q in range(QUAD)],
    )

    spread = [
        plane_swap(
            jnp.stack((cut(keys, h), cut(values, h))).reshape(2 * pieces, PIECE, part)
        )
        for h in range(HALVES)
    ]
    w_near, spread[0] = lax.optimization_barrier((w_near, spread[0]))
    w_far = lax.ppermute(w_near, "zh", SWAP)
    keeps_near = half == quad
    w_pair = jnp.stack(
        (jnp.where(keeps_near, w_near, w_far), jnp.where(keeps_near, w_far, w_near))
    )
    w_pair, spread[1] = lax.optimization_barrier((w_pair, spread[1]))
    w_all = lax.all_gather(w_pair, PLANE, axis=0, tiled=False)
    w_all = w_all.reshape(QUAD, seats // QUAD, 2, -1, width)

    wanted = lax.dynamic_slice_in_dim(plan, half * seats, seats, 1)
    place = ((wanted // seats ^ half) * seats + wanted % seats).T
    parts = []
    for h in range(HALVES):
        far = lax.ppermute(spread[h], "zh", SWAP)
        chosen = jnp.concatenate((spread[h], far)).at[place].get(mode="promise_in_bounds")
        routed = plane_swap(chosen)
        routed = routed.reshape(2, pieces, ROUNDS, PIECE, part).transpose(0, 2, 1, 3, 4)
        routed = routed.reshape(2, ROUNDS * tokens, part)
        attended = attend(
            cut(queries, h),
            jnp.concatenate((cut(keys, h), routed[0])),
            jnp.concatenate((cut(values, h), routed[1])),
        )
        parts += [attended] + [
            lax.ppermute(attended, "q", [(i, i ^ k) for i in range(QUAD)])
            for k in range(1, QUAD)
        ]

    order = member ^ jnp.arange(QUAD, dtype=jnp.int32)
    sent = project(order, parts, w_all, 1, jnp.bfloat16)
    arrived = lax.ppermute(sent, "p", SWAP)
    kept = project(order, parts, w_all, 0, jnp.float32)
    return (kept + arrived.astype(jnp.float32)).astype(jnp.bfloat16)


def solution(mesh):
    fine = Mesh(mesh.devices.reshape(SIZES), NAMES)
    return jax.shard_map(
        body,
        mesh=fine,
        in_specs=(P(CTX, HEAD), P(CTX, HEAD), P(CTX, HEAD), P(), P(HEAD, CTX)),
        out_specs=P(CTX, HEAD),
        check_vma=False,
    )
```

time: 190 us -> 196 us (1.032); the launches traced: 187 us -> 195 us
  starting transfers between devices: 58.1 us -> 89 us
  waiting for transfers between devices: 98.3 us -> 72.1 us
  local copies, waits for them, and re-layouts: 3.87 us -> 7.09 us
    all_to_all x2 -> x4, waiting for transfers between devices: 25.7 us -> 5.56 us  [body(): lax.all_to_all(sent, PLANE, split_axis=0, concat_axis=0, tiled=True)]
    ppermute x1 -> x2, starting transfers between devices: 1.92 us -> 14.7 us  [body(): far = lax.ppermute(spread[h], 'zh', SWAP)]
    all_to_all x2 -> x4, starting transfers between devices: 20.7 us -> 32.2 us  [body(): lax.all_to_all(sent, PLANE, split_axis=0, concat_axis=0, tiled=True)]
    ppermute x3 -> x6, starting transfers between devices: 10.1 us -> 20.2 us  [body(): lax.ppermute(attended, 'q', [(i, i ^ k) for i in range(QUAD)])]
    ppermute x3 -> x6, waiting for transfers between devices: 12.4 us -> 4.52 us  [body(): lax.ppermute(attended, 'q', [(i, i ^ k) for i in range(QUAD)])]
    slice x1 -> x8, local copies, waits for them, and re-layouts: 0.03 us -> 2.61 us  [the longest x6 2.57 us: body(): cut = lambda cols, h: cols[:, h * part:(h + 1) * part]]
    ppermute x1, waiting for transfers between devices: 5.35 us -> 7.87 us  [body(): lax.ppermute(w_out.T, ('x', 'q'), [(x * QUAD + q, q * QUAD + x) for x in...]
    ppermute x1, starting transfers between devices: 6.44 us -> 4.24 us  [body(): lax.ppermute(w_out.T, ('x', 'q'), [(x * QUAD + q, q * QUAD + x) for x in...]
  transfers between devices with their start and end apart: 10 -> 16, of which waited for: 6 -> 7; matrix products, arithmetic and copies ran while one was open for 4% -> 5% of each run, Pallas kernels for 2% -> 2%
where the time goes in v4:
time: 196 us; the launch traced here: 195 us
  starting transfers between devices  89 us (45%)
  waiting for transfers between devices  72.1 us (37%)
  between operations  13.8 us (7%)
  Pallas kernels  7.95 us (4%)
  local copies, waits for them, and re-layouts  7.09 us (4%)
  other arithmetic  3.98 us (2%)
    ppermute x2, waiting for transfers between devices, body(): far = lax.ppermute(spread[h], 'zh', SWAP)  38.8 us
    all_to_all x4, starting transfers between devices, body(): lax.all_to_all(sent, PLANE, split_axis=0, concat_axis=0, tiled=True)  32.2 us
    ppermute x6, starting transfers between devices, body(): lax.ppermute(attended, 'q', [(i, i ^ k) for i in range(QUAD)])  20.2 us
    ppermute x1, waiting for transfers between devices, body(): arrived = lax.ppermute(sent, 'p', SWAP)  15.3 us
    ppermute x2, starting transfers between devices, body(): far = lax.ppermute(spread[h], 'zh', SWAP)  14.7 us
    ppermute x1, starting transfers between devices, body(): w_far = lax.ppermute(w_near, 'zh', SWAP)  13.8 us
    pallas_call x2, Pallas kernels, project(): pl.pallas_call(functools.partial(project_kernel, side=side), in_specs=[pl...  7.95 us
    ppermute x1, waiting for transfers between devices, body(): lax.ppermute(w_out.T, ('x', 'q'), [(x * QUAD + q, q * QUAD + x) for x in...  7.87 us
  transfers between devices with their start and end apart: 16, of which 7 were waited for; matrix products, arithmetic and copies ran while one was open for 5% of the time, Pallas kernels for 2%

profile of v4, /device:TPU:6, one launch (start us, length us, event | category | flops | bytes accessed | tf_op | source)
XLA Modules:
  0.0 194.9 jit_solution(8364889035137621659)
XLA Ops:
  6.5 1.1 fusion.33
  7.6 0.7 pad_maximum_fusion.3
  8.3 9.5 %all-to-all-start = ((bf16[32,8,384]{2,1,0:T(8,128)(2,1)}), bf16[32,8,384]{2,1,0:T(8,128)(2,1)S(1)}, u32[]{:S(2)}, u32[]{:S(2)}) async-start(bf16[32,8,384]{2,1,0:T(8,128)(2,1)} %bitcast.4), calls=%async_computation | async-start | bytes 393216 | tf_op jit(solution)/shard_map/all_to_all | solution.py:95
  17.9 4.2 %collective-permute-start = (bf16[96,768]{1,0:T(8,128)(2,1)}, bf16[96,768]{1,0:T(8,128)(2,1)S(1)}, u32[]{:S(2)}, u32[]{:S(2)}) collective-permute-start(bf16[96,768]{1,0:T(8,128)(2,1)} %bitcast.76), channel_id=1, source_target_pairs={{0,0},{1,64},{2,128},{3,192},{64,1},{65,65},{66,129},{67,193},{128... | collective-permute-start | bytes 442376 | tf_op jit(solution)/shard_map/ppermute | solution.py:97
  22.1 7.9 %collective-permute-done = bf16[96,768]{1,0:T(8,128)(2,1)S(1)} collective-permute-done((bf16[96,768]{1,0:T(8,128)(2,1)}, bf16[96,768]{1,0:T(8,128)(2,1)S(1)}, u32[]{:S(2)}, u32[]{:S(2)}) %collective-permute-start) | collective-permute-done | bytes 147488 | tf_op jit(solution)/shard_map/ppermute | solution.py:97
  30.0 13.8 %collective-permute-start.5 = (bf16[96,768]{1,0:T(8,128)(2,1)S(1)}, bf16[96,768]{1,0:T(8,128)(2,1)S(1)}, u32[]{:S(2)}, u32[]{:S(2)}) collective-permute-start(bf16[96,768]{1,0:T(8,128)(2,1)S(1)} %collective-permute-done), channel_id=1, source_target_pairs={{0,256},{256,0},{1,257},{257,1},{2,258},{258,2},{3,259},{259,3},{4... | collective-permute-start | bytes 442376 | tf_op jit(solution)/shard_map/ppermute | solution.py:110
  43.8 0.7 pad_maximum_fusion.4
  44.5 9.8 %all-to-all-start.2 = ((bf16[32,8,384]{2,1,0:T(8,128)(2,1)}), bf16[32,8,384]{2,1,0:T(8,128)(2,1)S(1)}, u32[]{:S(2)}, u32[]{:S(2)}) async-start(bf16[32,8,384]{2,1,0:T(8,128)(2,1)} %bitcast.21), calls=%async_computation.2 | async-start | bytes 393216 | tf_op jit(solution)/shard_map/all_to_all | solution.py:95
  54.5 0.8 pad_maximum_fusion.2
  55.2 5.5 %all-to-all-done.2 = bf16[32,8,384]{2,1,0:T(8,128)(2,1)S(1)} async-done(((bf16[32,8,384]{2,1,0:T(8,128)(2,1)}), bf16[32,8,384]{2,1,0:T(8,128)(2,1)S(1)}, u32[]{:S(2)}, u32[]{:S(2)}) %all-to-all-start.2) | async-done | bytes 196640 | tf_op jit(solution)/shard_map/all_to_all | solution.py:95
  60.8 7.3 %collective-permute-start.1 = (bf16[32,8,384]{2,1,0:T(8,128)(2,1)S(1)}, bf16[32,8,384]{2,1,0:T(8,128)(2,1)S(1)}, u32[]{:S(2)}, u32[]{:S(2)}) collective-permute-start(bf16[32,8,384]{2,1,0:T(8,128)(2,1)S(1)} %all-to-all-done), channel_id=1, source_target_pairs={{0,256},{256,0},{1,257},{257,1},{2,258},{258,2},{3,259},{259,3},{4... | collective-permute-start | bytes 589832 | tf_op jit(solution)/shard_map/ppermute | solution.py:123
  68.1 0.8 compare_select_fusion
  69.1 20.6 %collective-permute-done.1 = bf16[32,8,384]{2,1,0:T(8,128)(2,1)S(1)} collective-permute-done((bf16[32,8,384]{2,1,0:T(8,128)(2,1)S(1)}, bf16[32,8,384]{2,1,0:T(8,128)(2,1)S(1)}, u32[]{:S(2)}, u32[]{:S(2)}) %collective-permute-start.1) | collective-permute-done | bytes 196640 | tf_op jit(solution)/shard_map/ppermute | solution.py:123
  89.8 1.4 gather_fusion
  91.2 5.4 %all-to-all-start.1 = ((bf16[32,2,8,384]{3,2,1,0:T(8,128)(2,1)}), bf16[32,2,8,384]{3,2,1,0:T(8,128)(2,1)S(1)}, u32[]{:S(2)}, u32[]{:S(2)}) async-start(bf16[32,2,8,384]{3,2,1,0:T(8,128)(2,1)} %bitcast.6), calls=%async_computation.1 | async-start | bytes 786432 | tf_op jit(solution)/shard_map/all_to_all | solution.py:95
  96.6 0.1 copy.92
  96.7 0.1 copy.94
  96.9 7.4 %collective-permute-start.6 = (bf16[32,8,384]{2,1,0:T(8,128)(2,1)S(1)}, bf16[32,8,384]{2,1,0:T(8,128)(2,1)S(1)}, u32[]{:S(2)}, u32[]{:S(2)}) collective-permute-start(bf16[32,8,384]{2,1,0:T(8,128)(2,1)S(1)} %all-to-all-done.2), channel_id=1, source_target_pairs={{0,256},{256,0},{1,257},{257,1},{2,258},{258,2},{3,259},{259,3},{4... | collective-permute-start | bytes 589832 | tf_op jit(solution)/shard_map/ppermute | solution.py:123
  104.3 1.0 fusion.35
  105.4 0.1 copy.89
  105.5 0.1 copy.79
  105.6 0.1 copy.81
  105.8 0.1 copy.110
  105.9 0.1 copy.75
  106.0 18.2 %collective-permute-done.6 = bf16[32,8,384]{2,1,0:T(8,128)(2,1)S(1)} collective-permute-done((bf16[32,8,384]{2,1,0:T(8,128)(2,1)S(1)}, bf16[32,8,384]{2,1,0:T(8,128)(2,1)S(1)}, u32[]{:S(2)}, u32[]{:S(2)}) %collective-permute-start.6) | collective-permute-done | bytes 196640 | tf_op jit(solution)/shard_map/ppermute | solution.py:123
  124.3 1.4 gather_fusion.1
  125.6 7.4 %all-to-all-start.3 = ((bf16[32,2,8,384]{3,2,1,0:T(8,128)(2,1)}), bf16[32,2,8,384]{3,2,1,0:T(8,128)(2,1)S(1)}, u32[]{:S(2)}, u32[]{:S(2)}) async-start(bf16[32,2,8,384]{3,2,1,0:T(8,128)(2,1)} %bitcast.22), calls=%async_computation.3 | async-start | bytes 786432 | tf_op jit(solution)/shard_map/all_to_all | solution.py:95
  133.2 0.2 fusion.36
  133.6 0.2 copy.78
  133.8 0.3 fusion.4
  134.1 0.1 copy.102.refs_0_
  134.2 1.9 collective-permute-start.2
  136.2 4.3 %collective-permute-start.3 = (bf16[128,384]{1,0:T(8,128)(2,1)S(1)}, bf16[128,384]{1,0:T(8,128)(2,1)S(1)}, u32[]{:S(2)}, u32[]{:S(2)}) collective-permute-start(bf16[128,384]{1,0:T(8,128)(2,1)S(1)} %copy.102.refs_0_), channel_id=1, source_target_pairs={{0,2},{1,3},{2,0},{3,1},{4,6},{5,7},{6,4},{7,5},{8,10},{9,11},{10,... | collective-permute-start | bytes 294920 | tf_op jit(solution)/shard_map/ppermute | solution.py:134
  140.5 3.9 %collective-permute-start.4 = (bf16[128,384]{1,0:T(8,128)(2,1)S(1)}, bf16[128,384]{1,0:T(8,128)(2,1)S(1)}, u32[]{:S(2)}, u32[]{:S(2)}) collective-permute-start(bf16[128,384]{1,0:T(8,128)(2,1)S(1)} %copy.102.refs_0_), channel_id=1, source_target_pairs={{0,3},{1,2},{2,1},{3,0},{4,7},{5,6},{6,5},{7,4},{8,11},{9,10},{10,... | collective-permute-start | bytes 294920 | tf_op jit(solution)/shard_map/ppermute | solution.py:134
  144.7 0.2 copy.91
  144.8 0.2 fusion.37
  145.2 0.3 fusion.5
  145.4 0.1 copy.103.refs_4_
  145.6 2.0 %collective-permute-start.7 = (bf16[128,384]{1,0:T(8,128)(2,1)S(1)}, bf16[128,384]{1,0:T(8,128)(2,1)S(1)}, u32[]{:S(2)}, u32[]{:S(2)}) collective-permute-start(bf16[128,384]{1,0:T(8,128)(2,1)S(1)} %copy.103.refs_4_), channel_id=1, source_target_pairs={{0,1},{1,0},{2,3},{3,2},{4,5},{5,4},{6,7},{7,6},{8,9},{9,8},{10,11... | collective-permute-start | bytes 294920 | tf_op jit(solution)/shard_map/ppermute | solution.py:134
  147.6 4.3 %collective-permute-start.8 = (bf16[128,384]{1,0:T(8,128)(2,1)S(1)}, bf16[128,384]{1,0:T(8,128)(2,1)S(1)}, u32[]{:S(2)}, u32[]{:S(2)}) collective-permute-start(bf16[128,384]{1,0:T(8,128)(2,1)S(1)} %copy.103.refs_4_), channel_id=1, source_target_pairs={{0,2},{1,3},{2,0},{3,1},{4,6},{5,7},{6,4},{7,5},{8,10},{9,11},{10,... | collective-permute-start | bytes 294920 | tf_op jit(solution)/shard_map/ppermute | solution.py:134
  151.8 3.9 %collective-permute-start.9 = (bf16[128,384]{1,0:T(8,128)(2,1)S(1)}, bf16[128,384]{1,0:T(8,128)(2,1)S(1)}, u32[]{:S(2)}, u32[]{:S(2)}) collective-permute-start(bf16[128,384]{1,0:T(8,128)(2,1)S(1)} %copy.103.refs_4_), channel_id=1, source_target_pairs={{0,3},{1,2},{2,1},{3,0},{4,7},{5,6},{6,5},{7,4},{8,11},{9,10},{10,... | collective-permute-start | bytes 294920 | tf_op jit(solution)/shard_map/ppermute | solution.py:134
  155.8 0.8 collective-permute-done.8.refs_6_
  156.5 3.7 %collective-permute-done.9.refs_7_ = bf16[128,384]{1,0:T(8,128)(2,1)S(1)} collective-permute-done((bf16[128,384]{1,0:T(8,128)(2,1)S(1)}, bf16[128,384]{1,0:T(8,128)(2,1)S(1)}, u32[]{:S(2)}, u32[]{:S(2)}) %collective-permute-start.9) | collective-permute-done | bytes 98336 | tf_op jit(solution)/shard_map/ppermute | solution.py:134
  160.3 4.0 %shard_map.56 = bf16[128,768]{1,0:T(8,128)(2,1)S(1)} custom-call(s32[4]{0:T(128)S(1)} %iota_xor_fusion.order_ref, bf16[128,384]{1,0:T(8,128)(2,1)S(1)} %copy.102.refs_0_, bf16[128,384]{1,0:T(8,128)(2,1)S(1)} %collective-permute-done.2.refs_1_, bf16[128,384]{1,0:T(8,128)(2,1)S(1)} %collective-permute-done.3.refs_2_, ...), custom_call_target="tpu_custom_call" | custom-call | flops 603979776 | bytes 5505024 | tf_op jit(solution)/shard_map/pallas_call | solution.py:50
  164.2 3.8 %collective-permute-start.10 = (bf16[128,768]{1,0:T(8,128)(2,1)S(1)}, bf16[128,768]{1,0:T(8,128)(2,1)S(1)}, u32[]{:S(2)}, u32[]{:S(2)}) collective-permute-start(bf16[128,768]{1,0:T(8,128)(2,1)S(1)} %shard_map.56), channel_id=1, source_target_pairs={{0,4},{4,0},{1,5},{5,1},{2,6},{6,2},{3,7},{7,3},{8,12},{12,8},{9,1... | collective-permute-start | bytes 589832 | tf_op jit(solution)/shard_map/ppermute | solution.py:140
  168.1 4.0 %shard_map.55 = f32[128,768]{1,0:T(8,128)S(1)} custom-call(s32[4]{0:T(128)S(1)} %iota_xor_fusion.order_ref, bf16[128,384]{1,0:T(8,128)(2,1)S(1)} %copy.102.refs_0_, bf16[128,384]{1,0:T(8,128)(2,1)S(1)} %collective-permute-done.2.refs_1_, bf16[128,384]{1,0:T(8,128)(2,1)S(1)} %collective-permute-done.3.refs_2_, ...), custom_call_target="tpu_custom_call" | custom-call | flops 603979776 | bytes 5505024 | tf_op jit(solution)/shard_map/pallas_call | solution.py:50
  172.1 15.3 %collective-permute-done.10 = bf16[128,768]{1,0:T(8,128)(2,1)S(1)} collective-permute-done((bf16[128,768]{1,0:T(8,128)(2,1)S(1)}, bf16[128,768]{1,0:T(8,128)(2,1)S(1)}, u32[]{:S(2)}, u32[]{:S(2)}) %collective-permute-start.10) | collective-permute-done | bytes 196640 | tf_op jit(solution)/shard_map/ppermute | solution.py:140
  187.4 0.7 add_convert_fusion
  (33 shorter events, 1.2 us)
Async XLA Ops:
  8.3 21.7 %all-to-all-start = ((bf16[32,8,384]{2,1,0:T(8,128)(2,1)}), bf16[32,8,384]{2,1,0:T(8,128)(2,1)S(1)}, u32[]{:S(2)}, u32[]{:S(2)}) async-start(bf16[32,8,384]{2,1,0:T(8,128)(2,1)} %bitcast.4), calls=%async_computation | async-start | bytes 393216 | tf_op jit(solution)/shard_map/all_to_all | solution.py:95
  17.9 12.1 %collective-permute-start = (bf16[96,768]{1,0:T(8,128)(2,1)}, bf16[96,768]{1,0:T(8,128)(2,1)S(1)}, u32[]{:S(2)}, u32[]{:S(2)}) collective-permute-start(bf16[96,768]{1,0:T(8,128)(2,1)} %bitcast.76), channel_id=1, source_target_pairs={{0,0},{1,64},{2,128},{3,192},{64,1},{65,65},{66,129},{67,193},{128... | collective-permute-start | bytes 442376 | tf_op jit(solution)/shard_map/ppermute | solution.py:97
  30.0 24.4 %collective-permute-start.5 = (bf16[96,768]{1,0:T(8,128)(2,1)S(1)}, bf16[96,768]{1,0:T(8,128)(2,1)S(1)}, u32[]{:S(2)}, u32[]{:S(2)}) collective-permute-start(bf16[96,768]{1,0:T(8,128)(2,1)S(1)} %collective-permute-done), channel_id=1, source_target_pairs={{0,256},{256,0},{1,257},{257,1},{2,258},{258,2},{3,259},{259,3},{4... | collective-permute-start | bytes 442376 | tf_op jit(solution)/shard_map/ppermute | solution.py:110
  44.5 16.2 %all-to-all-start.2 = ((bf16[32,8,384]{2,1,0:T(8,128)(2,1)}), bf16[32,8,384]{2,1,0:T(8,128)(2,1)S(1)}, u32[]{:S(2)}, u32[]{:S(2)}) async-start(bf16[32,8,384]{2,1,0:T(8,128)(2,1)} %bitcast.21), calls=%async_computation.2 | async-start | bytes 393216 | tf_op jit(solution)/shard_map/all_to_all | solution.py:95
  54.4 105.9 %all-gather.3.cloned.1.call-start = ((), (), s32[]{:S(2)}) async-start(), calls=%async_computation.4 | async-start | bytes 9732096 | tf_op jit(solution)/shard_map/all_gather | solution.py:116
  60.8 28.9 %collective-permute-start.1 = (bf16[32,8,384]{2,1,0:T(8,128)(2,1)S(1)}, bf16[32,8,384]{2,1,0:T(8,128)(2,1)S(1)}, u32[]{:S(2)}, u32[]{:S(2)}) collective-permute-start(bf16[32,8,384]{2,1,0:T(8,128)(2,1)S(1)} %all-to-all-done), channel_id=1, source_target_pairs={{0,256},{256,0},{1,257},{257,1},{2,258},{258,2},{3,259},{259,3},{4... | collective-permute-start | bytes 589832 | tf_op jit(solution)/shard_map/ppermute | solution.py:123
  91.2 34.5 %all-to-all-start.1 = ((bf16[32,2,8,384]{3,2,1,0:T(8,128)(2,1)}), bf16[32,2,8,384]{3,2,1,0:T(8,128)(2,1)S(1)}, u32[]{:S(2)}, u32[]{:S(2)}) async-start(bf16[32,2,8,384]{3,2,1,0:T(8,128)(2,1)} %bitcast.6), calls=%async_computation.1 | async-start | bytes 786432 | tf_op jit(solution)/shard_map/all_to_all | solution.py:95
  96.9 27.4 %collective-permute-start.6 = (bf16[32,8,384]{2,1,0:T(8,128)(2,1)S(1)}, bf16[32,8,384]{2,1,0:T(8,128)(2,1)S(1)}, u32[]{:S(2)}, u32[]{:S(2)}) collective-permute-start(bf16[32,8,384]{2,1,0:T(8,128)(2,1)S(1)} %all-to-all-done.2), channel_id=1, source_target_pairs={{0,256},{256,0},{1,257},{257,1},{2,258},{258,2},{3,259},{259,3},{4... | collective-permute-start | bytes 589832 | tf_op jit(solution)/shard_map/ppermute | solution.py:123
  125.6 18.7 %all-to-all-start.3 = ((bf16[32,2,8,384]{3,2,1,0:T(8,128)(2,1)}), bf16[32,2,8,384]{3,2,1,0:T(8,128)(2,1)S(1)}, u32[]{:S(2)}, u32[]{:S(2)}) async-start(bf16[32,2,8,384]{3,2,1,0:T(8,128)(2,1)} %bitcast.22), calls=%async_computation.3 | async-start | bytes 786432 | tf_op jit(solution)/shard_map/all_to_all | solution.py:95
  134.2 17.6 %collective-permute-start.2 = (bf16[128,384]{1,0:T(8,128)(2,1)S(1)}, bf16[128,384]{1,0:T(8,128)(2,1)S(1)}, u32[]{:S(2)}, u32[]{:S(2)}) collective-permute-start(bf16[128,384]{1,0:T(8,128)(2,1)S(1)} %copy.102.refs_0_), channel_id=1, source_target_pairs={{0,1},{1,0},{2,3},{3,2},{4,5},{5,4},{6,7},{7,6},{8,9},{9,8},{10,11... | collective-permute-start | bytes 294920 | tf_op jit(solution)/shard_map/ppermute | solution.py:134
  136.2 19.6 %collective-permute-start.3 = (bf16[128,384]{1,0:T(8,128)(2,1)S(1)}, bf16[128,384]{1,0:T(8,128)(2,1)S(1)}, u32[]{:S(2)}, u32[]{:S(2)}) collective-permute-start(bf16[128,384]{1,0:T(8,128)(2,1)S(1)} %copy.102.refs_0_), channel_id=1, source_target_pairs={{0,2},{1,3},{2,0},{3,1},{4,6},{5,7},{6,4},{7,5},{8,10},{9,11},{10,... | collective-permute-start | bytes 294920 | tf_op jit(solution)/shard_map/ppermute | solution.py:134
  140.5 15.2 %collective-permute-start.4 = (bf16[128,384]{1,0:T(8,128)(2,1)S(1)}, bf16[128,384]{1,0:T(8,128)(2,1)S(1)}, u32[]{:S(2)}, u32[]{:S(2)}) collective-permute-start(bf16[128,384]{1,0:T(8,128)(2,1)S(1)} %copy.102.refs_0_), channel_id=1, source_target_pairs={{0,3},{1,2},{2,1},{3,0},{4,7},{5,6},{6,5},{7,4},{8,11},{9,10},{10,... | collective-permute-start | bytes 294920 | tf_op jit(solution)/shard_map/ppermute | solution.py:134
  145.6 10.2 %collective-permute-start.7 = (bf16[128,384]{1,0:T(8,128)(2,1)S(1)}, bf16[128,384]{1,0:T(8,128)(2,1)S(1)}, u32[]{:S(2)}, u32[]{:S(2)}) collective-permute-start(bf16[128,384]{1,0:T(8,128)(2,1)S(1)} %copy.103.refs_4_), channel_id=1, source_target_pairs={{0,1},{1,0},{2,3},{3,2},{4,5},{5,4},{6,7},{7,6},{8,9},{9,8},{10,11... | collective-permute-start | bytes 294920 | tf_op jit(solution)/shard_map/ppermute | solution.py:134
  147.6 9.0 %collective-permute-start.8 = (bf16[128,384]{1,0:T(8,128)(2,1)S(1)}, bf16[128,384]{1,0:T(8,128)(2,1)S(1)}, u32[]{:S(2)}, u32[]{:S(2)}) collective-permute-start(bf16[128,384]{1,0:T(8,128)(2,1)S(1)} %copy.103.refs_4_), channel_id=1, source_target_pairs={{0,2},{1,3},{2,0},{3,1},{4,6},{5,7},{6,4},{7,5},{8,10},{9,11},{10,... | collective-permute-start | bytes 294920 | tf_op jit(solution)/shard_map/ppermute | solution.py:134
  151.8 8.4 %collective-permute-start.9 = (bf16[128,384]{1,0:T(8,128)(2,1)S(1)}, bf16[128,384]{1,0:T(8,128)(2,1)S(1)}, u32[]{:S(2)}, u32[]{:S(2)}) collective-permute-start(bf16[128,384]{1,0:T(8,128)(2,1)S(1)} %copy.103.refs_4_), channel_id=1, source_target_pairs={{0,3},{1,2},{2,1},{3,0},{4,7},{5,6},{6,5},{7,4},{8,11},{9,10},{10,... | collective-permute-start | bytes 294920 | tf_op jit(solution)/shard_map/ppermute | solution.py:134
  164.2 23.1 %collective-permute-start.10 = (bf16[128,768]{1,0:T(8,128)(2,1)S(1)}, bf16[128,768]{1,0:T(8,128)(2,1)S(1)}, u32[]{:S(2)}, u32[]{:S(2)}) collective-permute-start(bf16[128,768]{1,0:T(8,128)(2,1)S(1)} %shard_map.56), channel_id=1, source_target_pairs={{0,4},{4,0},{1,5},{5,1},{2,6},{6,2},{3,7},{7,3},{8,12},{12,8},{9,1... | collective-permute-start | bytes 589832 | tf_op jit(solution)/shard_map/ppermute | solution.py:140
Sparse Core Ops, SparseCore 0:
  60.9 70.0 all-gather.2

commit v5 on v3

--- a/solution.py
+++ b/solution.py
@@ -16,7 +16,9 @@
 PLANE = ("x", "y", "c")
 SWAP = ((0, 1), (1, 0))
 QUAD = 4
-PIECE = 8
+HINT_FLOPS, HINT_BYTES = 170 * 10**9, 10**6
+HALVES = 2
+PIECE = 16
 
 
 def project_kernel(order_ref, *refs, side):
@@ -64,13 +66,58 @@
     )(order, *parts, pltpu.with_memory_space_constraint(w_all, pltpu.HBM))
 
 
+def attend_kernel(q_ref, k_ref, v_ref, routed_ref, out_ref):
+    tokens, width = q_ref.shape
+    part = width // HALVES
+    for head in range(width // HEAD_DIM):
+        cols = slice(head * HEAD_DIM, (head + 1) * HEAD_DIM)
+        at, lane = divmod(head * HEAD_DIM, part)
+
+        def rows(kind, turn):
+            piece = routed_ref[kind * HALVES + at, :, turn, :, lane : lane + HEAD_DIM]
+            return piece.reshape(tokens, HEAD_DIM)
+
+        query = q_ref[:, cols]
+        scores = [
+            lax.dot_general(
+                query, keys, (((1,), (1,)), ((), ())), preferred_element_type=jnp.float32
+            )
+            * (1.0 / HEAD_DIM**0.5)
+            for keys in [k_ref[:, cols]] + [rows(0, turn) for turn in range(ROUNDS)]
+        ]
+        peak = functools.reduce(jnp.maximum, scores)
+        peak = jnp.max(peak, axis=-1, keepdims=True)
+        exponents = [jnp.exp(score - peak) for score in scores]
+        row_total = jnp.sum(functools.reduce(jnp.add, exponents), axis=-1, keepdims=True)
+        summed = 0.0
+        for exponent, values in zip(
+            exponents, [v_ref[:, cols]] + [rows(1, turn) for turn in range(ROUNDS)]
+        ):
+            summed += jnp.dot(
+                exponent.astype(jnp.bfloat16), values, preferred_element_type=jnp.float32
+            )
+        out_ref[:, cols] = (summed / row_total).astype(out_ref.dtype)
+
+
+def attend(queries, keys, values, routed):
+    in_vmem = pl.BlockSpec(memory_space=pltpu.VMEM)
+    return pl.pallas_call(
+        attend_kernel,
+        in_specs=[in_vmem] * 4,
+        out_specs=in_vmem,
+        out_shape=jax.ShapeDtypeStruct(queries.shape, queries.dtype),
+        compiler_params=pltpu.CompilerParams(vmem_limit_bytes=32 << 20),
+        cost_estimate=pl.CostEstimate(
+            flops=HINT_FLOPS, bytes_accessed=HINT_BYTES, transcendentals=0
+        ),
+    )(queries, keys, values, routed)
+
+
 def body(queries, keys, values, plan, w_out):
     tokens, width = queries.shape
-    heads = width // HEAD_DIM
     half = lax.axis_index("zh")
     quad, member = lax.axis_index("p"), lax.axis_index("q")
     seats = lax.axis_size(PLANE)
-    pieces = tokens // PIECE
 
     w_near = lax.ppermute(
         w_out.T,
@@ -83,36 +130,27 @@
         (jnp.where(keeps_near, w_near, w_far), jnp.where(keeps_near, w_far, w_near))
     )
 
-    own = jnp.stack((keys, values)).reshape(2 * pieces, PIECE, width)
-    spread = lax.all_to_all(own, PLANE, split_axis=0, concat_axis=0, tiled=True)
-    spread, w_pair = lax.optimization_barrier((spread, w_pair))
-    far = lax.ppermute(spread, "zh", SWAP)
+    part = width // HALVES
+    own = jnp.stack(
+        [rows[:, h * part : (h + 1) * part] for rows in (keys, values) for h in range(HALVES)]
+    )
+    own = own.reshape(1, seats, PIECE, part)
+    own = jnp.broadcast_to(own, (2, seats, PIECE, part)).reshape(2 * seats, PIECE, part)
+    spread = lax.all_to_all(own, CTX, split_axis=0, concat_axis=0, tiled=True)
+    spread, _ = lax.optimization_barrier((spread, w_pair))
 
     w_all = lax.all_gather(w_pair, PLANE, axis=0, tiled=False)
     w_all = w_all.reshape(QUAD, seats // QUAD, 2, -1, width)
 
     wanted = lax.dynamic_slice_in_dim(plan, half * seats, seats, 1)
-    place = (wanted // seats ^ half) * seats + wanted % seats
-    chosen = jnp.concatenate((spread, far)).at[place.T].get(mode="promise_in_bounds")
+    chosen = spread.at[wanted.T].get(mode="promise_in_bounds")
     routed = lax.all_to_all(chosen, PLANE, split_axis=0, concat_axis=0, tiled=True)
-    routed = routed.reshape(2, pieces, ROUNDS, PIECE, width).transpose(0, 2, 1, 3, 4)
-    routed = routed.reshape(2, ROUNDS * tokens, width)
-
-    key_rows = jnp.concatenate((keys, routed[0])).reshape(-1, heads, HEAD_DIM)
-    value_rows = jnp.concatenate((values, routed[1])).reshape(-1, heads, HEAD_DIM)
-    query_rows = queries.reshape(tokens, heads, HEAD_DIM)
-    scores = jnp.einsum(
-        "qhd,khd->hqk", query_rows, key_rows, preferred_element_type=jnp.float32
-    ) * (1.0 / HEAD_DIM**0.5)
-    exponent = jnp.exp(scores - jnp.max(scores, axis=-1, keepdims=True))
-    row_total = jnp.sum(exponent, axis=-1)
-    summed = jnp.einsum(
-        "hqk,khd->qhd",
-        exponent.astype(jnp.bfloat16),
-        value_rows,
-        preferred_element_type=jnp.float32,
+    attended = attend(
+        queries,
+        keys,
+        values,
+        routed.reshape(2 * HALVES, tokens // PIECE, ROUNDS, PIECE, part),
     )
-    attended = (summed / row_total.T[:, :, None]).astype(jnp.bfloat16).reshape(tokens, width)
 
     parts = [attended] + [
         lax.ppermute(attended, "q", [(i, i ^ k) for i in range(QUAD)]) for k in range(1, QUAD)

time: 190 us -> 216 us (1.14)
  blocking collectives: 0 us -> 31.5 us
  waiting for transfers between devices: 98.3 us -> 87.6 us
  starting transfers between devices: 58.1 us -> 63.5 us
    ppermute x1 -> x0, waiting for transfers between devices: 39.1 us -> none  [body(): far = lax.ppermute(spread, 'zh', SWAP)]
    all_to_all x0 -> x1, blocking collectives: none -> 31.5 us  [body(): lax.all_to_all(chosen, PLANE, split_axis=0, concat_axis=0, tiled=True)]
    all_to_all x2 -> x1, waiting for transfers between devices: 25.7 us -> 0.01 us  [body(): spread = lax.all_to_all(own, CTX, split_axis=0, concat_axis=0, tiled=True)]
    all_gather x1, waiting for transfers between devices: 0.01 us -> 24.7 us  [body(): w_all = lax.all_gather(w_pair, PLANE, axis=0, tiled=False)]
    ppermute x1, waiting for transfers between devices: 5.35 us -> 25 us  [body(): lax.ppermute(w_out.T, ('x', 'q'), [(x * QUAD + q, q * QUAD + x) for x in...]
    ppermute x1, waiting for transfers between devices: 0.01 us -> 12.5 us  [body(): w_far = lax.ppermute(w_near, 'zh', SWAP)]
    ppermute x3, starting transfers between devices: 10.1 us -> 18.2 us  [body(): lax.ppermute(attended, 'q', [(i, i ^ k) for i in range(QUAD)])]
    ppermute x1, starting transfers between devices: 3.25 us -> 7.64 us  [body(): arrived = lax.ppermute(sent, 'p', SWAP)]
  transfers between devices with their start and end apart: 10 -> 8, of which waited for: 6 -> 5; matrix products, arithmetic and copies ran while one was open for 4% -> 1% of each run, Pallas kernels for 2% -> 3%
where the time goes in v5:
time: 216 us; the launch traced here: 215 us
  waiting for transfers between devices  87.6 us (41%)
  starting transfers between devices  63.5 us (29%)
  blocking collectives  31.5 us (15%)
  between operations  13.6 us (6%)
  Pallas kernels  10.3 us (5%)
  local copies, waits for them, and re-layouts  5.74 us (3%)
  other arithmetic  2.34 us (1%)
    all_to_all x1, blocking collectives, body(): lax.all_to_all(chosen, PLANE, split_axis=0, concat_axis=0, tiled=True)  31.5 us
    ppermute x1, waiting for transfers between devices, body(): lax.ppermute(w_out.T, ('x', 'q'), [(x * QUAD + q, q * QUAD + x) for x in...  25 us
    all_gather x1, waiting for transfers between devices, body(): w_all = lax.all_gather(w_pair, PLANE, axis=0, tiled=False)  24.7 us
    all_to_all x1, starting transfers between devices, body(): spread = lax.all_to_all(own, CTX, split_axis=0, concat_axis=0, tiled=True)  21.3 us
    ppermute x3, starting transfers between devices, body(): lax.ppermute(attended, 'q', [(i, i ^ k) for i in range(QUAD)])  18.2 us
    ppermute x1, waiting for transfers between devices, body(): arrived = lax.ppermute(sent, 'p', SWAP)  13.8 us
    ppermute x1, starting transfers between devices, body(): w_far = lax.ppermute(w_near, 'zh', SWAP)  12.7 us
    ppermute x1, waiting for transfers between devices, body(): w_far = lax.ppermute(w_near, 'zh', SWAP)  12.5 us
  transfers between devices with their start and end apart: 8, of which 5 were waited for; matrix products, arithmetic and copies ran while one was open for 1% of the time, Pallas kernels for 3%

profile of v5, /device:TPU:6, one launch (start us, length us, event | category | flops | bytes accessed | tf_op | source)
XLA Modules:
  0.0 214.5 jit_solution(6804383515011395424)
XLA Ops:
  6.5 1.1 slice_bitcast_fusion.1
  7.6 0.1 pad_maximum_fusion
  7.7 1.0 broadcast_in_dim.11
  8.7 21.3 %all-to-all-start = ((bf16[64,16,384]{2,1,0:T(8,128)(2,1)}), bf16[64,16,384]{2,1,0:T(8,128)(2,1)S(1)}, u32[]{:S(2)}, u32[]{:S(2)}) async-start(bf16[64,16,384]{2,1,0:T(8,128)(2,1)} %bitcast.5), calls=%async_computation | async-start | bytes 1572864 | tf_op jit(solution)/shard_map/all_to_all | solution.py:139
  29.9 0.0 all-gather.3.cloned.1.call-start
  30.0 3.7 %collective-permute-start = (bf16[96,768]{1,0:T(8,128)(2,1)}, bf16[96,768]{1,0:T(8,128)(2,1)S(1)}, u32[]{:S(2)}, u32[]{:S(2)}) collective-permute-start(bf16[96,768]{1,0:T(8,128)(2,1)} %bitcast.25), channel_id=1, source_target_pairs={{0,0},{1,64},{2,128},{3,192},{64,1},{65,65},{66,129},{67,193},{128... | collective-permute-start | bytes 442376 | tf_op jit(solution)/shard_map/ppermute | solution.py:122
  33.7 25.0 %collective-permute-done = bf16[96,768]{1,0:T(8,128)(2,1)S(1)} collective-permute-done((bf16[96,768]{1,0:T(8,128)(2,1)}, bf16[96,768]{1,0:T(8,128)(2,1)S(1)}, u32[]{:S(2)}, u32[]{:S(2)}) %collective-permute-start) | collective-permute-done | bytes 147488 | tf_op jit(solution)/shard_map/ppermute | solution.py:122
  58.7 12.7 %collective-permute-start.1 = (bf16[96,768]{1,0:T(8,128)(2,1)S(1)}, bf16[96,768]{1,0:T(8,128)(2,1)S(1)}, u32[]{:S(2)}, u32[]{:S(2)}) collective-permute-start(bf16[96,768]{1,0:T(8,128)(2,1)S(1)} %collective-permute-done), channel_id=1, source_target_pairs={{0,256},{256,0},{1,257},{257,1},{2,258},{258,2},{3,259},{259,3},{4... | collective-permute-start | bytes 442376 | tf_op jit(solution)/shard_map/ppermute | solution.py:127
  71.4 12.5 %collective-permute-done.1 = bf16[96,768]{1,0:T(8,128)(2,1)S(1)} collective-permute-done((bf16[96,768]{1,0:T(8,128)(2,1)S(1)}, bf16[96,768]{1,0:T(8,128)(2,1)S(1)}, u32[]{:S(2)}, u32[]{:S(2)}) %collective-permute-start.1) | collective-permute-done | bytes 147488 | tf_op jit(solution)/shard_map/ppermute | solution.py:127
  83.9 0.8 pad_maximum_fusion.1
  84.7 0.0 all-gather.3.cloned.1.call-update
  84.7 0.8 compare_select_fusion
  85.5 0.1 copy.8
  85.6 0.1 reshape.16
  85.7 0.0 all-to-all-done
  85.7 0.7 gather_fusion
  86.4 31.5 %all_to_all.10 = bf16[32,2,16,384]{3,2,1,0:T(8,128)(2,1)S(1)} all-to-all(bf16[32,2,16,384]{3,2,1,0:T(8,128)(2,1)S(1)} %bitcast.23), channel_id=1, replica_groups=mesh['zh'=2,'x'=4,'y'=4,'c'=2,'p'=2,'q'=4] {'x','y','c'}, dimensions={0} | all-to-all | bytes 1572864 | tf_op jit(solution)/shard_map/all_to_all | solution.py:147
  117.9 0.0 copy-start
  117.9 0.9 copy-done
  118.9 0.0 copy-start.1
  118.9 0.9 copy-done.1
  119.8 0.0 copy-start.2
  119.8 0.9 copy-done.2
  120.7 1.9 shard_map.55.refs_0_
  122.6 12.0 %collective-permute-start.2 = (bf16[128,768]{1,0:T(8,128)(2,1)S(1)}, bf16[128,768]{1,0:T(8,128)(2,1)S(1)}, u32[]{:S(2)}, u32[]{:S(2)}) collective-permute-start(bf16[128,768]{1,0:T(8,128)(2,1)S(1)} %shard_map.55.refs_0_), channel_id=1, source_target_pairs={{0,1},{1,0},{2,3},{3,2},{4,5},{5,4},{6,7},{7,6},{8,9},{9,8},{10,11... | collective-permute-start | bytes 589832 | tf_op jit(solution)/shard_map/ppermute | solution.py:156
  134.6 1.9 collective-permute-start.3
  136.6 4.3 %collective-permute-start.4 = (bf16[128,768]{1,0:T(8,128)(2,1)S(1)}, bf16[128,768]{1,0:T(8,128)(2,1)S(1)}, u32[]{:S(2)}, u32[]{:S(2)}) collective-permute-start(bf16[128,768]{1,0:T(8,128)(2,1)S(1)} %shard_map.55.refs_0_), channel_id=1, source_target_pairs={{0,3},{1,2},{2,1},{3,0},{4,7},{5,6},{6,5},{7,4},{8,11},{9,10},{10,... | collective-permute-start | bytes 589832 | tf_op jit(solution)/shard_map/ppermute | solution.py:156
  140.9 0.0 collective-permute-done.2.refs_1_
  140.9 11.6 %collective-permute-done.3.refs_2_ = bf16[128,768]{1,0:T(8,128)(2,1)S(1)} collective-permute-done((bf16[128,768]{1,0:T(8,128)(2,1)S(1)}, bf16[128,768]{1,0:T(8,128)(2,1)S(1)}, u32[]{:S(2)}, u32[]{:S(2)}) %collective-permute-start.3) | collective-permute-done | bytes 196640 | tf_op jit(solution)/shard_map/ppermute | solution.py:156
  152.5 0.0 collective-permute-done.4.refs_3_
  152.5 24.7 %all-gather.3.cloned.1.call-done = bf16[64,96,768]{2,1,0:T(8,128)(2,1)} async-done(((bf16[2,96,768]{2,1,0:T(8,128)(2,1)}), bf16[64,96,768]{2,1,0:T(8,128)(2,1)}) %all-gather.3.cloned.1.call-update) | async-done | bytes 9437200 | tf_op jit(solution)/shard_map/all_gather | solution.py:142
  177.2 4.2 %shard_map.57 = bf16[128,768]{1,0:T(8,128)(2,1)S(1)} custom-call(s32[4]{0:T(128)S(1)} %iota_xor_fusion.order_ref, bf16[128,768]{1,0:T(8,128)(2,1)S(1)} %shard_map.55.refs_0_, bf16[128,768]{1,0:T(8,128)(2,1)S(1)} %collective-permute-done.2.refs_1_, bf16[128,768]{1,0:T(8,128)(2,1)S(1)} %collective-permute-done.3.refs_2_, ...), custom_call_target="tpu_custom_call" | custom-call | flops 603979776 | bytes 5505024 | tf_op jit(solution)/shard_map/pallas_call | solution.py:49
  181.4 7.6 %collective-permute-start.5 = (bf16[128,768]{1,0:T(8,128)(2,1)S(1)}, bf16[128,768]{1,0:T(8,128)(2,1)S(1)}, u32[]{:S(2)}, u32[]{:S(2)}) collective-permute-start(bf16[128,768]{1,0:T(8,128)(2,1)S(1)} %shard_map.57), channel_id=1, source_target_pairs={{0,4},{4,0},{1,5},{5,1},{2,6},{6,2},{3,7},{7,3},{8,12},{12,8},{9,1... | collective-permute-start | bytes 589832 | tf_op jit(solution)/shard_map/ppermute | solution.py:160
  189.0 4.2 %shard_map.56 = f32[128,768]{1,0:T(8,128)S(1)} custom-call(s32[4]{0:T(128)S(1)} %iota_xor_fusion.order_ref, bf16[128,768]{1,0:T(8,128)(2,1)S(1)} %shard_map.55.refs_0_, bf16[128,768]{1,0:T(8,128)(2,1)S(1)} %collective-permute-done.2.refs_1_, bf16[128,768]{1,0:T(8,128)(2,1)S(1)} %collective-permute-done.3.refs_2_, ...), custom_call_target="tpu_custom_call" | custom-call | flops 603979776 | bytes 5505024 | tf_op jit(solution)/shard_map/pallas_call | solution.py:49
  193.2 13.8 %collective-permute-done.5 = bf16[128,768]{1,0:T(8,128)(2,1)S(1)} collective-permute-done((bf16[128,768]{1,0:T(8,128)(2,1)S(1)}, bf16[128,768]{1,0:T(8,128)(2,1)S(1)}, u32[]{:S(2)}, u32[]{:S(2)}) %collective-permute-start.5) | collective-permute-done | bytes 196640 | tf_op jit(solution)/shard_map/ppermute | solution.py:160
  207.0 0.7 add_convert_fusion
  (3 shorter events, 0.0 us)
Async XLA Ops:
  8.7 77.0 %all-to-all-start = ((bf16[64,16,384]{2,1,0:T(8,128)(2,1)}), bf16[64,16,384]{2,1,0:T(8,128)(2,1)S(1)}, u32[]{:S(2)}, u32[]{:S(2)}) async-start(bf16[64,16,384]{2,1,0:T(8,128)(2,1)} %bitcast.5), calls=%async_computation | async-start | bytes 1572864 | tf_op jit(solution)/shard_map/all_to_all | solution.py:139
  29.9 147.2 %all-gather.3.cloned.1.call-start = ((), (), s32[]{:S(2)}) async-start(), calls=%async_computation.2 | async-start | bytes 9732096 | tf_op jit(solution)/shard_map/all_gather | solution.py:142
  30.0 28.7 %collective-permute-start = (bf16[96,768]{1,0:T(8,128)(2,1)}, bf16[96,768]{1,0:T(8,128)(2,1)S(1)}, u32[]{:S(2)}, u32[]{:S(2)}) collective-permute-start(bf16[96,768]{1,0:T(8,128)(2,1)} %bitcast.25), channel_id=1, source_target_pairs={{0,0},{1,64},{2,128},{3,192},{64,1},{65,65},{66,129},{67,193},{128... | collective-permute-start | bytes 442376 | tf_op jit(solution)/shard_map/ppermute | solution.py:122
  58.7 25.2 %collective-permute-start.1 = (bf16[96,768]{1,0:T(8,128)(2,1)S(1)}, bf16[96,768]{1,0:T(8,128)(2,1)S(1)}, u32[]{:S(2)}, u32[]{:S(2)}) collective-permute-start(bf16[96,768]{1,0:T(8,128)(2,1)S(1)} %collective-permute-done), channel_id=1, source_target_pairs={{0,256},{256,0},{1,257},{257,1},{2,258},{258,2},{3,259},{259,3},{4... | collective-permute-start | bytes 442376 | tf_op jit(solution)/shard_map/ppermute | solution.py:127
  117.9 0.9 copy-start
  118.9 0.9 copy-start.1
  119.8 0.9 copy-start.2
  122.6 18.3 %collective-permute-start.2 = (bf16[128,768]{1,0:T(8,128)(2,1)S(1)}, bf16[128,768]{1,0:T(8,128)(2,1)S(1)}, u32[]{:S(2)}, u32[]{:S(2)}) collective-permute-start(bf16[128,768]{1,0:T(8,128)(2,1)S(1)} %shard_map.55.refs_0_), channel_id=1, source_target_pairs={{0,1},{1,0},{2,3},{3,2},{4,5},{5,4},{6,7},{7,6},{8,9},{9,8},{10,11... | collective-permute-start | bytes 589832 | tf_op jit(solution)/shard_map/ppermute | solution.py:156
  134.6 17.9 %collective-permute-start.3 = (bf16[128,768]{1,0:T(8,128)(2,1)S(1)}, bf16[128,768]{1,0:T(8,128)(2,1)S(1)}, u32[]{:S(2)}, u32[]{:S(2)}) collective-permute-start(bf16[128,768]{1,0:T(8,128)(2,1)S(1)} %shard_map.55.refs_0_), channel_id=1, source_target_pairs={{0,2},{1,3},{2,0},{3,1},{4,6},{5,7},{6,4},{7,5},{8,10},{9,11},{10,... | collective-permute-start | bytes 589832 | tf_op jit(solution)/shard_map/ppermute | solution.py:156
  136.6 16.0 %collective-permute-start.4 = (bf16[128,768]{1,0:T(8,128)(2,1)S(1)}, bf16[128,768]{1,0:T(8,128)(2,1)S(1)}, u32[]{:S(2)}, u32[]{:S(2)}) collective-permute-start(bf16[128,768]{1,0:T(8,128)(2,1)S(1)} %shard_map.55.refs_0_), channel_id=1, source_target_pairs={{0,3},{1,2},{2,1},{3,0},{4,7},{5,6},{6,5},{7,4},{8,11},{9,10},{10,... | collective-permute-start | bytes 589832 | tf_op jit(solution)/shard_map/ppermute | solution.py:156
  181.4 25.6 %collective-permute-start.5 = (bf16[128,768]{1,0:T(8,128)(2,1)S(1)}, bf16[128,768]{1,0:T(8,128)(2,1)S(1)}, u32[]{:S(2)}, u32[]{:S(2)}) collective-permute-start(bf16[128,768]{1,0:T(8,128)(2,1)S(1)} %shard_map.57), channel_id=1, source_target_pairs={{0,4},{4,0},{1,5},{5,1},{2,6},{6,2},{3,7},{7,3},{8,12},{12,8},{9,1... | collective-permute-start | bytes 589832 | tf_op jit(solution)/shard_map/ppermute | solution.py:160
Sparse Core Ops, SparseCore 0:
  84.8 92.2 all-gather.2

commit v6 on v5

--- a/solution.py
+++ b/solution.py
@@ -16,7 +16,7 @@
 PLANE = ("x", "y", "c")
 SWAP = ((0, 1), (1, 0))
 QUAD = 4
-HINT_FLOPS, HINT_BYTES = 170 * 10**9, 10**6
+HINT_FLOPS, HINT_BYTES = 182 * 10**9, 10**6
 HALVES = 2
 PIECE = 16
 
@@ -124,26 +124,27 @@
         ("x", "q"),
         [(x * QUAD + q, q * QUAD + x) for x in range(QUAD) for q in range(QUAD)],
     )
-    w_far = lax.ppermute(w_near, "zh", SWAP)
-    keeps_near = half == quad
-    w_pair = jnp.stack(
-        (jnp.where(keeps_near, w_near, w_far), jnp.where(keeps_near, w_far, w_near))
-    )
 
     part = width // HALVES
     own = jnp.stack(
         [rows[:, h * part : (h + 1) * part] for rows in (keys, values) for h in range(HALVES)]
     )
-    own = own.reshape(1, seats, PIECE, part)
-    own = jnp.broadcast_to(own, (2, seats, PIECE, part)).reshape(2 * seats, PIECE, part)
-    spread = lax.all_to_all(own, CTX, split_axis=0, concat_axis=0, tiled=True)
-    spread, _ = lax.optimization_barrier((spread, w_pair))
+    own = own.reshape(seats, PIECE, part)
+    spread = lax.all_to_all(own, PLANE, split_axis=0, concat_axis=0, tiled=True)
+    spread, w_near = lax.optimization_barrier((spread, w_near))
 
+    w_far = lax.ppermute(w_near, "zh", SWAP)
+    far = lax.ppermute(spread, "zh", SWAP)
+    keeps_near = half == quad
+    w_pair = jnp.stack(
+        (jnp.where(keeps_near, w_near, w_far), jnp.where(keeps_near, w_far, w_near))
+    )
     w_all = lax.all_gather(w_pair, PLANE, axis=0, tiled=False)
     w_all = w_all.reshape(QUAD, seats // QUAD, 2, -1, width)
 
     wanted = lax.dynamic_slice_in_dim(plan, half * seats, seats, 1)
-    chosen = spread.at[wanted.T].get(mode="promise_in_bounds")
+    place = (wanted // seats ^ half) * seats + wanted % seats
+    chosen = jnp.concatenate((spread, far)).at[place.T].get(mode="promise_in_bounds")
     routed = lax.all_to_all(chosen, PLANE, split_axis=0, concat_axis=0, tiled=True)
     attended = attend(
         queries,

time: 216 us -> 188 us (0.87)
  starting transfers between devices: 63.5 us -> 47.3 us
  blocking collectives: 31.5 us -> 20.1 us
    ppermute x0 -> x1, waiting for transfers between devices: none -> 27.4 us  [body(): far = lax.ppermute(spread, 'zh', SWAP)]
    ppermute x1, waiting for transfers between devices: 25 us -> 7.88 us  [body(): lax.ppermute(w_out.T, ('x', 'q'), [(x * QUAD + q, q * QUAD + x) for x in...]
    all_gather x1, waiting for transfers between devices: 24.7 us -> 8.28 us  [body(): w_all = lax.all_gather(w_pair, PLANE, axis=0, tiled=False)]
    all_to_all x1, starting transfers between devices: 21.3 us -> 9.54 us  [body(): spread = lax.all_to_all(own, PLANE, split_axis=0, concat_axis=0, tiled=True)]
    all_to_all x1, blocking collectives: 31.5 us -> 20.1 us  [body(): lax.all_to_all(chosen, PLANE, split_axis=0, concat_axis=0, tiled=True)]
    ppermute x3, starting transfers between devices: 18.2 us -> 10.1 us  [body(): lax.ppermute(attended, 'q', [(i, i ^ k) for i in range(QUAD)])]
    ppermute x1, waiting for transfers between devices: 12.5 us -> 19.9 us  [body(): w_far = lax.ppermute(w_near, 'zh', SWAP)]
  transfers between devices with their start and end apart: 8 -> 9, of which waited for: 5 -> 7; matrix products, arithmetic and copies ran while one was open for 1% -> 1% of each run, Pallas kernels for 3% -> 3%
where the time goes in v6:
time: 188 us; the launch traced here: 187 us
  waiting for transfers between devices  88 us (47%)
  starting transfers between devices  47.3 us (25%)
  blocking collectives  20.1 us (11%)
  between operations  13.5 us (7%)
  Pallas kernels  10.3 us (5%)
  local copies, waits for them, and re-layouts  4.77 us (3%)
  other arithmetic  3.18 us (2%)
    ppermute x1, waiting for transfers between devices, body(): far = lax.ppermute(spread, 'zh', SWAP)  27.4 us
    all_to_all x1, blocking collectives, body(): lax.all_to_all(chosen, PLANE, split_axis=0, concat_axis=0, tiled=True)  20.1 us
    ppermute x1, waiting for transfers between devices, body(): w_far = lax.ppermute(w_near, 'zh', SWAP)  19.9 us
    ppermute x1, starting transfers between devices, body(): w_far = lax.ppermute(w_near, 'zh', SWAP)  13.8 us
    ppermute x1, waiting for transfers between devices, body(): arrived = lax.ppermute(sent, 'p', SWAP)  13.7 us
    ppermute x3, waiting for transfers between devices, body(): lax.ppermute(attended, 'q', [(i, i ^ k) for i in range(QUAD)])  10.8 us
    ppermute x3, starting transfers between devices, body(): lax.ppermute(attended, 'q', [(i, i ^ k) for i in range(QUAD)])  10.1 us
    all_to_all x1, starting transfers between devices, body(): spread = lax.all_to_all(own, PLANE, split_axis=0, concat_axis=0, tiled=True)  9.54 us
  transfers between devices with their start and end apart: 9, of which 7 were waited for; matrix products, arithmetic and copies ran while one was open for 1% of the time, Pallas kernels for 3%

profile of v6, /device:TPU:6, one launch (start us, length us, event | category | flops | bytes accessed | tf_op | source)
XLA Modules:
  0.0 187.1 jit_solution(2833329125068804669)
XLA Ops:
  6.5 1.1 slice_bitcast_fusion.1
  7.6 0.8 pad_maximum_fusion.1
  8.4 9.5 %all-to-all-start = ((bf16[32,16,384]{2,1,0:T(8,128)(2,1)}), bf16[32,16,384]{2,1,0:T(8,128)(2,1)S(1)}, u32[]{:S(2)}, u32[]{:S(2)}) async-start(bf16[32,16,384]{2,1,0:T(8,128)(2,1)} %bitcast.4), calls=%async_computation | async-start | bytes 786432 | tf_op jit(solution)/shard_map/all_to_all | solution.py:133
  18.0 0.0 all-gather.3.cloned.1.call-start
  18.0 4.2 %collective-permute-start = (bf16[96,768]{1,0:T(8,128)(2,1)}, bf16[96,768]{1,0:T(8,128)(2,1)S(1)}, u32[]{:S(2)}, u32[]{:S(2)}) collective-permute-start(bf16[96,768]{1,0:T(8,128)(2,1)} %bitcast.23), channel_id=1, source_target_pairs={{0,0},{1,64},{2,128},{3,192},{64,1},{65,65},{66,129},{67,193},{128... | collective-permute-start | bytes 442376 | tf_op jit(solution)/shard_map/ppermute | solution.py:122
  22.3 7.9 %collective-permute-done = bf16[96,768]{1,0:T(8,128)(2,1)S(1)} collective-permute-done((bf16[96,768]{1,0:T(8,128)(2,1)}, bf16[96,768]{1,0:T(8,128)(2,1)S(1)}, u32[]{:S(2)}, u32[]{:S(2)}) %collective-permute-start) | collective-permute-done | bytes 147488 | tf_op jit(solution)/shard_map/ppermute | solution.py:122
  30.2 0.0 all-to-all-done
  30.2 13.8 %collective-permute-start.5 = (bf16[96,768]{1,0:T(8,128)(2,1)S(1)}, bf16[96,768]{1,0:T(8,128)(2,1)S(1)}, u32[]{:S(2)}, u32[]{:S(2)}) collective-permute-start(bf16[96,768]{1,0:T(8,128)(2,1)S(1)} %collective-permute-done), channel_id=1, source_target_pairs={{0,256},{256,0},{1,257},{257,1},{2,258},{258,2},{3,259},{259,3},{4... | collective-permute-start | bytes 442376 | tf_op jit(solution)/shard_map/ppermute | solution.py:136
  44.0 1.9 %collective-permute-start.1 = (bf16[32,16,384]{2,1,0:T(8,128)(2,1)S(1)}, bf16[32,16,384]{2,1,0:T(8,128)(2,1)S(1)}, u32[]{:S(2)}, u32[]{:S(2)}) collective-permute-start(bf16[32,16,384]{2,1,0:T(8,128)(2,1)S(1)} %all-to-all-done), channel_id=1, source_target_pairs={{0,256},{256,0},{1,257},{257,1},{2,258},{258,2},{3,259},{259,3},{4... | collective-permute-start | bytes 1179656 | tf_op jit(solution)/shard_map/ppermute | solution.py:137
  45.9 19.9 %collective-permute-done.5 = bf16[96,768]{1,0:T(8,128)(2,1)S(1)} collective-permute-done((bf16[96,768]{1,0:T(8,128)(2,1)S(1)}, bf16[96,768]{1,0:T(8,128)(2,1)S(1)}, u32[]{:S(2)}, u32[]{:S(2)}) %collective-permute-start.5) | collective-permute-done | bytes 147488 | tf_op jit(solution)/shard_map/ppermute | solution.py:136
  65.8 0.7 pad_maximum_fusion.2
  66.5 0.0 all-gather.3.cloned.1.call-update
  66.5 0.8 compare_select_fusion
  67.3 0.1 copy.8
  67.4 0.1 reshape.14
  67.5 27.4 %collective-permute-done.1 = bf16[32,16,384]{2,1,0:T(8,128)(2,1)S(1)} collective-permute-done((bf16[32,16,384]{2,1,0:T(8,128)(2,1)S(1)}, bf16[32,16,384]{2,1,0:T(8,128)(2,1)S(1)}, u32[]{:S(2)}, u32[]{:S(2)}) %collective-permute-start.1) | collective-permute-done | bytes 393248 | tf_op jit(solution)/shard_map/ppermute | solution.py:137
  94.9 0.1 pad_maximum_fusion
  95.0 0.7 gather_fusion
  95.7 20.1 %all_to_all.10 = bf16[32,2,16,384]{3,2,1,0:T(8,128)(2,1)S(1)} all-to-all(bf16[32,2,16,384]{3,2,1,0:T(8,128)(2,1)S(1)} %bitcast.22), channel_id=1, replica_groups=mesh['zh'=2,'x'=4,'y'=4,'c'=2,'p'=2,'q'=4] {'x','y','c'}, dimensions={0} | all-to-all | bytes 1572864 | tf_op jit(solution)/shard_map/all_to_all | solution.py:148
  115.8 0.0 copy-start
  115.9 0.9 copy-done
  116.8 0.0 copy-start.1
  116.8 0.9 copy-done.1
  117.7 0.0 copy-start.2
  117.7 0.9 copy-done.2
  118.6 1.9 %shard_map.55.refs_0_ = bf16[128,768]{1,0:T(8,128)(2,1)S(1)} custom-call(bf16[128,768]{1,0:T(8,128)(2,1)S(1)} %copy-done.2, bf16[128,768]{1,0:T(8,128)(2,1)S(1)} %copy-done, bf16[128,768]{1,0:T(8,128)(2,1)S(1)} %copy-done.1, bf16[4,8,2,16,384]{4,3,2,1,0:T(8,128)(2,1)S(1)} %bitcast.19), custom_call_target="tpu_custom_call" | custom-call | flops 181999992832 | bytes 1000000 | tf_op jit(solution)/shard_map/pallas_call | solution.py:104
  120.5 1.9 %collective-permute-start.2 = (bf16[128,768]{1,0:T(8,128)(2,1)S(1)}, bf16[128,768]{1,0:T(8,128)(2,1)S(1)}, u32[]{:S(2)}, u32[]{:S(2)}) collective-permute-start(bf16[128,768]{1,0:T(8,128)(2,1)S(1)} %shard_map.55.refs_0_), channel_id=1, source_target_pairs={{0,1},{1,0},{2,3},{3,2},{4,5},{5,4},{6,7},{7,6},{8,9},{9,8},{10,11... | collective-permute-start | bytes 589832 | tf_op jit(solution)/shard_map/ppermute | solution.py:157
  122.4 1.9 %collective-permute-start.3 = (bf16[128,768]{1,0:T(8,128)(2,1)S(1)}, bf16[128,768]{1,0:T(8,128)(2,1)S(1)}, u32[]{:S(2)}, u32[]{:S(2)}) collective-permute-start(bf16[128,768]{1,0:T(8,128)(2,1)S(1)} %shard_map.55.refs_0_), channel_id=1, source_target_pairs={{0,2},{1,3},{2,0},{3,1},{4,6},{5,7},{6,4},{7,5},{8,10},{9,11},{10,... | collective-permute-start | bytes 589832 | tf_op jit(solution)/shard_map/ppermute | solution.py:157
  124.4 6.3 %collective-permute-start.4 = (bf16[128,768]{1,0:T(8,128)(2,1)S(1)}, bf16[128,768]{1,0:T(8,128)(2,1)S(1)}, u32[]{:S(2)}, u32[]{:S(2)}) collective-permute-start(bf16[128,768]{1,0:T(8,128)(2,1)S(1)} %shard_map.55.refs_0_), channel_id=1, source_target_pairs={{0,3},{1,2},{2,1},{3,0},{4,7},{5,6},{6,5},{7,4},{8,11},{9,10},{10,... | collective-permute-start | bytes 589832 | tf_op jit(solution)/shard_map/ppermute | solution.py:157
  130.7 0.1 collective-permute-done.2.refs_1_
  130.7 10.7 %collective-permute-done.3.refs_2_ = bf16[128,768]{1,0:T(8,128)(2,1)S(1)} collective-permute-done((bf16[128,768]{1,0:T(8,128)(2,1)S(1)}, bf16[128,768]{1,0:T(8,128)(2,1)S(1)}, u32[]{:S(2)}, u32[]{:S(2)}) %collective-permute-start.3) | collective-permute-done | bytes 196640 | tf_op jit(solution)/shard_map/ppermute | solution.py:157
  141.4 0.0 collective-permute-done.4.refs_3_
  141.4 8.3 %all-gather.3.cloned.1.call-done = bf16[64,96,768]{2,1,0:T(8,128)(2,1)} async-done(((bf16[2,96,768]{2,1,0:T(8,128)(2,1)}), bf16[64,96,768]{2,1,0:T(8,128)(2,1)}) %all-gather.3.cloned.1.call-update) | async-done | bytes 9437200 | tf_op jit(solution)/shard_map/all_gather | solution.py:142
  149.7 4.2 %shard_map.57 = bf16[128,768]{1,0:T(8,128)(2,1)S(1)} custom-call(s32[4]{0:T(128)S(1)} %iota_xor_fusion.order_ref, bf16[128,768]{1,0:T(8,128)(2,1)S(1)} %shard_map.55.refs_0_, bf16[128,768]{1,0:T(8,128)(2,1)S(1)} %collective-permute-done.2.refs_1_, bf16[128,768]{1,0:T(8,128)(2,1)S(1)} %collective-permute-done.3.refs_2_, ...), custom_call_target="tpu_custom_call" | custom-call | flops 603979776 | bytes 5505024 | tf_op jit(solution)/shard_map/pallas_call | solution.py:49
  153.9 7.6 %collective-permute-start.6 = (bf16[128,768]{1,0:T(8,128)(2,1)S(1)}, bf16[128,768]{1,0:T(8,128)(2,1)S(1)}, u32[]{:S(2)}, u32[]{:S(2)}) collective-permute-start(bf16[128,768]{1,0:T(8,128)(2,1)S(1)} %shard_map.57), channel_id=1, source_target_pairs={{0,4},{4,0},{1,5},{5,1},{2,6},{6,2},{3,7},{7,3},{8,12},{12,8},{9,1... | collective-permute-start | bytes 589832 | tf_op jit(solution)/shard_map/ppermute | solution.py:161
  161.6 4.2 %shard_map.56 = f32[128,768]{1,0:T(8,128)S(1)} custom-call(s32[4]{0:T(128)S(1)} %iota_xor_fusion.order_ref, bf16[128,768]{1,0:T(8,128)(2,1)S(1)} %shard_map.55.refs_0_, bf16[128,768]{1,0:T(8,128)(2,1)S(1)} %collective-permute-done.2.refs_1_, bf16[128,768]{1,0:T(8,128)(2,1)S(1)} %collective-permute-done.3.refs_2_, ...), custom_call_target="tpu_custom_call" | custom-call | flops 603979776 | bytes 5505024 | tf_op jit(solution)/shard_map/pallas_call | solution.py:49
  165.8 13.7 %collective-permute-done.6 = bf16[128,768]{1,0:T(8,128)(2,1)S(1)} collective-permute-done((bf16[128,768]{1,0:T(8,128)(2,1)S(1)}, bf16[128,768]{1,0:T(8,128)(2,1)S(1)}, u32[]{:S(2)}, u32[]{:S(2)}) %collective-permute-start.6) | collective-permute-done | bytes 196640 | tf_op jit(solution)/shard_map/ppermute | solution.py:161
  179.5 0.7 add_convert_fusion
  (3 shorter events, 0.0 us)
Async XLA Ops:
  8.4 21.7 %all-to-all-start = ((bf16[32,16,384]{2,1,0:T(8,128)(2,1)}), bf16[32,16,384]{2,1,0:T(8,128)(2,1)S(1)}, u32[]{:S(2)}, u32[]{:S(2)}) async-start(bf16[32,16,384]{2,1,0:T(8,128)(2,1)} %bitcast.4), calls=%async_computation | async-start | bytes 786432 | tf_op jit(solution)/shard_map/all_to_all | solution.py:133
  18.0 131.7 %all-gather.3.cloned.1.call-start = ((), (), s32[]{:S(2)}) async-start(), calls=%async_computation.2 | async-start | bytes 9732096 | tf_op jit(solution)/shard_map/all_gather | solution.py:142
  18.0 12.1 %collective-permute-start = (bf16[96,768]{1,0:T(8,128)(2,1)}, bf16[96,768]{1,0:T(8,128)(2,1)S(1)}, u32[]{:S(2)}, u32[]{:S(2)}) collective-permute-start(bf16[96,768]{1,0:T(8,128)(2,1)} %bitcast.23), channel_id=1, source_target_pairs={{0,0},{1,64},{2,128},{3,192},{64,1},{65,65},{66,129},{67,193},{128... | collective-permute-start | bytes 442376 | tf_op jit(solution)/shard_map/ppermute | solution.py:122
  30.2 35.6 %collective-permute-start.5 = (bf16[96,768]{1,0:T(8,128)(2,1)S(1)}, bf16[96,768]{1,0:T(8,128)(2,1)S(1)}, u32[]{:S(2)}, u32[]{:S(2)}) collective-permute-start(bf16[96,768]{1,0:T(8,128)(2,1)S(1)} %collective-permute-done), channel_id=1, source_target_pairs={{0,256},{256,0},{1,257},{257,1},{2,258},{258,2},{3,259},{259,3},{4... | collective-permute-start | bytes 442376 | tf_op jit(solution)/shard_map/ppermute | solution.py:136
  44.0 51.0 %collective-permute-start.1 = (bf16[32,16,384]{2,1,0:T(8,128)(2,1)S(1)}, bf16[32,16,384]{2,1,0:T(8,128)(2,1)S(1)}, u32[]{:S(2)}, u32[]{:S(2)}) collective-permute-start(bf16[32,16,384]{2,1,0:T(8,128)(2,1)S(1)} %all-to-all-done), channel_id=1, source_target_pairs={{0,256},{256,0},{1,257},{257,1},{2,258},{258,2},{3,259},{259,3},{4... | collective-permute-start | bytes 1179656 | tf_op jit(solution)/shard_map/ppermute | solution.py:137
  115.8 0.9 copy-start
  116.8 0.9 copy-start.1
  117.7 0.9 copy-start.2
  120.5 10.2 %collective-permute-start.2 = (bf16[128,768]{1,0:T(8,128)(2,1)S(1)}, bf16[128,768]{1,0:T(8,128)(2,1)S(1)}, u32[]{:S(2)}, u32[]{:S(2)}) collective-permute-start(bf16[128,768]{1,0:T(8,128)(2,1)S(1)} %shard_map.55.refs_0_), channel_id=1, source_target_pairs={{0,1},{1,0},{2,3},{3,2},{4,5},{5,4},{6,7},{7,6},{8,9},{9,8},{10,11... | collective-permute-start | bytes 589832 | tf_op jit(solution)/shard_map/ppermute | solution.py:157
  122.4 19.0 %collective-permute-start.3 = (bf16[128,768]{1,0:T(8,128)(2,1)S(1)}, bf16[128,768]{1,0:T(8,128)(2,1)S(1)}, u32[]{:S(2)}, u32[]{:S(2)}) collective-permute-start(bf16[128,768]{1,0:T(8,128)(2,1)S(1)} %shard_map.55.refs_0_), channel_id=1, source_target_pairs={{0,2},{1,3},{2,0},{3,1},{4,6},{5,7},{6,4},{7,5},{8,10},{9,11},{10,... | collective-permute-start | bytes 589832 | tf_op jit(solution)/shard_map/ppermute | solution.py:157
  124.4 17.1 %collective-permute-start.4 = (bf16[128,768]{1,0:T(8,128)(2,1)S(1)}, bf16[128,768]{1,0:T(8,128)(2,1)S(1)}, u32[]{:S(2)}, u32[]{:S(2)}) collective-permute-start(bf16[128,768]{1,0:T(8,128)(2,1)S(1)} %shard_map.55.refs_0_), channel_id=1, source_target_pairs={{0,3},{1,2},{2,1},{3,0},{4,7},{5,6},{6,5},{7,4},{8,11},{9,10},{10,... | collective-permute-start | bytes 589832 | tf_op jit(solution)/shard_map/ppermute | solution.py:157
  153.9 25.6 %collective-permute-start.6 = (bf16[128,768]{1,0:T(8,128)(2,1)S(1)}, bf16[128,768]{1,0:T(8,128)(2,1)S(1)}, u32[]{:S(2)}, u32[]{:S(2)}) collective-permute-start(bf16[128,768]{1,0:T(8,128)(2,1)S(1)} %shard_map.57), channel_id=1, source_target_pairs={{0,4},{4,0},{1,5},{5,1},{2,6},{6,2},{3,7},{7,3},{8,12},{12,8},{9,1... | collective-permute-start | bytes 589832 | tf_op jit(solution)/shard_map/ppermute | solution.py:161
Sparse Core Ops, SparseCore 0:
  66.7 83.0 all-gather.2

commit v7 on v6

--- a/solution.py
+++ b/solution.py
@@ -119,10 +119,11 @@
     quad, member = lax.axis_index("p"), lax.axis_index("q")
     seats = lax.axis_size(PLANE)
 
-    w_near = lax.ppermute(
-        w_out.T,
-        ("x", "q"),
-        [(x * QUAD + q, q * QUAD + x) for x in range(QUAD) for q in range(QUAD)],
+    w_near = w_out.T
+    w_far = lax.ppermute(w_near, "zh", SWAP)
+    keeps_near = half == quad
+    w_pair = jnp.stack(
+        (jnp.where(keeps_near, w_near, w_far), jnp.where(keeps_near, w_far, w_near))
     )
 
     part = width // HALVES
@@ -131,14 +132,14 @@
     )
     own = own.reshape(seats, PIECE, part)
     spread = lax.all_to_all(own, PLANE, split_axis=0, concat_axis=0, tiled=True)
-    spread, w_near = lax.optimization_barrier((spread, w_near))
+    spread, w_pair = lax.optimization_barrier((spread, w_pair))
 
-    w_far = lax.ppermute(w_near, "zh", SWAP)
+    w_pair = lax.ppermute(
+        w_pair,
+        ("x", "q"),
+        [(x * QUAD + q, q * QUAD + x) for x in range(QUAD) for q in range(QUAD)],
+    )
     far = lax.ppermute(spread, "zh", SWAP)
-    keeps_near = half == quad
-    w_pair = jnp.stack(
-        (jnp.where(keeps_near, w_near, w_far), jnp.where(keeps_near, w_far, w_near))
-    )
     w_all = lax.all_gather(w_pair, PLANE, axis=0, tiled=False)
     w_all = w_all.reshape(QUAD, seats // QUAD, 2, -1, width)
 

time: 188 us -> 199 us (1.059)
  waiting for transfers between devices: 88 us -> 71.3 us
  starting transfers between devices: 47.3 us -> 62 us
  blocking collectives: 20.1 us -> 32.2 us
    ppermute x1, waiting for transfers between devices: 19.9 us -> 0.01 us  [body(): w_far = lax.ppermute(w_near, 'zh', SWAP)]
    all_to_all x1, blocking collectives: 20.1 us -> 32.2 us  [body(): lax.all_to_all(chosen, PLANE, split_axis=0, concat_axis=0, tiled=True)]
    ppermute x1, waiting for transfers between devices: 27.4 us -> 18.6 us  [body(): far = lax.ppermute(spread, 'zh', SWAP)]
    ppermute x3, starting transfers between devices: 10.1 us -> 18.8 us  [body(): lax.ppermute(attended, 'q', [(i, i ^ k) for i in range(QUAD)])]
    all_gather x1, waiting for transfers between devices: 8.28 us -> 16.3 us  [body(): w_all = lax.all_gather(w_pair, PLANE, axis=0, tiled=False)]
    all_to_all x1, waiting for transfers between devices: 0.01 us -> 7.02 us  [body(): spread = lax.all_to_all(own, PLANE, split_axis=0, concat_axis=0, tiled=True)]
    ppermute x1, starting transfers between devices: 1.92 us -> 6.83 us  [body(): far = lax.ppermute(spread, 'zh', SWAP)]
    ppermute x1, waiting for transfers between devices: 7.88 us -> 3.61 us  [body(): lax.ppermute(w_pair, ('x', 'q'), [(x * QUAD + q, q * QUAD + x) for x in r...]
  transfers between devices with their start and end apart: 9 -> 9, of which waited for: 7 -> 6; matrix products, arithmetic and copies ran while one was open for 1% -> 2% of each run, Pallas kernels for 3% -> 3%
where the time goes in v7:
time: 199 us; the launch traced here: 198 us
  waiting for transfers between devices  71.3 us (36%)
  starting transfers between devices  62 us (31%)
  blocking collectives  32.2 us (16%)
  between operations  13.6 us (7%)
  Pallas kernels  10.3 us (5%)
  local copies, waits for them, and re-layouts  5.48 us (3%)
  other arithmetic  3.38 us (2%)
    all_to_all x1, blocking collectives, body(): lax.all_to_all(chosen, PLANE, split_axis=0, concat_axis=0, tiled=True)  32.2 us
    ppermute x3, starting transfers between devices, body(): lax.ppermute(attended, 'q', [(i, i ^ k) for i in range(QUAD)])  18.8 us
    ppermute x1, waiting for transfers between devices, body(): far = lax.ppermute(spread, 'zh', SWAP)  18.6 us
    all_gather x1, waiting for transfers between devices, body(): w_all = lax.all_gather(w_pair, PLANE, axis=0, tiled=False)  16.3 us
    ppermute x1, starting transfers between devices, body(): w_far = lax.ppermute(w_near, 'zh', SWAP)  15.7 us
    ppermute x1, waiting for transfers between devices, body(): arrived = lax.ppermute(sent, 'p', SWAP)  13.7 us
    ppermute x3, waiting for transfers between devices, body(): lax.ppermute(attended, 'q', [(i, i ^ k) for i in range(QUAD)])  12.1 us
    pallas_call x2, Pallas kernels, project(): pl.pallas_call(functools.partial(project_kernel, side=side), in_specs=[pl...  8.38 us
  transfers between devices with their start and end apart: 9, of which 6 were waited for; matrix products, arithmetic and copies ran while one was open for 2% of the time, Pallas kernels for 3%

profile of v7, /device:TPU:6, one launch (start us, length us, event | category | flops | bytes accessed | tf_op | source)
XLA Modules:
  0.0 198.2 jit_solution(15706313473170643394)
XLA Ops:
  6.5 15.7 %collective-permute-start = (bf16[96,768]{1,0:T(8,128)(2,1)}, bf16[96,768]{1,0:T(8,128)(2,1)S(1)}, u32[]{:S(2)}, u32[]{:S(2)}) collective-permute-start(bf16[96,768]{1,0:T(8,128)(2,1)} %bitcast.25), channel_id=1, source_target_pairs={{0,256},{256,0},{1,257},{257,1},{2,258},{258,2},{3,259},{259,3},{4... | collective-permute-start | bytes 442376 | tf_op jit(solution)/shard_map/ppermute | solution.py:123
  22.3 1.1 slice_bitcast_fusion.1
  23.3 0.8 pad_maximum_fusion.1
  24.2 7.6 %all-to-all-start = ((bf16[32,16,384]{2,1,0:T(8,128)(2,1)}), bf16[32,16,384]{2,1,0:T(8,128)(2,1)S(1)}, u32[]{:S(2)}, u32[]{:S(2)}) async-start(bf16[32,16,384]{2,1,0:T(8,128)(2,1)} %bitcast.4), calls=%async_computation | async-start | bytes 786432 | tf_op jit(solution)/shard_map/all_to_all | solution.py:134
  31.8 0.0 all-gather.3.cloned.1.call-start
  31.8 0.0 collective-permute-done
  31.8 0.9 select_bitcast_fusion.1
  32.8 7.0 %all-to-all-done = bf16[32,16,384]{2,1,0:T(8,128)(2,1)S(1)} async-done(((bf16[32,16,384]{2,1,0:T(8,128)(2,1)}), bf16[32,16,384]{2,1,0:T(8,128)(2,1)S(1)}, u32[]{:S(2)}, u32[]{:S(2)}) %all-to-all-start) | async-done | bytes 393248 | tf_op jit(solution)/shard_map/all_to_all | solution.py:134
  39.8 5.3 %collective-permute-start.5 = (bf16[2,96,768]{2,1,0:T(8,128)(2,1)S(1)}, bf16[2,96,768]{2,1,0:T(8,128)(2,1)S(1)}, u32[]{:S(2)}, u32[]{:S(2)}) collective-permute-start(bf16[2,96,768]{2,1,0:T(8,128)(2,1)S(1)} %pad_maximum_fusion.2), channel_id=1, source_target_pairs={{0,0},{1,64},{2,128},{3,192},{64,1},{65,65},{66,129},{67,193},{128... | collective-permute-start | bytes 884744 | tf_op jit(solution)/shard_map/ppermute | solution.py:137
  45.2 6.8 %collective-permute-start.1 = (bf16[32,16,384]{2,1,0:T(8,128)(2,1)S(1)}, bf16[32,16,384]{2,1,0:T(8,128)(2,1)S(1)}, u32[]{:S(2)}, u32[]{:S(2)}) collective-permute-start(bf16[32,16,384]{2,1,0:T(8,128)(2,1)S(1)} %all-to-all-done), channel_id=1, source_target_pairs={{0,256},{256,0},{1,257},{257,1},{2,258},{258,2},{3,259},{259,3},{4... | collective-permute-start | bytes 1179656 | tf_op jit(solution)/shard_map/ppermute | solution.py:142
  52.0 3.6 %collective-permute-done.5 = bf16[2,96,768]{2,1,0:T(8,128)(2,1)S(1)} collective-permute-done((bf16[2,96,768]{2,1,0:T(8,128)(2,1)S(1)}, bf16[2,96,768]{2,1,0:T(8,128)(2,1)S(1)}, u32[]{:S(2)}, u32[]{:S(2)}) %collective-permute-start.5) | collective-permute-done | bytes 294944 | tf_op jit(solution)/shard_map/ppermute | solution.py:137
  55.6 0.0 copy-start.3
  55.6 0.7 copy-done.3
  56.3 0.0 all-gather.3.cloned.1.call-update
  56.4 0.8 compare_select_fusion
  57.1 0.1 copy.8
  57.2 0.1 reshape.14
  57.3 18.6 %collective-permute-done.1 = bf16[32,16,384]{2,1,0:T(8,128)(2,1)S(1)} collective-permute-done((bf16[32,16,384]{2,1,0:T(8,128)(2,1)S(1)}, bf16[32,16,384]{2,1,0:T(8,128)(2,1)S(1)}, u32[]{:S(2)}, u32[]{:S(2)}) %collective-permute-start.1) | collective-permute-done | bytes 393248 | tf_op jit(solution)/shard_map/ppermute | solution.py:142
  75.9 0.1 pad_maximum_fusion
  76.0 0.7 gather_fusion
  76.7 32.2 %all_to_all.10 = bf16[32,2,16,384]{3,2,1,0:T(8,128)(2,1)S(1)} all-to-all(bf16[32,2,16,384]{3,2,1,0:T(8,128)(2,1)S(1)} %bitcast.24), channel_id=1, replica_groups=mesh['zh'=2,'x'=4,'y'=4,'c'=2,'p'=2,'q'=4] {'x','y','c'}, dimensions={0} | all-to-all | bytes 1572864 | tf_op jit(solution)/shard_map/all_to_all | solution.py:149
  108.9 0.0 copy-start
  108.9 0.9 copy-done
  109.9 0.0 copy-start.1
  109.9 0.9 copy-done.1
  110.8 0.0 copy-start.2
  110.8 0.9 copy-done.2
  111.7 1.9 shard_map.55.refs_0_
  113.6 12.6 %collective-permute-start.2 = (bf16[128,768]{1,0:T(8,128)(2,1)S(1)}, bf16[128,768]{1,0:T(8,128)(2,1)S(1)}, u32[]{:S(2)}, u32[]{:S(2)}) collective-permute-start(bf16[128,768]{1,0:T(8,128)(2,1)S(1)} %shard_map.55.refs_0_), channel_id=1, source_target_pairs={{0,1},{1,0},{2,3},{3,2},{4,5},{5,4},{6,7},{7,6},{8,9},{9,8},{10,11... | collective-permute-start | bytes 589832 | tf_op jit(solution)/shard_map/ppermute | solution.py:158
  126.3 1.9 collective-permute-start.3
  128.2 4.3 %collective-permute-start.4 = (bf16[128,768]{1,0:T(8,128)(2,1)S(1)}, bf16[128,768]{1,0:T(8,128)(2,1)S(1)}, u32[]{:S(2)}, u32[]{:S(2)}) collective-permute-start(bf16[128,768]{1,0:T(8,128)(2,1)S(1)} %shard_map.55.refs_0_), channel_id=1, source_target_pairs={{0,3},{1,2},{2,1},{3,0},{4,7},{5,6},{6,5},{7,4},{8,11},{9,10},{10,... | collective-permute-start | bytes 589832 | tf_op jit(solution)/shard_map/ppermute | solution.py:158
  132.5 0.0 collective-permute-done.2.refs_1_
  132.5 12.1 %collective-permute-done.3.refs_2_ = bf16[128,768]{1,0:T(8,128)(2,1)S(1)} collective-permute-done((bf16[128,768]{1,0:T(8,128)(2,1)S(1)}, bf16[128,768]{1,0:T(8,128)(2,1)S(1)}, u32[]{:S(2)}, u32[]{:S(2)}) %collective-permute-start.3) | collective-permute-done | bytes 196640 | tf_op jit(solution)/shard_map/ppermute | solution.py:158
  144.6 0.0 collective-permute-done.4.refs_3_
  144.6 16.3 %all-gather.3.cloned.1.call-done = bf16[64,96,768]{2,1,0:T(8,128)(2,1)} async-done(((bf16[2,96,768]{2,1,0:T(8,128)(2,1)}), bf16[64,96,768]{2,1,0:T(8,128)(2,1)}) %all-gather.3.cloned.1.call-update) | async-done | bytes 9437200 | tf_op jit(solution)/shard_map/all_gather | solution.py:143
  160.8 4.2 %shard_map.57 = bf16[128,768]{1,0:T(8,128)(2,1)S(1)} custom-call(s32[4]{0:T(128)S(1)} %iota_xor_fusion.order_ref, bf16[128,768]{1,0:T(8,128)(2,1)S(1)} %shard_map.55.refs_0_, bf16[128,768]{1,0:T(8,128)(2,1)S(1)} %collective-permute-done.2.refs_1_, bf16[128,768]{1,0:T(8,128)(2,1)S(1)} %collective-permute-done.3.refs_2_, ...), custom_call_target="tpu_custom_call" | custom-call | flops 603979776 | bytes 5505024 | tf_op jit(solution)/shard_map/pallas_call | solution.py:49
  165.0 7.7 %collective-permute-start.6 = (bf16[128,768]{1,0:T(8,128)(2,1)S(1)}, bf16[128,768]{1,0:T(8,128)(2,1)S(1)}, u32[]{:S(2)}, u32[]{:S(2)}) collective-permute-start(bf16[128,768]{1,0:T(8,128)(2,1)S(1)} %shard_map.57), channel_id=1, source_target_pairs={{0,4},{4,0},{1,5},{5,1},{2,6},{6,2},{3,7},{7,3},{8,12},{12,8},{9,1... | collective-permute-start | bytes 589832 | tf_op jit(solution)/shard_map/ppermute | solution.py:162
  172.7 4.2 %shard_map.56 = f32[128,768]{1,0:T(8,128)S(1)} custom-call(s32[4]{0:T(128)S(1)} %iota_xor_fusion.order_ref, bf16[128,768]{1,0:T(8,128)(2,1)S(1)} %shard_map.55.refs_0_, bf16[128,768]{1,0:T(8,128)(2,1)S(1)} %collective-permute-done.2.refs_1_, bf16[128,768]{1,0:T(8,128)(2,1)S(1)} %collective-permute-done.3.refs_2_, ...), custom_call_target="tpu_custom_call" | custom-call | flops 603979776 | bytes 5505024 | tf_op jit(solution)/shard_map/pallas_call | solution.py:49
  176.9 13.7 %collective-permute-done.6 = bf16[128,768]{1,0:T(8,128)(2,1)S(1)} collective-permute-done((bf16[128,768]{1,0:T(8,128)(2,1)S(1)}, bf16[128,768]{1,0:T(8,128)(2,1)S(1)}, u32[]{:S(2)}, u32[]{:S(2)}) %collective-permute-start.6) | collective-permute-done | bytes 196640 | tf_op jit(solution)/shard_map/ppermute | solution.py:162
  190.6 0.7 add_convert_fusion
  (3 shorter events, 0.0 us)
Async XLA Ops:
  6.5 25.3 %collective-permute-start = (bf16[96,768]{1,0:T(8,128)(2,1)}, bf16[96,768]{1,0:T(8,128)(2,1)S(1)}, u32[]{:S(2)}, u32[]{:S(2)}) collective-permute-start(bf16[96,768]{1,0:T(8,128)(2,1)} %bitcast.25), channel_id=1, source_target_pairs={{0,256},{256,0},{1,257},{257,1},{2,258},{258,2},{3,259},{259,3},{4... | collective-permute-start | bytes 442376 | tf_op jit(solution)/shard_map/ppermute | solution.py:123
  24.2 15.7 %all-to-all-start = ((bf16[32,16,384]{2,1,0:T(8,128)(2,1)}), bf16[32,16,384]{2,1,0:T(8,128)(2,1)S(1)}, u32[]{:S(2)}, u32[]{:S(2)}) async-start(bf16[32,16,384]{2,1,0:T(8,128)(2,1)} %bitcast.4), calls=%async_computation | async-start | bytes 786432 | tf_op jit(solution)/shard_map/all_to_all | solution.py:134
  31.8 129.1 %all-gather.3.cloned.1.call-start = ((), (), s32[]{:S(2)}) async-start(), calls=%async_computation.2 | async-start | bytes 9732096 | tf_op jit(solution)/shard_map/all_gather | solution.py:143
  39.8 15.8 %collective-permute-start.5 = (bf16[2,96,768]{2,1,0:T(8,128)(2,1)S(1)}, bf16[2,96,768]{2,1,0:T(8,128)(2,1)S(1)}, u32[]{:S(2)}, u32[]{:S(2)}) collective-permute-start(bf16[2,96,768]{2,1,0:T(8,128)(2,1)S(1)} %pad_maximum_fusion.2), channel_id=1, source_target_pairs={{0,0},{1,64},{2,128},{3,192},{64,1},{65,65},{66,129},{67,193},{128... | collective-permute-start | bytes 884744 | tf_op jit(solution)/shard_map/ppermute | solution.py:137
  45.2 30.7 %collective-permute-start.1 = (bf16[32,16,384]{2,1,0:T(8,128)(2,1)S(1)}, bf16[32,16,384]{2,1,0:T(8,128)(2,1)S(1)}, u32[]{:S(2)}, u32[]{:S(2)}) collective-permute-start(bf16[32,16,384]{2,1,0:T(8,128)(2,1)S(1)} %all-to-all-done), channel_id=1, source_target_pairs={{0,256},{256,0},{1,257},{257,1},{2,258},{258,2},{3,259},{259,3},{4... | collective-permute-start | bytes 1179656 | tf_op jit(solution)/shard_map/ppermute | solution.py:142
  55.6 0.7 copy-start.3
  108.9 0.9 copy-start
  109.9 0.9 copy-start.1
  110.8 0.9 copy-start.2
  113.6 18.9 %collective-permute-start.2 = (bf16[128,768]{1,0:T(8,128)(2,1)S(1)}, bf16[128,768]{1,0:T(8,128)(2,1)S(1)}, u32[]{:S(2)}, u32[]{:S(2)}) collective-permute-start(bf16[128,768]{1,0:T(8,128)(2,1)S(1)} %shard_map.55.refs_0_), channel_id=1, source_target_pairs={{0,1},{1,0},{2,3},{3,2},{4,5},{5,4},{6,7},{7,6},{8,9},{9,8},{10,11... | collective-permute-start | bytes 589832 | tf_op jit(solution)/shard_map/ppermute | solution.py:158
  126.3 18.3 %collective-permute-start.3 = (bf16[128,768]{1,0:T(8,128)(2,1)S(1)}, bf16[128,768]{1,0:T(8,128)(2,1)S(1)}, u32[]{:S(2)}, u32[]{:S(2)}) collective-permute-start(bf16[128,768]{1,0:T(8,128)(2,1)S(1)} %shard_map.55.refs_0_), channel_id=1, source_target_pairs={{0,2},{1,3},{2,0},{3,1},{4,6},{5,7},{6,4},{7,5},{8,10},{9,11},{10,... | collective-permute-start | bytes 589832 | tf_op jit(solution)/shard_map/ppermute | solution.py:158
  128.2 16.4 %collective-permute-start.4 = (bf16[128,768]{1,0:T(8,128)(2,1)S(1)}, bf16[128,768]{1,0:T(8,128)(2,1)S(1)}, u32[]{:S(2)}, u32[]{:S(2)}) collective-permute-start(bf16[128,768]{1,0:T(8,128)(2,1)S(1)} %shard_map.55.refs_0_), channel_id=1, source_target_pairs={{0,3},{1,2},{2,1},{3,0},{4,7},{5,6},{6,5},{7,4},{8,11},{9,10},{10,... | collective-permute-start | bytes 589832 | tf_op jit(solution)/shard_map/ppermute | solution.py:158
  165.0 25.6 %collective-permute-start.6 = (bf16[128,768]{1,0:T(8,128)(2,1)S(1)}, bf16[128,768]{1,0:T(8,128)(2,1)S(1)}, u32[]{:S(2)}, u32[]{:S(2)}) collective-permute-start(bf16[128,768]{1,0:T(8,128)(2,1)S(1)} %shard_map.57), channel_id=1, source_target_pairs={{0,4},{4,0},{1,5},{5,1},{2,6},{6,2},{3,7},{7,3},{8,12},{12,8},{9,1... | collective-permute-start | bytes 589832 | tf_op jit(solution)/shard_map/ppermute | solution.py:162
Sparse Core Ops, SparseCore 0:
  56.5 104.2 all-gather.2

commit v8 on v7

--- a/solution.py
+++ b/solution.py
@@ -16,7 +16,7 @@
 PLANE = ("x", "y", "c")
 SWAP = ((0, 1), (1, 0))
 QUAD = 4
-HINT_FLOPS, HINT_BYTES = 182 * 10**9, 10**6
+HINT_FLOPS, HINT_BYTES = 120 * 10**9, 10**6
 HALVES = 2
 PIECE = 16
 

time: 199 us -> 204 us (1.025)
  blocking collectives: 32.2 us -> 55.4 us
  starting transfers between devices: 62 us -> 48.6 us
  waiting for transfers between devices: 71.3 us -> 66.5 us
    all_to_all x1, blocking collectives: 32.2 us -> 55.4 us  [body(): lax.all_to_all(chosen, PLANE, split_axis=0, concat_axis=0, tiled=True)]
    all_gather x1, waiting for transfers between devices: 16.3 us -> 0.01 us  [body(): w_all = lax.all_gather(w_pair, PLANE, axis=0, tiled=False)]
    ppermute x1, waiting for transfers between devices: 3.61 us -> 10.1 us  [body(): lax.ppermute(w_pair, ('x', 'q'), [(x * QUAD + q, q * QUAD + x) for x in r...]
    ppermute x3, starting transfers between devices: 18.8 us -> 13.6 us  [body(): lax.ppermute(attended, 'q', [(i, i ^ k) for i in range(QUAD)])]
    ppermute x1, starting transfers between devices: 6.83 us -> 1.92 us  [body(): far = lax.ppermute(spread, 'zh', SWAP)]
    ppermute x1, starting transfers between devices: 7.65 us -> 4.4 us  [body(): arrived = lax.ppermute(sent, 'p', SWAP)]
    ppermute x1, waiting for transfers between devices: 18.6 us -> 21.6 us  [body(): far = lax.ppermute(spread, 'zh', SWAP)]
  transfers between devices with their start and end apart: 9 -> 9, of which waited for: 6 -> 5; matrix products, arithmetic and copies ran while one was open for 2% -> 2% of each run, Pallas kernels for 3% -> 3%
where the time goes in v8:
time: 204 us; the launch traced here: 203 us
  waiting for transfers between devices  66.5 us (33%)
  blocking collectives  55.4 us (27%)
  starting transfers between devices  48.6 us (24%)
  between operations  13.6 us (7%)
  Pallas kernels  10.3 us (5%)
  local copies, waits for them, and re-layouts  5.48 us (3%)
  other arithmetic  3.38 us (2%)
    all_to_all x1, blocking collectives, body(): lax.all_to_all(chosen, PLANE, split_axis=0, concat_axis=0, tiled=True)  55.4 us
    ppermute x1, waiting for transfers between devices, body(): far = lax.ppermute(spread, 'zh', SWAP)  21.6 us
    ppermute x1, starting transfers between devices, body(): w_far = lax.ppermute(w_near, 'zh', SWAP)  15.7 us
    ppermute x1, waiting for transfers between devices, body(): arrived = lax.ppermute(sent, 'p', SWAP)  15.4 us
    ppermute x3, starting transfers between devices, body(): lax.ppermute(attended, 'q', [(i, i ^ k) for i in range(QUAD)])  13.6 us
    ppermute x3, waiting for transfers between devices, body(): lax.ppermute(attended, 'q', [(i, i ^ k) for i in range(QUAD)])  12.3 us
    ppermute x1, waiting for transfers between devices, body(): lax.ppermute(w_pair, ('x', 'q'), [(x * QUAD + q, q * QUAD + x) for x in r...  10.1 us
    pallas_call x2, Pallas kernels, project(): pl.pallas_call(functools.partial(project_kernel, side=side), in_specs=[pl...  8.39 us
  transfers between devices with their start and end apart: 9, of which 5 were waited for; matrix products, arithmetic and copies ran while one was open for 2% of the time, Pallas kernels for 3%

profile of v8, /device:TPU:6, one launch (start us, length us, event | category | flops | bytes accessed | tf_op | source)
XLA Modules:
  0.0 203.2 jit_solution(3784027172137544961)
XLA Ops:
  6.5 15.7 %collective-permute-start = (bf16[96,768]{1,0:T(8,128)(2,1)}, bf16[96,768]{1,0:T(8,128)(2,1)S(1)}, u32[]{:S(2)}, u32[]{:S(2)}) collective-permute-start(bf16[96,768]{1,0:T(8,128)(2,1)} %bitcast.25), channel_id=1, source_target_pairs={{0,256},{256,0},{1,257},{257,1},{2,258},{258,2},{3,259},{259,3},{4... | collective-permute-start | bytes 442376 | tf_op jit(solution)/shard_map/ppermute | solution.py:123
  22.3 1.1 slice_bitcast_fusion.1
  23.3 0.8 pad_maximum_fusion.1
  24.2 7.6 %all-to-all-start = ((bf16[32,16,384]{2,1,0:T(8,128)(2,1)}), bf16[32,16,384]{2,1,0:T(8,128)(2,1)S(1)}, u32[]{:S(2)}, u32[]{:S(2)}) async-start(bf16[32,16,384]{2,1,0:T(8,128)(2,1)} %bitcast.4), calls=%async_computation | async-start | bytes 786432 | tf_op jit(solution)/shard_map/all_to_all | solution.py:134
  31.8 0.0 all-gather.3.cloned.1.call-start
  31.8 0.0 collective-permute-done
  31.8 0.9 select_bitcast_fusion.1
  32.8 7.0 %all-to-all-done = bf16[32,16,384]{2,1,0:T(8,128)(2,1)S(1)} async-done(((bf16[32,16,384]{2,1,0:T(8,128)(2,1)}), bf16[32,16,384]{2,1,0:T(8,128)(2,1)S(1)}, u32[]{:S(2)}, u32[]{:S(2)}) %all-to-all-start) | async-done | bytes 393248 | tf_op jit(solution)/shard_map/all_to_all | solution.py:134
  39.8 5.3 %collective-permute-start.5 = (bf16[2,96,768]{2,1,0:T(8,128)(2,1)S(1)}, bf16[2,96,768]{2,1,0:T(8,128)(2,1)S(1)}, u32[]{:S(2)}, u32[]{:S(2)}) collective-permute-start(bf16[2,96,768]{2,1,0:T(8,128)(2,1)S(1)} %pad_maximum_fusion.2), channel_id=1, source_target_pairs={{0,0},{1,64},{2,128},{3,192},{64,1},{65,65},{66,129},{67,193},{128... | collective-permute-start | bytes 884744 | tf_op jit(solution)/shard_map/ppermute | solution.py:137
  45.2 10.1 %collective-permute-done.5 = bf16[2,96,768]{2,1,0:T(8,128)(2,1)S(1)} collective-permute-done((bf16[2,96,768]{2,1,0:T(8,128)(2,1)S(1)}, bf16[2,96,768]{2,1,0:T(8,128)(2,1)S(1)}, u32[]{:S(2)}, u32[]{:S(2)}) %collective-permute-start.5) | collective-permute-done | bytes 294944 | tf_op jit(solution)/shard_map/ppermute | solution.py:137
  55.2 0.0 copy-start.3
  55.2 0.7 copy-done.3
  55.9 0.0 all-gather.3.cloned.1.call-update
  56.0 1.9 collective-permute-start.1
  57.9 0.8 compare_select_fusion
  58.7 0.1 copy.8
  58.8 0.1 reshape.14
  58.9 21.6 %collective-permute-done.1 = bf16[32,16,384]{2,1,0:T(8,128)(2,1)S(1)} collective-permute-done((bf16[32,16,384]{2,1,0:T(8,128)(2,1)S(1)}, bf16[32,16,384]{2,1,0:T(8,128)(2,1)S(1)}, u32[]{:S(2)}, u32[]{:S(2)}) %collective-permute-start.1) | collective-permute-done | bytes 393248 | tf_op jit(solution)/shard_map/ppermute | solution.py:142
  80.5 0.1 pad_maximum_fusion
  80.6 0.7 gather_fusion
  81.4 55.4 %all_to_all.10 = bf16[32,2,16,384]{3,2,1,0:T(8,128)(2,1)S(1)} all-to-all(bf16[32,2,16,384]{3,2,1,0:T(8,128)(2,1)S(1)} %bitcast.24), channel_id=1, replica_groups=mesh['zh'=2,'x'=4,'y'=4,'c'=2,'p'=2,'q'=4] {'x','y','c'}, dimensions={0} | all-to-all | bytes 1572864 | tf_op jit(solution)/shard_map/all_to_all | solution.py:149
  136.7 0.0 copy-start
  136.7 0.9 copy-done
  137.7 0.0 copy-start.1
  137.7 0.9 copy-done.1
  138.6 0.0 copy-start.2
  138.6 0.9 copy-done.2
  139.5 1.9 shard_map.55.refs_0_
  141.4 7.0 %collective-permute-start.2 = (bf16[128,768]{1,0:T(8,128)(2,1)S(1)}, bf16[128,768]{1,0:T(8,128)(2,1)S(1)}, u32[]{:S(2)}, u32[]{:S(2)}) collective-permute-start(bf16[128,768]{1,0:T(8,128)(2,1)S(1)} %shard_map.55.refs_0_), channel_id=1, source_target_pairs={{0,1},{1,0},{2,3},{3,2},{4,5},{5,4},{6,7},{7,6},{8,9},{9,8},{10,11... | collective-permute-start | bytes 589832 | tf_op jit(solution)/shard_map/ppermute | solution.py:158
  148.4 3.2 %collective-permute-start.3 = (bf16[128,768]{1,0:T(8,128)(2,1)S(1)}, bf16[128,768]{1,0:T(8,128)(2,1)S(1)}, u32[]{:S(2)}, u32[]{:S(2)}) collective-permute-start(bf16[128,768]{1,0:T(8,128)(2,1)S(1)} %shard_map.55.refs_0_), channel_id=1, source_target_pairs={{0,2},{1,3},{2,0},{3,1},{4,6},{5,7},{6,4},{7,5},{8,10},{9,11},{10,... | collective-permute-start | bytes 589832 | tf_op jit(solution)/shard_map/ppermute | solution.py:158
  151.7 3.4 %collective-permute-start.4 = (bf16[128,768]{1,0:T(8,128)(2,1)S(1)}, bf16[128,768]{1,0:T(8,128)(2,1)S(1)}, u32[]{:S(2)}, u32[]{:S(2)}) collective-permute-start(bf16[128,768]{1,0:T(8,128)(2,1)S(1)} %shard_map.55.refs_0_), channel_id=1, source_target_pairs={{0,3},{1,2},{2,1},{3,0},{4,7},{5,6},{6,5},{7,4},{8,11},{9,10},{10,... | collective-permute-start | bytes 589832 | tf_op jit(solution)/shard_map/ppermute | solution.py:158
  155.1 0.0 collective-permute-done.2.refs_1_
  155.1 12.3 %collective-permute-done.3.refs_2_ = bf16[128,768]{1,0:T(8,128)(2,1)S(1)} collective-permute-done((bf16[128,768]{1,0:T(8,128)(2,1)S(1)}, bf16[128,768]{1,0:T(8,128)(2,1)S(1)}, u32[]{:S(2)}, u32[]{:S(2)}) %collective-permute-start.3) | collective-permute-done | bytes 196640 | tf_op jit(solution)/shard_map/ppermute | solution.py:158
  167.4 0.0 collective-permute-done.4.refs_3_
  167.4 0.0 all-gather.3.cloned.1.call-done
  167.4 4.2 %shard_map.57 = bf16[128,768]{1,0:T(8,128)(2,1)S(1)} custom-call(s32[4]{0:T(128)S(1)} %iota_xor_fusion.order_ref, bf16[128,768]{1,0:T(8,128)(2,1)S(1)} %shard_map.55.refs_0_, bf16[128,768]{1,0:T(8,128)(2,1)S(1)} %collective-permute-done.2.refs_1_, bf16[128,768]{1,0:T(8,128)(2,1)S(1)} %collective-permute-done.3.refs_2_, ...), custom_call_target="tpu_custom_call" | custom-call | flops 603979776 | bytes 5505024 | tf_op jit(solution)/shard_map/pallas_call | solution.py:49
  171.6 4.4 %collective-permute-start.6 = (bf16[128,768]{1,0:T(8,128)(2,1)S(1)}, bf16[128,768]{1,0:T(8,128)(2,1)S(1)}, u32[]{:S(2)}, u32[]{:S(2)}) collective-permute-start(bf16[128,768]{1,0:T(8,128)(2,1)S(1)} %shard_map.57), channel_id=1, source_target_pairs={{0,4},{4,0},{1,5},{5,1},{2,6},{6,2},{3,7},{7,3},{8,12},{12,8},{9,1... | collective-permute-start | bytes 589832 | tf_op jit(solution)/shard_map/ppermute | solution.py:162
  176.0 4.2 %shard_map.56 = f32[128,768]{1,0:T(8,128)S(1)} custom-call(s32[4]{0:T(128)S(1)} %iota_xor_fusion.order_ref, bf16[128,768]{1,0:T(8,128)(2,1)S(1)} %shard_map.55.refs_0_, bf16[128,768]{1,0:T(8,128)(2,1)S(1)} %collective-permute-done.2.refs_1_, bf16[128,768]{1,0:T(8,128)(2,1)S(1)} %collective-permute-done.3.refs_2_, ...), custom_call_target="tpu_custom_call" | custom-call | flops 603979776 | bytes 5505024 | tf_op jit(solution)/shard_map/pallas_call | solution.py:49
  180.2 15.4 %collective-permute-done.6 = bf16[128,768]{1,0:T(8,128)(2,1)S(1)} collective-permute-done((bf16[128,768]{1,0:T(8,128)(2,1)S(1)}, bf16[128,768]{1,0:T(8,128)(2,1)S(1)}, u32[]{:S(2)}, u32[]{:S(2)}) %collective-permute-start.6) | collective-permute-done | bytes 196640 | tf_op jit(solution)/shard_map/ppermute | solution.py:162
  195.6 0.7 add_convert_fusion
  (3 shorter events, 0.0 us)
Async XLA Ops:
  6.5 25.3 %collective-permute-start = (bf16[96,768]{1,0:T(8,128)(2,1)}, bf16[96,768]{1,0:T(8,128)(2,1)S(1)}, u32[]{:S(2)}, u32[]{:S(2)}) collective-permute-start(bf16[96,768]{1,0:T(8,128)(2,1)} %bitcast.25), channel_id=1, source_target_pairs={{0,256},{256,0},{1,257},{257,1},{2,258},{258,2},{3,259},{259,3},{4... | collective-permute-start | bytes 442376 | tf_op jit(solution)/shard_map/ppermute | solution.py:123
  24.2 15.7 %all-to-all-start = ((bf16[32,16,384]{2,1,0:T(8,128)(2,1)}), bf16[32,16,384]{2,1,0:T(8,128)(2,1)S(1)}, u32[]{:S(2)}, u32[]{:S(2)}) async-start(bf16[32,16,384]{2,1,0:T(8,128)(2,1)} %bitcast.4), calls=%async_computation | async-start | bytes 786432 | tf_op jit(solution)/shard_map/all_to_all | solution.py:134
  31.8 135.6 %all-gather.3.cloned.1.call-start = ((), (), s32[]{:S(2)}) async-start(), calls=%async_computation.2 | async-start | bytes 9732096 | tf_op jit(solution)/shard_map/all_gather | solution.py:143
  39.8 15.4 %collective-permute-start.5 = (bf16[2,96,768]{2,1,0:T(8,128)(2,1)S(1)}, bf16[2,96,768]{2,1,0:T(8,128)(2,1)S(1)}, u32[]{:S(2)}, u32[]{:S(2)}) collective-permute-start(bf16[2,96,768]{2,1,0:T(8,128)(2,1)S(1)} %pad_maximum_fusion.2), channel_id=1, source_target_pairs={{0,0},{1,64},{2,128},{3,192},{64,1},{65,65},{66,129},{67,193},{128... | collective-permute-start | bytes 884744 | tf_op jit(solution)/shard_map/ppermute | solution.py:137
  55.2 0.7 copy-start.3
  56.0 24.6 %collective-permute-start.1 = (bf16[32,16,384]{2,1,0:T(8,128)(2,1)S(1)}, bf16[32,16,384]{2,1,0:T(8,128)(2,1)S(1)}, u32[]{:S(2)}, u32[]{:S(2)}) collective-permute-start(bf16[32,16,384]{2,1,0:T(8,128)(2,1)S(1)} %all-to-all-done), channel_id=1, source_target_pairs={{0,256},{256,0},{1,257},{257,1},{2,258},{258,2},{3,259},{259,3},{4... | collective-permute-start | bytes 1179656 | tf_op jit(solution)/shard_map/ppermute | solution.py:142
  136.7 0.9 copy-start
  137.7 0.9 copy-start.1
  138.6 0.9 copy-start.2
  141.4 13.7 %collective-permute-start.2 = (bf16[128,768]{1,0:T(8,128)(2,1)S(1)}, bf16[128,768]{1,0:T(8,128)(2,1)S(1)}, u32[]{:S(2)}, u32[]{:S(2)}) collective-permute-start(bf16[128,768]{1,0:T(8,128)(2,1)S(1)} %shard_map.55.refs_0_), channel_id=1, source_target_pairs={{0,1},{1,0},{2,3},{3,2},{4,5},{5,4},{6,7},{7,6},{8,9},{9,8},{10,11... | collective-permute-start | bytes 589832 | tf_op jit(solution)/shard_map/ppermute | solution.py:158
  148.4 19.0 %collective-permute-start.3 = (bf16[128,768]{1,0:T(8,128)(2,1)S(1)}, bf16[128,768]{1,0:T(8,128)(2,1)S(1)}, u32[]{:S(2)}, u32[]{:S(2)}) collective-permute-start(bf16[128,768]{1,0:T(8,128)(2,1)S(1)} %shard_map.55.refs_0_), channel_id=1, source_target_pairs={{0,2},{1,3},{2,0},{3,1},{4,6},{5,7},{6,4},{7,5},{8,10},{9,11},{10,... | collective-permute-start | bytes 589832 | tf_op jit(solution)/shard_map/ppermute | solution.py:158
  151.7 15.7 %collective-permute-start.4 = (bf16[128,768]{1,0:T(8,128)(2,1)S(1)}, bf16[128,768]{1,0:T(8,128)(2,1)S(1)}, u32[]{:S(2)}, u32[]{:S(2)}) collective-permute-start(bf16[128,768]{1,0:T(8,128)(2,1)S(1)} %shard_map.55.refs_0_), channel_id=1, source_target_pairs={{0,3},{1,2},{2,1},{3,0},{4,7},{5,6},{6,5},{7,4},{8,11},{9,10},{10,... | collective-permute-start | bytes 589832 | tf_op jit(solution)/shard_map/ppermute | solution.py:158
  171.6 24.0 %collective-permute-start.6 = (bf16[128,768]{1,0:T(8,128)(2,1)S(1)}, bf16[128,768]{1,0:T(8,128)(2,1)S(1)}, u32[]{:S(2)}, u32[]{:S(2)}) collective-permute-start(bf16[128,768]{1,0:T(8,128)(2,1)S(1)} %shard_map.57), channel_id=1, source_target_pairs={{0,4},{4,0},{1,5},{5,1},{2,6},{6,2},{3,7},{7,3},{8,12},{12,8},{9,1... | collective-permute-start | bytes 589832 | tf_op jit(solution)/shard_map/ppermute | solution.py:162
Sparse Core Ops, SparseCore 0:
  56.1 108.0 all-gather.2

commit v9 on v6

--- a/solution.py
+++ b/solution.py
@@ -16,23 +16,38 @@
 PLANE = ("x", "y", "c")
 SWAP = ((0, 1), (1, 0))
 QUAD = 4
-HINT_FLOPS, HINT_BYTES = 182 * 10**9, 10**6
 HALVES = 2
 PIECE = 16
 
 
-def project_kernel(order_ref, *refs, side):
-    parts, (w_ref, out_ref, held, arrivals) = refs[:QUAD], refs[QUAD:]
-    width = w_ref.shape[-1]
-    copies = [
-        pltpu.make_async_copy(w_ref.at[order_ref[k], :, side], held.at[k], arrivals.at[k])
-        for k in range(QUAD)
-    ]
-    for copy in copies:
-        copy.start()
+def project_kernel(place_ref, *refs):
+    parts, sides, (out_ref, held, arrivals) = refs[:QUAD], refs[QUAD:-3], refs[-3:]
+    width = held.shape[-1]
+    core = place_ref[QUAD + 1]
+
+    def copies(of_side):
+        return [
+            pltpu.make_async_copy(
+                of_side[other].at[place_ref[k]],
+                held.at[k, :, core ^ other],
+                arrivals.at[k, other],
+            )
+            for k in range(QUAD)
+            for other in range(2)
+        ]
+
+    for side in range(2):
+
+        @pl.when(place_ref[QUAD] == side)
+        def _(side=side):
+            for copy in copies(sides[2 * side : 2 * side + 2]):
+                copy.start()
+
     total = 0.0
+    waits = copies(sides[:2])
     for k in range(QUAD):
-        copies[k].wait()
+        for wait in waits[2 * k : 2 * k + 2]:
+            wait.wait()
         total += lax.dot_general(
             parts[k][...],
             held[k].reshape(-1, width),
@@ -42,28 +57,33 @@
     out_ref[...] = total.astype(out_ref.dtype)
 
 
-def project(order, parts, w_all, side, dtype):
+def project(order, side, core, parts, near, far, dtype):
     tokens, width = parts[0].shape
-    _, chunks, _, columns, _ = w_all.shape
+    _, chunks, columns, _ = near[0].shape
     in_vmem = pl.BlockSpec(memory_space=pltpu.VMEM)
+    place = jnp.concatenate((order, jnp.stack((side, core)).astype(jnp.int32)))
     return pl.pallas_call(
-        functools.partial(project_kernel, side=side),
+        project_kernel,
         in_specs=[pl.BlockSpec(memory_space=pltpu.SMEM)]
         + [in_vmem] * QUAD
-        + [pl.BlockSpec(memory_space=pltpu.HBM)],
+        + [pl.BlockSpec(memory_space=pltpu.HBM)] * 4,
         out_specs=in_vmem,
-        out_shape=jax.ShapeDtypeStruct((tokens, chunks * columns), dtype),
+        out_shape=jax.ShapeDtypeStruct((tokens, chunks * 2 * columns), dtype),
         scratch_shapes=[
-            pltpu.VMEM((QUAD, chunks, columns, width), w_all.dtype),
-            pltpu.SemaphoreType.DMA((QUAD,)),
+            pltpu.VMEM((QUAD, chunks, 2, columns, width), near[0].dtype),
+            pltpu.SemaphoreType.DMA((QUAD, 2)),
         ],
         compiler_params=pltpu.CompilerParams(vmem_limit_bytes=32 << 20),
         cost_estimate=pl.CostEstimate(
-            flops=2 * QUAD * tokens * width * chunks * columns,
-            bytes_accessed=2 * QUAD * width * (chunks * columns + tokens),
+            flops=4 * QUAD * tokens * width * chunks * columns,
+            bytes_accessed=2 * QUAD * width * (2 * chunks * columns + tokens),
             transcendentals=0,
         ),
-    )(order, *parts, pltpu.with_memory_space_constraint(w_all, pltpu.HBM))
+    )(
+        place,
+        *parts,
+        *[pltpu.with_memory_space_constraint(rows, pltpu.HBM) for rows in (*near, *far)],
+    )
 
 
 def attend_kernel(q_ref, k_ref, v_ref, routed_ref, out_ref):
@@ -108,7 +128,9 @@
         out_shape=jax.ShapeDtypeStruct(queries.shape, queries.dtype),
         compiler_params=pltpu.CompilerParams(vmem_limit_bytes=32 << 20),
         cost_estimate=pl.CostEstimate(
-            flops=HINT_FLOPS, bytes_accessed=HINT_BYTES, transcendentals=0
+            flops=4 * queries.size * (1 + ROUNDS) * queries.shape[0],
+            bytes_accessed=2 * (4 * queries.size + routed.size),
+            transcendentals=queries.size * (1 + ROUNDS),
         ),
     )(queries, keys, values, routed)
 
@@ -119,11 +141,19 @@
     quad, member = lax.axis_index("p"), lax.axis_index("q")
     seats = lax.axis_size(PLANE)
 
-    w_near = lax.ppermute(
-        w_out.T,
-        ("x", "q"),
-        [(x * QUAD + q, q * QUAD + x) for x in range(QUAD) for q in range(QUAD)],
-    )
+    w_near, w_far = [
+        lax.ppermute(
+            w_out.T,
+            ("zh", "x", "q"),
+            [
+                ((zh * QUAD + x) * QUAD + q, ((zh ^ flip) * QUAD + q) * QUAD + x)
+                for zh in range(2)
+                for x in range(QUAD)
+                for q in range(QUAD)
+            ],
+        )
+        for flip in range(2)
+    ]
 
     part = width // HALVES
     own = jnp.stack(
@@ -131,21 +161,26 @@
     )
     own = own.reshape(seats, PIECE, part)
     spread = lax.all_to_all(own, PLANE, split_axis=0, concat_axis=0, tiled=True)
-    spread, w_near = lax.optimization_barrier((spread, w_near))
-
-    w_far = lax.ppermute(w_near, "zh", SWAP)
     far = lax.ppermute(spread, "zh", SWAP)
-    keeps_near = half == quad
-    w_pair = jnp.stack(
-        (jnp.where(keeps_near, w_near, w_far), jnp.where(keeps_near, w_far, w_near))
-    )
-    w_all = lax.all_gather(w_pair, PLANE, axis=0, tiled=False)
-    w_all = w_all.reshape(QUAD, seats // QUAD, 2, -1, width)
+
+    def gather(chunk):
+        to_all = jnp.broadcast_to(chunk, (QUAD * QUAD,) + chunk.shape)
+        return lax.all_to_all(to_all, ("x", "y"), split_axis=0, concat_axis=0, tiled=True)
+
+    def with_other_core(chunks):
+        other = lax.ppermute(chunks, "c", SWAP)
+        return [rows.reshape(QUAD, QUAD, *rows.shape[1:]) for rows in (chunks, other)]
+
+    w_near = gather(w_near)
+    far, w_near = lax.optimization_barrier((far, w_near))
+    w_near = with_other_core(w_near)
 
     wanted = lax.dynamic_slice_in_dim(plan, half * seats, seats, 1)
     place = (wanted // seats ^ half) * seats + wanted % seats
     chosen = jnp.concatenate((spread, far)).at[place.T].get(mode="promise_in_bounds")
     routed = lax.all_to_all(chosen, PLANE, split_axis=0, concat_axis=0, tiled=True)
+    routed, w_far = lax.optimization_barrier((routed, w_far))
+    w_far = gather(w_far)
     attended = attend(
         queries,
         keys,
@@ -156,10 +191,14 @@
     parts = [attended] + [
         lax.ppermute(attended, "q", [(i, i ^ k) for i in range(QUAD)]) for k in range(1, QUAD)
     ]
+    w_far, parts = lax.optimization_barrier((w_far, parts))
+    w_far = with_other_core(w_far)
     order = member ^ jnp.arange(QUAD, dtype=jnp.int32)
-    sent = project(order, parts, w_all, 1, jnp.bfloat16)
+    core = lax.axis_index("c")
+    keeps_far = (half != quad).astype(jnp.int32)
+    sent = project(order, 1 - keeps_far, core, parts, w_near, w_far, jnp.bfloat16)
     arrived = lax.ppermute(sent, "p", SWAP)
-    kept = project(order, parts, w_all, 0, jnp.float32)
+    kept = project(order, keeps_far, core, parts, w_near, w_far, jnp.float32)
     return (kept + arrived.astype(jnp.float32)).astype(jnp.bfloat16)
 
 

time: 188 us -> 194 us (1.032)
  the two profiles are of different devices: /device:TPU:6 before, /device:TPU:5 now
where the time goes in v9:
time: 194 us; the launch traced here: 193 us
  starting transfers between devices  129 us (66%)
  waiting for transfers between devices  43.6 us (22%)
  Pallas kernels  10.3 us (5%)
  local copies, waits for them, and re-layouts  6.97 us (4%)
  other arithmetic  3.05 us (2%)
    ppermute x2, starting transfers between devices, body(): lax.ppermute(w_out.T, ('zh', 'x', 'q'), [((zh * QUAD + x) * QUAD + q, ((z...  28.4 us
    ppermute x2, starting transfers between devices, with_other_core(): other = lax.ppermute(chunks, 'c', SWAP)  21.2 us
    all_to_all x2, starting transfers between devices, gather(): lax.all_to_all(to_all, ('x', 'y'), split_axis=0, concat_axis=0, tiled=True)  17.5 us
    ppermute x2, waiting for transfers between devices, body(): lax.ppermute(w_out.T, ('zh', 'x', 'q'), [((zh * QUAD + x) * QUAD + q, ((z...  16.9 us
    ppermute x1, starting transfers between devices, body(): arrived = lax.ppermute(sent, 'p', SWAP)  16.2 us
    ppermute x1, starting transfers between devices, body(): far = lax.ppermute(spread, 'zh', SWAP)  13.5 us
    ppermute x3, starting transfers between devices, body(): lax.ppermute(attended, 'q', [(i, i ^ k) for i in range(QUAD)])  12.1 us
    ppermute x1, waiting for transfers between devices, body(): far = lax.ppermute(spread, 'zh', SWAP)  11.6 us
  transfers between devices with their start and end apart: 13, of which 6 were waited for; matrix products, arithmetic and copies ran while one was open for 0% of the time, Pallas kernels for 3%

profile of v9, /device:TPU:5, one launch (start us, length us, event | category | flops | bytes accessed | tf_op | source)
XLA Modules:
  0.0 193.3 jit_solution(2600272078749039896)
XLA Ops:
  0.0 1.1 slice_bitcast_fusion.1
  1.1 0.8 pad_maximum_fusion.1
  1.9 9.8 %all-to-all-start = ((bf16[32,16,384]{2,1,0:T(8,128)(2,1)}), bf16[32,16,384]{2,1,0:T(8,128)(2,1)S(1)}, u32[]{:S(2)}, u32[]{:S(2)}) async-start(bf16[32,16,384]{2,1,0:T(8,128)(2,1)} %bitcast.6), calls=%async_computation | async-start | bytes 786432 | tf_op jit(solution)/shard_map/all_to_all | solution.py:163
  11.8 0.0 copy-done.7
  11.8 2.8 %collective-permute-start.1 = (bf16[96,768]{1,0:T(8,128)(2,1)S(1)}, bf16[96,768]{1,0:T(8,128)(2,1)S(1)}, u32[]{:S(2)}, u32[]{:S(2)}) collective-permute-start(bf16[96,768]{1,0:T(8,128)(2,1)S(1)} %bitcast.27), channel_id=1, source_target_pairs={{0,0},{1,64},{2,128},{3,192},{64,1},{65,65},{66,129},{67,193},{128... | collective-permute-start | bytes 442376 | tf_op jit(solution)/shard_map/ppermute | solution.py:145
  14.6 10.8 %collective-permute-done.1 = bf16[96,768]{1,0:T(8,128)(2,1)S(1)} collective-permute-done((bf16[96,768]{1,0:T(8,128)(2,1)S(1)}, bf16[96,768]{1,0:T(8,128)(2,1)S(1)}, u32[]{:S(2)}, u32[]{:S(2)}) %collective-permute-start.1) | collective-permute-done | bytes 147488 | tf_op jit(solution)/shard_map/ppermute | solution.py:145
  25.3 0.0 all-to-all-done
  25.3 1.7 broadcast_in_dim.9
  27.0 6.8 %all-to-all-start.1 = ((bf16[16,96,768]{2,1,0:T(8,128)(2,1)}), bf16[16,96,768]{2,1,0:T(8,128)(2,1)S(1)}, u32[]{:S(2)}, u32[]{:S(2)}) async-start(bf16[16,96,768]{2,1,0:T(8,128)(2,1)} %broadcast_in_dim.9), calls=%async_computation.1 | async-start | bytes 4718592 | tf_op jit(solution)/shard_map/all_to_all | solution.py:168
  33.8 13.5 %collective-permute-start = (bf16[32,16,384]{2,1,0:T(8,128)(2,1)S(1)}, bf16[32,16,384]{2,1,0:T(8,128)(2,1)S(1)}, u32[]{:S(2)}, u32[]{:S(2)}) collective-permute-start(bf16[32,16,384]{2,1,0:T(8,128)(2,1)S(1)} %all-to-all-done), channel_id=1, source_target_pairs={{0,256},{256,0},{1,257},{257,1},{2,258},{258,2},{3,259},{259,3},{4... | collective-permute-start | bytes 1179656 | tf_op jit(solution)/shard_map/ppermute | solution.py:164
  47.3 0.0 copy-done.6
  47.3 0.1 compare_select_fusion
  47.4 0.1 copy.7
  47.5 0.1 reshape.26
  47.6 11.6 %collective-permute-done = bf16[32,16,384]{2,1,0:T(8,128)(2,1)S(1)} collective-permute-done((bf16[32,16,384]{2,1,0:T(8,128)(2,1)S(1)}, bf16[32,16,384]{2,1,0:T(8,128)(2,1)S(1)}, u32[]{:S(2)}, u32[]{:S(2)}) %collective-permute-start) | collective-permute-done | bytes 393248 | tf_op jit(solution)/shard_map/ppermute | solution.py:164
  59.2 0.8 copy-done.5
  60.0 1.6 all-to-all-done.1
  61.5 1.3 pad_maximum_fusion
  62.9 1.6 gather_fusion
  64.4 0.0 copy-done.3
  64.4 10.5 %all-to-all-start.2 = ((bf16[32,2,16,384]{3,2,1,0:T(8,128)(2,1)}), bf16[32,2,16,384]{3,2,1,0:T(8,128)(2,1)S(1)}, u32[]{:S(2)}, u32[]{:S(2)}) async-start(bf16[32,2,16,384]{3,2,1,0:T(8,128)(2,1)} %bitcast.9), calls=%async_computation.2 | async-start | bytes 1572864 | tf_op jit(solution)/shard_map/all_to_all | solution.py:181
  74.9 25.6 %collective-permute-start.2 = (bf16[96,768]{1,0:T(8,128)(2,1)}, bf16[96,768]{1,0:T(8,128)(2,1)S(1)}, u32[]{:S(2)}, u32[]{:S(2)}) collective-permute-start(bf16[96,768]{1,0:T(8,128)(2,1)} %bitcast.26), channel_id=1, source_target_pairs={{0,256},{1,320},{2,384},{3,448},{64,257},{65,321},{66,385},{67,449... | collective-permute-start | bytes 442376 | tf_op jit(solution)/shard_map/ppermute | solution.py:145
  100.5 6.2 %collective-permute-done.2 = bf16[96,768]{1,0:T(8,128)(2,1)S(1)} collective-permute-done((bf16[96,768]{1,0:T(8,128)(2,1)}, bf16[96,768]{1,0:T(8,128)(2,1)S(1)}, u32[]{:S(2)}, u32[]{:S(2)}) %collective-permute-start.2) | collective-permute-done | bytes 147488 | tf_op jit(solution)/shard_map/ppermute | solution.py:145
  106.7 0.0 all-to-all-done.2
  106.7 1.7 broadcast_in_dim.11
  108.4 10.7 %all-to-all-start.3 = ((bf16[16,96,768]{2,1,0:T(8,128)(2,1)}), bf16[16,96,768]{2,1,0:T(8,128)(2,1)}, u32[]{:S(2)}, u32[]{:S(2)}) async-start(bf16[16,96,768]{2,1,0:T(8,128)(2,1)} %broadcast_in_dim.11), calls=%async_computation.3 | async-start | bytes 4718592 | tf_op jit(solution)/shard_map/all_to_all | solution.py:168
  119.1 0.0 copy-done
  119.1 0.0 copy-done.1
  119.1 0.0 copy-done.2
  119.1 1.9 shard_map.55.refs_0_
  121.0 8.0 %collective-permute-start.5 = (bf16[128,768]{1,0:T(8,128)(2,1)S(1)}, bf16[128,768]{1,0:T(8,128)(2,1)S(1)}, u32[]{:S(2)}, u32[]{:S(2)}) collective-permute-start(bf16[128,768]{1,0:T(8,128)(2,1)S(1)} %shard_map.55.refs_0_), channel_id=1, source_target_pairs={{0,3},{1,2},{2,1},{3,0},{4,7},{5,6},{6,5},{7,4},{8,11},{9,10},{10,... | collective-permute-start | bytes 589832 | tf_op jit(solution)/shard_map/ppermute | solution.py:192
  129.0 1.9 collective-permute-start.4
  130.9 2.2 %collective-permute-start.3 = (bf16[128,768]{1,0:T(8,128)(2,1)S(1)}, bf16[128,768]{1,0:T(8,128)(2,1)S(1)}, u32[]{:S(2)}, u32[]{:S(2)}) collective-permute-start(bf16[128,768]{1,0:T(8,128)(2,1)S(1)} %shard_map.55.refs_0_), channel_id=1, source_target_pairs={{0,1},{1,0},{2,3},{3,2},{4,5},{5,4},{6,7},{7,6},{8,9},{9,8},{10,11... | collective-permute-start | bytes 589832 | tf_op jit(solution)/shard_map/ppermute | solution.py:192
  133.1 13.9 %collective-permute-start.6 = (bf16[16,96,768]{2,1,0:T(8,128)(2,1)}, bf16[16,96,768]{2,1,0:T(8,128)(2,1)S(1)}, u32[]{:S(2)}, u32[]{:S(2)}) collective-permute-start(bf16[16,96,768]{2,1,0:T(8,128)(2,1)} %copy-done.3), channel_id=1, source_target_pairs={{0,8},{8,0},{1,9},{9,1},{2,10},{10,2},{3,11},{11,3},{4,12},{12,4},... | collective-permute-start | bytes 7077896 | tf_op jit(solution)/shard_map/ppermute | solution.py:171
  147.0 0.0 collective-permute-done.5.refs_3_
  147.1 0.0 collective-permute-done.4.refs_2_
  147.1 0.0 collective-permute-done.3.refs_1_
  147.1 0.0 all-to-all-done.3
  147.1 7.2 %collective-permute-start.7 = (bf16[16,96,768]{2,1,0:T(8,128)(2,1)}, bf16[16,96,768]{2,1,0:T(8,128)(2,1)}, u32[]{:S(2)}, u32[]{:S(2)}) collective-permute-start(bf16[16,96,768]{2,1,0:T(8,128)(2,1)} %all-to-all-done.3), channel_id=1, source_target_pairs={{0,8},{8,0},{1,9},{9,1},{2,10},{10,2},{3,11},{11,3},{4,12},{12,4},... | collective-permute-start | bytes 7077896 | tf_op jit(solution)/shard_map/ppermute | solution.py:171
  154.3 0.1 add_add_fusion.1
  154.4 0.0 collective-permute-done.6
  154.4 4.4 %collective-permute-done.7 = bf16[16,96,768]{2,1,0:T(8,128)(2,1)} collective-permute-done((bf16[16,96,768]{2,1,0:T(8,128)(2,1)}, bf16[16,96,768]{2,1,0:T(8,128)(2,1)}, u32[]{:S(2)}, u32[]{:S(2)}) %collective-permute-start.7) | collective-permute-done | bytes 2359328 | tf_op jit(solution)/shard_map/ppermute | solution.py:171
  158.8 0.0 copy-done.4
  158.8 4.2 %shard_map.57 = bf16[128,768]{1,0:T(8,128)(2,1)S(1)} custom-call(s32[6]{0:T(128)S(1)} %get-tuple-element.27.place_ref, bf16[128,768]{1,0:T(8,128)(2,1)S(1)} %shard_map.55.refs_0_, bf16[128,768]{1,0:T(8,128)(2,1)S(1)} %collective-permute-done.3.refs_1_, bf16[128,768]{1,0:T(8,128)(2,1)S(1)} %collective-permute-done.4.refs_2_, ...), custom_call_target="tpu_custom_call" | custom-call | flops 603979776 | bytes 5505024 | tf_op jit(solution)/shard_map/pallas_call | solution.py:65
  163.0 16.2 %collective-permute-start.8 = (bf16[128,768]{1,0:T(8,128)(2,1)S(1)}, bf16[128,768]{1,0:T(8,128)(2,1)S(1)}, u32[]{:S(2)}, u32[]{:S(2)}) collective-permute-start(bf16[128,768]{1,0:T(8,128)(2,1)S(1)} %shard_map.57), channel_id=1, source_target_pairs={{0,4},{4,0},{1,5},{5,1},{2,6},{6,2},{3,7},{7,3},{8,12},{12,8},{9,1... | collective-permute-start | bytes 589832 | tf_op jit(solution)/shard_map/ppermute | solution.py:200
  179.2 4.2 %shard_map.56 = f32[128,768]{1,0:T(8,128)S(1)} custom-call(s32[6]{0:T(128)S(1)} %get-tuple-element.28.place_ref, bf16[128,768]{1,0:T(8,128)(2,1)S(1)} %shard_map.55.refs_0_, bf16[128,768]{1,0:T(8,128)(2,1)S(1)} %collective-permute-done.3.refs_1_, bf16[128,768]{1,0:T(8,128)(2,1)S(1)} %collective-permute-done.4.refs_2_, ...), custom_call_target="tpu_custom_call" | custom-call | flops 603979776 | bytes 5505024 | tf_op jit(solution)/shard_map/pallas_call | solution.py:65
  183.4 9.1 %collective-permute-done.8 = bf16[128,768]{1,0:T(8,128)(2,1)S(1)} collective-permute-done((bf16[128,768]{1,0:T(8,128)(2,1)S(1)}, bf16[128,768]{1,0:T(8,128)(2,1)S(1)}, u32[]{:S(2)}, u32[]{:S(2)}) %collective-permute-start.8) | collective-permute-done | bytes 196640 | tf_op jit(solution)/shard_map/ppermute | solution.py:200
  192.5 0.7 add_convert_fusion
  (10 shorter events, 0.0 us)
Async XLA Ops:
  0.0 11.8 %copy-start.7 = (bf16[768,96]{0,1:T(8,128)(2,1)S(1)}, bf16[768,96]{0,1:T(8,128)(2,1)}, u32[]{:S(2)}) copy-start(bf16[768,96]{0,1:T(8,128)(2,1)} %param.9) | copy-start | bytes 442372
  1.9 23.4 %all-to-all-start = ((bf16[32,16,384]{2,1,0:T(8,128)(2,1)}), bf16[32,16,384]{2,1,0:T(8,128)(2,1)S(1)}, u32[]{:S(2)}, u32[]{:S(2)}) async-start(bf16[32,16,384]{2,1,0:T(8,128)(2,1)} %bitcast.6), calls=%async_computation | async-start | bytes 786432 | tf_op jit(solution)/shard_map/all_to_all | solution.py:163
  11.8 13.5 %collective-permute-start.1 = (bf16[96,768]{1,0:T(8,128)(2,1)S(1)}, bf16[96,768]{1,0:T(8,128)(2,1)S(1)}, u32[]{:S(2)}, u32[]{:S(2)}) collective-permute-start(bf16[96,768]{1,0:T(8,128)(2,1)S(1)} %bitcast.27), channel_id=1, source_target_pairs={{0,0},{1,64},{2,128},{3,192},{64,1},{65,65},{66,129},{67,193},{128... | collective-permute-start | bytes 442376 | tf_op jit(solution)/shard_map/ppermute | solution.py:145
  27.0 20.3 %copy-start.6 = (s32[2,64]{1,0:T(2,128)S(1)}, s32[2,64]{1,0:T(2,128)}, u32[]{:S(2)}) copy-start(s32[2,64]{1,0:T(2,128)} %param.8) | copy-start | bytes 1540
  27.0 34.5 %all-to-all-start.1 = ((bf16[16,96,768]{2,1,0:T(8,128)(2,1)}), bf16[16,96,768]{2,1,0:T(8,128)(2,1)S(1)}, u32[]{:S(2)}, u32[]{:S(2)}) async-start(bf16[16,96,768]{2,1,0:T(8,128)(2,1)} %broadcast_in_dim.9), calls=%async_computation.1 | async-start | bytes 4718592 | tf_op jit(solution)/shard_map/all_to_all | solution.py:168
  33.8 25.4 %collective-permute-start = (bf16[32,16,384]{2,1,0:T(8,128)(2,1)S(1)}, bf16[32,16,384]{2,1,0:T(8,128)(2,1)S(1)}, u32[]{:S(2)}, u32[]{:S(2)}) collective-permute-start(bf16[32,16,384]{2,1,0:T(8,128)(2,1)S(1)} %all-to-all-done), channel_id=1, source_target_pairs={{0,256},{256,0},{1,257},{257,1},{2,258},{258,2},{3,259},{259,3},{4... | collective-permute-start | bytes 1179656 | tf_op jit(solution)/shard_map/ppermute | solution.py:164
  59.2 0.8 copy-start.5
  61.5 2.9 %copy-start.3 = (bf16[16,96,768]{2,1,0:T(8,128)(2,1)}, bf16[16,96,768]{2,1,0:T(8,128)(2,1)S(1)}, u32[]{:S(2)}) copy-start(bf16[16,96,768]{2,1,0:T(8,128)(2,1)S(1)} %all-to-all-done.1) | copy-start | bytes 7077892
  64.4 42.3 %all-to-all-start.2 = ((bf16[32,2,16,384]{3,2,1,0:T(8,128)(2,1)}), bf16[32,2,16,384]{3,2,1,0:T(8,128)(2,1)S(1)}, u32[]{:S(2)}, u32[]{:S(2)}) async-start(bf16[32,2,16,384]{3,2,1,0:T(8,128)(2,1)} %bitcast.9), calls=%async_computation.2 | async-start | bytes 1572864 | tf_op jit(solution)/shard_map/all_to_all | solution.py:181
  74.9 31.8 %collective-permute-start.2 = (bf16[96,768]{1,0:T(8,128)(2,1)}, bf16[96,768]{1,0:T(8,128)(2,1)S(1)}, u32[]{:S(2)}, u32[]{:S(2)}) collective-permute-start(bf16[96,768]{1,0:T(8,128)(2,1)} %bitcast.26), channel_id=1, source_target_pairs={{0,256},{1,320},{2,384},{3,448},{64,257},{65,321},{66,385},{67,449... | collective-permute-start | bytes 442376 | tf_op jit(solution)/shard_map/ppermute | solution.py:145
  108.4 10.7 %copy-start = (bf16[128,768]{1,0:T(8,128)(2,1)S(1)}, bf16[128,768]{1,0:T(8,128)(2,1)}, u32[]{:S(2)}) copy-start(bf16[128,768]{1,0:T(8,128)(2,1)} %k_ref.1) | copy-start | bytes 589828
  108.4 10.7 %copy-start.1 = (bf16[128,768]{1,0:T(8,128)(2,1)S(1)}, bf16[128,768]{1,0:T(8,128)(2,1)}, u32[]{:S(2)}) copy-start(bf16[128,768]{1,0:T(8,128)(2,1)} %v_ref.1) | copy-start | bytes 589828
  108.4 10.7 %copy-start.2 = (bf16[128,768]{1,0:T(8,128)(2,1)S(1)}, bf16[128,768]{1,0:T(8,128)(2,1)}, u32[]{:S(2)}) copy-start(bf16[128,768]{1,0:T(8,128)(2,1)} %q_ref.1) | copy-start | bytes 589828
  108.4 38.7 %all-to-all-start.3 = ((bf16[16,96,768]{2,1,0:T(8,128)(2,1)}), bf16[16,96,768]{2,1,0:T(8,128)(2,1)}, u32[]{:S(2)}, u32[]{:S(2)}) async-start(bf16[16,96,768]{2,1,0:T(8,128)(2,1)} %broadcast_in_dim.11), calls=%async_computation.3 | async-start | bytes 4718592 | tf_op jit(solution)/shard_map/all_to_all | solution.py:168
  121.0 26.1 %collective-permute-start.5 = (bf16[128,768]{1,0:T(8,128)(2,1)S(1)}, bf16[128,768]{1,0:T(8,128)(2,1)S(1)}, u32[]{:S(2)}, u32[]{:S(2)}) collective-permute-start(bf16[128,768]{1,0:T(8,128)(2,1)S(1)} %shard_map.55.refs_0_), channel_id=1, source_target_pairs={{0,3},{1,2},{2,1},{3,0},{4,7},{5,6},{6,5},{7,4},{8,11},{9,10},{10,... | collective-permute-start | bytes 589832 | tf_op jit(solution)/shard_map/ppermute | solution.py:192
  129.0 18.1 %collective-permute-start.4 = (bf16[128,768]{1,0:T(8,128)(2,1)S(1)}, bf16[128,768]{1,0:T(8,128)(2,1)S(1)}, u32[]{:S(2)}, u32[]{:S(2)}) collective-permute-start(bf16[128,768]{1,0:T(8,128)(2,1)S(1)} %shard_map.55.refs_0_), channel_id=1, source_target_pairs={{0,2},{1,3},{2,0},{3,1},{4,6},{5,7},{6,4},{7,5},{8,10},{9,11},{10,... | collective-permute-start | bytes 589832 | tf_op jit(solution)/shard_map/ppermute | solution.py:192
  130.9 16.2 %collective-permute-start.3 = (bf16[128,768]{1,0:T(8,128)(2,1)S(1)}, bf16[128,768]{1,0:T(8,128)(2,1)S(1)}, u32[]{:S(2)}, u32[]{:S(2)}) collective-permute-start(bf16[128,768]{1,0:T(8,128)(2,1)S(1)} %shard_map.55.refs_0_), channel_id=1, source_target_pairs={{0,1},{1,0},{2,3},{3,2},{4,5},{5,4},{6,7},{7,6},{8,9},{9,8},{10,11... | collective-permute-start | bytes 589832 | tf_op jit(solution)/shard_map/ppermute | solution.py:192
  133.1 21.3 %collective-permute-start.6 = (bf16[16,96,768]{2,1,0:T(8,128)(2,1)}, bf16[16,96,768]{2,1,0:T(8,128)(2,1)S(1)}, u32[]{:S(2)}, u32[]{:S(2)}) collective-permute-start(bf16[16,96,768]{2,1,0:T(8,128)(2,1)} %copy-done.3), channel_id=1, source_target_pairs={{0,8},{8,0},{1,9},{9,1},{2,10},{10,2},{3,11},{11,3},{4,12},{12,4},... | collective-permute-start | bytes 7077896 | tf_op jit(solution)/shard_map/ppermute | solution.py:171
  147.1 11.7 %collective-permute-start.7 = (bf16[16,96,768]{2,1,0:T(8,128)(2,1)}, bf16[16,96,768]{2,1,0:T(8,128)(2,1)}, u32[]{:S(2)}, u32[]{:S(2)}) collective-permute-start(bf16[16,96,768]{2,1,0:T(8,128)(2,1)} %all-to-all-done.3), channel_id=1, source_target_pairs={{0,8},{8,0},{1,9},{9,1},{2,10},{10,2},{3,11},{11,3},{4,12},{12,4},... | collective-permute-start | bytes 7077896 | tf_op jit(solution)/shard_map/ppermute | solution.py:171
  154.4 4.4 %copy-start.4 = (bf16[16,96,768]{2,1,0:T(8,128)(2,1)}, bf16[16,96,768]{2,1,0:T(8,128)(2,1)S(1)}, u32[]{:S(2)}) copy-start(bf16[16,96,768]{2,1,0:T(8,128)(2,1)S(1)} %collective-permute-done.6) | copy-start | bytes 7077892
  163.0 29.5 %collective-permute-start.8 = (bf16[128,768]{1,0:T(8,128)(2,1)S(1)}, bf16[128,768]{1,0:T(8,128)(2,1)S(1)}, u32[]{:S(2)}, u32[]{:S(2)}) collective-permute-start(bf16[128,768]{1,0:T(8,128)(2,1)S(1)} %shard_map.57), channel_id=1, source_target_pairs={{0,4},{4,0},{1,5},{5,1},{2,6},{6,2},{3,7},{7,3},{8,12},{12,8},{9,1... | collective-permute-start | bytes 589832 | tf_op jit(solution)/shard_map/ppermute | solution.py:200

commit v10 on v9

--- a/solution.py
+++ b/solution.py
@@ -20,34 +20,28 @@
 PIECE = 16
 
 
-def project_kernel(place_ref, *refs):
-    parts, sides, (out_ref, held, arrivals) = refs[:QUAD], refs[QUAD:-3], refs[-3:]
+def project_kernel(place_ref, *refs, side):
+    parts, gathered, (out_ref, held, arrivals) = refs[:QUAD], refs[QUAD:-3], refs[-3:]
     width = held.shape[-1]
-    core = place_ref[QUAD + 1]
-
-    def copies(of_side):
-        return [
+    core = place_ref[QUAD]
+    copies = [
+        [
             pltpu.make_async_copy(
-                of_side[other].at[place_ref[k]],
+                rows.at[place_ref[k], :, side],
                 held.at[k, :, core ^ other],
                 arrivals.at[k, other],
             )
-            for k in range(QUAD)
-            for other in range(2)
+            for other, rows in enumerate(gathered)
         ]
-
-    for side in range(2):
-
-        @pl.when(place_ref[QUAD] == side)
-        def _(side=side):
-            for copy in copies(sides[2 * side : 2 * side + 2]):
-                copy.start()
-
+        for k in range(QUAD)
+    ]
+    for k in range(QUAD):
+        for copy in copies[k]:
+            copy.start()
     total = 0.0
-    waits = copies(sides[:2])
     for k in range(QUAD):
-        for wait in waits[2 * k : 2 * k + 2]:
-            wait.wait()
+        for copy in copies[k]:
+            copy.wait()
         total += lax.dot_general(
             parts[k][...],
             held[k].reshape(-1, width),
@@ -57,20 +51,19 @@
     out_ref[...] = total.astype(out_ref.dtype)
 
 
-def project(order, side, core, parts, near, far, dtype):
+def project(place, parts, gathered, side, dtype):
     tokens, width = parts[0].shape
-    _, chunks, columns, _ = near[0].shape
+    _, chunks, _, columns, _ = gathered[0].shape
     in_vmem = pl.BlockSpec(memory_space=pltpu.VMEM)
-    place = jnp.concatenate((order, jnp.stack((side, core)).astype(jnp.int32)))
     return pl.pallas_call(
-        project_kernel,
+        functools.partial(project_kernel, side=side),
         in_specs=[pl.BlockSpec(memory_space=pltpu.SMEM)]
         + [in_vmem] * QUAD
-        + [pl.BlockSpec(memory_space=pltpu.HBM)] * 4,
+        + [pl.BlockSpec(memory_space=pltpu.HBM)] * 2,
         out_specs=in_vmem,
         out_shape=jax.ShapeDtypeStruct((tokens, chunks * 2 * columns), dtype),
         scratch_shapes=[
-            pltpu.VMEM((QUAD, chunks, 2, columns, width), near[0].dtype),
+            pltpu.VMEM((QUAD, chunks, 2, columns, width), gathered[0].dtype),
             pltpu.SemaphoreType.DMA((QUAD, 2)),
         ],
         compiler_params=pltpu.CompilerParams(vmem_limit_bytes=32 << 20),
@@ -82,7 +75,7 @@
     )(
         place,
         *parts,
-        *[pltpu.with_memory_space_constraint(rows, pltpu.HBM) for rows in (*near, *far)],
+        *[pltpu.with_memory_space_constraint(rows, pltpu.HBM) for rows in gathered],
     )
 
 
@@ -163,24 +156,26 @@
     spread = lax.all_to_all(own, PLANE, split_axis=0, concat_axis=0, tiled=True)
     far = lax.ppermute(spread, "zh", SWAP)
 
-    def gather(chunk):
-        to_all = jnp.broadcast_to(chunk, (QUAD * QUAD,) + chunk.shape)
-        return lax.all_to_all(to_all, ("x", "y"), split_axis=0, concat_axis=0, tiled=True)
-
-    def with_other_core(chunks):
-        other = lax.ppermute(chunks, "c", SWAP)
-        return [rows.reshape(QUAD, QUAD, *rows.shape[1:]) for rows in (chunks, other)]
-
-    w_near = gather(w_near)
-    far, w_near = lax.optimization_barrier((far, w_near))
-    w_near = with_other_core(w_near)
+    keeps_near = half == quad
+    w_pair = jnp.stack(
+        (jnp.where(keeps_near, w_near, w_far), jnp.where(keeps_near, w_far, w_near))
+    )
+    w_all = lax.all_to_all(
+        jnp.broadcast_to(w_pair, (QUAD * QUAD,) + w_pair.shape),
+        ("x", "y"),
+        split_axis=0,
+        concat_axis=0,
+        tiled=True,
+    )
+    far, w_all = lax.optimization_barrier((far, w_all))
 
     wanted = lax.dynamic_slice_in_dim(plan, half * seats, seats, 1)
     place = (wanted // seats ^ half) * seats + wanted % seats
     chosen = jnp.concatenate((spread, far)).at[place.T].get(mode="promise_in_bounds")
     routed = lax.all_to_all(chosen, PLANE, split_axis=0, concat_axis=0, tiled=True)
-    routed, w_far = lax.optimization_barrier((routed, w_far))
-    w_far = gather(w_far)
+    gathered = [
+        rows.reshape(QUAD, QUAD, *w_pair.shape) for rows in (w_all, lax.ppermute(w_all, "c", SWAP))
+    ]
     attended = attend(
         queries,
         keys,
@@ -191,14 +186,12 @@
     parts = [attended] + [
         lax.ppermute(attended, "q", [(i, i ^ k) for i in range(QUAD)]) for k in range(1, QUAD)
     ]
-    w_far, parts = lax.optimization_barrier((w_far, parts))
-    w_far = with_other_core(w_far)
-    order = member ^ jnp.arange(QUAD, dtype=jnp.int32)
-    core = lax.axis_index("c")
-    keeps_far = (half != quad).astype(jnp.int32)
-    sent = project(order, 1 - keeps_far, core, parts, w_near, w_far, jnp.bfloat16)
+    place = jnp.append(
+        member ^ jnp.arange(QUAD, dtype=jnp.int32), lax.axis_index("c").astype(jnp.int32)
+    )
+    sent = project(place, parts, gathered, 1, jnp.bfloat16)
     arrived = lax.ppermute(sent, "p", SWAP)
-    kept = project(order, keeps_far, core, parts, w_near, w_far, jnp.float32)
+    kept = project(place, parts, gathered, 0, jnp.float32)
     return (kept + arrived.astype(jnp.float32)).astype(jnp.bfloat16)
 
 

time: 194 us -> 205 us (1.057)
  the two profiles are of different devices: /device:TPU:5 before, /device:TPU:6 now
where the time goes in v10:
time: 205 us; the launch traced here: 202 us
  waiting for transfers between devices  98.3 us (48%)
  starting transfers between devices  85.5 us (42%)
  Pallas kernels  10.3 us (5%)
  local copies, waits for them, and re-layouts  5.54 us (3%)
    all_to_all x1, waiting for transfers between devices, body(): lax.all_to_all(jnp.broadcast_to(w_pair, (QUAD * QUAD,) + w_pair.shape), (...  32.2 us
    ppermute x1, waiting for transfers between devices, body(): far = lax.ppermute(spread, 'zh', SWAP)  21.9 us
    ppermute x2, starting transfers between devices, body(): lax.ppermute(w_out.T, ('zh', 'x', 'q'), [((zh * QUAD + x) * QUAD + q, ((z...  20.3 us
    ppermute x3, starting transfers between devices, body(): lax.ppermute(attended, 'q', [(i, i ^ k) for i in range(QUAD)])  18.5 us
    ppermute x1, starting transfers between devices, body(): far = lax.ppermute(spread, 'zh', SWAP)  15.2 us
    ppermute x1, waiting for transfers between devices, body(): arrived = lax.ppermute(sent, 'p', SWAP)  13.6 us
    all_to_all x1, waiting for transfers between devices, body(): lax.all_to_all(chosen, PLANE, split_axis=0, concat_axis=0, tiled=True)  12 us
    ppermute x3, waiting for transfers between devices, body(): lax.ppermute(attended, 'q', [(i, i ^ k) for i in range(QUAD)])  10.6 us
  transfers between devices with their start and end apart: 11, of which 8 were waited for; matrix products, arithmetic and copies ran while one was open for 2% of the time, Pallas kernels for 3%

profile of v10, /device:TPU:6, one launch (start us, length us, event | category | flops | bytes accessed | tf_op | source)
XLA Modules:
  0.0 201.7 jit_solution(15432685886288186950)
XLA Ops:
  0.0 14.3 %collective-permute-start.2 = (bf16[96,768]{1,0:T(8,128)(2,1)}, bf16[96,768]{1,0:T(8,128)(2,1)S(1)}, u32[]{:S(2)}, u32[]{:S(2)}) collective-permute-start(bf16[96,768]{1,0:T(8,128)(2,1)} %bitcast.22), channel_id=1, source_target_pairs={{0,256},{1,320},{2,384},{3,448},{64,257},{65,321},{66,385},{67,449... | collective-permute-start | bytes 442376 | tf_op jit(solution)/shard_map/ppermute | solution.py:138
  14.3 6.0 %collective-permute-start.1 = (bf16[96,768]{1,0:T(8,128)(2,1)}, bf16[96,768]{1,0:T(8,128)(2,1)S(1)}, u32[]{:S(2)}, u32[]{:S(2)}) collective-permute-start(bf16[96,768]{1,0:T(8,128)(2,1)} %bitcast.23), channel_id=1, source_target_pairs={{0,0},{1,64},{2,128},{3,192},{64,1},{65,65},{66,129},{67,193},{128... | collective-permute-start | bytes 442376 | tf_op jit(solution)/shard_map/ppermute | solution.py:138
  20.3 1.1 slice_bitcast_fusion.1
  21.4 0.8 pad_maximum_fusion.1
  22.2 7.9 %all-to-all-start = ((bf16[32,16,384]{2,1,0:T(8,128)(2,1)}), bf16[32,16,384]{2,1,0:T(8,128)(2,1)S(1)}, u32[]{:S(2)}, u32[]{:S(2)}) async-start(bf16[32,16,384]{2,1,0:T(8,128)(2,1)} %bitcast.5), calls=%async_computation | async-start | bytes 786432 | tf_op jit(solution)/shard_map/all_to_all | solution.py:156
  30.1 5.8 %collective-permute-done.2 = bf16[96,768]{1,0:T(8,128)(2,1)S(1)} collective-permute-done((bf16[96,768]{1,0:T(8,128)(2,1)}, bf16[96,768]{1,0:T(8,128)(2,1)S(1)}, u32[]{:S(2)}, u32[]{:S(2)}) %collective-permute-start.2) | collective-permute-done | bytes 147488 | tf_op jit(solution)/shard_map/ppermute | solution.py:138
  35.9 0.0 collective-permute-done.1
  36.0 2.2 %all-to-all-done = bf16[32,16,384]{2,1,0:T(8,128)(2,1)S(1)} async-done(((bf16[32,16,384]{2,1,0:T(8,128)(2,1)}), bf16[32,16,384]{2,1,0:T(8,128)(2,1)S(1)}, u32[]{:S(2)}, u32[]{:S(2)}) %all-to-all-start) | async-done | bytes 393248 | tf_op jit(solution)/shard_map/all_to_all | solution.py:156
  38.2 2.7 %broadcast_in_dim.6 = bf16[16,2,96,768]{3,2,1,0:T(8,128)(2,1)} broadcast(bf16[2,96,768]{2,1,0:T(8,128)(2,1)S(1)} %pad_maximum_fusion.2), dimensions={1,2,3} | broadcast | bytes 5013504 | tf_op jit(solution)/shard_map/broadcast_in_dim | solution.py:164
  40.9 0.0 copy-start.3
  40.9 6.8 %all-to-all-start.1 = ((bf16[16,2,96,768]{3,2,1,0:T(8,128)(2,1)}), bf16[16,2,96,768]{3,2,1,0:T(8,128)(2,1)}, u32[]{:S(2)}, u32[]{:S(2)}) async-start(bf16[16,2,96,768]{3,2,1,0:T(8,128)(2,1)} %broadcast_in_dim.6), calls=%async_computation.1 | async-start | bytes 9437184 | tf_op jit(solution)/shard_map/all_to_all | solution.py:163
  47.7 0.0 copy-start
  47.7 0.0 copy-start.1
  47.7 0.0 copy-start.2
  47.7 15.2 %collective-permute-start = (bf16[32,16,384]{2,1,0:T(8,128)(2,1)S(1)}, bf16[32,16,384]{2,1,0:T(8,128)(2,1)S(1)}, u32[]{:S(2)}, u32[]{:S(2)}) collective-permute-start(bf16[32,16,384]{2,1,0:T(8,128)(2,1)S(1)} %all-to-all-done), channel_id=1, source_target_pairs={{0,256},{256,0},{1,257},{257,1},{2,258},{258,2},{3,259},{259,3},{4... | collective-permute-start | bytes 1179656 | tf_op jit(solution)/shard_map/ppermute | solution.py:157
  62.9 21.9 %collective-permute-done = bf16[32,16,384]{2,1,0:T(8,128)(2,1)S(1)} collective-permute-done((bf16[32,16,384]{2,1,0:T(8,128)(2,1)S(1)}, bf16[32,16,384]{2,1,0:T(8,128)(2,1)S(1)}, u32[]{:S(2)}, u32[]{:S(2)}) %collective-permute-start) | collective-permute-done | bytes 393248 | tf_op jit(solution)/shard_map/ppermute | solution.py:157
  84.8 32.2 %all-to-all-done.1 = bf16[16,2,96,768]{3,2,1,0:T(8,128)(2,1)} async-done(((bf16[16,2,96,768]{3,2,1,0:T(8,128)(2,1)}), bf16[16,2,96,768]{3,2,1,0:T(8,128)(2,1)}, u32[]{:S(2)}, u32[]{:S(2)}) %all-to-all-start.1) | async-done | bytes 4718624 | tf_op jit(solution)/shard_map/all_to_all | solution.py:163
  117.0 1.9 collective-permute-start.6
  119.0 0.0 copy-done.3
  119.0 0.1 compare_select_fusion
  119.1 0.1 copy.7
  119.1 0.1 reshape.23
  119.3 0.1 pad_maximum_fusion
  119.4 1.5 gather_fusion
  120.9 8.8 %all-to-all-start.2 = ((bf16[32,2,16,384]{3,2,1,0:T(8,128)(2,1)}), bf16[32,2,16,384]{3,2,1,0:T(8,128)(2,1)S(1)}, u32[]{:S(2)}, u32[]{:S(2)}) async-start(bf16[32,2,16,384]{3,2,1,0:T(8,128)(2,1)} %bitcast.10), calls=%async_computation.2 | async-start | bytes 1572864 | tf_op jit(solution)/shard_map/all_to_all | solution.py:175
  129.7 12.0 %all-to-all-done.2 = bf16[32,2,16,384]{3,2,1,0:T(8,128)(2,1)S(1)} async-done(((bf16[32,2,16,384]{3,2,1,0:T(8,128)(2,1)}), bf16[32,2,16,384]{3,2,1,0:T(8,128)(2,1)S(1)}, u32[]{:S(2)}, u32[]{:S(2)}) %all-to-all-start.2) | async-done | bytes 786464 | tf_op jit(solution)/shard_map/all_to_all | solution.py:175
  141.7 0.0 copy-done
  141.8 0.0 copy-done.1
  141.8 0.0 copy-done.2
  141.8 1.9 shard_map.55.refs_0_
  143.6 10.8 %collective-permute-start.5 = (bf16[128,768]{1,0:T(8,128)(2,1)S(1)}, bf16[128,768]{1,0:T(8,128)(2,1)S(1)}, u32[]{:S(2)}, u32[]{:S(2)}) collective-permute-start(bf16[128,768]{1,0:T(8,128)(2,1)S(1)} %shard_map.55.refs_0_), channel_id=1, source_target_pairs={{0,3},{1,2},{2,1},{3,0},{4,7},{5,6},{6,5},{7,4},{8,11},{9,10},{10,... | collective-permute-start | bytes 589832 | tf_op jit(solution)/shard_map/ppermute | solution.py:187
  154.4 5.8 %collective-permute-start.4 = (bf16[128,768]{1,0:T(8,128)(2,1)S(1)}, bf16[128,768]{1,0:T(8,128)(2,1)S(1)}, u32[]{:S(2)}, u32[]{:S(2)}) collective-permute-start(bf16[128,768]{1,0:T(8,128)(2,1)S(1)} %shard_map.55.refs_0_), channel_id=1, source_target_pairs={{0,2},{1,3},{2,0},{3,1},{4,6},{5,7},{6,4},{7,5},{8,10},{9,11},{10,... | collective-permute-start | bytes 589832 | tf_op jit(solution)/shard_map/ppermute | solution.py:187
  160.2 1.9 collective-permute-start.3
  162.2 0.1 pad_add_fusion.place_ref
  162.2 0.0 collective-permute-done.5.refs_3_
  162.3 10.3 %collective-permute-done.4.refs_2_ = bf16[128,768]{1,0:T(8,128)(2,1)S(1)} collective-permute-done((bf16[128,768]{1,0:T(8,128)(2,1)S(1)}, bf16[128,768]{1,0:T(8,128)(2,1)S(1)}, u32[]{:S(2)}, u32[]{:S(2)}) %collective-permute-start.4) | collective-permute-done | bytes 196640 | tf_op jit(solution)/shard_map/ppermute | solution.py:187
  172.5 0.3 collective-permute-done.3.refs_1_
  172.9 0.0 collective-permute-done.6
  172.9 4.2 %shard_map.57 = bf16[128,768]{1,0:T(8,128)(2,1)S(1)} custom-call(s32[5]{0:T(128)S(1)} %pad_add_fusion.place_ref, bf16[128,768]{1,0:T(8,128)(2,1)S(1)} %shard_map.55.refs_0_, bf16[128,768]{1,0:T(8,128)(2,1)S(1)} %collective-permute-done.3.refs_1_, bf16[128,768]{1,0:T(8,128)(2,1)S(1)} %collective-permute-done.4.refs_2_, ...), custom_call_target="tpu_custom_call" | custom-call | flops 603979776 | bytes 5505024 | tf_op jit(solution)/shard_map/pallas_call | solution.py:58
  177.1 6.0 %collective-permute-start.7 = (bf16[128,768]{1,0:T(8,128)(2,1)S(1)}, bf16[128,768]{1,0:T(8,128)(2,1)S(1)}, u32[]{:S(2)}, u32[]{:S(2)}) collective-permute-start(bf16[128,768]{1,0:T(8,128)(2,1)S(1)} %shard_map.57), channel_id=1, source_target_pairs={{0,4},{4,0},{1,5},{5,1},{2,6},{6,2},{3,7},{7,3},{8,12},{12,8},{9,1... | collective-permute-start | bytes 589832 | tf_op jit(solution)/shard_map/ppermute | solution.py:193
  183.1 4.2 %shard_map.56 = f32[128,768]{1,0:T(8,128)S(1)} custom-call(s32[5]{0:T(128)S(1)} %pad_add_fusion.place_ref, bf16[128,768]{1,0:T(8,128)(2,1)S(1)} %shard_map.55.refs_0_, bf16[128,768]{1,0:T(8,128)(2,1)S(1)} %collective-permute-done.3.refs_1_, bf16[128,768]{1,0:T(8,128)(2,1)S(1)} %collective-permute-done.4.refs_2_, ...), custom_call_target="tpu_custom_call" | custom-call | flops 603979776 | bytes 5505024 | tf_op jit(solution)/shard_map/pallas_call | solution.py:58
  187.3 13.6 %collective-permute-done.7 = bf16[128,768]{1,0:T(8,128)(2,1)S(1)} collective-permute-done((bf16[128,768]{1,0:T(8,128)(2,1)S(1)}, bf16[128,768]{1,0:T(8,128)(2,1)S(1)}, u32[]{:S(2)}, u32[]{:S(2)}) %collective-permute-start.7) | collective-permute-done | bytes 196640 | tf_op jit(solution)/shard_map/ppermute | solution.py:193
  201.0 0.7 add_convert_fusion
  (4 shorter events, 0.1 us)
Async XLA Ops:
  0.0 35.9 %collective-permute-start.2 = (bf16[96,768]{1,0:T(8,128)(2,1)}, bf16[96,768]{1,0:T(8,128)(2,1)S(1)}, u32[]{:S(2)}, u32[]{:S(2)}) collective-permute-start(bf16[96,768]{1,0:T(8,128)(2,1)} %bitcast.22), channel_id=1, source_target_pairs={{0,256},{1,320},{2,384},{3,448},{64,257},{65,321},{66,385},{67,449... | collective-permute-start | bytes 442376 | tf_op jit(solution)/shard_map/ppermute | solution.py:138
  14.3 21.6 %collective-permute-start.1 = (bf16[96,768]{1,0:T(8,128)(2,1)}, bf16[96,768]{1,0:T(8,128)(2,1)S(1)}, u32[]{:S(2)}, u32[]{:S(2)}) collective-permute-start(bf16[96,768]{1,0:T(8,128)(2,1)} %bitcast.23), channel_id=1, source_target_pairs={{0,0},{1,64},{2,128},{3,192},{64,1},{65,65},{66,129},{67,193},{128... | collective-permute-start | bytes 442376 | tf_op jit(solution)/shard_map/ppermute | solution.py:138
  22.2 16.0 %all-to-all-start = ((bf16[32,16,384]{2,1,0:T(8,128)(2,1)}), bf16[32,16,384]{2,1,0:T(8,128)(2,1)S(1)}, u32[]{:S(2)}, u32[]{:S(2)}) async-start(bf16[32,16,384]{2,1,0:T(8,128)(2,1)} %bitcast.5), calls=%async_computation | async-start | bytes 786432 | tf_op jit(solution)/shard_map/all_to_all | solution.py:156
  40.9 78.0 %copy-start.3 = (s32[2,64]{1,0:T(2,128)S(1)}, s32[2,64]{1,0:T(2,128)}, u32[]{:S(2)}) copy-start(s32[2,64]{1,0:T(2,128)} %param.8) | copy-start | bytes 1540
  40.9 76.1 %all-to-all-start.1 = ((bf16[16,2,96,768]{3,2,1,0:T(8,128)(2,1)}), bf16[16,2,96,768]{3,2,1,0:T(8,128)(2,1)}, u32[]{:S(2)}, u32[]{:S(2)}) async-start(bf16[16,2,96,768]{3,2,1,0:T(8,128)(2,1)} %broadcast_in_dim.6), calls=%async_computation.1 | async-start | bytes 9437184 | tf_op jit(solution)/shard_map/all_to_all | solution.py:163
  47.7 94.1 %copy-start = (bf16[128,768]{1,0:T(8,128)(2,1)S(1)}, bf16[128,768]{1,0:T(8,128)(2,1)}, u32[]{:S(2)}) copy-start(bf16[128,768]{1,0:T(8,128)(2,1)} %k_ref.1) | copy-start | bytes 589828
  47.7 94.1 %copy-start.1 = (bf16[128,768]{1,0:T(8,128)(2,1)S(1)}, bf16[128,768]{1,0:T(8,128)(2,1)}, u32[]{:S(2)}) copy-start(bf16[128,768]{1,0:T(8,128)(2,1)} %v_ref.1) | copy-start | bytes 589828
  47.7 94.1 %copy-start.2 = (bf16[128,768]{1,0:T(8,128)(2,1)S(1)}, bf16[128,768]{1,0:T(8,128)(2,1)}, u32[]{:S(2)}) copy-start(bf16[128,768]{1,0:T(8,128)(2,1)} %q_ref.1) | copy-start | bytes 589828
  47.7 37.1 %collective-permute-start = (bf16[32,16,384]{2,1,0:T(8,128)(2,1)S(1)}, bf16[32,16,384]{2,1,0:T(8,128)(2,1)S(1)}, u32[]{:S(2)}, u32[]{:S(2)}) collective-permute-start(bf16[32,16,384]{2,1,0:T(8,128)(2,1)S(1)} %all-to-all-done), channel_id=1, source_target_pairs={{0,256},{256,0},{1,257},{257,1},{2,258},{258,2},{3,259},{259,3},{4... | collective-permute-start | bytes 1179656 | tf_op jit(solution)/shard_map/ppermute | solution.py:157
  117.0 55.8 %collective-permute-start.6 = (bf16[16,2,96,768]{3,2,1,0:T(8,128)(2,1)}, bf16[16,2,96,768]{3,2,1,0:T(8,128)(2,1)}, u32[]{:S(2)}, u32[]{:S(2)}) collective-permute-start(bf16[16,2,96,768]{3,2,1,0:T(8,128)(2,1)} %all-to-all-done.1), channel_id=1, source_target_pairs={{0,8},{8,0},{1,9},{9,1},{2,10},{10,2},{3,11},{11,3},{4,12},{12,4},... | collective-permute-start | bytes 14155784 | tf_op jit(solution)/shard_map/ppermute | solution.py:177
  120.9 20.9 %all-to-all-start.2 = ((bf16[32,2,16,384]{3,2,1,0:T(8,128)(2,1)}), bf16[32,2,16,384]{3,2,1,0:T(8,128)(2,1)S(1)}, u32[]{:S(2)}, u32[]{:S(2)}) async-start(bf16[32,2,16,384]{3,2,1,0:T(8,128)(2,1)} %bitcast.10), calls=%async_computation.2 | async-start | bytes 1572864 | tf_op jit(solution)/shard_map/all_to_all | solution.py:175
  143.6 18.6 %collective-permute-start.5 = (bf16[128,768]{1,0:T(8,128)(2,1)S(1)}, bf16[128,768]{1,0:T(8,128)(2,1)S(1)}, u32[]{:S(2)}, u32[]{:S(2)}) collective-permute-start(bf16[128,768]{1,0:T(8,128)(2,1)S(1)} %shard_map.55.refs_0_), channel_id=1, source_target_pairs={{0,3},{1,2},{2,1},{3,0},{4,7},{5,6},{6,5},{7,4},{8,11},{9,10},{10,... | collective-permute-start | bytes 589832 | tf_op jit(solution)/shard_map/ppermute | solution.py:187
  154.4 18.1 %collective-permute-start.4 = (bf16[128,768]{1,0:T(8,128)(2,1)S(1)}, bf16[128,768]{1,0:T(8,128)(2,1)S(1)}, u32[]{:S(2)}, u32[]{:S(2)}) collective-permute-start(bf16[128,768]{1,0:T(8,128)(2,1)S(1)} %shard_map.55.refs_0_), channel_id=1, source_target_pairs={{0,2},{1,3},{2,0},{3,1},{4,6},{5,7},{6,4},{7,5},{8,10},{9,11},{10,... | collective-permute-start | bytes 589832 | tf_op jit(solution)/shard_map/ppermute | solution.py:187
  160.2 12.6 %collective-permute-start.3 = (bf16[128,768]{1,0:T(8,128)(2,1)S(1)}, bf16[128,768]{1,0:T(8,128)(2,1)S(1)}, u32[]{:S(2)}, u32[]{:S(2)}) collective-permute-start(bf16[128,768]{1,0:T(8,128)(2,1)S(1)} %shard_map.55.refs_0_), channel_id=1, source_target_pairs={{0,1},{1,0},{2,3},{3,2},{4,5},{5,4},{6,7},{7,6},{8,9},{9,8},{10,11... | collective-permute-start | bytes 589832 | tf_op jit(solution)/shard_map/ppermute | solution.py:187
  177.1 23.9 %collective-permute-start.7 = (bf16[128,768]{1,0:T(8,128)(2,1)S(1)}, bf16[128,768]{1,0:T(8,128)(2,1)S(1)}, u32[]{:S(2)}, u32[]{:S(2)}) collective-permute-start(bf16[128,768]{1,0:T(8,128)(2,1)S(1)} %shard_map.57), channel_id=1, source_target_pairs={{0,4},{4,0},{1,5},{5,1},{2,6},{6,2},{3,7},{7,3},{8,12},{12,8},{9,1... | collective-permute-start | bytes 589832 | tf_op jit(solution)/shard_map/ppermute | solution.py:193

commit v11 on v8

--- a/solution.py
+++ b/solution.py
@@ -16,7 +16,6 @@
 PLANE = ("x", "y", "c")
 SWAP = ((0, 1), (1, 0))
 QUAD = 4
-HINT_FLOPS, HINT_BYTES = 120 * 10**9, 10**6
 HALVES = 2
 PIECE = 16
 
@@ -108,7 +107,9 @@
         out_shape=jax.ShapeDtypeStruct(queries.shape, queries.dtype),
         compiler_params=pltpu.CompilerParams(vmem_limit_bytes=32 << 20),
         cost_estimate=pl.CostEstimate(
-            flops=HINT_FLOPS, bytes_accessed=HINT_BYTES, transcendentals=0
+            flops=4 * queries.size * (1 + ROUNDS) * queries.shape[0],
+            bytes_accessed=2 * (4 * queries.size + routed.size),
+            transcendentals=queries.size * (1 + ROUNDS),
         ),
     )(queries, keys, values, routed)
 
@@ -119,8 +120,19 @@
     quad, member = lax.axis_index("p"), lax.axis_index("q")
     seats = lax.axis_size(PLANE)
 
-    w_near = w_out.T
-    w_far = lax.ppermute(w_near, "zh", SWAP)
+    w_near, w_far = [
+        lax.ppermute(
+            w_out.T,
+            ("zh", "x", "q"),
+            [
+                ((zh * QUAD + x) * QUAD + q, ((zh ^ flip) * QUAD + q) * QUAD + x)
+                for zh in range(2)
+                for x in range(QUAD)
+                for q in range(QUAD)
+            ],
+        )
+        for flip in range(2)
+    ]
     keeps_near = half == quad
     w_pair = jnp.stack(
         (jnp.where(keeps_near, w_near, w_far), jnp.where(keeps_near, w_far, w_near))
@@ -132,13 +144,11 @@
     )
     own = own.reshape(seats, PIECE, part)
     spread = lax.all_to_all(own, PLANE, split_axis=0, concat_axis=0, tiled=True)
-    spread, w_pair = lax.optimization_barrier((spread, w_pair))
 
-    w_pair = lax.ppermute(
-        w_pair,
-        ("x", "q"),
-        [(x * QUAD + q, q * QUAD + x) for x in range(QUAD) for q in range(QUAD)],
-    )
+    token = jnp.zeros((seats, 8, 128), jnp.bfloat16)
+    token, w_pair, spread = lax.optimization_barrier((token, w_pair, spread))
+    token = lax.all_to_all(token, PLANE, split_axis=0, concat_axis=0, tiled=True)
+    spread = spread + token[0, 0, 0]
     far = lax.ppermute(spread, "zh", SWAP)
     w_all = lax.all_gather(w_pair, PLANE, axis=0, tiled=False)
     w_all = w_all.reshape(QUAD, seats // QUAD, 2, -1, width)

time: 204 us -> 189 us (0.926)
  blocking collectives: 55.4 us -> 32.7 us
  waiting for transfers between devices: 66.5 us -> 72 us
  starting transfers between devices: 48.6 us -> 52 us
  local copies, waits for them, and re-layouts: 5.48 us -> 2.53 us
    all_to_all x1, blocking collectives: 55.4 us -> 20 us  [body(): lax.all_to_all(chosen, PLANE, split_axis=0, concat_axis=0, tiled=True)]
    all_to_all x0 -> x1, blocking collectives: none -> 12.8 us  [body(): lax.all_to_all(token, PLANE, split_axis=0, concat_axis=0, tiled=True)]
    ppermute x1, starting transfers between devices: 1.92 us -> 11.6 us  [body(): far = lax.ppermute(spread, 'zh', SWAP)]
    ppermute x1, waiting for transfers between devices: 21.6 us -> 30.7 us  [body(): far = lax.ppermute(spread, 'zh', SWAP)]
    all_to_all x1, waiting for transfers between devices: 7.02 us -> 0.01 us  [body(): spread = lax.all_to_all(own, PLANE, split_axis=0, concat_axis=0, tiled=True)]
    ppermute x3, starting transfers between devices: 13.6 us -> 10.1 us  [body(): lax.ppermute(attended, 'q', [(i, i ^ k) for i in range(QUAD)])]
    unnamed x8 -> x6, local copies, waits for them, and re-layouts: 3.49 us -> 0.01 us
    ppermute x1, starting transfers between devices: 4.4 us -> 1.92 us  [body(): arrived = lax.ppermute(sent, 'p', SWAP)]
  transfers between devices with their start and end apart: 9 -> 9, of which waited for: 5 -> 4; matrix products, arithmetic and copies ran while one was open for 2% -> 3% of each run, Pallas kernels for 3% -> 3%
where the time goes in v11:
time: 189 us; the launch traced here: 187 us
  waiting for transfers between devices  72 us (38%)
  starting transfers between devices  52 us (28%)
  blocking collectives  32.7 us (17%)
  between operations  13.6 us (7%)
  Pallas kernels  10.3 us (5%)
  other arithmetic  3.86 us (2%)
  local copies, waits for them, and re-layouts  2.53 us (1%)
    ppermute x1, waiting for transfers between devices, body(): far = lax.ppermute(spread, 'zh', SWAP)  30.7 us
    ppermute x2, starting transfers between devices, body(): lax.ppermute(w_out.T, ('zh', 'x', 'q'), [((zh * QUAD + x) * QUAD + q, ((z...  20.4 us
    all_to_all x1, blocking collectives, body(): lax.all_to_all(chosen, PLANE, split_axis=0, concat_axis=0, tiled=True)  20 us
    ppermute x1, waiting for transfers between devices, body(): arrived = lax.ppermute(sent, 'p', SWAP)  17 us
    all_to_all x1, blocking collectives, body(): lax.all_to_all(token, PLANE, split_axis=0, concat_axis=0, tiled=True)  12.8 us
    ppermute x2, waiting for transfers between devices, body(): lax.ppermute(w_out.T, ('zh', 'x', 'q'), [((zh * QUAD + x) * QUAD + q, ((z...  12.3 us
    ppermute x3, waiting for transfers between devices, body(): lax.ppermute(attended, 'q', [(i, i ^ k) for i in range(QUAD)])  12 us
    ppermute x1, starting transfers between devices, body(): far = lax.ppermute(spread, 'zh', SWAP)  11.6 us
  transfers between devices with their start and end apart: 9, of which 4 were waited for; matrix products, arithmetic and copies ran while one was open for 3% of the time, Pallas kernels for 3%

profile of v11, /device:TPU:6, one launch (start us, length us, event | category | flops | bytes accessed | tf_op | source)
XLA Modules:
  0.0 186.9 jit_solution(11990426408475812733)
XLA Ops:
  6.5 0.0 copy-start
  6.5 0.0 copy-start.1
  6.5 0.0 copy-start.2
  6.5 6.6 %collective-permute-start = (bf16[96,768]{1,0:T(8,128)(2,1)}, bf16[96,768]{1,0:T(8,128)(2,1)S(1)}, u32[]{:S(2)}, u32[]{:S(2)}) collective-permute-start(bf16[96,768]{1,0:T(8,128)(2,1)} %bitcast.24), channel_id=1, source_target_pairs={{0,0},{1,64},{2,128},{3,192},{64,1},{65,65},{66,129},{67,193},{128... | collective-permute-start | bytes 442376 | tf_op jit(solution)/shard_map/ppermute | solution.py:124
  13.1 13.9 %collective-permute-start.1 = (bf16[96,768]{1,0:T(8,128)(2,1)}, bf16[96,768]{1,0:T(8,128)(2,1)S(1)}, u32[]{:S(2)}, u32[]{:S(2)}) collective-permute-start(bf16[96,768]{1,0:T(8,128)(2,1)} %bitcast.25), channel_id=1, source_target_pairs={{0,256},{1,320},{2,384},{3,448},{64,257},{65,321},{66,385},{67,449... | collective-permute-start | bytes 442376 | tf_op jit(solution)/shard_map/ppermute | solution.py:124
  27.0 1.1 slice_bitcast_fusion.1
  28.1 0.8 pad_maximum_fusion.1
  28.9 7.9 %all-to-all-start = ((bf16[32,16,384]{2,1,0:T(8,128)(2,1)}), bf16[32,16,384]{2,1,0:T(8,128)(2,1)S(1)}, u32[]{:S(2)}, u32[]{:S(2)}) async-start(bf16[32,16,384]{2,1,0:T(8,128)(2,1)} %bitcast.7), calls=%async_computation | async-start | bytes 786432 | tf_op jit(solution)/shard_map/all_to_all | solution.py:146
  36.8 0.0 all-gather.3.cloned.1.call-start
  36.9 0.0 collective-permute-done
  36.9 12.3 %collective-permute-done.1 = bf16[96,768]{1,0:T(8,128)(2,1)S(1)} collective-permute-done((bf16[96,768]{1,0:T(8,128)(2,1)}, bf16[96,768]{1,0:T(8,128)(2,1)S(1)}, u32[]{:S(2)}, u32[]{:S(2)}) %collective-permute-start.1) | collective-permute-done | bytes 147488 | tf_op jit(solution)/shard_map/ppermute | solution.py:124
  49.2 0.7 pad_maximum_fusion.2
  49.9 0.0 all-to-all-done
  49.9 0.0 all-gather.3.cloned.1.call-update
  49.9 12.8 %all_to_all.15 = bf16[32,8,128]{2,1,0:T(8,128)(2,1)S(1)} all-to-all(bf16[32,8,128]{2,1,0:T(8,128)(2,1)S(1)} %broadcast_in_dim.6), channel_id=1, replica_groups=mesh['zh'=2,'x'=4,'y'=4,'c'=2,'p'=2,'q'=4] {'x','y','c'}, dimensions={0} | all-to-all | bytes 131072 | tf_op jit(solution)/shard_map/all_to_all | solution.py:150
  62.7 0.5 slice.22
  63.2 0.7 broadcast_add_fusion
  63.9 11.6 %collective-permute-start.2 = (bf16[32,16,384]{2,1,0:T(8,128)(2,1)S(1)}, bf16[32,16,384]{2,1,0:T(8,128)(2,1)S(1)}, u32[]{:S(2)}, u32[]{:S(2)}) collective-permute-start(bf16[32,16,384]{2,1,0:T(8,128)(2,1)S(1)} %broadcast_add_fusion), channel_id=1, source_target_pairs={{0,256},{256,0},{1,257},{257,1},{2,258},{258,2},{3,259},{259,3},{4... | collective-permute-start | bytes 1179656 | tf_op jit(solution)/shard_map/ppermute | solution.py:152
  75.5 0.8 compare_select_fusion
  76.3 0.1 copy.8
  76.4 0.1 reshape.14
  76.5 30.7 %collective-permute-done.2 = bf16[32,16,384]{2,1,0:T(8,128)(2,1)S(1)} collective-permute-done((bf16[32,16,384]{2,1,0:T(8,128)(2,1)S(1)}, bf16[32,16,384]{2,1,0:T(8,128)(2,1)S(1)}, u32[]{:S(2)}, u32[]{:S(2)}) %collective-permute-start.2) | collective-permute-done | bytes 393248 | tf_op jit(solution)/shard_map/ppermute | solution.py:152
  107.2 0.1 pad_maximum_fusion
  107.3 0.7 gather_fusion
  108.0 20.0 %all_to_all.16 = bf16[32,2,16,384]{3,2,1,0:T(8,128)(2,1)S(1)} all-to-all(bf16[32,2,16,384]{3,2,1,0:T(8,128)(2,1)S(1)} %bitcast.23), channel_id=1, replica_groups=mesh['zh'=2,'x'=4,'y'=4,'c'=2,'p'=2,'q'=4] {'x','y','c'}, dimensions={0} | all-to-all | bytes 1572864 | tf_op jit(solution)/shard_map/all_to_all | solution.py:159
  128.0 0.0 copy-done
  128.0 0.0 copy-done.1
  128.0 0.0 copy-done.2
  128.0 1.9 %shard_map.55.refs_0_ = bf16[128,768]{1,0:T(8,128)(2,1)S(1)} custom-call(bf16[128,768]{1,0:T(8,128)(2,1)S(1)} %copy-done.2, bf16[128,768]{1,0:T(8,128)(2,1)S(1)} %copy-done, bf16[128,768]{1,0:T(8,128)(2,1)S(1)} %copy-done.1, bf16[4,8,2,16,384]{4,3,2,1,0:T(8,128)(2,1)S(1)} %bitcast.20), custom_call_target="tpu_custom_call" | custom-call | flops 150994944 | bytes 1572864 | tf_op jit(solution)/shard_map/pallas_call | solution.py:103
  129.9 1.9 %collective-permute-start.3 = (bf16[128,768]{1,0:T(8,128)(2,1)S(1)}, bf16[128,768]{1,0:T(8,128)(2,1)S(1)}, u32[]{:S(2)}, u32[]{:S(2)}) collective-permute-start(bf16[128,768]{1,0:T(8,128)(2,1)S(1)} %shard_map.55.refs_0_), channel_id=1, source_target_pairs={{0,1},{1,0},{2,3},{3,2},{4,5},{5,4},{6,7},{7,6},{8,9},{9,8},{10,11... | collective-permute-start | bytes 589832 | tf_op jit(solution)/shard_map/ppermute | solution.py:168
  131.8 6.0 %collective-permute-start.4 = (bf16[128,768]{1,0:T(8,128)(2,1)S(1)}, bf16[128,768]{1,0:T(8,128)(2,1)S(1)}, u32[]{:S(2)}, u32[]{:S(2)}) collective-permute-start(bf16[128,768]{1,0:T(8,128)(2,1)S(1)} %shard_map.55.refs_0_), channel_id=1, source_target_pairs={{0,2},{1,3},{2,0},{3,1},{4,6},{5,7},{6,4},{7,5},{8,10},{9,11},{10,... | collective-permute-start | bytes 589832 | tf_op jit(solution)/shard_map/ppermute | solution.py:168
  137.8 2.2 %collective-permute-start.5 = (bf16[128,768]{1,0:T(8,128)(2,1)S(1)}, bf16[128,768]{1,0:T(8,128)(2,1)S(1)}, u32[]{:S(2)}, u32[]{:S(2)}) collective-permute-start(bf16[128,768]{1,0:T(8,128)(2,1)S(1)} %shard_map.55.refs_0_), channel_id=1, source_target_pairs={{0,3},{1,2},{2,1},{3,0},{4,7},{5,6},{6,5},{7,4},{8,11},{9,10},{10,... | collective-permute-start | bytes 589832 | tf_op jit(solution)/shard_map/ppermute | solution.py:168
  140.0 0.0 collective-permute-done.3.refs_1_
  140.0 12.0 %collective-permute-done.4.refs_2_ = bf16[128,768]{1,0:T(8,128)(2,1)S(1)} collective-permute-done((bf16[128,768]{1,0:T(8,128)(2,1)S(1)}, bf16[128,768]{1,0:T(8,128)(2,1)S(1)}, u32[]{:S(2)}, u32[]{:S(2)}) %collective-permute-start.4) | collective-permute-done | bytes 196640 | tf_op jit(solution)/shard_map/ppermute | solution.py:168
  152.0 0.0 collective-permute-done.5.refs_3_
  152.0 0.0 all-gather.3.cloned.1.call-done
  152.0 4.2 %shard_map.57 = bf16[128,768]{1,0:T(8,128)(2,1)S(1)} custom-call(s32[4]{0:T(128)S(1)} %iota_xor_fusion.order_ref, bf16[128,768]{1,0:T(8,128)(2,1)S(1)} %shard_map.55.refs_0_, bf16[128,768]{1,0:T(8,128)(2,1)S(1)} %collective-permute-done.3.refs_1_, bf16[128,768]{1,0:T(8,128)(2,1)S(1)} %collective-permute-done.4.refs_2_, ...), custom_call_target="tpu_custom_call" | custom-call | flops 603979776 | bytes 5505024 | tf_op jit(solution)/shard_map/pallas_call | solution.py:48
  156.2 1.9 %collective-permute-start.6 = (bf16[128,768]{1,0:T(8,128)(2,1)S(1)}, bf16[128,768]{1,0:T(8,128)(2,1)S(1)}, u32[]{:S(2)}, u32[]{:S(2)}) collective-permute-start(bf16[128,768]{1,0:T(8,128)(2,1)S(1)} %shard_map.57), channel_id=1, source_target_pairs={{0,4},{4,0},{1,5},{5,1},{2,6},{6,2},{3,7},{7,3},{8,12},{12,8},{9,1... | collective-permute-start | bytes 589832 | tf_op jit(solution)/shard_map/ppermute | solution.py:172
  158.1 4.2 %shard_map.56 = f32[128,768]{1,0:T(8,128)S(1)} custom-call(s32[4]{0:T(128)S(1)} %iota_xor_fusion.order_ref, bf16[128,768]{1,0:T(8,128)(2,1)S(1)} %shard_map.55.refs_0_, bf16[128,768]{1,0:T(8,128)(2,1)S(1)} %collective-permute-done.3.refs_1_, bf16[128,768]{1,0:T(8,128)(2,1)S(1)} %collective-permute-done.4.refs_2_, ...), custom_call_target="tpu_custom_call" | custom-call | flops 603979776 | bytes 5505024 | tf_op jit(solution)/shard_map/pallas_call | solution.py:48
  162.3 17.0 %collective-permute-done.6 = bf16[128,768]{1,0:T(8,128)(2,1)S(1)} collective-permute-done((bf16[128,768]{1,0:T(8,128)(2,1)S(1)}, bf16[128,768]{1,0:T(8,128)(2,1)S(1)}, u32[]{:S(2)}, u32[]{:S(2)}) %collective-permute-start.6) | collective-permute-done | bytes 196640 | tf_op jit(solution)/shard_map/ppermute | solution.py:172
  179.3 0.7 add_convert_fusion
  (4 shorter events, 0.0 us)
Async XLA Ops:
  6.5 121.5 %copy-start = (bf16[128,768]{1,0:T(8,128)(2,1)S(1)}, bf16[128,768]{1,0:T(8,128)(2,1)}, u32[]{:S(2)}) copy-start(bf16[128,768]{1,0:T(8,128)(2,1)} %k_ref.1) | copy-start | bytes 589828
  6.5 121.5 %copy-start.1 = (bf16[128,768]{1,0:T(8,128)(2,1)S(1)}, bf16[128,768]{1,0:T(8,128)(2,1)}, u32[]{:S(2)}) copy-start(bf16[128,768]{1,0:T(8,128)(2,1)} %v_ref.1) | copy-start | bytes 589828
  6.5 121.5 %copy-start.2 = (bf16[128,768]{1,0:T(8,128)(2,1)S(1)}, bf16[128,768]{1,0:T(8,128)(2,1)}, u32[]{:S(2)}) copy-start(bf16[128,768]{1,0:T(8,128)(2,1)} %q_ref.1) | copy-start | bytes 589828
  6.5 30.3 %collective-permute-start = (bf16[96,768]{1,0:T(8,128)(2,1)}, bf16[96,768]{1,0:T(8,128)(2,1)S(1)}, u32[]{:S(2)}, u32[]{:S(2)}) collective-permute-start(bf16[96,768]{1,0:T(8,128)(2,1)} %bitcast.24), channel_id=1, source_target_pairs={{0,0},{1,64},{2,128},{3,192},{64,1},{65,65},{66,129},{67,193},{128... | collective-permute-start | bytes 442376 | tf_op jit(solution)/shard_map/ppermute | solution.py:124
  13.1 36.0 %collective-permute-start.1 = (bf16[96,768]{1,0:T(8,128)(2,1)}, bf16[96,768]{1,0:T(8,128)(2,1)S(1)}, u32[]{:S(2)}, u32[]{:S(2)}) collective-permute-start(bf16[96,768]{1,0:T(8,128)(2,1)} %bitcast.25), channel_id=1, source_target_pairs={{0,256},{1,320},{2,384},{3,448},{64,257},{65,321},{66,385},{67,449... | collective-permute-start | bytes 442376 | tf_op jit(solution)/shard_map/ppermute | solution.py:124
  28.9 21.0 %all-to-all-start = ((bf16[32,16,384]{2,1,0:T(8,128)(2,1)}), bf16[32,16,384]{2,1,0:T(8,128)(2,1)S(1)}, u32[]{:S(2)}, u32[]{:S(2)}) async-start(bf16[32,16,384]{2,1,0:T(8,128)(2,1)} %bitcast.7), calls=%async_computation | async-start | bytes 786432 | tf_op jit(solution)/shard_map/all_to_all | solution.py:146
  36.8 115.2 %all-gather.3.cloned.1.call-start = ((), (), s32[]{:S(2)}) async-start(), calls=%async_computation.3 | async-start | bytes 9732096 | tf_op jit(solution)/shard_map/all_gather | solution.py:153
  63.9 43.3 %collective-permute-start.2 = (bf16[32,16,384]{2,1,0:T(8,128)(2,1)S(1)}, bf16[32,16,384]{2,1,0:T(8,128)(2,1)S(1)}, u32[]{:S(2)}, u32[]{:S(2)}) collective-permute-start(bf16[32,16,384]{2,1,0:T(8,128)(2,1)S(1)} %broadcast_add_fusion), channel_id=1, source_target_pairs={{0,256},{256,0},{1,257},{257,1},{2,258},{258,2},{3,259},{259,3},{4... | collective-permute-start | bytes 1179656 | tf_op jit(solution)/shard_map/ppermute | solution.py:152
  129.9 10.2 %collective-permute-start.3 = (bf16[128,768]{1,0:T(8,128)(2,1)S(1)}, bf16[128,768]{1,0:T(8,128)(2,1)S(1)}, u32[]{:S(2)}, u32[]{:S(2)}) collective-permute-start(bf16[128,768]{1,0:T(8,128)(2,1)S(1)} %shard_map.55.refs_0_), channel_id=1, source_target_pairs={{0,1},{1,0},{2,3},{3,2},{4,5},{5,4},{6,7},{7,6},{8,9},{9,8},{10,11... | collective-permute-start | bytes 589832 | tf_op jit(solution)/shard_map/ppermute | solution.py:168
  131.8 20.2 %collective-permute-start.4 = (bf16[128,768]{1,0:T(8,128)(2,1)S(1)}, bf16[128,768]{1,0:T(8,128)(2,1)S(1)}, u32[]{:S(2)}, u32[]{:S(2)}) collective-permute-start(bf16[128,768]{1,0:T(8,128)(2,1)S(1)} %shard_map.55.refs_0_), channel_id=1, source_target_pairs={{0,2},{1,3},{2,0},{3,1},{4,6},{5,7},{6,4},{7,5},{8,10},{9,11},{10,... | collective-permute-start | bytes 589832 | tf_op jit(solution)/shard_map/ppermute | solution.py:168
  137.8 14.2 %collective-permute-start.5 = (bf16[128,768]{1,0:T(8,128)(2,1)S(1)}, bf16[128,768]{1,0:T(8,128)(2,1)S(1)}, u32[]{:S(2)}, u32[]{:S(2)}) collective-permute-start(bf16[128,768]{1,0:T(8,128)(2,1)S(1)} %shard_map.55.refs_0_), channel_id=1, source_target_pairs={{0,3},{1,2},{2,1},{3,0},{4,7},{5,6},{6,5},{7,4},{8,11},{9,10},{10,... | collective-permute-start | bytes 589832 | tf_op jit(solution)/shard_map/ppermute | solution.py:168
  156.2 23.1 %collective-permute-start.6 = (bf16[128,768]{1,0:T(8,128)(2,1)S(1)}, bf16[128,768]{1,0:T(8,128)(2,1)S(1)}, u32[]{:S(2)}, u32[]{:S(2)}) collective-permute-start(bf16[128,768]{1,0:T(8,128)(2,1)S(1)} %shard_map.57), channel_id=1, source_target_pairs={{0,4},{4,0},{1,5},{5,1},{2,6},{6,2},{3,7},{7,3},{8,12},{12,8},{9,1... | collective-permute-start | bytes 589832 | tf_op jit(solution)/shard_map/ppermute | solution.py:172
Sparse Core Ops, SparseCore 0:
  50.0 78.6 all-gather.2

commit v12 on v6

--- a/solution.py
+++ b/solution.py
@@ -16,7 +16,7 @@
 PLANE = ("x", "y", "c")
 SWAP = ((0, 1), (1, 0))
 QUAD = 4
-HINT_FLOPS, HINT_BYTES = 182 * 10**9, 10**6
+HINT_FLOPS, HINT_BYTES = 183 * 10**9, 10**6
 HALVES = 2
 PIECE = 16
 
@@ -134,17 +134,20 @@
     spread, w_near = lax.optimization_barrier((spread, w_near))
 
     w_far = lax.ppermute(w_near, "zh", SWAP)
-    far = lax.ppermute(spread, "zh", SWAP)
     keeps_near = half == quad
     w_pair = jnp.stack(
         (jnp.where(keeps_near, w_near, w_far), jnp.where(keeps_near, w_far, w_near))
     )
+    spread = jnp.split(spread, 2)
+    far = [lax.ppermute(spread[0], "zh", SWAP)]
+    spread[1], w_pair = lax.optimization_barrier((spread[1], w_pair))
+    far.append(lax.ppermute(spread[1], "zh", SWAP))
     w_all = lax.all_gather(w_pair, PLANE, axis=0, tiled=False)
     w_all = w_all.reshape(QUAD, seats // QUAD, 2, -1, width)
 
     wanted = lax.dynamic_slice_in_dim(plan, half * seats, seats, 1)
     place = (wanted // seats ^ half) * seats + wanted % seats
-    chosen = jnp.concatenate((spread, far)).at[place.T].get(mode="promise_in_bounds")
+    chosen = jnp.concatenate((*spread, *far)).at[place.T].get(mode="promise_in_bounds")
     routed = lax.all_to_all(chosen, PLANE, split_axis=0, concat_axis=0, tiled=True)
     attended = attend(
         queries,

time: 188 us -> 190 us (1.011)
  waiting for transfers between devices: 88 us -> 72.3 us
  starting transfers between devices: 47.3 us -> 60.8 us
  blocking collectives: 20.1 us -> 26.7 us
  local copies, waits for them, and re-layouts: 4.77 us -> 2.11 us
    ppermute x1 -> x2, waiting for transfers between devices: 27.4 us -> 7.32 us  [the longest x1 4.03 us: body(): far = [lax.ppermute(spread[0], 'zh', SWAP)]]
    ppermute x1 -> x2, starting transfers between devices: 1.92 us -> 15.5 us  [the longest x1 13.6 us: body(): far.append(lax.ppermute(spread[1], 'zh', SWAP))]
    all_to_all x1, blocking collectives: 20.1 us -> 26.7 us  [body(): lax.all_to_all(chosen, PLANE, split_axis=0, concat_axis=0, tiled=True)]
    all_gather x1, waiting for transfers between devices: 8.28 us -> 12.7 us  [body(): w_all = lax.all_gather(w_pair, PLANE, axis=0, tiled=False)]
    unnamed x6, local copies, waits for them, and re-layouts: 2.78 us -> 0.01 us
  transfers between devices with their start and end apart: 9 -> 10, of which waited for: 7 -> 8; matrix products, arithmetic and copies ran while one was open for 1% -> 1% of each run, Pallas kernels for 3% -> 3%
where the time goes in v12:
time: 190 us; the launch traced here: 189 us
  waiting for transfers between devices  72.3 us (38%)
  starting transfers between devices  60.8 us (32%)
  blocking collectives  26.7 us (14%)
  between operations  13.6 us (7%)
  Pallas kernels  10.3 us (5%)
  other arithmetic  3.21 us (2%)
  local copies, waits for them, and re-layouts  2.11 us (1%)
    all_to_all x1, blocking collectives, body(): lax.all_to_all(chosen, PLANE, split_axis=0, concat_axis=0, tiled=True)  26.7 us
    ppermute x1, waiting for transfers between devices, body(): w_far = lax.ppermute(w_near, 'zh', SWAP)  19.8 us
    ppermute x1, starting transfers between devices, body(): w_far = lax.ppermute(w_near, 'zh', SWAP)  13.8 us
    ppermute x1, waiting for transfers between devices, body(): arrived = lax.ppermute(sent, 'p', SWAP)  13.7 us
    ppermute x1, starting transfers between devices, body(): far.append(lax.ppermute(spread[1], 'zh', SWAP))  13.6 us
    all_gather x1, waiting for transfers between devices, body(): w_all = lax.all_gather(w_pair, PLANE, axis=0, tiled=False)  12.7 us
    ppermute x3, waiting for transfers between devices, body(): lax.ppermute(attended, 'q', [(i, i ^ k) for i in range(QUAD)])  10.8 us
    ppermute x3, starting transfers between devices, body(): lax.ppermute(attended, 'q', [(i, i ^ k) for i in range(QUAD)])  10.1 us
  transfers between devices with their start and end apart: 10, of which 8 were waited for; matrix products, arithmetic and copies ran while one was open for 1% of the time, Pallas kernels for 3%

profile of v12, /device:TPU:6, one launch (start us, length us, event | category | flops | bytes accessed | tf_op | source)
XLA Modules:
  0.0 188.9 jit_solution(1988123088921383162)
XLA Ops:
  6.5 0.0 copy-start
  6.5 0.0 copy-start.1
  6.5 0.0 copy-start.2
  6.5 1.1 slice_bitcast_fusion.1
  7.7 0.8 pad_maximum_fusion.1
  8.5 9.5 %all-to-all-start = ((bf16[32,16,384]{2,1,0:T(8,128)(2,1)}), bf16[32,16,384]{2,1,0:T(8,128)(2,1)S(1)}, u32[]{:S(2)}, u32[]{:S(2)}) async-start(bf16[32,16,384]{2,1,0:T(8,128)(2,1)} %bitcast.4), calls=%async_computation | async-start | bytes 786432 | tf_op jit(solution)/shard_map/all_to_all | solution.py:133
  18.0 0.0 all-gather.3.cloned.1.call-start
  18.1 4.2 %collective-permute-start = (bf16[96,768]{1,0:T(8,128)(2,1)}, bf16[96,768]{1,0:T(8,128)(2,1)S(1)}, u32[]{:S(2)}, u32[]{:S(2)}) collective-permute-start(bf16[96,768]{1,0:T(8,128)(2,1)} %bitcast.23), channel_id=1, source_target_pairs={{0,0},{1,64},{2,128},{3,192},{64,1},{65,65},{66,129},{67,193},{128... | collective-permute-start | bytes 442376 | tf_op jit(solution)/shard_map/ppermute | solution.py:122
  22.3 7.9 %collective-permute-done = bf16[96,768]{1,0:T(8,128)(2,1)S(1)} collective-permute-done((bf16[96,768]{1,0:T(8,128)(2,1)}, bf16[96,768]{1,0:T(8,128)(2,1)S(1)}, u32[]{:S(2)}, u32[]{:S(2)}) %collective-permute-start) | collective-permute-done | bytes 147488 | tf_op jit(solution)/shard_map/ppermute | solution.py:122
  30.2 0.0 all-to-all-done
  30.2 13.8 %collective-permute-start.1 = (bf16[96,768]{1,0:T(8,128)(2,1)S(1)}, bf16[96,768]{1,0:T(8,128)(2,1)S(1)}, u32[]{:S(2)}, u32[]{:S(2)}) collective-permute-start(bf16[96,768]{1,0:T(8,128)(2,1)S(1)} %collective-permute-done), channel_id=1, source_target_pairs={{0,256},{256,0},{1,257},{257,1},{2,258},{258,2},{3,259},{259,3},{4... | collective-permute-start | bytes 442376 | tf_op jit(solution)/shard_map/ppermute | solution.py:136
  44.1 1.9 %collective-permute-start.2 = (bf16[16,16,384]{2,1,0:T(8,128)(2,1)S(1)}, bf16[16,16,384]{2,1,0:T(8,128)(2,1)S(1)}, u32[]{:S(2)}, u32[]{:S(2)}) collective-permute-start(bf16[16,16,384]{2,1,0:T(8,128)(2,1)S(1)} %get-tuple-element.13), channel_id=1, source_target_pairs={{0,256},{256,0},{1,257},{257,1},{2,258},{258,2},{3,259},{259,3},{4... | collective-permute-start | bytes 589832 | tf_op jit(solution)/shard_map/ppermute | solution.py:142
  46.0 19.8 %collective-permute-done.1 = bf16[96,768]{1,0:T(8,128)(2,1)S(1)} collective-permute-done((bf16[96,768]{1,0:T(8,128)(2,1)S(1)}, bf16[96,768]{1,0:T(8,128)(2,1)S(1)}, u32[]{:S(2)}, u32[]{:S(2)}) %collective-permute-start.1) | collective-permute-done | bytes 147488 | tf_op jit(solution)/shard_map/ppermute | solution.py:136
  65.8 0.7 pad_maximum_fusion.2
  66.5 13.6 %collective-permute-start.3 = (bf16[16,16,384]{2,1,0:T(8,128)(2,1)S(1)}, bf16[16,16,384]{2,1,0:T(8,128)(2,1)S(1)}, u32[]{:S(2)}, u32[]{:S(2)}) collective-permute-start(bf16[16,16,384]{2,1,0:T(8,128)(2,1)S(1)} %get-tuple-element.11), channel_id=1, source_target_pairs={{0,256},{256,0},{1,257},{257,1},{2,258},{258,2},{3,259},{259,3},{4... | collective-permute-start | bytes 589832 | tf_op jit(solution)/shard_map/ppermute | solution.py:144
  80.1 0.8 compare_select_fusion
  80.9 0.1 copy.8
  81.0 0.1 reshape.14
  81.1 0.0 all-gather.3.cloned.1.call-update
  81.1 4.0 %collective-permute-done.2 = bf16[16,16,384]{2,1,0:T(8,128)(2,1)S(1)} collective-permute-done((bf16[16,16,384]{2,1,0:T(8,128)(2,1)S(1)}, bf16[16,16,384]{2,1,0:T(8,128)(2,1)S(1)}, u32[]{:S(2)}, u32[]{:S(2)}) %collective-permute-start.2) | collective-permute-done | bytes 196640 | tf_op jit(solution)/shard_map/ppermute | solution.py:142
  85.2 3.3 %collective-permute-done.3 = bf16[16,16,384]{2,1,0:T(8,128)(2,1)S(1)} collective-permute-done((bf16[16,16,384]{2,1,0:T(8,128)(2,1)S(1)}, bf16[16,16,384]{2,1,0:T(8,128)(2,1)S(1)}, u32[]{:S(2)}, u32[]{:S(2)}) %collective-permute-start.3) | collective-permute-done | bytes 196640 | tf_op jit(solution)/shard_map/ppermute | solution.py:144
  88.5 0.1 pad_maximum_fusion
  88.6 0.7 gather_fusion
  89.3 26.7 %all_to_all.10 = bf16[32,2,16,384]{3,2,1,0:T(8,128)(2,1)S(1)} all-to-all(bf16[32,2,16,384]{3,2,1,0:T(8,128)(2,1)S(1)} %bitcast.22), channel_id=1, replica_groups=mesh['zh'=2,'x'=4,'y'=4,'c'=2,'p'=2,'q'=4] {'x','y','c'}, dimensions={0} | all-to-all | bytes 1572864 | tf_op jit(solution)/shard_map/all_to_all | solution.py:151
  116.0 0.0 copy-done
  116.0 0.0 copy-done.1
  116.0 0.0 copy-done.2
  116.0 1.9 shard_map.55.refs_0_
  117.9 1.9 %collective-permute-start.4 = (bf16[128,768]{1,0:T(8,128)(2,1)S(1)}, bf16[128,768]{1,0:T(8,128)(2,1)S(1)}, u32[]{:S(2)}, u32[]{:S(2)}) collective-permute-start(bf16[128,768]{1,0:T(8,128)(2,1)S(1)} %shard_map.55.refs_0_), channel_id=1, source_target_pairs={{0,1},{1,0},{2,3},{3,2},{4,5},{5,4},{6,7},{7,6},{8,9},{9,8},{10,11... | collective-permute-start | bytes 589832 | tf_op jit(solution)/shard_map/ppermute | solution.py:160
  119.8 3.3 %collective-permute-start.5 = (bf16[128,768]{1,0:T(8,128)(2,1)S(1)}, bf16[128,768]{1,0:T(8,128)(2,1)S(1)}, u32[]{:S(2)}, u32[]{:S(2)}) collective-permute-start(bf16[128,768]{1,0:T(8,128)(2,1)S(1)} %shard_map.55.refs_0_), channel_id=1, source_target_pairs={{0,2},{1,3},{2,0},{3,1},{4,6},{5,7},{6,4},{7,5},{8,10},{9,11},{10,... | collective-permute-start | bytes 589832 | tf_op jit(solution)/shard_map/ppermute | solution.py:160
  123.1 4.9 %collective-permute-start.6 = (bf16[128,768]{1,0:T(8,128)(2,1)S(1)}, bf16[128,768]{1,0:T(8,128)(2,1)S(1)}, u32[]{:S(2)}, u32[]{:S(2)}) collective-permute-start(bf16[128,768]{1,0:T(8,128)(2,1)S(1)} %shard_map.55.refs_0_), channel_id=1, source_target_pairs={{0,3},{1,2},{2,1},{3,0},{4,7},{5,6},{6,5},{7,4},{8,11},{9,10},{10,... | collective-permute-start | bytes 589832 | tf_op jit(solution)/shard_map/ppermute | solution.py:160
  128.0 0.1 collective-permute-done.4.refs_1_
  128.1 10.7 %collective-permute-done.5.refs_2_ = bf16[128,768]{1,0:T(8,128)(2,1)S(1)} collective-permute-done((bf16[128,768]{1,0:T(8,128)(2,1)S(1)}, bf16[128,768]{1,0:T(8,128)(2,1)S(1)}, u32[]{:S(2)}, u32[]{:S(2)}) %collective-permute-start.5) | collective-permute-done | bytes 196640 | tf_op jit(solution)/shard_map/ppermute | solution.py:160
  138.8 0.0 collective-permute-done.6.refs_3_
  138.8 12.7 %all-gather.3.cloned.1.call-done = bf16[64,96,768]{2,1,0:T(8,128)(2,1)} async-done(((bf16[2,96,768]{2,1,0:T(8,128)(2,1)}), bf16[64,96,768]{2,1,0:T(8,128)(2,1)}) %all-gather.3.cloned.1.call-update) | async-done | bytes 9437200 | tf_op jit(solution)/shard_map/all_gather | solution.py:145
  151.5 4.2 %shard_map.57 = bf16[128,768]{1,0:T(8,128)(2,1)S(1)} custom-call(s32[4]{0:T(128)S(1)} %iota_xor_fusion.order_ref, bf16[128,768]{1,0:T(8,128)(2,1)S(1)} %shard_map.55.refs_0_, bf16[128,768]{1,0:T(8,128)(2,1)S(1)} %collective-permute-done.4.refs_1_, bf16[128,768]{1,0:T(8,128)(2,1)S(1)} %collective-permute-done.5.refs_2_, ...), custom_call_target="tpu_custom_call" | custom-call | flops 603979776 | bytes 5505024 | tf_op jit(solution)/shard_map/pallas_call | solution.py:49
  155.7 7.6 %collective-permute-start.7 = (bf16[128,768]{1,0:T(8,128)(2,1)S(1)}, bf16[128,768]{1,0:T(8,128)(2,1)S(1)}, u32[]{:S(2)}, u32[]{:S(2)}) collective-permute-start(bf16[128,768]{1,0:T(8,128)(2,1)S(1)} %shard_map.57), channel_id=1, source_target_pairs={{0,4},{4,0},{1,5},{5,1},{2,6},{6,2},{3,7},{7,3},{8,12},{12,8},{9,1... | collective-permute-start | bytes 589832 | tf_op jit(solution)/shard_map/ppermute | solution.py:164
  163.4 4.2 %shard_map.56 = f32[128,768]{1,0:T(8,128)S(1)} custom-call(s32[4]{0:T(128)S(1)} %iota_xor_fusion.order_ref, bf16[128,768]{1,0:T(8,128)(2,1)S(1)} %shard_map.55.refs_0_, bf16[128,768]{1,0:T(8,128)(2,1)S(1)} %collective-permute-done.4.refs_1_, bf16[128,768]{1,0:T(8,128)(2,1)S(1)} %collective-permute-done.5.refs_2_, ...), custom_call_target="tpu_custom_call" | custom-call | flops 603979776 | bytes 5505024 | tf_op jit(solution)/shard_map/pallas_call | solution.py:49
  167.6 13.7 %collective-permute-done.7 = bf16[128,768]{1,0:T(8,128)(2,1)S(1)} collective-permute-done((bf16[128,768]{1,0:T(8,128)(2,1)S(1)}, bf16[128,768]{1,0:T(8,128)(2,1)S(1)}, u32[]{:S(2)}, u32[]{:S(2)}) %collective-permute-start.7) | collective-permute-done | bytes 196640 | tf_op jit(solution)/shard_map/ppermute | solution.py:164
  181.3 0.7 add_convert_fusion
  (4 shorter events, 0.1 us)
Async XLA Ops:
  6.5 109.4 %copy-start = (bf16[128,768]{1,0:T(8,128)(2,1)S(1)}, bf16[128,768]{1,0:T(8,128)(2,1)}, u32[]{:S(2)}) copy-start(bf16[128,768]{1,0:T(8,128)(2,1)} %k_ref.1) | copy-start | bytes 589828
  6.5 109.4 %copy-start.1 = (bf16[128,768]{1,0:T(8,128)(2,1)S(1)}, bf16[128,768]{1,0:T(8,128)(2,1)}, u32[]{:S(2)}) copy-start(bf16[128,768]{1,0:T(8,128)(2,1)} %v_ref.1) | copy-start | bytes 589828
  6.5 109.4 %copy-start.2 = (bf16[128,768]{1,0:T(8,128)(2,1)S(1)}, bf16[128,768]{1,0:T(8,128)(2,1)}, u32[]{:S(2)}) copy-start(bf16[128,768]{1,0:T(8,128)(2,1)} %q_ref.1) | copy-start | bytes 589828
  8.5 21.7 %all-to-all-start = ((bf16[32,16,384]{2,1,0:T(8,128)(2,1)}), bf16[32,16,384]{2,1,0:T(8,128)(2,1)S(1)}, u32[]{:S(2)}, u32[]{:S(2)}) async-start(bf16[32,16,384]{2,1,0:T(8,128)(2,1)} %bitcast.4), calls=%async_computation | async-start | bytes 786432 | tf_op jit(solution)/shard_map/all_to_all | solution.py:133
  18.0 133.5 %all-gather.3.cloned.1.call-start = ((), (), s32[]{:S(2)}) async-start(), calls=%async_computation.2 | async-start | bytes 9732096 | tf_op jit(solution)/shard_map/all_gather | solution.py:145
  18.1 12.1 %collective-permute-start = (bf16[96,768]{1,0:T(8,128)(2,1)}, bf16[96,768]{1,0:T(8,128)(2,1)S(1)}, u32[]{:S(2)}, u32[]{:S(2)}) collective-permute-start(bf16[96,768]{1,0:T(8,128)(2,1)} %bitcast.23), channel_id=1, source_target_pairs={{0,0},{1,64},{2,128},{3,192},{64,1},{65,65},{66,129},{67,193},{128... | collective-permute-start | bytes 442376 | tf_op jit(solution)/shard_map/ppermute | solution.py:122
  30.2 35.6 %collective-permute-start.1 = (bf16[96,768]{1,0:T(8,128)(2,1)S(1)}, bf16[96,768]{1,0:T(8,128)(2,1)S(1)}, u32[]{:S(2)}, u32[]{:S(2)}) collective-permute-start(bf16[96,768]{1,0:T(8,128)(2,1)S(1)} %collective-permute-done), channel_id=1, source_target_pairs={{0,256},{256,0},{1,257},{257,1},{2,258},{258,2},{3,259},{259,3},{4... | collective-permute-start | bytes 442376 | tf_op jit(solution)/shard_map/ppermute | solution.py:136
  44.1 41.1 %collective-permute-start.2 = (bf16[16,16,384]{2,1,0:T(8,128)(2,1)S(1)}, bf16[16,16,384]{2,1,0:T(8,128)(2,1)S(1)}, u32[]{:S(2)}, u32[]{:S(2)}) collective-permute-start(bf16[16,16,384]{2,1,0:T(8,128)(2,1)S(1)} %get-tuple-element.13), channel_id=1, source_target_pairs={{0,256},{256,0},{1,257},{257,1},{2,258},{258,2},{3,259},{259,3},{4... | collective-permute-start | bytes 589832 | tf_op jit(solution)/shard_map/ppermute | solution.py:142
  66.5 21.9 %collective-permute-start.3 = (bf16[16,16,384]{2,1,0:T(8,128)(2,1)S(1)}, bf16[16,16,384]{2,1,0:T(8,128)(2,1)S(1)}, u32[]{:S(2)}, u32[]{:S(2)}) collective-permute-start(bf16[16,16,384]{2,1,0:T(8,128)(2,1)S(1)} %get-tuple-element.11), channel_id=1, source_target_pairs={{0,256},{256,0},{1,257},{257,1},{2,258},{258,2},{3,259},{259,3},{4... | collective-permute-start | bytes 589832 | tf_op jit(solution)/shard_map/ppermute | solution.py:144
  117.9 10.2 %collective-permute-start.4 = (bf16[128,768]{1,0:T(8,128)(2,1)S(1)}, bf16[128,768]{1,0:T(8,128)(2,1)S(1)}, u32[]{:S(2)}, u32[]{:S(2)}) collective-permute-start(bf16[128,768]{1,0:T(8,128)(2,1)S(1)} %shard_map.55.refs_0_), channel_id=1, source_target_pairs={{0,1},{1,0},{2,3},{3,2},{4,5},{5,4},{6,7},{7,6},{8,9},{9,8},{10,11... | collective-permute-start | bytes 589832 | tf_op jit(solution)/shard_map/ppermute | solution.py:160
  119.8 19.0 %collective-permute-start.5 = (bf16[128,768]{1,0:T(8,128)(2,1)S(1)}, bf16[128,768]{1,0:T(8,128)(2,1)S(1)}, u32[]{:S(2)}, u32[]{:S(2)}) collective-permute-start(bf16[128,768]{1,0:T(8,128)(2,1)S(1)} %shard_map.55.refs_0_), channel_id=1, source_target_pairs={{0,2},{1,3},{2,0},{3,1},{4,6},{5,7},{6,4},{7,5},{8,10},{9,11},{10,... | collective-permute-start | bytes 589832 | tf_op jit(solution)/shard_map/ppermute | solution.py:160
  123.1 15.6 %collective-permute-start.6 = (bf16[128,768]{1,0:T(8,128)(2,1)S(1)}, bf16[128,768]{1,0:T(8,128)(2,1)S(1)}, u32[]{:S(2)}, u32[]{:S(2)}) collective-permute-start(bf16[128,768]{1,0:T(8,128)(2,1)S(1)} %shard_map.55.refs_0_), channel_id=1, source_target_pairs={{0,3},{1,2},{2,1},{3,0},{4,7},{5,6},{6,5},{7,4},{8,11},{9,10},{10,... | collective-permute-start | bytes 589832 | tf_op jit(solution)/shard_map/ppermute | solution.py:160
  155.7 25.6 %collective-permute-start.7 = (bf16[128,768]{1,0:T(8,128)(2,1)S(1)}, bf16[128,768]{1,0:T(8,128)(2,1)S(1)}, u32[]{:S(2)}, u32[]{:S(2)}) collective-permute-start(bf16[128,768]{1,0:T(8,128)(2,1)S(1)} %shard_map.57), channel_id=1, source_target_pairs={{0,4},{4,0},{1,5},{5,1},{2,6},{6,2},{3,7},{7,3},{8,12},{12,8},{9,1... | collective-permute-start | bytes 589832 | tf_op jit(solution)/shard_map/ppermute | solution.py:164
Sparse Core Ops, SparseCore 0:
  81.2 70.2 all-gather.2

commit v13 on v6

--- a/solution.py
+++ b/solution.py
@@ -16,7 +16,6 @@
 PLANE = ("x", "y", "c")
 SWAP = ((0, 1), (1, 0))
 QUAD = 4
-HINT_FLOPS, HINT_BYTES = 182 * 10**9, 10**6
 HALVES = 2
 PIECE = 16
 
@@ -108,7 +107,9 @@
         out_shape=jax.ShapeDtypeStruct(queries.shape, queries.dtype),
         compiler_params=pltpu.CompilerParams(vmem_limit_bytes=32 << 20),
         cost_estimate=pl.CostEstimate(
-            flops=HINT_FLOPS, bytes_accessed=HINT_BYTES, transcendentals=0
+            flops=4 * queries.size * (1 + ROUNDS) * queries.shape[0],
+            bytes_accessed=2 * (4 * queries.size + routed.size),
+            transcendentals=queries.size * (1 + ROUNDS),
         ),
     )(queries, keys, values, routed)
 

time: 188 us -> 187 us (level)
  waiting for transfers between devices: 88 us -> 54.5 us
  blocking collectives: 20.1 us -> 39 us
  starting transfers between devices: 47.3 us -> 59.9 us
    all_to_all x1, blocking collectives: 20.1 us -> 39 us  [body(): lax.all_to_all(chosen, PLANE, split_axis=0, concat_axis=0, tiled=True)]
    ppermute x1, waiting for transfers between devices: 27.4 us -> 12.4 us  [body(): far = lax.ppermute(spread, 'zh', SWAP)]
    ppermute x1, starting transfers between devices: 1.92 us -> 13.1 us  [body(): far = lax.ppermute(spread, 'zh', SWAP)]
    ppermute x1, waiting for transfers between devices: 19.9 us -> 10.5 us  [body(): w_far = lax.ppermute(w_near, 'zh', SWAP)]
    all_gather x1, waiting for transfers between devices: 8.28 us -> 0.01 us  [body(): w_all = lax.all_gather(w_pair, PLANE, axis=0, tiled=False)]
  transfers between devices with their start and end apart: 9 -> 9, of which waited for: 7 -> 6; matrix products, arithmetic and copies ran while one was open for 1% -> 1% of each run, Pallas kernels for 3% -> 3%
where the time goes in v13:
time: 187 us; the launch traced here: 185 us
  starting transfers between devices  59.9 us (32%)
  waiting for transfers between devices  54.5 us (29%)
  blocking collectives  39 us (21%)
  between operations  13.5 us (7%)
  Pallas kernels  10.3 us (6%)
  local copies, waits for them, and re-layouts  4.82 us (3%)
  other arithmetic  3.18 us (2%)
    all_to_all x1, blocking collectives, body(): lax.all_to_all(chosen, PLANE, split_axis=0, concat_axis=0, tiled=True)  39 us
    ppermute x1, starting transfers between devices, body(): w_far = lax.ppermute(w_near, 'zh', SWAP)  13.8 us
    ppermute x1, starting transfers between devices, body(): far = lax.ppermute(spread, 'zh', SWAP)  13.1 us
    ppermute x1, waiting for transfers between devices, body(): arrived = lax.ppermute(sent, 'p', SWAP)  12.9 us
    ppermute x1, waiting for transfers between devices, body(): far = lax.ppermute(spread, 'zh', SWAP)  12.4 us
    ppermute x3, waiting for transfers between devices, body(): lax.ppermute(attended, 'q', [(i, i ^ k) for i in range(QUAD)])  10.7 us
    ppermute x1, waiting for transfers between devices, body(): w_far = lax.ppermute(w_near, 'zh', SWAP)  10.5 us
    ppermute x3, starting transfers between devices, body(): lax.ppermute(attended, 'q', [(i, i ^ k) for i in range(QUAD)])  10.1 us
  transfers between devices with their start and end apart: 9, of which 6 were waited for; matrix products, arithmetic and copies ran while one was open for 1% of the time, Pallas kernels for 3%

profile of v13, /device:TPU:6, one launch (start us, length us, event | category | flops | bytes accessed | tf_op | source)
XLA Modules:
  0.0 185.2 jit_solution(11875295689732253772)
XLA Ops:
  6.5 1.1 slice_bitcast_fusion.1
  7.6 0.8 pad_maximum_fusion.1
  8.4 9.5 %all-to-all-start = ((bf16[32,16,384]{2,1,0:T(8,128)(2,1)}), bf16[32,16,384]{2,1,0:T(8,128)(2,1)S(1)}, u32[]{:S(2)}, u32[]{:S(2)}) async-start(bf16[32,16,384]{2,1,0:T(8,128)(2,1)} %bitcast.4), calls=%async_computation | async-start | bytes 786432 | tf_op jit(solution)/shard_map/all_to_all | solution.py:134
  18.0 0.0 all-gather.3.cloned.1.call-start
  18.0 4.2 %collective-permute-start = (bf16[96,768]{1,0:T(8,128)(2,1)}, bf16[96,768]{1,0:T(8,128)(2,1)S(1)}, u32[]{:S(2)}, u32[]{:S(2)}) collective-permute-start(bf16[96,768]{1,0:T(8,128)(2,1)} %bitcast.23), channel_id=1, source_target_pairs={{0,0},{1,64},{2,128},{3,192},{64,1},{65,65},{66,129},{67,193},{128... | collective-permute-start | bytes 442376 | tf_op jit(solution)/shard_map/ppermute | solution.py:123
  22.3 7.9 %collective-permute-done = bf16[96,768]{1,0:T(8,128)(2,1)S(1)} collective-permute-done((bf16[96,768]{1,0:T(8,128)(2,1)}, bf16[96,768]{1,0:T(8,128)(2,1)S(1)}, u32[]{:S(2)}, u32[]{:S(2)}) %collective-permute-start) | collective-permute-done | bytes 147488 | tf_op jit(solution)/shard_map/ppermute | solution.py:123
  30.2 0.0 all-to-all-done
  30.2 13.8 %collective-permute-start.5 = (bf16[96,768]{1,0:T(8,128)(2,1)S(1)}, bf16[96,768]{1,0:T(8,128)(2,1)S(1)}, u32[]{:S(2)}, u32[]{:S(2)}) collective-permute-start(bf16[96,768]{1,0:T(8,128)(2,1)S(1)} %collective-permute-done), channel_id=1, source_target_pairs={{0,256},{256,0},{1,257},{257,1},{2,258},{258,2},{3,259},{259,3},{4... | collective-permute-start | bytes 442376 | tf_op jit(solution)/shard_map/ppermute | solution.py:137
  44.0 10.5 %collective-permute-done.5 = bf16[96,768]{1,0:T(8,128)(2,1)S(1)} collective-permute-done((bf16[96,768]{1,0:T(8,128)(2,1)S(1)}, bf16[96,768]{1,0:T(8,128)(2,1)S(1)}, u32[]{:S(2)}, u32[]{:S(2)}) %collective-permute-start.5) | collective-permute-done | bytes 147488 | tf_op jit(solution)/shard_map/ppermute | solution.py:137
  54.5 0.7 pad_maximum_fusion.2
  55.2 0.0 all-gather.3.cloned.1.call-update
  55.2 13.1 %collective-permute-start.1 = (bf16[32,16,384]{2,1,0:T(8,128)(2,1)S(1)}, bf16[32,16,384]{2,1,0:T(8,128)(2,1)S(1)}, u32[]{:S(2)}, u32[]{:S(2)}) collective-permute-start(bf16[32,16,384]{2,1,0:T(8,128)(2,1)S(1)} %all-to-all-done), channel_id=1, source_target_pairs={{0,256},{256,0},{1,257},{257,1},{2,258},{258,2},{3,259},{259,3},{4... | collective-permute-start | bytes 1179656 | tf_op jit(solution)/shard_map/ppermute | solution.py:138
  68.3 0.8 compare_select_fusion
  69.1 0.1 copy.8
  69.2 0.1 reshape.14
  69.3 12.4 %collective-permute-done.1 = bf16[32,16,384]{2,1,0:T(8,128)(2,1)S(1)} collective-permute-done((bf16[32,16,384]{2,1,0:T(8,128)(2,1)S(1)}, bf16[32,16,384]{2,1,0:T(8,128)(2,1)S(1)}, u32[]{:S(2)}, u32[]{:S(2)}) %collective-permute-start.1) | collective-permute-done | bytes 393248 | tf_op jit(solution)/shard_map/ppermute | solution.py:138
  81.8 0.1 pad_maximum_fusion
  81.9 0.7 gather_fusion
  82.6 39.0 %all_to_all.10 = bf16[32,2,16,384]{3,2,1,0:T(8,128)(2,1)S(1)} all-to-all(bf16[32,2,16,384]{3,2,1,0:T(8,128)(2,1)S(1)} %bitcast.22), channel_id=1, replica_groups=mesh['zh'=2,'x'=4,'y'=4,'c'=2,'p'=2,'q'=4] {'x','y','c'}, dimensions={0} | all-to-all | bytes 1572864 | tf_op jit(solution)/shard_map/all_to_all | solution.py:149
  121.5 0.0 copy-start
  121.5 0.9 copy-done
  122.5 0.0 copy-start.1
  122.5 1.0 copy-done.1
  123.4 0.0 copy-start.2
  123.4 0.9 copy-done.2
  124.4 1.9 %shard_map.55.refs_0_ = bf16[128,768]{1,0:T(8,128)(2,1)S(1)} custom-call(bf16[128,768]{1,0:T(8,128)(2,1)S(1)} %copy-done.2, bf16[128,768]{1,0:T(8,128)(2,1)S(1)} %copy-done, bf16[128,768]{1,0:T(8,128)(2,1)S(1)} %copy-done.1, bf16[4,8,2,16,384]{4,3,2,1,0:T(8,128)(2,1)S(1)} %bitcast.19), custom_call_target="tpu_custom_call" | custom-call | flops 150994944 | bytes 1572864 | tf_op jit(solution)/shard_map/pallas_call | solution.py:103
  126.3 1.9 %collective-permute-start.2 = (bf16[128,768]{1,0:T(8,128)(2,1)S(1)}, bf16[128,768]{1,0:T(8,128)(2,1)S(1)}, u32[]{:S(2)}, u32[]{:S(2)}) collective-permute-start(bf16[128,768]{1,0:T(8,128)(2,1)S(1)} %shard_map.55.refs_0_), channel_id=1, source_target_pairs={{0,1},{1,0},{2,3},{3,2},{4,5},{5,4},{6,7},{7,6},{8,9},{9,8},{10,11... | collective-permute-start | bytes 589832 | tf_op jit(solution)/shard_map/ppermute | solution.py:158
  128.2 2.9 %collective-permute-start.3 = (bf16[128,768]{1,0:T(8,128)(2,1)S(1)}, bf16[128,768]{1,0:T(8,128)(2,1)S(1)}, u32[]{:S(2)}, u32[]{:S(2)}) collective-permute-start(bf16[128,768]{1,0:T(8,128)(2,1)S(1)} %shard_map.55.refs_0_), channel_id=1, source_target_pairs={{0,2},{1,3},{2,0},{3,1},{4,6},{5,7},{6,4},{7,5},{8,10},{9,11},{10,... | collective-permute-start | bytes 589832 | tf_op jit(solution)/shard_map/ppermute | solution.py:158
  131.1 5.3 %collective-permute-start.4 = (bf16[128,768]{1,0:T(8,128)(2,1)S(1)}, bf16[128,768]{1,0:T(8,128)(2,1)S(1)}, u32[]{:S(2)}, u32[]{:S(2)}) collective-permute-start(bf16[128,768]{1,0:T(8,128)(2,1)S(1)} %shard_map.55.refs_0_), channel_id=1, source_target_pairs={{0,3},{1,2},{2,1},{3,0},{4,7},{5,6},{6,5},{7,4},{8,11},{9,10},{10,... | collective-permute-start | bytes 589832 | tf_op jit(solution)/shard_map/ppermute | solution.py:158
  136.4 0.3 collective-permute-done.2.refs_1_
  136.7 10.5 %collective-permute-done.3.refs_2_ = bf16[128,768]{1,0:T(8,128)(2,1)S(1)} collective-permute-done((bf16[128,768]{1,0:T(8,128)(2,1)S(1)}, bf16[128,768]{1,0:T(8,128)(2,1)S(1)}, u32[]{:S(2)}, u32[]{:S(2)}) %collective-permute-start.3) | collective-permute-done | bytes 196640 | tf_op jit(solution)/shard_map/ppermute | solution.py:158
  147.1 0.0 collective-permute-done.4.refs_3_
  147.1 0.0 all-gather.3.cloned.1.call-done
  147.2 4.2 %shard_map.57 = bf16[128,768]{1,0:T(8,128)(2,1)S(1)} custom-call(s32[4]{0:T(128)S(1)} %iota_xor_fusion.order_ref, bf16[128,768]{1,0:T(8,128)(2,1)S(1)} %shard_map.55.refs_0_, bf16[128,768]{1,0:T(8,128)(2,1)S(1)} %collective-permute-done.2.refs_1_, bf16[128,768]{1,0:T(8,128)(2,1)S(1)} %collective-permute-done.3.refs_2_, ...), custom_call_target="tpu_custom_call" | custom-call | flops 603979776 | bytes 5505024 | tf_op jit(solution)/shard_map/pallas_call | solution.py:48
  151.3 9.1 %collective-permute-start.6 = (bf16[128,768]{1,0:T(8,128)(2,1)S(1)}, bf16[128,768]{1,0:T(8,128)(2,1)S(1)}, u32[]{:S(2)}, u32[]{:S(2)}) collective-permute-start(bf16[128,768]{1,0:T(8,128)(2,1)S(1)} %shard_map.57), channel_id=1, source_target_pairs={{0,4},{4,0},{1,5},{5,1},{2,6},{6,2},{3,7},{7,3},{8,12},{12,8},{9,1... | collective-permute-start | bytes 589832 | tf_op jit(solution)/shard_map/ppermute | solution.py:162
  160.4 4.2 %shard_map.56 = f32[128,768]{1,0:T(8,128)S(1)} custom-call(s32[4]{0:T(128)S(1)} %iota_xor_fusion.order_ref, bf16[128,768]{1,0:T(8,128)(2,1)S(1)} %shard_map.55.refs_0_, bf16[128,768]{1,0:T(8,128)(2,1)S(1)} %collective-permute-done.2.refs_1_, bf16[128,768]{1,0:T(8,128)(2,1)S(1)} %collective-permute-done.3.refs_2_, ...), custom_call_target="tpu_custom_call" | custom-call | flops 603979776 | bytes 5505024 | tf_op jit(solution)/shard_map/pallas_call | solution.py:48
  164.7 12.9 %collective-permute-done.6 = bf16[128,768]{1,0:T(8,128)(2,1)S(1)} collective-permute-done((bf16[128,768]{1,0:T(8,128)(2,1)S(1)}, bf16[128,768]{1,0:T(8,128)(2,1)S(1)}, u32[]{:S(2)}, u32[]{:S(2)}) %collective-permute-start.6) | collective-permute-done | bytes 196640 | tf_op jit(solution)/shard_map/ppermute | solution.py:162
  177.6 0.7 add_convert_fusion
  (3 shorter events, 0.0 us)
Async XLA Ops:
  8.4 21.7 %all-to-all-start = ((bf16[32,16,384]{2,1,0:T(8,128)(2,1)}), bf16[32,16,384]{2,1,0:T(8,128)(2,1)S(1)}, u32[]{:S(2)}, u32[]{:S(2)}) async-start(bf16[32,16,384]{2,1,0:T(8,128)(2,1)} %bitcast.4), calls=%async_computation | async-start | bytes 786432 | tf_op jit(solution)/shard_map/all_to_all | solution.py:134
  18.0 129.2 %all-gather.3.cloned.1.call-start = ((), (), s32[]{:S(2)}) async-start(), calls=%async_computation.2 | async-start | bytes 9732096 | tf_op jit(solution)/shard_map/all_gather | solution.py:143
  18.0 12.1 %collective-permute-start = (bf16[96,768]{1,0:T(8,128)(2,1)}, bf16[96,768]{1,0:T(8,128)(2,1)S(1)}, u32[]{:S(2)}, u32[]{:S(2)}) collective-permute-start(bf16[96,768]{1,0:T(8,128)(2,1)} %bitcast.23), channel_id=1, source_target_pairs={{0,0},{1,64},{2,128},{3,192},{64,1},{65,65},{66,129},{67,193},{128... | collective-permute-start | bytes 442376 | tf_op jit(solution)/shard_map/ppermute | solution.py:123
  30.2 24.3 %collective-permute-start.5 = (bf16[96,768]{1,0:T(8,128)(2,1)S(1)}, bf16[96,768]{1,0:T(8,128)(2,1)S(1)}, u32[]{:S(2)}, u32[]{:S(2)}) collective-permute-start(bf16[96,768]{1,0:T(8,128)(2,1)S(1)} %collective-permute-done), channel_id=1, source_target_pairs={{0,256},{256,0},{1,257},{257,1},{2,258},{258,2},{3,259},{259,3},{4... | collective-permute-start | bytes 442376 | tf_op jit(solution)/shard_map/ppermute | solution.py:137
  55.2 26.5 %collective-permute-start.1 = (bf16[32,16,384]{2,1,0:T(8,128)(2,1)S(1)}, bf16[32,16,384]{2,1,0:T(8,128)(2,1)S(1)}, u32[]{:S(2)}, u32[]{:S(2)}) collective-permute-start(bf16[32,16,384]{2,1,0:T(8,128)(2,1)S(1)} %all-to-all-done), channel_id=1, source_target_pairs={{0,256},{256,0},{1,257},{257,1},{2,258},{258,2},{3,259},{259,3},{4... | collective-permute-start | bytes 1179656 | tf_op jit(solution)/shard_map/ppermute | solution.py:138
  121.5 0.9 copy-start
  122.5 1.0 copy-start.1
  123.4 0.9 copy-start.2
  126.3 10.4 %collective-permute-start.2 = (bf16[128,768]{1,0:T(8,128)(2,1)S(1)}, bf16[128,768]{1,0:T(8,128)(2,1)S(1)}, u32[]{:S(2)}, u32[]{:S(2)}) collective-permute-start(bf16[128,768]{1,0:T(8,128)(2,1)S(1)} %shard_map.55.refs_0_), channel_id=1, source_target_pairs={{0,1},{1,0},{2,3},{3,2},{4,5},{5,4},{6,7},{7,6},{8,9},{9,8},{10,11... | collective-permute-start | bytes 589832 | tf_op jit(solution)/shard_map/ppermute | solution.py:158
  128.2 19.0 %collective-permute-start.3 = (bf16[128,768]{1,0:T(8,128)(2,1)S(1)}, bf16[128,768]{1,0:T(8,128)(2,1)S(1)}, u32[]{:S(2)}, u32[]{:S(2)}) collective-permute-start(bf16[128,768]{1,0:T(8,128)(2,1)S(1)} %shard_map.55.refs_0_), channel_id=1, source_target_pairs={{0,2},{1,3},{2,0},{3,1},{4,6},{5,7},{6,4},{7,5},{8,10},{9,11},{10,... | collective-permute-start | bytes 589832 | tf_op jit(solution)/shard_map/ppermute | solution.py:158
  131.1 16.1 %collective-permute-start.4 = (bf16[128,768]{1,0:T(8,128)(2,1)S(1)}, bf16[128,768]{1,0:T(8,128)(2,1)S(1)}, u32[]{:S(2)}, u32[]{:S(2)}) collective-permute-start(bf16[128,768]{1,0:T(8,128)(2,1)S(1)} %shard_map.55.refs_0_), channel_id=1, source_target_pairs={{0,3},{1,2},{2,1},{3,0},{4,7},{5,6},{6,5},{7,4},{8,11},{9,10},{10,... | collective-permute-start | bytes 589832 | tf_op jit(solution)/shard_map/ppermute | solution.py:158
  151.3 26.2 %collective-permute-start.6 = (bf16[128,768]{1,0:T(8,128)(2,1)S(1)}, bf16[128,768]{1,0:T(8,128)(2,1)S(1)}, u32[]{:S(2)}, u32[]{:S(2)}) collective-permute-start(bf16[128,768]{1,0:T(8,128)(2,1)S(1)} %shard_map.57), channel_id=1, source_target_pairs={{0,4},{4,0},{1,5},{5,1},{2,6},{6,2},{3,7},{7,3},{8,12},{12,8},{9,1... | collective-permute-start | bytes 589832 | tf_op jit(solution)/shard_map/ppermute | solution.py:162
Sparse Core Ops, SparseCore 0:
  55.3 81.1 all-gather.2

commit v14 on v9

--- a/solution.py
+++ b/solution.py
@@ -141,19 +141,11 @@
     quad, member = lax.axis_index("p"), lax.axis_index("q")
     seats = lax.axis_size(PLANE)
 
-    w_near, w_far = [
-        lax.ppermute(
-            w_out.T,
-            ("zh", "x", "q"),
-            [
-                ((zh * QUAD + x) * QUAD + q, ((zh ^ flip) * QUAD + q) * QUAD + x)
-                for zh in range(2)
-                for x in range(QUAD)
-                for q in range(QUAD)
-            ],
-        )
-        for flip in range(2)
-    ]
+    w_near = lax.ppermute(
+        w_out.T,
+        ("x", "q"),
+        [(x * QUAD + q, q * QUAD + x) for x in range(QUAD) for q in range(QUAD)],
+    )
 
     part = width // HALVES
     own = jnp.stack(
@@ -163,6 +155,8 @@
     spread = lax.all_to_all(own, PLANE, split_axis=0, concat_axis=0, tiled=True)
     far = lax.ppermute(spread, "zh", SWAP)
 
+    w_far = lax.ppermute(w_near, "zh", SWAP)
+
     def gather(chunk):
         to_all = jnp.broadcast_to(chunk, (QUAD * QUAD,) + chunk.shape)
         return lax.all_to_all(to_all, ("x", "y"), split_axis=0, concat_axis=0, tiled=True)
@@ -172,7 +166,7 @@
         return [rows.reshape(QUAD, QUAD, *rows.shape[1:]) for rows in (chunks, other)]
 
     w_near = gather(w_near)
-    far, w_near = lax.optimization_barrier((far, w_near))
+    far, w_near, w_far = lax.optimization_barrier((far, w_near, w_far))
     w_near = with_other_core(w_near)
 
     wanted = lax.dynamic_slice_in_dim(plan, half * seats, seats, 1)

time: 194 us -> 189 us (0.974)
  the two profiles are of different devices: /device:TPU:5 before, /device:TPU:32 now
where the time goes in v14:
time: 189 us
  waiting for transfers between devices  92.9 us (49%)
  starting transfers between devices  53.6 us (28%)
  blocking collectives  21.1 us (11%)
  Pallas kernels  10.3 us (5%)
  local copies, waits for them, and re-layouts  7.63 us (4%)
  other arithmetic  3.05 us (2%)
    ppermute x1, waiting for transfers between devices, body(): w_far = lax.ppermute(w_near, 'zh', SWAP)  41.6 us
    all_to_all x1, blocking collectives, body(): lax.all_to_all(chosen, PLANE, split_axis=0, concat_axis=0, tiled=True)  21.1 us
    ppermute x1, waiting for transfers between devices, body(): arrived = lax.ppermute(sent, 'p', SWAP)  15 us
    all_to_all x2, waiting for transfers between devices, gather(): lax.all_to_all(to_all, ('x', 'y'), split_axis=0, concat_axis=0, tiled=True)  14.8 us
    ppermute x1, starting transfers between devices, body(): far = lax.ppermute(spread, 'zh', SWAP)  14.8 us
    ppermute x1, waiting for transfers between devices, body(): lax.ppermute(w_out.T, ('x', 'q'), [(x * QUAD + q, q * QUAD + x) for x in...  9.74 us
    all_to_all x2, starting transfers between devices, gather(): lax.all_to_all(to_all, ('x', 'y'), split_axis=0, concat_axis=0, tiled=True)  9.45 us
    ppermute x3, starting transfers between devices, body(): lax.ppermute(attended, 'q', [(i, i ^ k) for i in range(QUAD)])  9.23 us
  transfers between devices with their start and end apart: 12, of which 9 were waited for; matrix products, arithmetic and copies ran while one was open for 0% of the time, Pallas kernels for 3%

profile of v14, /device:TPU:32, one launch (start us, length us, event | category | flops | bytes accessed | tf_op | source)
XLA Modules:
  0.0 188.7 jit_solution(11123406626193287597)
XLA Ops:
  0.0 1.1 slice_bitcast_fusion.1
  1.1 0.8 pad_maximum_fusion.1
  1.9 7.3 %all-to-all-start = ((bf16[32,16,384]{2,1,0:T(8,128)(2,1)}), bf16[32,16,384]{2,1,0:T(8,128)(2,1)S(1)}, u32[]{:S(2)}, u32[]{:S(2)}) async-start(bf16[32,16,384]{2,1,0:T(8,128)(2,1)} %bitcast.6), calls=%async_computation | async-start | bytes 786432 | tf_op jit(solution)/shard_map/all_to_all | solution.py:155
  9.3 0.0 copy-done.9
  9.3 5.1 %collective-permute-start.1 = (bf16[96,768]{1,0:T(8,128)(2,1)S(1)}, bf16[96,768]{1,0:T(8,128)(2,1)S(1)}, u32[]{:S(2)}, u32[]{:S(2)}) collective-permute-start(bf16[96,768]{1,0:T(8,128)(2,1)S(1)} %bitcast.27), channel_id=1, source_target_pairs={{0,0},{1,64},{2,128},{3,192},{64,1},{65,65},{66,129},{67,193},{128... | collective-permute-start | bytes 442376 | tf_op jit(solution)/shard_map/ppermute | solution.py:144
  14.4 9.7 %collective-permute-done.1 = bf16[96,768]{1,0:T(8,128)(2,1)S(1)} collective-permute-done((bf16[96,768]{1,0:T(8,128)(2,1)S(1)}, bf16[96,768]{1,0:T(8,128)(2,1)S(1)}, u32[]{:S(2)}, u32[]{:S(2)}) %collective-permute-start.1) | collective-permute-done | bytes 147488 | tf_op jit(solution)/shard_map/ppermute | solution.py:144
  24.1 0.3 all-to-all-done
  24.4 1.7 broadcast_in_dim.9
  26.1 4.9 %all-to-all-start.1 = ((bf16[16,96,768]{2,1,0:T(8,128)(2,1)}), bf16[16,96,768]{2,1,0:T(8,128)(2,1)S(1)}, u32[]{:S(2)}, u32[]{:S(2)}) async-start(bf16[16,96,768]{2,1,0:T(8,128)(2,1)} %broadcast_in_dim.9), calls=%async_computation.1 | async-start | bytes 4718592 | tf_op jit(solution)/shard_map/all_to_all | solution.py:162
  31.0 14.8 %collective-permute-start = (bf16[32,16,384]{2,1,0:T(8,128)(2,1)S(1)}, bf16[32,16,384]{2,1,0:T(8,128)(2,1)S(1)}, u32[]{:S(2)}, u32[]{:S(2)}) collective-permute-start(bf16[32,16,384]{2,1,0:T(8,128)(2,1)S(1)} %all-to-all-done), channel_id=1, source_target_pairs={{0,256},{256,0},{1,257},{257,1},{2,258},{258,2},{3,259},{259,3},{4... | collective-permute-start | bytes 1179656 | tf_op jit(solution)/shard_map/ppermute | solution.py:156
  45.8 1.9 %collective-permute-start.2 = (bf16[96,768]{1,0:T(8,128)(2,1)S(1)}, bf16[96,768]{1,0:T(8,128)(2,1)S(1)}, u32[]{:S(2)}, u32[]{:S(2)}) collective-permute-start(bf16[96,768]{1,0:T(8,128)(2,1)S(1)} %collective-permute-done.1), channel_id=1, source_target_pairs={{0,256},{256,0},{1,257},{257,1},{2,258},{258,2},{3,259},{259,3},{4... | collective-permute-start | bytes 442376 | tf_op jit(solution)/shard_map/ppermute | solution.py:158
  47.7 0.0 copy-done.8
  47.7 0.1 compare_select_fusion
  47.8 0.1 copy.7
  47.9 0.1 reshape.26
  48.0 41.6 %collective-permute-done.2 = bf16[96,768]{1,0:T(8,128)(2,1)S(1)} collective-permute-done((bf16[96,768]{1,0:T(8,128)(2,1)S(1)}, bf16[96,768]{1,0:T(8,128)(2,1)S(1)}, u32[]{:S(2)}, u32[]{:S(2)}) %collective-permute-start.2) | collective-permute-done | bytes 147488 | tf_op jit(solution)/shard_map/ppermute | solution.py:158
  89.6 0.0 collective-permute-done
  89.6 0.7 copy-done.6
  90.3 0.8 copy-done.5
  91.0 0.0 all-to-all-done.1
  91.0 1.3 pad_maximum_fusion
  92.4 0.0 copy-start.7
  92.4 1.5 gather_fusion
  94.0 0.0 copy-done.3
  94.0 21.1 %all_to_all.20 = bf16[32,2,16,384]{3,2,1,0:T(8,128)(2,1)S(1)} all-to-all(bf16[32,2,16,384]{3,2,1,0:T(8,128)(2,1)} %bitcast.26), channel_id=1, replica_groups=mesh['zh'=2,'x'=4,'y'=4,'c'=2,'p'=2,'q'=4] {'x','y','c'}, dimensions={0} | all-to-all | bytes 1572864 | tf_op jit(solution)/shard_map/all_to_all | solution.py:175
  115.0 0.0 copy-done.7
  115.0 1.7 broadcast_in_dim.11
  116.7 4.6 %all-to-all-start.3 = ((bf16[16,96,768]{2,1,0:T(8,128)(2,1)}), bf16[16,96,768]{2,1,0:T(8,128)(2,1)}, u32[]{:S(2)}, u32[]{:S(2)}) async-start(bf16[16,96,768]{2,1,0:T(8,128)(2,1)} %broadcast_in_dim.11), calls=%async_computation.3 | async-start | bytes 4718592 | tf_op jit(solution)/shard_map/all_to_all | solution.py:162
  121.3 0.0 copy-done
  121.3 0.0 copy-done.1
  121.3 1.9 shard_map.55.refs_0_
  123.2 1.9 %collective-permute-start.5 = (bf16[128,768]{1,0:T(8,128)(2,1)S(1)}, bf16[128,768]{1,0:T(8,128)(2,1)S(1)}, u32[]{:S(2)}, u32[]{:S(2)}) collective-permute-start(bf16[128,768]{1,0:T(8,128)(2,1)S(1)} %shard_map.55.refs_0_), channel_id=1, source_target_pairs={{0,3},{1,2},{2,1},{3,0},{4,7},{5,6},{6,5},{7,4},{8,11},{9,10},{10,... | collective-permute-start | bytes 589832 | tf_op jit(solution)/shard_map/ppermute | solution.py:186
  125.1 1.9 %collective-permute-start.4 = (bf16[128,768]{1,0:T(8,128)(2,1)S(1)}, bf16[128,768]{1,0:T(8,128)(2,1)S(1)}, u32[]{:S(2)}, u32[]{:S(2)}) collective-permute-start(bf16[128,768]{1,0:T(8,128)(2,1)S(1)} %shard_map.55.refs_0_), channel_id=1, source_target_pairs={{0,2},{1,3},{2,0},{3,1},{4,6},{5,7},{6,4},{7,5},{8,10},{9,11},{10,... | collective-permute-start | bytes 589832 | tf_op jit(solution)/shard_map/ppermute | solution.py:186
  127.0 5.4 %collective-permute-start.3 = (bf16[128,768]{1,0:T(8,128)(2,1)S(1)}, bf16[128,768]{1,0:T(8,128)(2,1)S(1)}, u32[]{:S(2)}, u32[]{:S(2)}) collective-permute-start(bf16[128,768]{1,0:T(8,128)(2,1)S(1)} %shard_map.55.refs_0_), channel_id=1, source_target_pairs={{0,1},{1,0},{2,3},{3,2},{4,5},{5,4},{6,7},{7,6},{8,9},{9,8},{10,11... | collective-permute-start | bytes 589832 | tf_op jit(solution)/shard_map/ppermute | solution.py:186
  132.4 1.9 %collective-permute-start.6 = (bf16[16,96,768]{2,1,0:T(8,128)(2,1)}, bf16[16,96,768]{2,1,0:T(8,128)(2,1)S(1)}, u32[]{:S(2)}, u32[]{:S(2)}) collective-permute-start(bf16[16,96,768]{2,1,0:T(8,128)(2,1)} %copy-done.3), channel_id=1, source_target_pairs={{0,8},{8,0},{1,9},{9,1},{2,10},{10,2},{3,11},{11,3},{4,12},{12,4},... | collective-permute-start | bytes 7077896 | tf_op jit(solution)/shard_map/ppermute | solution.py:165
  134.4 2.7 %collective-permute-done.5.refs_3_ = bf16[128,768]{1,0:T(8,128)(2,1)S(1)} collective-permute-done((bf16[128,768]{1,0:T(8,128)(2,1)S(1)}, bf16[128,768]{1,0:T(8,128)(2,1)S(1)}, u32[]{:S(2)}, u32[]{:S(2)}) %collective-permute-start.5) | collective-permute-done | bytes 196640 | tf_op jit(solution)/shard_map/ppermute | solution.py:186
  137.1 3.7 %collective-permute-done.4.refs_2_ = bf16[128,768]{1,0:T(8,128)(2,1)S(1)} collective-permute-done((bf16[128,768]{1,0:T(8,128)(2,1)S(1)}, bf16[128,768]{1,0:T(8,128)(2,1)S(1)}, u32[]{:S(2)}, u32[]{:S(2)}) %collective-permute-start.4) | collective-permute-done | bytes 196640 | tf_op jit(solution)/shard_map/ppermute | solution.py:186
  140.7 0.3 collective-permute-done.3.refs_1_
  141.0 14.8 %all-to-all-done.3 = bf16[16,96,768]{2,1,0:T(8,128)(2,1)} async-done(((bf16[16,96,768]{2,1,0:T(8,128)(2,1)}), bf16[16,96,768]{2,1,0:T(8,128)(2,1)}, u32[]{:S(2)}, u32[]{:S(2)}) %all-to-all-start.3) | async-done | bytes 2359328 | tf_op jit(solution)/shard_map/all_to_all | solution.py:162
  155.9 1.9 %collective-permute-start.7 = (bf16[16,96,768]{2,1,0:T(8,128)(2,1)}, bf16[16,96,768]{2,1,0:T(8,128)(2,1)}, u32[]{:S(2)}, u32[]{:S(2)}) collective-permute-start(bf16[16,96,768]{2,1,0:T(8,128)(2,1)} %all-to-all-done.3), channel_id=1, source_target_pairs={{0,8},{8,0},{1,9},{9,1},{2,10},{10,2},{3,11},{11,3},{4,12},{12,4},... | collective-permute-start | bytes 7077896 | tf_op jit(solution)/shard_map/ppermute | solution.py:165
  157.8 0.1 add_add_fusion.1
  157.9 0.0 collective-permute-done.6
  157.9 4.7 %collective-permute-done.7 = bf16[16,96,768]{2,1,0:T(8,128)(2,1)} collective-permute-done((bf16[16,96,768]{2,1,0:T(8,128)(2,1)}, bf16[16,96,768]{2,1,0:T(8,128)(2,1)}, u32[]{:S(2)}, u32[]{:S(2)}) %collective-permute-start.7) | collective-permute-done | bytes 2359328 | tf_op jit(solution)/shard_map/ppermute | solution.py:165
  162.6 4.2 %shard_map.57 = bf16[128,768]{1,0:T(8,128)(2,1)S(1)} custom-call(s32[6]{0:T(128)S(1)} %get-tuple-element.29.place_ref, bf16[128,768]{1,0:T(8,128)(2,1)S(1)} %shard_map.55.refs_0_, bf16[128,768]{1,0:T(8,128)(2,1)S(1)} %collective-permute-done.3.refs_1_, bf16[128,768]{1,0:T(8,128)(2,1)S(1)} %collective-permute-done.4.refs_2_, ...), custom_call_target="tpu_custom_call" | custom-call | flops 603979776 | bytes 5505024 | tf_op jit(solution)/shard_map/pallas_call | solution.py:65
  166.8 1.9 %collective-permute-start.8 = (bf16[128,768]{1,0:T(8,128)(2,1)S(1)}, bf16[128,768]{1,0:T(8,128)(2,1)S(1)}, u32[]{:S(2)}, u32[]{:S(2)}) collective-permute-start(bf16[128,768]{1,0:T(8,128)(2,1)S(1)} %shard_map.57), channel_id=1, source_target_pairs={{0,4},{4,0},{1,5},{5,1},{2,6},{6,2},{3,7},{7,3},{8,12},{12,8},{9,1... | collective-permute-start | bytes 589832 | tf_op jit(solution)/shard_map/ppermute | solution.py:194
  168.8 4.2 %shard_map.56 = f32[128,768]{1,0:T(8,128)S(1)} custom-call(s32[6]{0:T(128)S(1)} %get-tuple-element.30.place_ref, bf16[128,768]{1,0:T(8,128)(2,1)S(1)} %shard_map.55.refs_0_, bf16[128,768]{1,0:T(8,128)(2,1)S(1)} %collective-permute-done.3.refs_1_, bf16[128,768]{1,0:T(8,128)(2,1)S(1)} %collective-permute-done.4.refs_2_, ...), custom_call_target="tpu_custom_call" | custom-call | flops 603979776 | bytes 5505024 | tf_op jit(solution)/shard_map/pallas_call | solution.py:65
  173.0 15.0 %collective-permute-done.8 = bf16[128,768]{1,0:T(8,128)(2,1)S(1)} collective-permute-done((bf16[128,768]{1,0:T(8,128)(2,1)S(1)}, bf16[128,768]{1,0:T(8,128)(2,1)S(1)}, u32[]{:S(2)}, u32[]{:S(2)}) %collective-permute-start.8) | collective-permute-done | bytes 196640 | tf_op jit(solution)/shard_map/ppermute | solution.py:194
  188.0 0.7 add_convert_fusion
  (13 shorter events, 0.0 us)
Async XLA Ops:
  0.0 9.3 %copy-start.9 = (bf16[768,96]{0,1:T(8,128)(2,1)S(1)}, bf16[768,96]{0,1:T(8,128)(2,1)}, u32[]{:S(2)}) copy-start(bf16[768,96]{0,1:T(8,128)(2,1)} %param.9) | copy-start | bytes 442372
  1.9 22.5 %all-to-all-start = ((bf16[32,16,384]{2,1,0:T(8,128)(2,1)}), bf16[32,16,384]{2,1,0:T(8,128)(2,1)S(1)}, u32[]{:S(2)}, u32[]{:S(2)}) async-start(bf16[32,16,384]{2,1,0:T(8,128)(2,1)} %bitcast.6), calls=%async_computation | async-start | bytes 786432 | tf_op jit(solution)/shard_map/all_to_all | solution.py:155
  9.3 14.9 %collective-permute-start.1 = (bf16[96,768]{1,0:T(8,128)(2,1)S(1)}, bf16[96,768]{1,0:T(8,128)(2,1)S(1)}, u32[]{:S(2)}, u32[]{:S(2)}) collective-permute-start(bf16[96,768]{1,0:T(8,128)(2,1)S(1)} %bitcast.27), channel_id=1, source_target_pairs={{0,0},{1,64},{2,128},{3,192},{64,1},{65,65},{66,129},{67,193},{128... | collective-permute-start | bytes 442376 | tf_op jit(solution)/shard_map/ppermute | solution.py:144
  26.1 21.7 %copy-start.8 = (s32[2,64]{1,0:T(2,128)S(1)}, s32[2,64]{1,0:T(2,128)}, u32[]{:S(2)}) copy-start(s32[2,64]{1,0:T(2,128)} %param.8) | copy-start | bytes 1540
  26.1 65.0 %all-to-all-start.1 = ((bf16[16,96,768]{2,1,0:T(8,128)(2,1)}), bf16[16,96,768]{2,1,0:T(8,128)(2,1)S(1)}, u32[]{:S(2)}, u32[]{:S(2)}) async-start(bf16[16,96,768]{2,1,0:T(8,128)(2,1)} %broadcast_in_dim.9), calls=%async_computation.1 | async-start | bytes 4718592 | tf_op jit(solution)/shard_map/all_to_all | solution.py:162
  31.0 58.7 %collective-permute-start = (bf16[32,16,384]{2,1,0:T(8,128)(2,1)S(1)}, bf16[32,16,384]{2,1,0:T(8,128)(2,1)S(1)}, u32[]{:S(2)}, u32[]{:S(2)}) collective-permute-start(bf16[32,16,384]{2,1,0:T(8,128)(2,1)S(1)} %all-to-all-done), channel_id=1, source_target_pairs={{0,256},{256,0},{1,257},{257,1},{2,258},{258,2},{3,259},{259,3},{4... | collective-permute-start | bytes 1179656 | tf_op jit(solution)/shard_map/ppermute | solution.py:156
  45.8 43.8 %collective-permute-start.2 = (bf16[96,768]{1,0:T(8,128)(2,1)S(1)}, bf16[96,768]{1,0:T(8,128)(2,1)S(1)}, u32[]{:S(2)}, u32[]{:S(2)}) collective-permute-start(bf16[96,768]{1,0:T(8,128)(2,1)S(1)} %collective-permute-done.1), channel_id=1, source_target_pairs={{0,256},{256,0},{1,257},{257,1},{2,258},{258,2},{3,259},{259,3},{4... | collective-permute-start | bytes 442376 | tf_op jit(solution)/shard_map/ppermute | solution.py:158
  89.6 0.7 copy-start.6
  90.3 0.8 copy-start.5
  91.0 2.9 %copy-start.3 = (bf16[16,96,768]{2,1,0:T(8,128)(2,1)}, bf16[16,96,768]{2,1,0:T(8,128)(2,1)S(1)}, u32[]{:S(2)}) copy-start(bf16[16,96,768]{2,1,0:T(8,128)(2,1)S(1)} %all-to-all-done.1) | copy-start | bytes 7077892
  92.4 22.6 %copy-start.7 = (bf16[96,768]{1,0:T(8,128)(2,1)S(1)}, bf16[96,768]{1,0:T(8,128)(2,1)}, u32[]{:S(2)}) copy-start(bf16[96,768]{1,0:T(8,128)(2,1)} %copy-done.6) | copy-start | bytes 442372
  116.7 4.6 %copy-start = (bf16[128,768]{1,0:T(8,128)(2,1)S(1)}, bf16[128,768]{1,0:T(8,128)(2,1)}, u32[]{:S(2)}) copy-start(bf16[128,768]{1,0:T(8,128)(2,1)} %k_ref.1) | copy-start | bytes 589828
  116.7 4.6 %copy-start.1 = (bf16[128,768]{1,0:T(8,128)(2,1)S(1)}, bf16[128,768]{1,0:T(8,128)(2,1)}, u32[]{:S(2)}) copy-start(bf16[128,768]{1,0:T(8,128)(2,1)} %v_ref.1) | copy-start | bytes 589828
  116.7 4.6 %copy-start.2 = (bf16[128,768]{1,0:T(8,128)(2,1)S(1)}, bf16[128,768]{1,0:T(8,128)(2,1)}, u32[]{:S(2)}) copy-start(bf16[128,768]{1,0:T(8,128)(2,1)} %q_ref.1) | copy-start | bytes 589828
  116.7 39.2 %all-to-all-start.3 = ((bf16[16,96,768]{2,1,0:T(8,128)(2,1)}), bf16[16,96,768]{2,1,0:T(8,128)(2,1)}, u32[]{:S(2)}, u32[]{:S(2)}) async-start(bf16[16,96,768]{2,1,0:T(8,128)(2,1)} %broadcast_in_dim.11), calls=%async_computation.3 | async-start | bytes 4718592 | tf_op jit(solution)/shard_map/all_to_all | solution.py:162
  123.2 13.9 %collective-permute-start.5 = (bf16[128,768]{1,0:T(8,128)(2,1)S(1)}, bf16[128,768]{1,0:T(8,128)(2,1)S(1)}, u32[]{:S(2)}, u32[]{:S(2)}) collective-permute-start(bf16[128,768]{1,0:T(8,128)(2,1)S(1)} %shard_map.55.refs_0_), channel_id=1, source_target_pairs={{0,3},{1,2},{2,1},{3,0},{4,7},{5,6},{6,5},{7,4},{8,11},{9,10},{10,... | collective-permute-start | bytes 589832 | tf_op jit(solution)/shard_map/ppermute | solution.py:186
  125.1 15.6 %collective-permute-start.4 = (bf16[128,768]{1,0:T(8,128)(2,1)S(1)}, bf16[128,768]{1,0:T(8,128)(2,1)S(1)}, u32[]{:S(2)}, u32[]{:S(2)}) collective-permute-start(bf16[128,768]{1,0:T(8,128)(2,1)S(1)} %shard_map.55.refs_0_), channel_id=1, source_target_pairs={{0,2},{1,3},{2,0},{3,1},{4,6},{5,7},{6,4},{7,5},{8,10},{9,11},{10,... | collective-permute-start | bytes 589832 | tf_op jit(solution)/shard_map/ppermute | solution.py:186
  127.0 14.0 %collective-permute-start.3 = (bf16[128,768]{1,0:T(8,128)(2,1)S(1)}, bf16[128,768]{1,0:T(8,128)(2,1)S(1)}, u32[]{:S(2)}, u32[]{:S(2)}) collective-permute-start(bf16[128,768]{1,0:T(8,128)(2,1)S(1)} %shard_map.55.refs_0_), channel_id=1, source_target_pairs={{0,1},{1,0},{2,3},{3,2},{4,5},{5,4},{6,7},{7,6},{8,9},{9,8},{10,11... | collective-permute-start | bytes 589832 | tf_op jit(solution)/shard_map/ppermute | solution.py:186
  132.4 25.5 %collective-permute-start.6 = (bf16[16,96,768]{2,1,0:T(8,128)(2,1)}, bf16[16,96,768]{2,1,0:T(8,128)(2,1)S(1)}, u32[]{:S(2)}, u32[]{:S(2)}) collective-permute-start(bf16[16,96,768]{2,1,0:T(8,128)(2,1)} %copy-done.3), channel_id=1, source_target_pairs={{0,8},{8,0},{1,9},{9,1},{2,10},{10,2},{3,11},{11,3},{4,12},{12,4},... | collective-permute-start | bytes 7077896 | tf_op jit(solution)/shard_map/ppermute | solution.py:165
  155.9 6.8 %collective-permute-start.7 = (bf16[16,96,768]{2,1,0:T(8,128)(2,1)}, bf16[16,96,768]{2,1,0:T(8,128)(2,1)}, u32[]{:S(2)}, u32[]{:S(2)}) collective-permute-start(bf16[16,96,768]{2,1,0:T(8,128)(2,1)} %all-to-all-done.3), channel_id=1, source_target_pairs={{0,8},{8,0},{1,9},{9,1},{2,10},{10,2},{3,11},{11,3},{4,12},{12,4},... | collective-permute-start | bytes 7077896 | tf_op jit(solution)/shard_map/ppermute | solution.py:165
  157.9 4.7 %copy-start.4 = (bf16[16,96,768]{2,1,0:T(8,128)(2,1)}, bf16[16,96,768]{2,1,0:T(8,128)(2,1)S(1)}, u32[]{:S(2)}) copy-start(bf16[16,96,768]{2,1,0:T(8,128)(2,1)S(1)} %collective-permute-done.6) | copy-start | bytes 7077892
  166.8 21.2 %collective-permute-start.8 = (bf16[128,768]{1,0:T(8,128)(2,1)S(1)}, bf16[128,768]{1,0:T(8,128)(2,1)S(1)}, u32[]{:S(2)}, u32[]{:S(2)}) collective-permute-start(bf16[128,768]{1,0:T(8,128)(2,1)S(1)} %shard_map.57), channel_id=1, source_target_pairs={{0,4},{4,0},{1,5},{5,1},{2,6},{6,2},{3,7},{7,3},{8,12},{12,8},{9,1... | collective-permute-start | bytes 589832 | tf_op jit(solution)/shard_map/ppermute | solution.py:194

commit v15 on v6

--- a/solution.py
+++ b/solution.py
@@ -16,7 +16,6 @@
 PLANE = ("x", "y", "c")
 SWAP = ((0, 1), (1, 0))
 QUAD = 4
-HINT_FLOPS, HINT_BYTES = 182 * 10**9, 10**6
 HALVES = 2
 PIECE = 16
 
@@ -34,12 +33,12 @@
     for k in range(QUAD):
         copies[k].wait()
         total += lax.dot_general(
+            held[k].reshape(-1, width),
             parts[k][...],
-            held[k].reshape(-1, width),
             (((1,), (1,)), ((), ())),
             preferred_element_type=jnp.float32,
         )
-    out_ref[...] = total.astype(out_ref.dtype)
+    out_ref[...] = total.T.astype(out_ref.dtype)
 
 
 def project(order, parts, w_all, side, dtype):
@@ -66,8 +65,8 @@
     )(order, *parts, pltpu.with_memory_space_constraint(w_all, pltpu.HBM))
 
 
-def attend_kernel(q_ref, k_ref, v_ref, routed_ref, out_ref):
-    tokens, width = q_ref.shape
+def attend_kernel(own_ref, routed_ref, out_ref):
+    _, tokens, width = own_ref.shape
     part = width // HALVES
     for head in range(width // HEAD_DIM):
         cols = slice(head * HEAD_DIM, (head + 1) * HEAD_DIM)
@@ -77,13 +76,13 @@
             piece = routed_ref[kind * HALVES + at, :, turn, :, lane : lane + HEAD_DIM]
             return piece.reshape(tokens, HEAD_DIM)
 
-        query = q_ref[:, cols]
+        query = own_ref[0, :, cols]
         scores = [
             lax.dot_general(
                 query, keys, (((1,), (1,)), ((), ())), preferred_element_type=jnp.float32
             )
             * (1.0 / HEAD_DIM**0.5)
-            for keys in [k_ref[:, cols]] + [rows(0, turn) for turn in range(ROUNDS)]
+            for keys in [own_ref[1, :, cols]] + [rows(0, turn) for turn in range(ROUNDS)]
         ]
         peak = functools.reduce(jnp.maximum, scores)
         peak = jnp.max(peak, axis=-1, keepdims=True)
@@ -91,7 +90,7 @@
         row_total = jnp.sum(functools.reduce(jnp.add, exponents), axis=-1, keepdims=True)
         summed = 0.0
         for exponent, values in zip(
-            exponents, [v_ref[:, cols]] + [rows(1, turn) for turn in range(ROUNDS)]
+            exponents, [own_ref[2, :, cols]] + [rows(1, turn) for turn in range(ROUNDS)]
         ):
             summed += jnp.dot(
                 exponent.astype(jnp.bfloat16), values, preferred_element_type=jnp.float32
@@ -99,18 +98,21 @@
         out_ref[:, cols] = (summed / row_total).astype(out_ref.dtype)
 
 
-def attend(queries, keys, values, routed):
+def attend(own, routed):
+    _, tokens, width = own.shape
     in_vmem = pl.BlockSpec(memory_space=pltpu.VMEM)
     return pl.pallas_call(
         attend_kernel,
-        in_specs=[in_vmem] * 4,
+        in_specs=[in_vmem] * 2,
         out_specs=in_vmem,
-        out_shape=jax.ShapeDtypeStruct(queries.shape, queries.dtype),
+        out_shape=jax.ShapeDtypeStruct((tokens, width), own.dtype),
         compiler_params=pltpu.CompilerParams(vmem_limit_bytes=32 << 20),
         cost_estimate=pl.CostEstimate(
-            flops=HINT_FLOPS, bytes_accessed=HINT_BYTES, transcendentals=0
+            flops=4 * tokens * width * (1 + ROUNDS) * tokens,
+            bytes_accessed=2 * (own.size + routed.size + tokens * width),
+            transcendentals=tokens * width * (1 + ROUNDS),
         ),
-    )(queries, keys, values, routed)
+    )(own, routed)
 
 
 def body(queries, keys, values, plan, w_out):
@@ -142,15 +144,15 @@
     w_all = lax.all_gather(w_pair, PLANE, axis=0, tiled=False)
     w_all = w_all.reshape(QUAD, seats // QUAD, 2, -1, width)
 
+    block = jnp.stack((queries, keys, values))
+    far, block = lax.optimization_barrier((far, block))
+
     wanted = lax.dynamic_slice_in_dim(plan, half * seats, seats, 1)
     place = (wanted // seats ^ half) * seats + wanted % seats
     chosen = jnp.concatenate((spread, far)).at[place.T].get(mode="promise_in_bounds")
     routed = lax.all_to_all(chosen, PLANE, split_axis=0, concat_axis=0, tiled=True)
     attended = attend(
-        queries,
-        keys,
-        values,
-        routed.reshape(2 * HALVES, tokens // PIECE, ROUNDS, PIECE, part),
+        block, routed.reshape(2 * HALVES, tokens // PIECE, ROUNDS, PIECE, part)
     )
 
     parts = [attended] + [

time: 188 us -> 185 us (0.984)
  waiting for transfers between devices: 88 us -> 52.4 us
  blocking collectives: 20.1 us -> 39 us
  starting transfers between devices: 47.3 us -> 59.9 us
  local copies, waits for them, and re-layouts: 4.77 us -> 1.99 us
    all_to_all x1, blocking collectives: 20.1 us -> 39 us  [body(): lax.all_to_all(chosen, PLANE, split_axis=0, concat_axis=0, tiled=True)]
    ppermute x1, waiting for transfers between devices: 27.4 us -> 11.2 us  [body(): far = lax.ppermute(spread, 'zh', SWAP)]
    ppermute x1, starting transfers between devices: 1.92 us -> 13.1 us  [body(): far = lax.ppermute(spread, 'zh', SWAP)]
    ppermute x1, waiting for transfers between devices: 19.9 us -> 10.5 us  [body(): w_far = lax.ppermute(w_near, 'zh', SWAP)]
    all_gather x1, waiting for transfers between devices: 8.28 us -> 0.01 us  [body(): w_all = lax.all_gather(w_pair, PLANE, axis=0, tiled=False)]
    unnamed x6 -> x0, local copies, waits for them, and re-layouts: 2.78 us -> none
  transfers between devices with their start and end apart: 9 -> 9, of which waited for: 7 -> 6; matrix products, arithmetic and copies ran while one was open for 1% -> 2% of each run, Pallas kernels for 3% -> 4%
where the time goes in v15:
time: 185 us; the launch traced here: 183 us
  starting transfers between devices  59.9 us (32%)
  waiting for transfers between devices  52.4 us (28%)
  blocking collectives  39 us (21%)
  between operations  13.5 us (7%)
  Pallas kernels  11.9 us (6%)
  other arithmetic  4.36 us (2%)
  local copies, waits for them, and re-layouts  1.99 us (1%)
    all_to_all x1, blocking collectives, body(): lax.all_to_all(chosen, PLANE, split_axis=0, concat_axis=0, tiled=True)  39 us
    ppermute x1, starting transfers between devices, body(): w_far = lax.ppermute(w_near, 'zh', SWAP)  13.8 us
    ppermute x1, starting transfers between devices, body(): far = lax.ppermute(spread, 'zh', SWAP)  13.1 us
    ppermute x1, waiting for transfers between devices, body(): arrived = lax.ppermute(sent, 'p', SWAP)  12.1 us
    ppermute x1, waiting for transfers between devices, body(): far = lax.ppermute(spread, 'zh', SWAP)  11.2 us
    ppermute x3, waiting for transfers between devices, body(): lax.ppermute(attended, 'q', [(i, i ^ k) for i in range(QUAD)])  10.7 us
    ppermute x1, waiting for transfers between devices, body(): w_far = lax.ppermute(w_near, 'zh', SWAP)  10.5 us
    ppermute x3, starting transfers between devices, body(): lax.ppermute(attended, 'q', [(i, i ^ k) for i in range(QUAD)])  10.1 us
  transfers between devices with their start and end apart: 9, of which 6 were waited for; matrix products, arithmetic and copies ran while one was open for 2% of the time, Pallas kernels for 4%

profile of v15, /device:TPU:6, one launch (start us, length us, event | category | flops | bytes accessed | tf_op | source)
XLA Modules:
  0.0 183.1 jit_solution(5825511488803140188)
XLA Ops:
  6.5 1.1 slice_bitcast_fusion.1
  7.6 0.8 pad_maximum_fusion.2
  8.4 9.5 %all-to-all-start = ((bf16[32,16,384]{2,1,0:T(8,128)(2,1)}), bf16[32,16,384]{2,1,0:T(8,128)(2,1)S(1)}, u32[]{:S(2)}, u32[]{:S(2)}) async-start(bf16[32,16,384]{2,1,0:T(8,128)(2,1)} %bitcast.4), calls=%async_computation | async-start | bytes 786432 | tf_op jit(solution)/shard_map/all_to_all | solution.py:135
  18.0 0.0 all-gather.3.cloned.1.call-start
  18.0 4.2 %collective-permute-start = (bf16[96,768]{1,0:T(8,128)(2,1)}, bf16[96,768]{1,0:T(8,128)(2,1)S(1)}, u32[]{:S(2)}, u32[]{:S(2)}) collective-permute-start(bf16[96,768]{1,0:T(8,128)(2,1)} %bitcast.29), channel_id=1, source_target_pairs={{0,0},{1,64},{2,128},{3,192},{64,1},{65,65},{66,129},{67,193},{128... | collective-permute-start | bytes 442376 | tf_op jit(solution)/shard_map/ppermute | solution.py:124
  22.3 7.9 %collective-permute-done = bf16[96,768]{1,0:T(8,128)(2,1)S(1)} collective-permute-done((bf16[96,768]{1,0:T(8,128)(2,1)}, bf16[96,768]{1,0:T(8,128)(2,1)S(1)}, u32[]{:S(2)}, u32[]{:S(2)}) %collective-permute-start) | collective-permute-done | bytes 147488 | tf_op jit(solution)/shard_map/ppermute | solution.py:124
  30.1 0.0 all-to-all-done
  30.1 13.8 %collective-permute-start.5 = (bf16[96,768]{1,0:T(8,128)(2,1)S(1)}, bf16[96,768]{1,0:T(8,128)(2,1)S(1)}, u32[]{:S(2)}, u32[]{:S(2)}) collective-permute-start(bf16[96,768]{1,0:T(8,128)(2,1)S(1)} %collective-permute-done), channel_id=1, source_target_pairs={{0,256},{256,0},{1,257},{257,1},{2,258},{258,2},{3,259},{259,3},{4... | collective-permute-start | bytes 442376 | tf_op jit(solution)/shard_map/ppermute | solution.py:138
  43.9 10.5 %collective-permute-done.5 = bf16[96,768]{1,0:T(8,128)(2,1)S(1)} collective-permute-done((bf16[96,768]{1,0:T(8,128)(2,1)S(1)}, bf16[96,768]{1,0:T(8,128)(2,1)S(1)}, u32[]{:S(2)}, u32[]{:S(2)}) %collective-permute-start.5) | collective-permute-done | bytes 147488 | tf_op jit(solution)/shard_map/ppermute | solution.py:138
  54.4 0.8 pad_maximum_fusion.3
  55.2 0.0 all-gather.3.cloned.1.call-update
  55.2 13.1 %collective-permute-start.1 = (bf16[32,16,384]{2,1,0:T(8,128)(2,1)S(1)}, bf16[32,16,384]{2,1,0:T(8,128)(2,1)S(1)}, u32[]{:S(2)}, u32[]{:S(2)}) collective-permute-start(bf16[32,16,384]{2,1,0:T(8,128)(2,1)S(1)} %all-to-all-done), channel_id=1, source_target_pairs={{0,256},{256,0},{1,257},{257,1},{2,258},{258,2},{3,259},{259,3},{4... | collective-permute-start | bytes 1179656 | tf_op jit(solution)/shard_map/ppermute | solution.py:139
  68.3 0.8 compare_select_fusion
  69.1 0.1 copy.8
  69.2 0.1 reshape.14
  69.3 1.2 pad_maximum_fusion.1.own_ref
  70.5 11.2 %collective-permute-done.1 = bf16[32,16,384]{2,1,0:T(8,128)(2,1)S(1)} collective-permute-done((bf16[32,16,384]{2,1,0:T(8,128)(2,1)S(1)}, bf16[32,16,384]{2,1,0:T(8,128)(2,1)S(1)}, u32[]{:S(2)}, u32[]{:S(2)}) %collective-permute-start.1) | collective-permute-done | bytes 393248 | tf_op jit(solution)/shard_map/ppermute | solution.py:139
  81.7 0.1 pad_maximum_fusion
  81.8 0.7 gather_fusion
  82.6 39.0 %all_to_all.10 = bf16[32,2,16,384]{3,2,1,0:T(8,128)(2,1)S(1)} all-to-all(bf16[32,2,16,384]{3,2,1,0:T(8,128)(2,1)S(1)} %bitcast.25), channel_id=1, replica_groups=mesh['zh'=2,'x'=4,'y'=4,'c'=2,'p'=2,'q'=4] {'x','y','c'}, dimensions={0} | all-to-all | bytes 1572864 | tf_op jit(solution)/shard_map/all_to_all | solution.py:153
  121.5 1.9 %shard_map.55.refs_0_ = bf16[128,768]{1,0:T(8,128)(2,1)S(1)} custom-call(bf16[3,128,768]{2,1,0:T(8,128)(2,1)S(1)} %pad_maximum_fusion.1.own_ref, bf16[4,8,2,16,384]{4,3,2,1,0:T(8,128)(2,1)S(1)} %bitcast.22), custom_call_target="tpu_custom_call" | custom-call | flops 150994944 | bytes 1572864 | tf_op jit(solution)/shard_map/pallas_call | solution.py:104
  123.4 1.9 %collective-permute-start.2 = (bf16[128,768]{1,0:T(8,128)(2,1)S(1)}, bf16[128,768]{1,0:T(8,128)(2,1)S(1)}, u32[]{:S(2)}, u32[]{:S(2)}) collective-permute-start(bf16[128,768]{1,0:T(8,128)(2,1)S(1)} %shard_map.55.refs_0_), channel_id=1, source_target_pairs={{0,1},{1,0},{2,3},{3,2},{4,5},{5,4},{6,7},{7,6},{8,9},{9,8},{10,11... | collective-permute-start | bytes 589832 | tf_op jit(solution)/shard_map/ppermute | solution.py:159
  125.3 2.8 %collective-permute-start.3 = (bf16[128,768]{1,0:T(8,128)(2,1)S(1)}, bf16[128,768]{1,0:T(8,128)(2,1)S(1)}, u32[]{:S(2)}, u32[]{:S(2)}) collective-permute-start(bf16[128,768]{1,0:T(8,128)(2,1)S(1)} %shard_map.55.refs_0_), channel_id=1, source_target_pairs={{0,2},{1,3},{2,0},{3,1},{4,6},{5,7},{6,4},{7,5},{8,10},{9,11},{10,... | collective-permute-start | bytes 589832 | tf_op jit(solution)/shard_map/ppermute | solution.py:159
  128.2 5.4 %collective-permute-start.4 = (bf16[128,768]{1,0:T(8,128)(2,1)S(1)}, bf16[128,768]{1,0:T(8,128)(2,1)S(1)}, u32[]{:S(2)}, u32[]{:S(2)}) collective-permute-start(bf16[128,768]{1,0:T(8,128)(2,1)S(1)} %shard_map.55.refs_0_), channel_id=1, source_target_pairs={{0,3},{1,2},{2,1},{3,0},{4,7},{5,6},{6,5},{7,4},{8,11},{9,10},{10,... | collective-permute-start | bytes 589832 | tf_op jit(solution)/shard_map/ppermute | solution.py:159
  133.6 0.3 collective-permute-done.2.refs_1_
  133.9 10.4 %collective-permute-done.3.refs_2_ = bf16[128,768]{1,0:T(8,128)(2,1)S(1)} collective-permute-done((bf16[128,768]{1,0:T(8,128)(2,1)S(1)}, bf16[128,768]{1,0:T(8,128)(2,1)S(1)}, u32[]{:S(2)}, u32[]{:S(2)}) %collective-permute-start.3) | collective-permute-done | bytes 196640 | tf_op jit(solution)/shard_map/ppermute | solution.py:159
  144.3 0.0 collective-permute-done.4.refs_3_
  144.3 0.0 all-gather.3.cloned.1.call-done
  144.3 5.0 %shard_map.57 = bf16[128,768]{1,0:T(8,128)(2,1)S(1)} custom-call(s32[4]{0:T(128)S(1)} %iota_xor_fusion.order_ref, bf16[128,768]{1,0:T(8,128)(2,1)S(1)} %shard_map.55.refs_0_, bf16[128,768]{1,0:T(8,128)(2,1)S(1)} %collective-permute-done.2.refs_1_, bf16[128,768]{1,0:T(8,128)(2,1)S(1)} %collective-permute-done.3.refs_2_, ...), custom_call_target="tpu_custom_call" | custom-call | flops 603979776 | bytes 5505024 | tf_op jit(solution)/shard_map/pallas_call | solution.py:48
  149.4 9.1 %collective-permute-start.6 = (bf16[128,768]{1,0:T(8,128)(2,1)S(1)}, bf16[128,768]{1,0:T(8,128)(2,1)S(1)}, u32[]{:S(2)}, u32[]{:S(2)}) collective-permute-start(bf16[128,768]{1,0:T(8,128)(2,1)S(1)} %shard_map.57), channel_id=1, source_target_pairs={{0,4},{4,0},{1,5},{5,1},{2,6},{6,2},{3,7},{7,3},{8,12},{12,8},{9,1... | collective-permute-start | bytes 589832 | tf_op jit(solution)/shard_map/ppermute | solution.py:163
  158.4 5.0 %shard_map.56 = f32[128,768]{1,0:T(8,128)S(1)} custom-call(s32[4]{0:T(128)S(1)} %iota_xor_fusion.order_ref, bf16[128,768]{1,0:T(8,128)(2,1)S(1)} %shard_map.55.refs_0_, bf16[128,768]{1,0:T(8,128)(2,1)S(1)} %collective-permute-done.2.refs_1_, bf16[128,768]{1,0:T(8,128)(2,1)S(1)} %collective-permute-done.3.refs_2_, ...), custom_call_target="tpu_custom_call" | custom-call | flops 603979776 | bytes 5505024 | tf_op jit(solution)/shard_map/pallas_call | solution.py:48
  163.5 12.1 %collective-permute-done.6 = bf16[128,768]{1,0:T(8,128)(2,1)S(1)} collective-permute-done((bf16[128,768]{1,0:T(8,128)(2,1)S(1)}, bf16[128,768]{1,0:T(8,128)(2,1)S(1)}, u32[]{:S(2)}, u32[]{:S(2)}) %collective-permute-start.6) | collective-permute-done | bytes 196640 | tf_op jit(solution)/shard_map/ppermute | solution.py:163
  175.6 0.7 add_convert_fusion
  (3 shorter events, 0.0 us)
Async XLA Ops:
  8.4 21.7 %all-to-all-start = ((bf16[32,16,384]{2,1,0:T(8,128)(2,1)}), bf16[32,16,384]{2,1,0:T(8,128)(2,1)S(1)}, u32[]{:S(2)}, u32[]{:S(2)}) async-start(bf16[32,16,384]{2,1,0:T(8,128)(2,1)} %bitcast.4), calls=%async_computation | async-start | bytes 786432 | tf_op jit(solution)/shard_map/all_to_all | solution.py:135
  18.0 126.3 %all-gather.3.cloned.1.call-start = ((), (), s32[]{:S(2)}) async-start(), calls=%async_computation.2 | async-start | bytes 9732096 | tf_op jit(solution)/shard_map/all_gather | solution.py:144
  18.0 12.1 %collective-permute-start = (bf16[96,768]{1,0:T(8,128)(2,1)}, bf16[96,768]{1,0:T(8,128)(2,1)S(1)}, u32[]{:S(2)}, u32[]{:S(2)}) collective-permute-start(bf16[96,768]{1,0:T(8,128)(2,1)} %bitcast.29), channel_id=1, source_target_pairs={{0,0},{1,64},{2,128},{3,192},{64,1},{65,65},{66,129},{67,193},{128... | collective-permute-start | bytes 442376 | tf_op jit(solution)/shard_map/ppermute | solution.py:124
  30.1 24.3 %collective-permute-start.5 = (bf16[96,768]{1,0:T(8,128)(2,1)S(1)}, bf16[96,768]{1,0:T(8,128)(2,1)S(1)}, u32[]{:S(2)}, u32[]{:S(2)}) collective-permute-start(bf16[96,768]{1,0:T(8,128)(2,1)S(1)} %collective-permute-done), channel_id=1, source_target_pairs={{0,256},{256,0},{1,257},{257,1},{2,258},{258,2},{3,259},{259,3},{4... | collective-permute-start | bytes 442376 | tf_op jit(solution)/shard_map/ppermute | solution.py:138
  55.2 26.5 %collective-permute-start.1 = (bf16[32,16,384]{2,1,0:T(8,128)(2,1)S(1)}, bf16[32,16,384]{2,1,0:T(8,128)(2,1)S(1)}, u32[]{:S(2)}, u32[]{:S(2)}) collective-permute-start(bf16[32,16,384]{2,1,0:T(8,128)(2,1)S(1)} %all-to-all-done), channel_id=1, source_target_pairs={{0,256},{256,0},{1,257},{257,1},{2,258},{258,2},{3,259},{259,3},{4... | collective-permute-start | bytes 1179656 | tf_op jit(solution)/shard_map/ppermute | solution.py:139
  123.4 10.5 %collective-permute-start.2 = (bf16[128,768]{1,0:T(8,128)(2,1)S(1)}, bf16[128,768]{1,0:T(8,128)(2,1)S(1)}, u32[]{:S(2)}, u32[]{:S(2)}) collective-permute-start(bf16[128,768]{1,0:T(8,128)(2,1)S(1)} %shard_map.55.refs_0_), channel_id=1, source_target_pairs={{0,1},{1,0},{2,3},{3,2},{4,5},{5,4},{6,7},{7,6},{8,9},{9,8},{10,11... | collective-permute-start | bytes 589832 | tf_op jit(solution)/shard_map/ppermute | solution.py:159
  125.3 19.0 %collective-permute-start.3 = (bf16[128,768]{1,0:T(8,128)(2,1)S(1)}, bf16[128,768]{1,0:T(8,128)(2,1)S(1)}, u32[]{:S(2)}, u32[]{:S(2)}) collective-permute-start(bf16[128,768]{1,0:T(8,128)(2,1)S(1)} %shard_map.55.refs_0_), channel_id=1, source_target_pairs={{0,2},{1,3},{2,0},{3,1},{4,6},{5,7},{6,4},{7,5},{8,10},{9,11},{10,... | collective-permute-start | bytes 589832 | tf_op jit(solution)/shard_map/ppermute | solution.py:159
  128.2 16.1 %collective-permute-start.4 = (bf16[128,768]{1,0:T(8,128)(2,1)S(1)}, bf16[128,768]{1,0:T(8,128)(2,1)S(1)}, u32[]{:S(2)}, u32[]{:S(2)}) collective-permute-start(bf16[128,768]{1,0:T(8,128)(2,1)S(1)} %shard_map.55.refs_0_), channel_id=1, source_target_pairs={{0,3},{1,2},{2,1},{3,0},{4,7},{5,6},{6,5},{7,4},{8,11},{9,10},{10,... | collective-permute-start | bytes 589832 | tf_op jit(solution)/shard_map/ppermute | solution.py:159
  149.4 26.2 %collective-permute-start.6 = (bf16[128,768]{1,0:T(8,128)(2,1)S(1)}, bf16[128,768]{1,0:T(8,128)(2,1)S(1)}, u32[]{:S(2)}, u32[]{:S(2)}) collective-permute-start(bf16[128,768]{1,0:T(8,128)(2,1)S(1)} %shard_map.57), channel_id=1, source_target_pairs={{0,4},{4,0},{1,5},{5,1},{2,6},{6,2},{3,7},{7,3},{8,12},{12,8},{9,1... | collective-permute-start | bytes 589832 | tf_op jit(solution)/shard_map/ppermute | solution.py:163
Sparse Core Ops, SparseCore 0:
  55.3 81.1 all-gather.2

commit v16 on v15

--- a/solution.py
+++ b/solution.py
@@ -17,6 +17,7 @@
 SWAP = ((0, 1), (1, 0))
 QUAD = 4
 HALVES = 2
+HINT_FLOPS, FIRST = 180 * 10**9, 20
 PIECE = 16
 
 
@@ -33,12 +34,12 @@
     for k in range(QUAD):
         copies[k].wait()
         total += lax.dot_general(
+            parts[k][...],
             held[k].reshape(-1, width),
-            parts[k][...],
             (((1,), (1,)), ((), ())),
             preferred_element_type=jnp.float32,
         )
-    out_ref[...] = total.T.astype(out_ref.dtype)
+    out_ref[...] = total.astype(out_ref.dtype)
 
 
 def project(order, parts, w_all, side, dtype):
@@ -107,11 +108,7 @@
         out_specs=in_vmem,
         out_shape=jax.ShapeDtypeStruct((tokens, width), own.dtype),
         compiler_params=pltpu.CompilerParams(vmem_limit_bytes=32 << 20),
-        cost_estimate=pl.CostEstimate(
-            flops=4 * tokens * width * (1 + ROUNDS) * tokens,
-            bytes_accessed=2 * (own.size + routed.size + tokens * width),
-            transcendentals=tokens * width * (1 + ROUNDS),
-        ),
+        cost_estimate=pl.CostEstimate(flops=HINT_FLOPS, bytes_accessed=10**6, transcendentals=0),
     )(own, routed)
 
 
@@ -136,11 +133,14 @@
     spread, w_near = lax.optimization_barrier((spread, w_near))
 
     w_far = lax.ppermute(w_near, "zh", SWAP)
-    far = lax.ppermute(spread, "zh", SWAP)
     keeps_near = half == quad
     w_pair = jnp.stack(
         (jnp.where(keeps_near, w_near, w_far), jnp.where(keeps_near, w_far, w_near))
     )
+    spread = jnp.split(spread, (FIRST,))
+    far = [lax.ppermute(spread[0], "zh", SWAP)]
+    spread[1], w_pair = lax.optimization_barrier((spread[1], w_pair))
+    far.append(lax.ppermute(spread[1], "zh", SWAP))
     w_all = lax.all_gather(w_pair, PLANE, axis=0, tiled=False)
     w_all = w_all.reshape(QUAD, seats // QUAD, 2, -1, width)
 
@@ -149,7 +149,7 @@
 
     wanted = lax.dynamic_slice_in_dim(plan, half * seats, seats, 1)
     place = (wanted // seats ^ half) * seats + wanted % seats
-    chosen = jnp.concatenate((spread, far)).at[place.T].get(mode="promise_in_bounds")
+    chosen = jnp.concatenate((*spread, *far)).at[place.T].get(mode="promise_in_bounds")
     routed = lax.all_to_all(chosen, PLANE, split_axis=0, concat_axis=0, tiled=True)
     attended = attend(
         block, routed.reshape(2 * HALVES, tokens // PIECE, ROUNDS, PIECE, part)

time: 185 us -> 187 us (1.011)
  waiting for transfers between devices: 52.4 us -> 74.9 us
  blocking collectives: 39 us -> 20.4 us
    all_to_all x1, blocking collectives: 39 us -> 20.4 us  [body(): lax.all_to_all(chosen, PLANE, split_axis=0, concat_axis=0, tiled=True)]
    all_gather x1, waiting for transfers between devices: 0.01 us -> 10.2 us  [body(): w_all = lax.all_gather(w_pair, PLANE, axis=0, tiled=False)]
    ppermute x1, waiting for transfers between devices: 10.5 us -> 19.8 us  [body(): w_far = lax.ppermute(w_near, 'zh', SWAP)]
    ppermute x1 -> x2, starting transfers between devices: 13.1 us -> 15.4 us  [the longest x1 13.5 us: body(): far.append(lax.ppermute(spread[1], 'zh', SWAP))]
    ppermute x1 -> x2, waiting for transfers between devices: 11.2 us -> 12.4 us  [the longest x1 7.51 us: body(): far.append(lax.ppermute(spread[1], 'zh', SWAP))]
  transfers between devices with their start and end apart: 9 -> 10, of which waited for: 6 -> 8; matrix products, arithmetic and copies ran while one was open for 2% -> 2% of each run, Pallas kernels for 4% -> 3%
where the time goes in v16:
time: 187 us; the launch traced here: 186 us
  waiting for transfers between devices  74.9 us (40%)
  starting transfers between devices  60.8 us (33%)
  blocking collectives  20.4 us (11%)
  between operations  13.6 us (7%)
  Pallas kernels  10.3 us (6%)
  other arithmetic  4.39 us (2%)
  local copies, waits for them, and re-layouts  2.03 us (1%)
    all_to_all x1, blocking collectives, body(): lax.all_to_all(chosen, PLANE, split_axis=0, concat_axis=0, tiled=True)  20.4 us
    ppermute x1, waiting for transfers between devices, body(): w_far = lax.ppermute(w_near, 'zh', SWAP)  19.8 us
    ppermute x1, starting transfers between devices, body(): w_far = lax.ppermute(w_near, 'zh', SWAP)  13.8 us
    ppermute x1, waiting for transfers between devices, body(): arrived = lax.ppermute(sent, 'p', SWAP)  13.8 us
    ppermute x1, starting transfers between devices, body(): far.append(lax.ppermute(spread[1], 'zh', SWAP))  13.5 us
    ppermute x3, waiting for transfers between devices, body(): lax.ppermute(attended, 'q', [(i, i ^ k) for i in range(QUAD)])  10.8 us
    all_gather x1, waiting for transfers between devices, body(): w_all = lax.all_gather(w_pair, PLANE, axis=0, tiled=False)  10.2 us
    ppermute x3, starting transfers between devices, body(): lax.ppermute(attended, 'q', [(i, i ^ k) for i in range(QUAD)])  10.1 us
  transfers between devices with their start and end apart: 10, of which 8 were waited for; matrix products, arithmetic and copies ran while one was open for 2% of the time, Pallas kernels for 3%

profile of v16, /device:TPU:6, one launch (start us, length us, event | category | flops | bytes accessed | tf_op | source)
XLA Modules:
  0.0 186.3 jit_solution(15453135499280099902)
XLA Ops:
  6.5 1.1 slice_bitcast_fusion.1
  7.6 0.8 pad_maximum_fusion.2
  8.4 9.5 %all-to-all-start = ((bf16[32,16,384]{2,1,0:T(8,128)(2,1)}), bf16[32,16,384]{2,1,0:T(8,128)(2,1)S(1)}, u32[]{:S(2)}, u32[]{:S(2)}) async-start(bf16[32,16,384]{2,1,0:T(8,128)(2,1)} %bitcast.4), calls=%async_computation | async-start | bytes 786432 | tf_op jit(solution)/shard_map/all_to_all | solution.py:132
  18.0 0.0 all-gather.3.cloned.1.call-start
  18.0 4.2 %collective-permute-start = (bf16[96,768]{1,0:T(8,128)(2,1)}, bf16[96,768]{1,0:T(8,128)(2,1)S(1)}, u32[]{:S(2)}, u32[]{:S(2)}) collective-permute-start(bf16[96,768]{1,0:T(8,128)(2,1)} %bitcast.29), channel_id=1, source_target_pairs={{0,0},{1,64},{2,128},{3,192},{64,1},{65,65},{66,129},{67,193},{128... | collective-permute-start | bytes 442376 | tf_op jit(solution)/shard_map/ppermute | solution.py:121
  22.3 7.9 %collective-permute-done = bf16[96,768]{1,0:T(8,128)(2,1)S(1)} collective-permute-done((bf16[96,768]{1,0:T(8,128)(2,1)}, bf16[96,768]{1,0:T(8,128)(2,1)S(1)}, u32[]{:S(2)}, u32[]{:S(2)}) %collective-permute-start) | collective-permute-done | bytes 147488 | tf_op jit(solution)/shard_map/ppermute | solution.py:121
  30.1 0.0 all-to-all-done
  30.1 13.8 %collective-permute-start.2 = (bf16[96,768]{1,0:T(8,128)(2,1)S(1)}, bf16[96,768]{1,0:T(8,128)(2,1)S(1)}, u32[]{:S(2)}, u32[]{:S(2)}) collective-permute-start(bf16[96,768]{1,0:T(8,128)(2,1)S(1)} %collective-permute-done), channel_id=1, source_target_pairs={{0,256},{256,0},{1,257},{257,1},{2,258},{258,2},{3,259},{259,3},{4... | collective-permute-start | bytes 442376 | tf_op jit(solution)/shard_map/ppermute | solution.py:135
  44.0 1.9 %collective-permute-start.1 = (bf16[20,16,384]{2,1,0:T(8,128)(2,1)S(1)}, bf16[20,16,384]{2,1,0:T(8,128)(2,1)S(1)}, u32[]{:S(2)}, u32[]{:S(2)}) collective-permute-start(bf16[20,16,384]{2,1,0:T(8,128)(2,1)S(1)} %split.6), channel_id=1, source_target_pairs={{0,256},{256,0},{1,257},{257,1},{2,258},{258,2},{3,259},{259,3},{4... | collective-permute-start | bytes 737288 | tf_op jit(solution)/shard_map/ppermute | solution.py:141
  45.9 19.8 %collective-permute-done.2 = bf16[96,768]{1,0:T(8,128)(2,1)S(1)} collective-permute-done((bf16[96,768]{1,0:T(8,128)(2,1)S(1)}, bf16[96,768]{1,0:T(8,128)(2,1)S(1)}, u32[]{:S(2)}, u32[]{:S(2)}) %collective-permute-start.2) | collective-permute-done | bytes 147488 | tf_op jit(solution)/shard_map/ppermute | solution.py:135
  65.8 0.7 pad_maximum_fusion.3
  66.5 0.0 all-gather.3.cloned.1.call-update
  66.5 0.8 compare_select_fusion
  67.3 0.1 copy.8
  67.4 0.1 reshape.14
  67.5 13.5 %collective-permute-start.3 = (bf16[12,16,384]{2,1,0:T(8,128)(2,1)S(1)}, bf16[12,16,384]{2,1,0:T(8,128)(2,1)S(1)}, u32[]{:S(2)}, u32[]{:S(2)}) collective-permute-start(bf16[12,16,384]{2,1,0:T(8,128)(2,1)S(1)} %split.7), channel_id=1, source_target_pairs={{0,256},{256,0},{1,257},{257,1},{2,258},{258,2},{3,259},{259,3},{4... | collective-permute-start | bytes 442376 | tf_op jit(solution)/shard_map/ppermute | solution.py:143
  81.0 1.2 pad_maximum_fusion.1.own_ref
  82.2 4.9 %collective-permute-done.1 = bf16[20,16,384]{2,1,0:T(8,128)(2,1)S(1)} collective-permute-done((bf16[20,16,384]{2,1,0:T(8,128)(2,1)S(1)}, bf16[20,16,384]{2,1,0:T(8,128)(2,1)S(1)}, u32[]{:S(2)}, u32[]{:S(2)}) %collective-permute-start.1) | collective-permute-done | bytes 245792 | tf_op jit(solution)/shard_map/ppermute | solution.py:141
  87.1 7.5 %collective-permute-done.3 = bf16[12,16,384]{2,1,0:T(8,128)(2,1)S(1)} collective-permute-done((bf16[12,16,384]{2,1,0:T(8,128)(2,1)S(1)}, bf16[12,16,384]{2,1,0:T(8,128)(2,1)S(1)}, u32[]{:S(2)}, u32[]{:S(2)}) %collective-permute-start.3) | collective-permute-done | bytes 147488 | tf_op jit(solution)/shard_map/ppermute | solution.py:143
  94.7 0.1 pad_maximum_fusion
  94.8 0.7 gather_fusion
  95.5 20.4 %all_to_all.10 = bf16[32,2,16,384]{3,2,1,0:T(8,128)(2,1)S(1)} all-to-all(bf16[32,2,16,384]{3,2,1,0:T(8,128)(2,1)S(1)} %bitcast.25), channel_id=1, replica_groups=mesh['zh'=2,'x'=4,'y'=4,'c'=2,'p'=2,'q'=4] {'x','y','c'}, dimensions={0} | all-to-all | bytes 1572864 | tf_op jit(solution)/shard_map/all_to_all | solution.py:153
  115.9 1.9 %shard_map.55.refs_0_ = bf16[128,768]{1,0:T(8,128)(2,1)S(1)} custom-call(bf16[3,128,768]{2,1,0:T(8,128)(2,1)S(1)} %pad_maximum_fusion.1.own_ref, bf16[4,8,2,16,384]{4,3,2,1,0:T(8,128)(2,1)S(1)} %bitcast.22), custom_call_target="tpu_custom_call" | custom-call | flops 179999997952 | bytes 1000000 | tf_op jit(solution)/shard_map/pallas_call | solution.py:105
  117.8 1.9 %collective-permute-start.4 = (bf16[128,768]{1,0:T(8,128)(2,1)S(1)}, bf16[128,768]{1,0:T(8,128)(2,1)S(1)}, u32[]{:S(2)}, u32[]{:S(2)}) collective-permute-start(bf16[128,768]{1,0:T(8,128)(2,1)S(1)} %shard_map.55.refs_0_), channel_id=1, source_target_pairs={{0,1},{1,0},{2,3},{3,2},{4,5},{5,4},{6,7},{7,6},{8,9},{9,8},{10,11... | collective-permute-start | bytes 589832 | tf_op jit(solution)/shard_map/ppermute | solution.py:159
  119.7 1.9 %collective-permute-start.5 = (bf16[128,768]{1,0:T(8,128)(2,1)S(1)}, bf16[128,768]{1,0:T(8,128)(2,1)S(1)}, u32[]{:S(2)}, u32[]{:S(2)}) collective-permute-start(bf16[128,768]{1,0:T(8,128)(2,1)S(1)} %shard_map.55.refs_0_), channel_id=1, source_target_pairs={{0,2},{1,3},{2,0},{3,1},{4,6},{5,7},{6,4},{7,5},{8,10},{9,11},{10,... | collective-permute-start | bytes 589832 | tf_op jit(solution)/shard_map/ppermute | solution.py:159
  121.7 6.3 %collective-permute-start.6 = (bf16[128,768]{1,0:T(8,128)(2,1)S(1)}, bf16[128,768]{1,0:T(8,128)(2,1)S(1)}, u32[]{:S(2)}, u32[]{:S(2)}) collective-permute-start(bf16[128,768]{1,0:T(8,128)(2,1)S(1)} %shard_map.55.refs_0_), channel_id=1, source_target_pairs={{0,3},{1,2},{2,1},{3,0},{4,7},{5,6},{6,5},{7,4},{8,11},{9,10},{10,... | collective-permute-start | bytes 589832 | tf_op jit(solution)/shard_map/ppermute | solution.py:159
  128.0 0.1 collective-permute-done.4.refs_1_
  128.0 10.7 %collective-permute-done.5.refs_2_ = bf16[128,768]{1,0:T(8,128)(2,1)S(1)} collective-permute-done((bf16[128,768]{1,0:T(8,128)(2,1)S(1)}, bf16[128,768]{1,0:T(8,128)(2,1)S(1)}, u32[]{:S(2)}, u32[]{:S(2)}) %collective-permute-start.5) | collective-permute-done | bytes 196640 | tf_op jit(solution)/shard_map/ppermute | solution.py:159
  138.7 0.0 collective-permute-done.6.refs_3_
  138.7 10.2 %all-gather.3.cloned.1.call-done = bf16[64,96,768]{2,1,0:T(8,128)(2,1)} async-done(((bf16[2,96,768]{2,1,0:T(8,128)(2,1)}), bf16[64,96,768]{2,1,0:T(8,128)(2,1)}) %all-gather.3.cloned.1.call-update) | async-done | bytes 9437200 | tf_op jit(solution)/shard_map/all_gather | solution.py:144
  148.9 4.2 %shard_map.57 = bf16[128,768]{1,0:T(8,128)(2,1)S(1)} custom-call(s32[4]{0:T(128)S(1)} %iota_xor_fusion.order_ref, bf16[128,768]{1,0:T(8,128)(2,1)S(1)} %shard_map.55.refs_0_, bf16[128,768]{1,0:T(8,128)(2,1)S(1)} %collective-permute-done.4.refs_1_, bf16[128,768]{1,0:T(8,128)(2,1)S(1)} %collective-permute-done.5.refs_2_, ...), custom_call_target="tpu_custom_call" | custom-call | flops 603979776 | bytes 5505024 | tf_op jit(solution)/shard_map/pallas_call | solution.py:49
  153.1 7.6 %collective-permute-start.7 = (bf16[128,768]{1,0:T(8,128)(2,1)S(1)}, bf16[128,768]{1,0:T(8,128)(2,1)S(1)}, u32[]{:S(2)}, u32[]{:S(2)}) collective-permute-start(bf16[128,768]{1,0:T(8,128)(2,1)S(1)} %shard_map.57), channel_id=1, source_target_pairs={{0,4},{4,0},{1,5},{5,1},{2,6},{6,2},{3,7},{7,3},{8,12},{12,8},{9,1... | collective-permute-start | bytes 589832 | tf_op jit(solution)/shard_map/ppermute | solution.py:163
  160.8 4.2 %shard_map.56 = f32[128,768]{1,0:T(8,128)S(1)} custom-call(s32[4]{0:T(128)S(1)} %iota_xor_fusion.order_ref, bf16[128,768]{1,0:T(8,128)(2,1)S(1)} %shard_map.55.refs_0_, bf16[128,768]{1,0:T(8,128)(2,1)S(1)} %collective-permute-done.4.refs_1_, bf16[128,768]{1,0:T(8,128)(2,1)S(1)} %collective-permute-done.5.refs_2_, ...), custom_call_target="tpu_custom_call" | custom-call | flops 603979776 | bytes 5505024 | tf_op jit(solution)/shard_map/pallas_call | solution.py:49
  165.0 13.8 %collective-permute-done.7 = bf16[128,768]{1,0:T(8,128)(2,1)S(1)} collective-permute-done((bf16[128,768]{1,0:T(8,128)(2,1)S(1)}, bf16[128,768]{1,0:T(8,128)(2,1)S(1)}, u32[]{:S(2)}, u32[]{:S(2)}) %collective-permute-start.7) | collective-permute-done | bytes 196640 | tf_op jit(solution)/shard_map/ppermute | solution.py:163
  178.7 0.7 add_convert_fusion
  (5 shorter events, 0.1 us)
Async XLA Ops:
  8.4 21.7 %all-to-all-start = ((bf16[32,16,384]{2,1,0:T(8,128)(2,1)}), bf16[32,16,384]{2,1,0:T(8,128)(2,1)S(1)}, u32[]{:S(2)}, u32[]{:S(2)}) async-start(bf16[32,16,384]{2,1,0:T(8,128)(2,1)} %bitcast.4), calls=%async_computation | async-start | bytes 786432 | tf_op jit(solution)/shard_map/all_to_all | solution.py:132
  18.0 130.9 %all-gather.3.cloned.1.call-start = ((), (), s32[]{:S(2)}) async-start(), calls=%async_computation.2 | async-start | bytes 9732096 | tf_op jit(solution)/shard_map/all_gather | solution.py:144
  18.0 12.1 %collective-permute-start = (bf16[96,768]{1,0:T(8,128)(2,1)}, bf16[96,768]{1,0:T(8,128)(2,1)S(1)}, u32[]{:S(2)}, u32[]{:S(2)}) collective-permute-start(bf16[96,768]{1,0:T(8,128)(2,1)} %bitcast.29), channel_id=1, source_target_pairs={{0,0},{1,64},{2,128},{3,192},{64,1},{65,65},{66,129},{67,193},{128... | collective-permute-start | bytes 442376 | tf_op jit(solution)/shard_map/ppermute | solution.py:121
  30.1 35.6 %collective-permute-start.2 = (bf16[96,768]{1,0:T(8,128)(2,1)S(1)}, bf16[96,768]{1,0:T(8,128)(2,1)S(1)}, u32[]{:S(2)}, u32[]{:S(2)}) collective-permute-start(bf16[96,768]{1,0:T(8,128)(2,1)S(1)} %collective-permute-done), channel_id=1, source_target_pairs={{0,256},{256,0},{1,257},{257,1},{2,258},{258,2},{3,259},{259,3},{4... | collective-permute-start | bytes 442376 | tf_op jit(solution)/shard_map/ppermute | solution.py:135
  44.0 43.2 %collective-permute-start.1 = (bf16[20,16,384]{2,1,0:T(8,128)(2,1)S(1)}, bf16[20,16,384]{2,1,0:T(8,128)(2,1)S(1)}, u32[]{:S(2)}, u32[]{:S(2)}) collective-permute-start(bf16[20,16,384]{2,1,0:T(8,128)(2,1)S(1)} %split.6), channel_id=1, source_target_pairs={{0,256},{256,0},{1,257},{257,1},{2,258},{258,2},{3,259},{259,3},{4... | collective-permute-start | bytes 737288 | tf_op jit(solution)/shard_map/ppermute | solution.py:141
  67.5 27.1 %collective-permute-start.3 = (bf16[12,16,384]{2,1,0:T(8,128)(2,1)S(1)}, bf16[12,16,384]{2,1,0:T(8,128)(2,1)S(1)}, u32[]{:S(2)}, u32[]{:S(2)}) collective-permute-start(bf16[12,16,384]{2,1,0:T(8,128)(2,1)S(1)} %split.7), channel_id=1, source_target_pairs={{0,256},{256,0},{1,257},{257,1},{2,258},{258,2},{3,259},{259,3},{4... | collective-permute-start | bytes 442376 | tf_op jit(solution)/shard_map/ppermute | solution.py:143
  117.8 10.2 %collective-permute-start.4 = (bf16[128,768]{1,0:T(8,128)(2,1)S(1)}, bf16[128,768]{1,0:T(8,128)(2,1)S(1)}, u32[]{:S(2)}, u32[]{:S(2)}) collective-permute-start(bf16[128,768]{1,0:T(8,128)(2,1)S(1)} %shard_map.55.refs_0_), channel_id=1, source_target_pairs={{0,1},{1,0},{2,3},{3,2},{4,5},{5,4},{6,7},{7,6},{8,9},{9,8},{10,11... | collective-permute-start | bytes 589832 | tf_op jit(solution)/shard_map/ppermute | solution.py:159
  119.7 19.0 %collective-permute-start.5 = (bf16[128,768]{1,0:T(8,128)(2,1)S(1)}, bf16[128,768]{1,0:T(8,128)(2,1)S(1)}, u32[]{:S(2)}, u32[]{:S(2)}) collective-permute-start(bf16[128,768]{1,0:T(8,128)(2,1)S(1)} %shard_map.55.refs_0_), channel_id=1, source_target_pairs={{0,2},{1,3},{2,0},{3,1},{4,6},{5,7},{6,4},{7,5},{8,10},{9,11},{10,... | collective-permute-start | bytes 589832 | tf_op jit(solution)/shard_map/ppermute | solution.py:159
  121.7 17.1 %collective-permute-start.6 = (bf16[128,768]{1,0:T(8,128)(2,1)S(1)}, bf16[128,768]{1,0:T(8,128)(2,1)S(1)}, u32[]{:S(2)}, u32[]{:S(2)}) collective-permute-start(bf16[128,768]{1,0:T(8,128)(2,1)S(1)} %shard_map.55.refs_0_), channel_id=1, source_target_pairs={{0,3},{1,2},{2,1},{3,0},{4,7},{5,6},{6,5},{7,4},{8,11},{9,10},{10,... | collective-permute-start | bytes 589832 | tf_op jit(solution)/shard_map/ppermute | solution.py:159
  153.1 25.6 %collective-permute-start.7 = (bf16[128,768]{1,0:T(8,128)(2,1)S(1)}, bf16[128,768]{1,0:T(8,128)(2,1)S(1)}, u32[]{:S(2)}, u32[]{:S(2)}) collective-permute-start(bf16[128,768]{1,0:T(8,128)(2,1)S(1)} %shard_map.57), channel_id=1, source_target_pairs={{0,4},{4,0},{1,5},{5,1},{2,6},{6,2},{3,7},{7,3},{8,12},{12,8},{9,1... | collective-permute-start | bytes 589832 | tf_op jit(solution)/shard_map/ppermute | solution.py:163
Sparse Core Ops, SparseCore 0:
  66.7 82.2 all-gather.2

commit v17 on v15

--- a/solution.py
+++ b/solution.py
@@ -33,12 +33,12 @@
     for k in range(QUAD):
         copies[k].wait()
         total += lax.dot_general(
+            parts[k][...],
             held[k].reshape(-1, width),
-            parts[k][...],
             (((1,), (1,)), ((), ())),
             preferred_element_type=jnp.float32,
         )
-    out_ref[...] = total.T.astype(out_ref.dtype)
+    out_ref[...] = total.astype(out_ref.dtype)
 
 
 def project(order, parts, w_all, side, dtype):
@@ -65,6 +65,40 @@
     )(order, *parts, pltpu.with_memory_space_constraint(w_all, pltpu.HBM))
 
 
+def cut_kernel(keys_ref, values_ref, out_ref, arrivals):
+    part = out_ref.shape[-1]
+    copies = [
+        pltpu.make_async_copy(
+            rows.at[:, pl.ds(h * part, part)],
+            out_ref.at[kind * HALVES + h],
+            arrivals.at[kind, h],
+        )
+        for kind, rows in enumerate((keys_ref, values_ref))
+        for h in range(HALVES)
+    ]
+    for copy in copies:
+        copy.start()
+    for copy in copies:
+        copy.wait()
+
+
+def cut(keys, values):
+    tokens, width = keys.shape
+    return pl.pallas_call(
+        cut_kernel,
+        in_specs=[pl.BlockSpec(memory_space=pltpu.HBM)] * 2,
+        out_specs=pl.BlockSpec(memory_space=pltpu.VMEM),
+        out_shape=jax.ShapeDtypeStruct((2 * HALVES, tokens, width // HALVES), keys.dtype),
+        scratch_shapes=[pltpu.SemaphoreType.DMA((2, HALVES))],
+        compiler_params=pltpu.CompilerParams(vmem_limit_bytes=16 << 20),
+        cost_estimate=pl.CostEstimate(
+            flops=0, bytes_accessed=8 * tokens * width, transcendentals=0
+        ),
+    )(
+        *[pltpu.with_memory_space_constraint(rows, pltpu.HBM) for rows in (keys, values)],
+    )
+
+
 def attend_kernel(own_ref, routed_ref, out_ref):
     _, tokens, width = own_ref.shape
     part = width // HALVES
@@ -128,10 +162,7 @@
     )
 
     part = width // HALVES
-    own = jnp.stack(
-        [rows[:, h * part : (h + 1) * part] for rows in (keys, values) for h in range(HALVES)]
-    )
-    own = own.reshape(seats, PIECE, part)
+    own = cut(keys, values).reshape(seats, PIECE, part)
     spread = lax.all_to_all(own, PLANE, split_axis=0, concat_axis=0, tiled=True)
     spread, w_near = lax.optimization_barrier((spread, w_near))
 

time: 185 us -> 184 us (level)
  transfers between devices with their start and end apart: 9 -> 9, of which waited for: 6 -> 6; matrix products, arithmetic and copies ran while one was open for 2% -> 2% of each run, Pallas kernels for 4% -> 3%
where the time goes in v17:
time: 184 us; the launch traced here: 182 us
  starting transfers between devices  59.9 us (33%)
  waiting for transfers between devices  53.3 us (29%)
  blocking collectives  39 us (21%)
  between operations  13.5 us (7%)
  Pallas kernels  12.1 us (7%)
  other arithmetic  3.54 us (2%)
    all_to_all x1, blocking collectives, body(): lax.all_to_all(chosen, PLANE, split_axis=0, concat_axis=0, tiled=True)  39 us
    ppermute x1, starting transfers between devices, body(): w_far = lax.ppermute(w_near, 'zh', SWAP)  13.8 us
    ppermute x1, starting transfers between devices, body(): far = lax.ppermute(spread, 'zh', SWAP)  13.1 us
    ppermute x1, waiting for transfers between devices, body(): arrived = lax.ppermute(sent, 'p', SWAP)  12.9 us
    ppermute x1, waiting for transfers between devices, body(): far = lax.ppermute(spread, 'zh', SWAP)  11.3 us
    ppermute x3, waiting for transfers between devices, body(): lax.ppermute(attended, 'q', [(i, i ^ k) for i in range(QUAD)])  10.7 us
    ppermute x1, waiting for transfers between devices, body(): w_far = lax.ppermute(w_near, 'zh', SWAP)  10.5 us
    ppermute x3, starting transfers between devices, body(): lax.ppermute(attended, 'q', [(i, i ^ k) for i in range(QUAD)])  10.1 us
  transfers between devices with their start and end apart: 9, of which 6 were waited for; matrix products, arithmetic and copies ran while one was open for 2% of the time, Pallas kernels for 3%

profile of v17, /device:TPU:6, one launch (start us, length us, event | category | flops | bytes accessed | tf_op | source)
XLA Modules:
  0.0 182.2 jit_solution(9304421053215910344)
XLA Ops:
  6.5 1.8 shard_map.55
  8.3 9.6 %all-to-all-start = ((bf16[32,16,384]{2,1,0:T(8,128)(2,1)}), bf16[32,16,384]{2,1,0:T(8,128)(2,1)S(1)}, u32[]{:S(2)}, u32[]{:S(2)}) async-start(bf16[32,16,384]{2,1,0:T(8,128)(2,1)} %bitcast), calls=%async_computation | async-start | bytes 786432 | tf_op jit(solution)/shard_map/all_to_all | solution.py:166
  17.9 0.0 all-gather.3.cloned.1.call-start
  18.0 4.2 %collective-permute-start = (bf16[96,768]{1,0:T(8,128)(2,1)}, bf16[96,768]{1,0:T(8,128)(2,1)S(1)}, u32[]{:S(2)}, u32[]{:S(2)}) collective-permute-start(bf16[96,768]{1,0:T(8,128)(2,1)} %bitcast.21), channel_id=1, source_target_pairs={{0,0},{1,64},{2,128},{3,192},{64,1},{65,65},{66,129},{67,193},{128... | collective-permute-start | bytes 442376 | tf_op jit(solution)/shard_map/ppermute | solution.py:158
  22.2 7.9 %collective-permute-done = bf16[96,768]{1,0:T(8,128)(2,1)S(1)} collective-permute-done((bf16[96,768]{1,0:T(8,128)(2,1)}, bf16[96,768]{1,0:T(8,128)(2,1)S(1)}, u32[]{:S(2)}, u32[]{:S(2)}) %collective-permute-start) | collective-permute-done | bytes 147488 | tf_op jit(solution)/shard_map/ppermute | solution.py:158
  30.1 0.0 all-to-all-done
  30.1 13.8 %collective-permute-start.5 = (bf16[96,768]{1,0:T(8,128)(2,1)S(1)}, bf16[96,768]{1,0:T(8,128)(2,1)S(1)}, u32[]{:S(2)}, u32[]{:S(2)}) collective-permute-start(bf16[96,768]{1,0:T(8,128)(2,1)S(1)} %collective-permute-done), channel_id=1, source_target_pairs={{0,256},{256,0},{1,257},{257,1},{2,258},{258,2},{3,259},{259,3},{4... | collective-permute-start | bytes 442376 | tf_op jit(solution)/shard_map/ppermute | solution.py:169
  43.9 10.5 %collective-permute-done.5 = bf16[96,768]{1,0:T(8,128)(2,1)S(1)} collective-permute-done((bf16[96,768]{1,0:T(8,128)(2,1)S(1)}, bf16[96,768]{1,0:T(8,128)(2,1)S(1)}, u32[]{:S(2)}, u32[]{:S(2)}) %collective-permute-start.5) | collective-permute-done | bytes 147488 | tf_op jit(solution)/shard_map/ppermute | solution.py:169
  54.4 0.7 pad_maximum_fusion.2
  55.1 0.0 all-gather.3.cloned.1.call-update
  55.1 13.1 %collective-permute-start.1 = (bf16[32,16,384]{2,1,0:T(8,128)(2,1)S(1)}, bf16[32,16,384]{2,1,0:T(8,128)(2,1)S(1)}, u32[]{:S(2)}, u32[]{:S(2)}) collective-permute-start(bf16[32,16,384]{2,1,0:T(8,128)(2,1)S(1)} %all-to-all-done), channel_id=1, source_target_pairs={{0,256},{256,0},{1,257},{257,1},{2,258},{258,2},{3,259},{259,3},{4... | collective-permute-start | bytes 1179656 | tf_op jit(solution)/shard_map/ppermute | solution.py:170
  68.3 0.8 compare_select_fusion
  69.0 0.1 copy.8
  69.1 0.1 reshape.14
  69.2 1.2 pad_maximum_fusion.1.own_ref
  70.4 11.3 %collective-permute-done.1 = bf16[32,16,384]{2,1,0:T(8,128)(2,1)S(1)} collective-permute-done((bf16[32,16,384]{2,1,0:T(8,128)(2,1)S(1)}, bf16[32,16,384]{2,1,0:T(8,128)(2,1)S(1)}, u32[]{:S(2)}, u32[]{:S(2)}) %collective-permute-start.1) | collective-permute-done | bytes 393248 | tf_op jit(solution)/shard_map/ppermute | solution.py:170
  81.7 0.1 pad_maximum_fusion
  81.8 0.7 gather_fusion
  82.5 39.0 %all_to_all.10 = bf16[32,2,16,384]{3,2,1,0:T(8,128)(2,1)S(1)} all-to-all(bf16[32,2,16,384]{3,2,1,0:T(8,128)(2,1)S(1)} %bitcast.17), channel_id=1, replica_groups=mesh['zh'=2,'x'=4,'y'=4,'c'=2,'p'=2,'q'=4] {'x','y','c'}, dimensions={0} | all-to-all | bytes 1572864 | tf_op jit(solution)/shard_map/all_to_all | solution.py:184
  121.5 1.9 %shard_map.56.refs_0_ = bf16[128,768]{1,0:T(8,128)(2,1)S(1)} custom-call(bf16[3,128,768]{2,1,0:T(8,128)(2,1)S(1)} %pad_maximum_fusion.1.own_ref, bf16[4,8,2,16,384]{4,3,2,1,0:T(8,128)(2,1)S(1)} %bitcast.14), custom_call_target="tpu_custom_call" | custom-call | flops 150994944 | bytes 1572864 | tf_op jit(solution)/shard_map/pallas_call | solution.py:138
  123.3 1.9 %collective-permute-start.2 = (bf16[128,768]{1,0:T(8,128)(2,1)S(1)}, bf16[128,768]{1,0:T(8,128)(2,1)S(1)}, u32[]{:S(2)}, u32[]{:S(2)}) collective-permute-start(bf16[128,768]{1,0:T(8,128)(2,1)S(1)} %shard_map.56.refs_0_), channel_id=1, source_target_pairs={{0,1},{1,0},{2,3},{3,2},{4,5},{5,4},{6,7},{7,6},{8,9},{9,8},{10,11... | collective-permute-start | bytes 589832 | tf_op jit(solution)/shard_map/ppermute | solution.py:190
  125.3 2.8 %collective-permute-start.3 = (bf16[128,768]{1,0:T(8,128)(2,1)S(1)}, bf16[128,768]{1,0:T(8,128)(2,1)S(1)}, u32[]{:S(2)}, u32[]{:S(2)}) collective-permute-start(bf16[128,768]{1,0:T(8,128)(2,1)S(1)} %shard_map.56.refs_0_), channel_id=1, source_target_pairs={{0,2},{1,3},{2,0},{3,1},{4,6},{5,7},{6,4},{7,5},{8,10},{9,11},{10,... | collective-permute-start | bytes 589832 | tf_op jit(solution)/shard_map/ppermute | solution.py:190
  128.1 5.3 %collective-permute-start.4 = (bf16[128,768]{1,0:T(8,128)(2,1)S(1)}, bf16[128,768]{1,0:T(8,128)(2,1)S(1)}, u32[]{:S(2)}, u32[]{:S(2)}) collective-permute-start(bf16[128,768]{1,0:T(8,128)(2,1)S(1)} %shard_map.56.refs_0_), channel_id=1, source_target_pairs={{0,3},{1,2},{2,1},{3,0},{4,7},{5,6},{6,5},{7,4},{8,11},{9,10},{10,... | collective-permute-start | bytes 589832 | tf_op jit(solution)/shard_map/ppermute | solution.py:190
  133.5 0.3 collective-permute-done.2.refs_1_
  133.8 10.4 %collective-permute-done.3.refs_2_ = bf16[128,768]{1,0:T(8,128)(2,1)S(1)} collective-permute-done((bf16[128,768]{1,0:T(8,128)(2,1)S(1)}, bf16[128,768]{1,0:T(8,128)(2,1)S(1)}, u32[]{:S(2)}, u32[]{:S(2)}) %collective-permute-start.3) | collective-permute-done | bytes 196640 | tf_op jit(solution)/shard_map/ppermute | solution.py:190
  144.2 0.0 collective-permute-done.4.refs_3_
  144.2 0.0 all-gather.3.cloned.1.call-done
  144.2 4.2 %shard_map.58 = bf16[128,768]{1,0:T(8,128)(2,1)S(1)} custom-call(s32[4]{0:T(128)S(1)} %iota_xor_fusion.order_ref, bf16[128,768]{1,0:T(8,128)(2,1)S(1)} %shard_map.56.refs_0_, bf16[128,768]{1,0:T(8,128)(2,1)S(1)} %collective-permute-done.2.refs_1_, bf16[128,768]{1,0:T(8,128)(2,1)S(1)} %collective-permute-done.3.refs_2_, ...), custom_call_target="tpu_custom_call" | custom-call | flops 603979776 | bytes 5505024 | tf_op jit(solution)/shard_map/pallas_call | solution.py:48
  148.4 9.1 %collective-permute-start.6 = (bf16[128,768]{1,0:T(8,128)(2,1)S(1)}, bf16[128,768]{1,0:T(8,128)(2,1)S(1)}, u32[]{:S(2)}, u32[]{:S(2)}) collective-permute-start(bf16[128,768]{1,0:T(8,128)(2,1)S(1)} %shard_map.58), channel_id=1, source_target_pairs={{0,4},{4,0},{1,5},{5,1},{2,6},{6,2},{3,7},{7,3},{8,12},{12,8},{9,1... | collective-permute-start | bytes 589832 | tf_op jit(solution)/shard_map/ppermute | solution.py:194
  157.5 4.2 %shard_map.57 = f32[128,768]{1,0:T(8,128)S(1)} custom-call(s32[4]{0:T(128)S(1)} %iota_xor_fusion.order_ref, bf16[128,768]{1,0:T(8,128)(2,1)S(1)} %shard_map.56.refs_0_, bf16[128,768]{1,0:T(8,128)(2,1)S(1)} %collective-permute-done.2.refs_1_, bf16[128,768]{1,0:T(8,128)(2,1)S(1)} %collective-permute-done.3.refs_2_, ...), custom_call_target="tpu_custom_call" | custom-call | flops 603979776 | bytes 5505024 | tf_op jit(solution)/shard_map/pallas_call | solution.py:48
  161.7 12.9 %collective-permute-done.6 = bf16[128,768]{1,0:T(8,128)(2,1)S(1)} collective-permute-done((bf16[128,768]{1,0:T(8,128)(2,1)S(1)}, bf16[128,768]{1,0:T(8,128)(2,1)S(1)}, u32[]{:S(2)}, u32[]{:S(2)}) %collective-permute-start.6) | collective-permute-done | bytes 196640 | tf_op jit(solution)/shard_map/ppermute | solution.py:194
  174.6 0.7 add_convert_fusion
  (3 shorter events, 0.0 us)
Async XLA Ops:
  8.3 21.7 %all-to-all-start = ((bf16[32,16,384]{2,1,0:T(8,128)(2,1)}), bf16[32,16,384]{2,1,0:T(8,128)(2,1)S(1)}, u32[]{:S(2)}, u32[]{:S(2)}) async-start(bf16[32,16,384]{2,1,0:T(8,128)(2,1)} %bitcast), calls=%async_computation | async-start | bytes 786432 | tf_op jit(solution)/shard_map/all_to_all | solution.py:166
  17.9 126.3 %all-gather.3.cloned.1.call-start = ((), (), s32[]{:S(2)}) async-start(), calls=%async_computation.2 | async-start | bytes 9732096 | tf_op jit(solution)/shard_map/all_gather | solution.py:175
  18.0 12.1 %collective-permute-start = (bf16[96,768]{1,0:T(8,128)(2,1)}, bf16[96,768]{1,0:T(8,128)(2,1)S(1)}, u32[]{:S(2)}, u32[]{:S(2)}) collective-permute-start(bf16[96,768]{1,0:T(8,128)(2,1)} %bitcast.21), channel_id=1, source_target_pairs={{0,0},{1,64},{2,128},{3,192},{64,1},{65,65},{66,129},{67,193},{128... | collective-permute-start | bytes 442376 | tf_op jit(solution)/shard_map/ppermute | solution.py:158
  30.1 24.3 %collective-permute-start.5 = (bf16[96,768]{1,0:T(8,128)(2,1)S(1)}, bf16[96,768]{1,0:T(8,128)(2,1)S(1)}, u32[]{:S(2)}, u32[]{:S(2)}) collective-permute-start(bf16[96,768]{1,0:T(8,128)(2,1)S(1)} %collective-permute-done), channel_id=1, source_target_pairs={{0,256},{256,0},{1,257},{257,1},{2,258},{258,2},{3,259},{259,3},{4... | collective-permute-start | bytes 442376 | tf_op jit(solution)/shard_map/ppermute | solution.py:169
  55.1 26.5 %collective-permute-start.1 = (bf16[32,16,384]{2,1,0:T(8,128)(2,1)S(1)}, bf16[32,16,384]{2,1,0:T(8,128)(2,1)S(1)}, u32[]{:S(2)}, u32[]{:S(2)}) collective-permute-start(bf16[32,16,384]{2,1,0:T(8,128)(2,1)S(1)} %all-to-all-done), channel_id=1, source_target_pairs={{0,256},{256,0},{1,257},{257,1},{2,258},{258,2},{3,259},{259,3},{4... | collective-permute-start | bytes 1179656 | tf_op jit(solution)/shard_map/ppermute | solution.py:170
  123.3 10.5 %collective-permute-start.2 = (bf16[128,768]{1,0:T(8,128)(2,1)S(1)}, bf16[128,768]{1,0:T(8,128)(2,1)S(1)}, u32[]{:S(2)}, u32[]{:S(2)}) collective-permute-start(bf16[128,768]{1,0:T(8,128)(2,1)S(1)} %shard_map.56.refs_0_), channel_id=1, source_target_pairs={{0,1},{1,0},{2,3},{3,2},{4,5},{5,4},{6,7},{7,6},{8,9},{9,8},{10,11... | collective-permute-start | bytes 589832 | tf_op jit(solution)/shard_map/ppermute | solution.py:190
  125.3 19.0 %collective-permute-start.3 = (bf16[128,768]{1,0:T(8,128)(2,1)S(1)}, bf16[128,768]{1,0:T(8,128)(2,1)S(1)}, u32[]{:S(2)}, u32[]{:S(2)}) collective-permute-start(bf16[128,768]{1,0:T(8,128)(2,1)S(1)} %shard_map.56.refs_0_), channel_id=1, source_target_pairs={{0,2},{1,3},{2,0},{3,1},{4,6},{5,7},{6,4},{7,5},{8,10},{9,11},{10,... | collective-permute-start | bytes 589832 | tf_op jit(solution)/shard_map/ppermute | solution.py:190
  128.1 16.1 %collective-permute-start.4 = (bf16[128,768]{1,0:T(8,128)(2,1)S(1)}, bf16[128,768]{1,0:T(8,128)(2,1)S(1)}, u32[]{:S(2)}, u32[]{:S(2)}) collective-permute-start(bf16[128,768]{1,0:T(8,128)(2,1)S(1)} %shard_map.56.refs_0_), channel_id=1, source_target_pairs={{0,3},{1,2},{2,1},{3,0},{4,7},{5,6},{6,5},{7,4},{8,11},{9,10},{10,... | collective-permute-start | bytes 589832 | tf_op jit(solution)/shard_map/ppermute | solution.py:190
  148.4 26.2 %collective-permute-start.6 = (bf16[128,768]{1,0:T(8,128)(2,1)S(1)}, bf16[128,768]{1,0:T(8,128)(2,1)S(1)}, u32[]{:S(2)}, u32[]{:S(2)}) collective-permute-start(bf16[128,768]{1,0:T(8,128)(2,1)S(1)} %shard_map.58), channel_id=1, source_target_pairs={{0,4},{4,0},{1,5},{5,1},{2,6},{6,2},{3,7},{7,3},{8,12},{12,8},{9,1... | collective-permute-start | bytes 589832 | tf_op jit(solution)/shard_map/ppermute | solution.py:194
Sparse Core Ops, SparseCore 0:
  55.3 81.1 all-gather.2

commit v18 on v17

--- a/solution.py
+++ b/solution.py
@@ -20,11 +20,13 @@
 PIECE = 16
 
 
-def project_kernel(order_ref, *refs, side):
+def project_kernel(order_ref, *refs, side, first):
     parts, (w_ref, out_ref, held, arrivals) = refs[:QUAD], refs[QUAD:]
     width = w_ref.shape[-1]
     copies = [
-        pltpu.make_async_copy(w_ref.at[order_ref[k], :, side], held.at[k], arrivals.at[k])
+        pltpu.make_async_copy(
+            w_ref.at[order_ref[k], pl.ds(first, held.shape[1]), side], held.at[k], arrivals.at[k]
+        )
         for k in range(QUAD)
     ]
     for copy in copies:
@@ -41,12 +43,13 @@
     out_ref[...] = total.astype(out_ref.dtype)
 
 
-def project(order, parts, w_all, side, dtype):
+def project(order, parts, w_all, side, dtype, first=0, chunks=None):
     tokens, width = parts[0].shape
-    _, chunks, _, columns, _ = w_all.shape
+    columns = w_all.shape[3]
+    chunks = chunks or w_all.shape[1]
     in_vmem = pl.BlockSpec(memory_space=pltpu.VMEM)
     return pl.pallas_call(
-        functools.partial(project_kernel, side=side),
+        functools.partial(project_kernel, side=side, first=first),
         in_specs=[pl.BlockSpec(memory_space=pltpu.SMEM)]
         + [in_vmem] * QUAD
         + [pl.BlockSpec(memory_space=pltpu.HBM)],
@@ -186,12 +189,19 @@
         block, routed.reshape(2 * HALVES, tokens // PIECE, ROUNDS, PIECE, part)
     )
 
+    steps = (0, 2, 3, 1)
     parts = [attended] + [
-        lax.ppermute(attended, "q", [(i, i ^ k) for i in range(QUAD)]) for k in range(1, QUAD)
-    ]
-    order = member ^ jnp.arange(QUAD, dtype=jnp.int32)
-    sent = project(order, parts, w_all, 1, jnp.bfloat16)
-    arrived = lax.ppermute(sent, "p", SWAP)
+        lax.ppermute(attended, "q", [(i, i ^ k) for i in range(QUAD)]) for k in steps[1:]
+    ]
+    order = member ^ jnp.array(steps, jnp.int32)
+    chunks = w_all.shape[1] // 2
+    arrived = [
+        lax.ppermute(
+            project(order, parts, w_all, 1, jnp.bfloat16, h * chunks, chunks), "p", SWAP
+        )
+        for h in range(2)
+    ]
+    arrived = jnp.concatenate(arrived, 1)
     kept = project(order, parts, w_all, 0, jnp.float32)
     return (kept + arrived.astype(jnp.float32)).astype(jnp.bfloat16)
 

time: 184 us -> 186 us (1.011)
  blocking collectives: 39 us -> 0 us
  starting transfers between devices: 59.9 us -> 80.8 us
  waiting for transfers between devices: 53.3 us -> 69.6 us
    all_to_all x1 -> x0, blocking collectives: 39 us -> none  [body(): lax.all_to_all(chosen, PLANE, split_axis=0, concat_axis=0, tiled=True)]
    all_to_all x0 -> x1, starting transfers between devices: none -> 21.1 us  [body(): lax.all_to_all(chosen, PLANE, split_axis=0, concat_axis=0, tiled=True)]
    all_to_all x0 -> x1, waiting for transfers between devices: none -> 19.2 us  [body(): lax.all_to_all(chosen, PLANE, split_axis=0, concat_axis=0, tiled=True)]
    ppermute x1 -> x2, waiting for transfers between devices: 12.9 us -> 9.67 us  [body(): lax.ppermute(project(order, parts, w_all, 1, jnp.bfloat16, h * chunks, ch...]
    pallas_call x2 -> x3, Pallas kernels: 8.38 us -> 9.95 us  [project(): pl.pallas_call(functools.partial(project_kernel, side=side, first=first),...]
    ppermute x1 -> x2, starting transfers between devices: 9.07 us -> 9.75 us  [body(): lax.ppermute(project(order, parts, w_all, 1, jnp.bfloat16, h * chunks, ch...]
  transfers between devices with their start and end apart: 9 -> 11, of which waited for: 6 -> 7; matrix products, arithmetic and copies ran while one was open for 2% -> 2% of each run, Pallas kernels for 3% -> 5%
where the time goes in v18:
time: 186 us; the launch traced here: 183 us
  starting transfers between devices  80.8 us (43%)
  waiting for transfers between devices  69.6 us (37%)
  Pallas kernels  13.7 us (7%)
  between operations  13.6 us (7%)
  other arithmetic  3.56 us (2%)
    all_to_all x1, starting transfers between devices, body(): lax.all_to_all(chosen, PLANE, split_axis=0, concat_axis=0, tiled=True)  21.1 us
    all_to_all x1, waiting for transfers between devices, body(): lax.all_to_all(chosen, PLANE, split_axis=0, concat_axis=0, tiled=True)  19.2 us
    ppermute x1, starting transfers between devices, body(): w_far = lax.ppermute(w_near, 'zh', SWAP)  13.8 us
    ppermute x1, starting transfers between devices, body(): far = lax.ppermute(spread, 'zh', SWAP)  13.1 us
    ppermute x1, waiting for transfers between devices, body(): far = lax.ppermute(spread, 'zh', SWAP)  11.2 us
    ppermute x3, waiting for transfers between devices, body(): lax.ppermute(attended, 'q', [(i, i ^ k) for i in range(QUAD)])  11.1 us
    ppermute x1, waiting for transfers between devices, body(): w_far = lax.ppermute(w_near, 'zh', SWAP)  10.5 us
    pallas_call x3, Pallas kernels, project(): pl.pallas_call(functools.partial(project_kernel, side=side, first=first),...  9.95 us
  transfers between devices with their start and end apart: 11, of which 7 were waited for; matrix products, arithmetic and copies ran while one was open for 2% of the time, Pallas kernels for 5%

profile of v18, /device:TPU:6, one launch (start us, length us, event | category | flops | bytes accessed | tf_op | source)
XLA Modules:
  0.0 183.0 jit_solution(11929127496577084284)
XLA Ops:
  6.5 0.0 copy-start
  6.5 1.8 %shard_map.64 = bf16[4,128,384]{2,1,0:T(8,128)(2,1)} custom-call(bf16[128,768]{1,0:T(8,128)(2,1)} %keys_ref.1, bf16[128,768]{1,0:T(8,128)(2,1)} %values_ref.1), custom_call_target="tpu_custom_call" | custom-call | bytes 786432 | tf_op jit(solution)/shard_map/pallas_call | solution.py:90
  8.4 9.6 %all-to-all-start = ((bf16[32,16,384]{2,1,0:T(8,128)(2,1)}), bf16[32,16,384]{2,1,0:T(8,128)(2,1)S(1)}, u32[]{:S(2)}, u32[]{:S(2)}) async-start(bf16[32,16,384]{2,1,0:T(8,128)(2,1)} %bitcast), calls=%async_computation | async-start | bytes 786432 | tf_op jit(solution)/shard_map/all_to_all | solution.py:169
  17.9 0.0 all-gather.3.cloned.1.call-start
  18.0 4.2 %collective-permute-start = (bf16[96,768]{1,0:T(8,128)(2,1)}, bf16[96,768]{1,0:T(8,128)(2,1)S(1)}, u32[]{:S(2)}, u32[]{:S(2)}) collective-permute-start(bf16[96,768]{1,0:T(8,128)(2,1)} %bitcast.21), channel_id=1, source_target_pairs={{0,0},{1,64},{2,128},{3,192},{64,1},{65,65},{66,129},{67,193},{128... | collective-permute-start | bytes 442376 | tf_op jit(solution)/shard_map/ppermute | solution.py:161
  22.2 7.9 %collective-permute-done = bf16[96,768]{1,0:T(8,128)(2,1)S(1)} collective-permute-done((bf16[96,768]{1,0:T(8,128)(2,1)}, bf16[96,768]{1,0:T(8,128)(2,1)S(1)}, u32[]{:S(2)}, u32[]{:S(2)}) %collective-permute-start) | collective-permute-done | bytes 147488 | tf_op jit(solution)/shard_map/ppermute | solution.py:161
  30.1 0.0 all-to-all-done
  30.1 13.8 %collective-permute-start.5 = (bf16[96,768]{1,0:T(8,128)(2,1)S(1)}, bf16[96,768]{1,0:T(8,128)(2,1)S(1)}, u32[]{:S(2)}, u32[]{:S(2)}) collective-permute-start(bf16[96,768]{1,0:T(8,128)(2,1)S(1)} %collective-permute-done), channel_id=1, source_target_pairs={{0,256},{256,0},{1,257},{257,1},{2,258},{258,2},{3,259},{259,3},{4... | collective-permute-start | bytes 442376 | tf_op jit(solution)/shard_map/ppermute | solution.py:172
  43.9 10.5 %collective-permute-done.5 = bf16[96,768]{1,0:T(8,128)(2,1)S(1)} collective-permute-done((bf16[96,768]{1,0:T(8,128)(2,1)S(1)}, bf16[96,768]{1,0:T(8,128)(2,1)S(1)}, u32[]{:S(2)}, u32[]{:S(2)}) %collective-permute-start.5) | collective-permute-done | bytes 147488 | tf_op jit(solution)/shard_map/ppermute | solution.py:172
  54.4 0.8 pad_maximum_fusion.2
  55.2 0.0 all-gather.3.cloned.1.call-update
  55.2 13.1 %collective-permute-start.1 = (bf16[32,16,384]{2,1,0:T(8,128)(2,1)S(1)}, bf16[32,16,384]{2,1,0:T(8,128)(2,1)S(1)}, u32[]{:S(2)}, u32[]{:S(2)}) collective-permute-start(bf16[32,16,384]{2,1,0:T(8,128)(2,1)S(1)} %all-to-all-done), channel_id=1, source_target_pairs={{0,256},{256,0},{1,257},{257,1},{2,258},{258,2},{3,259},{259,3},{4... | collective-permute-start | bytes 1179656 | tf_op jit(solution)/shard_map/ppermute | solution.py:173
  68.3 0.8 compare_select_fusion
  69.1 0.1 copy.9
  69.2 0.1 reshape.14
  69.3 1.2 pad_maximum_fusion.1.own_ref
  70.5 11.2 %collective-permute-done.1 = bf16[32,16,384]{2,1,0:T(8,128)(2,1)S(1)} collective-permute-done((bf16[32,16,384]{2,1,0:T(8,128)(2,1)S(1)}, bf16[32,16,384]{2,1,0:T(8,128)(2,1)S(1)}, u32[]{:S(2)}, u32[]{:S(2)}) %collective-permute-start.1) | collective-permute-done | bytes 393248 | tf_op jit(solution)/shard_map/ppermute | solution.py:173
  81.7 0.1 pad_maximum_fusion
  81.8 1.6 gather_fusion
  83.4 21.1 %all-to-all-start.1 = ((bf16[32,2,16,384]{3,2,1,0:T(8,128)(2,1)}), bf16[32,2,16,384]{3,2,1,0:T(8,128)(2,1)S(1)}, u32[]{:S(2)}, u32[]{:S(2)}) async-start(bf16[32,2,16,384]{3,2,1,0:T(8,128)(2,1)} %bitcast.6), calls=%async_computation.1 | async-start | bytes 1572864 | tf_op jit(solution)/shard_map/all_to_all | solution.py:187
  104.5 19.2 %all-to-all-done.1 = bf16[32,2,16,384]{3,2,1,0:T(8,128)(2,1)S(1)} async-done(((bf16[32,2,16,384]{3,2,1,0:T(8,128)(2,1)}), bf16[32,2,16,384]{3,2,1,0:T(8,128)(2,1)S(1)}, u32[]{:S(2)}, u32[]{:S(2)}) %all-to-all-start.1) | async-done | bytes 786464 | tf_op jit(solution)/shard_map/all_to_all | solution.py:187
  123.7 1.9 %shard_map.65.refs_0_ = bf16[128,768]{1,0:T(8,128)(2,1)S(1)} custom-call(bf16[3,128,768]{2,1,0:T(8,128)(2,1)S(1)} %pad_maximum_fusion.1.own_ref, bf16[4,8,2,16,384]{4,3,2,1,0:T(8,128)(2,1)S(1)} %bitcast.14), custom_call_target="tpu_custom_call" | custom-call | flops 150994944 | bytes 1572864 | tf_op jit(solution)/shard_map/pallas_call | solution.py:141
  125.6 1.9 %collective-permute-start.2 = (bf16[128,768]{1,0:T(8,128)(2,1)S(1)}, bf16[128,768]{1,0:T(8,128)(2,1)S(1)}, u32[]{:S(2)}, u32[]{:S(2)}) collective-permute-start(bf16[128,768]{1,0:T(8,128)(2,1)S(1)} %shard_map.65.refs_0_), channel_id=1, source_target_pairs={{0,2},{1,3},{2,0},{3,1},{4,6},{5,7},{6,4},{7,5},{8,10},{9,11},{10,... | collective-permute-start | bytes 589832 | tf_op jit(solution)/shard_map/ppermute | solution.py:194
  127.5 2.1 %collective-permute-start.3 = (bf16[128,768]{1,0:T(8,128)(2,1)S(1)}, bf16[128,768]{1,0:T(8,128)(2,1)S(1)}, u32[]{:S(2)}, u32[]{:S(2)}) collective-permute-start(bf16[128,768]{1,0:T(8,128)(2,1)S(1)} %shard_map.65.refs_0_), channel_id=1, source_target_pairs={{0,3},{1,2},{2,1},{3,0},{4,7},{5,6},{6,5},{7,4},{8,11},{9,10},{10,... | collective-permute-start | bytes 589832 | tf_op jit(solution)/shard_map/ppermute | solution.py:194
  129.7 5.2 %collective-permute-start.4 = (bf16[128,768]{1,0:T(8,128)(2,1)S(1)}, bf16[128,768]{1,0:T(8,128)(2,1)S(1)}, u32[]{:S(2)}, u32[]{:S(2)}) collective-permute-start(bf16[128,768]{1,0:T(8,128)(2,1)S(1)} %shard_map.65.refs_0_), channel_id=1, source_target_pairs={{0,1},{1,0},{2,3},{3,2},{4,5},{5,4},{6,7},{7,6},{8,9},{9,8},{10,11... | collective-permute-start | bytes 589832 | tf_op jit(solution)/shard_map/ppermute | solution.py:194
  134.9 0.0 copy-done
  134.9 7.0 %collective-permute-done.2.refs_1_ = bf16[128,768]{1,0:T(8,128)(2,1)S(1)} collective-permute-done((bf16[128,768]{1,0:T(8,128)(2,1)S(1)}, bf16[128,768]{1,0:T(8,128)(2,1)S(1)}, u32[]{:S(2)}, u32[]{:S(2)}) %collective-permute-start.2) | collective-permute-done | bytes 196640 | tf_op jit(solution)/shard_map/ppermute | solution.py:194
  141.9 0.0 collective-permute-done.3.refs_2_
  141.9 4.1 %collective-permute-done.4.refs_3_ = bf16[128,768]{1,0:T(8,128)(2,1)S(1)} collective-permute-done((bf16[128,768]{1,0:T(8,128)(2,1)S(1)}, bf16[128,768]{1,0:T(8,128)(2,1)S(1)}, u32[]{:S(2)}, u32[]{:S(2)}) %collective-permute-start.4) | collective-permute-done | bytes 196640 | tf_op jit(solution)/shard_map/ppermute | solution.py:194
  146.0 0.0 all-gather.3.cloned.1.call-done
  146.0 2.9 %shard_map.67 = bf16[128,384]{1,0:T(8,128)(2,1)S(1)} custom-call(s32[4]{0:T(128)S(1)} %broadcast_xor_fusion.order_ref, bf16[128,768]{1,0:T(8,128)(2,1)S(1)} %shard_map.65.refs_0_, bf16[128,768]{1,0:T(8,128)(2,1)S(1)} %collective-permute-done.2.refs_1_, bf16[128,768]{1,0:T(8,128)(2,1)S(1)} %collective-permute-done.3.refs_2_, ...), custom_call_target="tpu_custom_call" | custom-call | flops 301989888 | bytes 3145728 | tf_op jit(solution)/shard_map/pallas_call | solution.py:51
  148.9 7.1 %collective-permute-start.6 = (bf16[128,384]{1,0:T(8,128)(2,1)S(1)}, bf16[128,384]{1,0:T(8,128)(2,1)S(1)}, u32[]{:S(2)}, u32[]{:S(2)}) collective-permute-start(bf16[128,384]{1,0:T(8,128)(2,1)S(1)} %shard_map.67), channel_id=1, source_target_pairs={{0,4},{4,0},{1,5},{5,1},{2,6},{6,2},{3,7},{7,3},{8,12},{12,8},{9,1... | collective-permute-start | bytes 294920 | tf_op jit(solution)/shard_map/ppermute | solution.py:199
  156.0 2.9 %shard_map.68 = bf16[128,384]{1,0:T(8,128)(2,1)S(1)} custom-call(s32[4]{0:T(128)S(1)} %broadcast_xor_fusion.order_ref, bf16[128,768]{1,0:T(8,128)(2,1)S(1)} %shard_map.65.refs_0_, bf16[128,768]{1,0:T(8,128)(2,1)S(1)} %collective-permute-done.2.refs_1_, bf16[128,768]{1,0:T(8,128)(2,1)S(1)} %collective-permute-done.3.refs_2_, ...), custom_call_target="tpu_custom_call" | custom-call | flops 301989888 | bytes 3145728 | tf_op jit(solution)/shard_map/pallas_call | solution.py:51
  158.9 2.6 %collective-permute-start.7 = (bf16[128,384]{1,0:T(8,128)(2,1)S(1)}, bf16[128,384]{1,0:T(8,128)(2,1)S(1)}, u32[]{:S(2)}, u32[]{:S(2)}) collective-permute-start(bf16[128,384]{1,0:T(8,128)(2,1)S(1)} %shard_map.68), channel_id=1, source_target_pairs={{0,4},{4,0},{1,5},{5,1},{2,6},{6,2},{3,7},{7,3},{8,12},{12,8},{9,1... | collective-permute-start | bytes 294920 | tf_op jit(solution)/shard_map/ppermute | solution.py:199
  161.5 4.2 %shard_map.66 = f32[128,768]{1,0:T(8,128)S(1)} custom-call(s32[4]{0:T(128)S(1)} %broadcast_xor_fusion.order_ref, bf16[128,768]{1,0:T(8,128)(2,1)S(1)} %shard_map.65.refs_0_, bf16[128,768]{1,0:T(8,128)(2,1)S(1)} %collective-permute-done.2.refs_1_, bf16[128,768]{1,0:T(8,128)(2,1)S(1)} %collective-permute-done.3.refs_2_, ...), custom_call_target="tpu_custom_call" | custom-call | flops 603979776 | bytes 5505024 | tf_op jit(solution)/shard_map/pallas_call | solution.py:51
  165.7 0.0 collective-permute-done.6
  165.8 9.7 %collective-permute-done.7 = bf16[128,384]{1,0:T(8,128)(2,1)S(1)} collective-permute-done((bf16[128,384]{1,0:T(8,128)(2,1)S(1)}, bf16[128,384]{1,0:T(8,128)(2,1)S(1)}, u32[]{:S(2)}, u32[]{:S(2)}) %collective-permute-start.7) | collective-permute-done | bytes 98336 | tf_op jit(solution)/shard_map/ppermute | solution.py:199
  175.4 0.7 add_convert_fusion
  (3 shorter events, 0.0 us)
Async XLA Ops:
  6.5 128.3 %copy-start = (s32[4]{0:T(128)S(1)}, s32[4]{0:T(128)}, u32[]{:S(2)}) copy-start(s32[4]{0:T(128)} %constant.49.clone) | copy-start | bytes 52
  8.4 21.7 %all-to-all-start = ((bf16[32,16,384]{2,1,0:T(8,128)(2,1)}), bf16[32,16,384]{2,1,0:T(8,128)(2,1)S(1)}, u32[]{:S(2)}, u32[]{:S(2)}) async-start(bf16[32,16,384]{2,1,0:T(8,128)(2,1)} %bitcast), calls=%async_computation | async-start | bytes 786432 | tf_op jit(solution)/shard_map/all_to_all | solution.py:169
  17.9 128.1 %all-gather.3.cloned.1.call-start = ((), (), s32[]{:S(2)}) async-start(), calls=%async_computation.2 | async-start | bytes 9732096 | tf_op jit(solution)/shard_map/all_gather | solution.py:178
  18.0 12.1 %collective-permute-start = (bf16[96,768]{1,0:T(8,128)(2,1)}, bf16[96,768]{1,0:T(8,128)(2,1)S(1)}, u32[]{:S(2)}, u32[]{:S(2)}) collective-permute-start(bf16[96,768]{1,0:T(8,128)(2,1)} %bitcast.21), channel_id=1, source_target_pairs={{0,0},{1,64},{2,128},{3,192},{64,1},{65,65},{66,129},{67,193},{128... | collective-permute-start | bytes 442376 | tf_op jit(solution)/shard_map/ppermute | solution.py:161
  30.1 24.3 %collective-permute-start.5 = (bf16[96,768]{1,0:T(8,128)(2,1)S(1)}, bf16[96,768]{1,0:T(8,128)(2,1)S(1)}, u32[]{:S(2)}, u32[]{:S(2)}) collective-permute-start(bf16[96,768]{1,0:T(8,128)(2,1)S(1)} %collective-permute-done), channel_id=1, source_target_pairs={{0,256},{256,0},{1,257},{257,1},{2,258},{258,2},{3,259},{259,3},{4... | collective-permute-start | bytes 442376 | tf_op jit(solution)/shard_map/ppermute | solution.py:172
  55.2 26.5 %collective-permute-start.1 = (bf16[32,16,384]{2,1,0:T(8,128)(2,1)S(1)}, bf16[32,16,384]{2,1,0:T(8,128)(2,1)S(1)}, u32[]{:S(2)}, u32[]{:S(2)}) collective-permute-start(bf16[32,16,384]{2,1,0:T(8,128)(2,1)S(1)} %all-to-all-done), channel_id=1, source_target_pairs={{0,256},{256,0},{1,257},{257,1},{2,258},{258,2},{3,259},{259,3},{4... | collective-permute-start | bytes 1179656 | tf_op jit(solution)/shard_map/ppermute | solution.py:173
  83.4 40.4 %all-to-all-start.1 = ((bf16[32,2,16,384]{3,2,1,0:T(8,128)(2,1)}), bf16[32,2,16,384]{3,2,1,0:T(8,128)(2,1)S(1)}, u32[]{:S(2)}, u32[]{:S(2)}) async-start(bf16[32,2,16,384]{3,2,1,0:T(8,128)(2,1)} %bitcast.6), calls=%async_computation.1 | async-start | bytes 1572864 | tf_op jit(solution)/shard_map/all_to_all | solution.py:187
  125.6 16.3 %collective-permute-start.2 = (bf16[128,768]{1,0:T(8,128)(2,1)S(1)}, bf16[128,768]{1,0:T(8,128)(2,1)S(1)}, u32[]{:S(2)}, u32[]{:S(2)}) collective-permute-start(bf16[128,768]{1,0:T(8,128)(2,1)S(1)} %shard_map.65.refs_0_), channel_id=1, source_target_pairs={{0,2},{1,3},{2,0},{3,1},{4,6},{5,7},{6,4},{7,5},{8,10},{9,11},{10,... | collective-permute-start | bytes 589832 | tf_op jit(solution)/shard_map/ppermute | solution.py:194
  127.5 14.3 %collective-permute-start.3 = (bf16[128,768]{1,0:T(8,128)(2,1)S(1)}, bf16[128,768]{1,0:T(8,128)(2,1)S(1)}, u32[]{:S(2)}, u32[]{:S(2)}) collective-permute-start(bf16[128,768]{1,0:T(8,128)(2,1)S(1)} %shard_map.65.refs_0_), channel_id=1, source_target_pairs={{0,3},{1,2},{2,1},{3,0},{4,7},{5,6},{6,5},{7,4},{8,11},{9,10},{10,... | collective-permute-start | bytes 589832 | tf_op jit(solution)/shard_map/ppermute | solution.py:194
  129.7 16.3 %collective-permute-start.4 = (bf16[128,768]{1,0:T(8,128)(2,1)S(1)}, bf16[128,768]{1,0:T(8,128)(2,1)S(1)}, u32[]{:S(2)}, u32[]{:S(2)}) collective-permute-start(bf16[128,768]{1,0:T(8,128)(2,1)S(1)} %shard_map.65.refs_0_), channel_id=1, source_target_pairs={{0,1},{1,0},{2,3},{3,2},{4,5},{5,4},{6,7},{7,6},{8,9},{9,8},{10,11... | collective-permute-start | bytes 589832 | tf_op jit(solution)/shard_map/ppermute | solution.py:194
  148.9 16.9 %collective-permute-start.6 = (bf16[128,384]{1,0:T(8,128)(2,1)S(1)}, bf16[128,384]{1,0:T(8,128)(2,1)S(1)}, u32[]{:S(2)}, u32[]{:S(2)}) collective-permute-start(bf16[128,384]{1,0:T(8,128)(2,1)S(1)} %shard_map.67), channel_id=1, source_target_pairs={{0,4},{4,0},{1,5},{5,1},{2,6},{6,2},{3,7},{7,3},{8,12},{12,8},{9,1... | collective-permute-start | bytes 294920 | tf_op jit(solution)/shard_map/ppermute | solution.py:199
  158.9 16.5 %collective-permute-start.7 = (bf16[128,384]{1,0:T(8,128)(2,1)S(1)}, bf16[128,384]{1,0:T(8,128)(2,1)S(1)}, u32[]{:S(2)}, u32[]{:S(2)}) collective-permute-start(bf16[128,384]{1,0:T(8,128)(2,1)S(1)} %shard_map.68), channel_id=1, source_target_pairs={{0,4},{4,0},{1,5},{5,1},{2,6},{6,2},{3,7},{7,3},{8,12},{12,8},{9,1... | collective-permute-start | bytes 294920 | tf_op jit(solution)/shard_map/ppermute | solution.py:199
Sparse Core Ops, SparseCore 0:
  55.3 82.2 all-gather.2

commit v19 on v17

--- a/solution.py
+++ b/solution.py
@@ -27,11 +27,13 @@
         pltpu.make_async_copy(w_ref.at[order_ref[k], :, side], held.at[k], arrivals.at[k])
         for k in range(QUAD)
     ]
-    for copy in copies:
-        copy.start()
+    copies[0].start()
+    copies[1].start()
     total = 0.0
     for k in range(QUAD):
         copies[k].wait()
+        if k + 2 < QUAD:
+            copies[k + 2].start()
         total += lax.dot_general(
             parts[k][...],
             held[k].reshape(-1, width),

time: 184 us -> 184 us (level)
  no operation moved by 1% of the time
where the time goes in v19:
time: 184 us; the launch traced here: 182 us
  starting transfers between devices  59.9 us (33%)
  waiting for transfers between devices  53.2 us (29%)
  blocking collectives  39 us (21%)
  between operations  13.5 us (7%)
  Pallas kernels  12.3 us (7%)
  other arithmetic  3.54 us (2%)
    all_to_all x1, blocking collectives, body(): lax.all_to_all(chosen, PLANE, split_axis=0, concat_axis=0, tiled=True)  39 us
    ppermute x1, starting transfers between devices, body(): w_far = lax.ppermute(w_near, 'zh', SWAP)  13.8 us
    ppermute x1, starting transfers between devices, body(): far = lax.ppermute(spread, 'zh', SWAP)  13.1 us
    ppermute x1, waiting for transfers between devices, body(): arrived = lax.ppermute(sent, 'p', SWAP)  12.8 us
    ppermute x1, waiting for transfers between devices, body(): far = lax.ppermute(spread, 'zh', SWAP)  11.3 us
    ppermute x3, waiting for transfers between devices, body(): lax.ppermute(attended, 'q', [(i, i ^ k) for i in range(QUAD)])  10.7 us
    ppermute x1, waiting for transfers between devices, body(): w_far = lax.ppermute(w_near, 'zh', SWAP)  10.5 us
    ppermute x3, starting transfers between devices, body(): lax.ppermute(attended, 'q', [(i, i ^ k) for i in range(QUAD)])  10.1 us
  transfers between devices with their start and end apart: 9, of which 6 were waited for; matrix products, arithmetic and copies ran while one was open for 2% of the time, Pallas kernels for 3%

profile of v19, /device:TPU:6, one launch (start us, length us, event | category | flops | bytes accessed | tf_op | source)
XLA Modules:
  0.0 182.3 jit_solution(15536384451640128469)
XLA Ops:
  6.5 1.8 shard_map.55
  8.3 9.6 %all-to-all-start = ((bf16[32,16,384]{2,1,0:T(8,128)(2,1)}), bf16[32,16,384]{2,1,0:T(8,128)(2,1)S(1)}, u32[]{:S(2)}, u32[]{:S(2)}) async-start(bf16[32,16,384]{2,1,0:T(8,128)(2,1)} %bitcast), calls=%async_computation | async-start | bytes 786432 | tf_op jit(solution)/shard_map/all_to_all | solution.py:168
  17.9 0.0 all-gather.3.cloned.1.call-start
  18.0 4.2 %collective-permute-start = (bf16[96,768]{1,0:T(8,128)(2,1)}, bf16[96,768]{1,0:T(8,128)(2,1)S(1)}, u32[]{:S(2)}, u32[]{:S(2)}) collective-permute-start(bf16[96,768]{1,0:T(8,128)(2,1)} %bitcast.21), channel_id=1, source_target_pairs={{0,0},{1,64},{2,128},{3,192},{64,1},{65,65},{66,129},{67,193},{128... | collective-permute-start | bytes 442376 | tf_op jit(solution)/shard_map/ppermute | solution.py:160
  22.2 7.9 %collective-permute-done = bf16[96,768]{1,0:T(8,128)(2,1)S(1)} collective-permute-done((bf16[96,768]{1,0:T(8,128)(2,1)}, bf16[96,768]{1,0:T(8,128)(2,1)S(1)}, u32[]{:S(2)}, u32[]{:S(2)}) %collective-permute-start) | collective-permute-done | bytes 147488 | tf_op jit(solution)/shard_map/ppermute | solution.py:160
  30.1 0.0 all-to-all-done
  30.1 13.8 %collective-permute-start.5 = (bf16[96,768]{1,0:T(8,128)(2,1)S(1)}, bf16[96,768]{1,0:T(8,128)(2,1)S(1)}, u32[]{:S(2)}, u32[]{:S(2)}) collective-permute-start(bf16[96,768]{1,0:T(8,128)(2,1)S(1)} %collective-permute-done), channel_id=1, source_target_pairs={{0,256},{256,0},{1,257},{257,1},{2,258},{258,2},{3,259},{259,3},{4... | collective-permute-start | bytes 442376 | tf_op jit(solution)/shard_map/ppermute | solution.py:171
  43.9 10.5 %collective-permute-done.5 = bf16[96,768]{1,0:T(8,128)(2,1)S(1)} collective-permute-done((bf16[96,768]{1,0:T(8,128)(2,1)S(1)}, bf16[96,768]{1,0:T(8,128)(2,1)S(1)}, u32[]{:S(2)}, u32[]{:S(2)}) %collective-permute-start.5) | collective-permute-done | bytes 147488 | tf_op jit(solution)/shard_map/ppermute | solution.py:171
  54.4 0.7 pad_maximum_fusion.2
  55.1 0.0 all-gather.3.cloned.1.call-update
  55.1 13.1 %collective-permute-start.1 = (bf16[32,16,384]{2,1,0:T(8,128)(2,1)S(1)}, bf16[32,16,384]{2,1,0:T(8,128)(2,1)S(1)}, u32[]{:S(2)}, u32[]{:S(2)}) collective-permute-start(bf16[32,16,384]{2,1,0:T(8,128)(2,1)S(1)} %all-to-all-done), channel_id=1, source_target_pairs={{0,256},{256,0},{1,257},{257,1},{2,258},{258,2},{3,259},{259,3},{4... | collective-permute-start | bytes 1179656 | tf_op jit(solution)/shard_map/ppermute | solution.py:172
  68.3 0.8 compare_select_fusion
  69.0 0.1 copy.8
  69.1 0.1 reshape.14
  69.2 1.2 pad_maximum_fusion.1.own_ref
  70.4 11.3 %collective-permute-done.1 = bf16[32,16,384]{2,1,0:T(8,128)(2,1)S(1)} collective-permute-done((bf16[32,16,384]{2,1,0:T(8,128)(2,1)S(1)}, bf16[32,16,384]{2,1,0:T(8,128)(2,1)S(1)}, u32[]{:S(2)}, u32[]{:S(2)}) %collective-permute-start.1) | collective-permute-done | bytes 393248 | tf_op jit(solution)/shard_map/ppermute | solution.py:172
  81.7 0.1 pad_maximum_fusion
  81.8 0.7 gather_fusion
  82.5 39.0 %all_to_all.10 = bf16[32,2,16,384]{3,2,1,0:T(8,128)(2,1)S(1)} all-to-all(bf16[32,2,16,384]{3,2,1,0:T(8,128)(2,1)S(1)} %bitcast.17), channel_id=1, replica_groups=mesh['zh'=2,'x'=4,'y'=4,'c'=2,'p'=2,'q'=4] {'x','y','c'}, dimensions={0} | all-to-all | bytes 1572864 | tf_op jit(solution)/shard_map/all_to_all | solution.py:186
  121.5 1.9 %shard_map.56.refs_0_ = bf16[128,768]{1,0:T(8,128)(2,1)S(1)} custom-call(bf16[3,128,768]{2,1,0:T(8,128)(2,1)S(1)} %pad_maximum_fusion.1.own_ref, bf16[4,8,2,16,384]{4,3,2,1,0:T(8,128)(2,1)S(1)} %bitcast.14), custom_call_target="tpu_custom_call" | custom-call | flops 150994944 | bytes 1572864 | tf_op jit(solution)/shard_map/pallas_call | solution.py:140
  123.3 1.9 %collective-permute-start.2 = (bf16[128,768]{1,0:T(8,128)(2,1)S(1)}, bf16[128,768]{1,0:T(8,128)(2,1)S(1)}, u32[]{:S(2)}, u32[]{:S(2)}) collective-permute-start(bf16[128,768]{1,0:T(8,128)(2,1)S(1)} %shard_map.56.refs_0_), channel_id=1, source_target_pairs={{0,1},{1,0},{2,3},{3,2},{4,5},{5,4},{6,7},{7,6},{8,9},{9,8},{10,11... | collective-permute-start | bytes 589832 | tf_op jit(solution)/shard_map/ppermute | solution.py:192
  125.3 2.8 %collective-permute-start.3 = (bf16[128,768]{1,0:T(8,128)(2,1)S(1)}, bf16[128,768]{1,0:T(8,128)(2,1)S(1)}, u32[]{:S(2)}, u32[]{:S(2)}) collective-permute-start(bf16[128,768]{1,0:T(8,128)(2,1)S(1)} %shard_map.56.refs_0_), channel_id=1, source_target_pairs={{0,2},{1,3},{2,0},{3,1},{4,6},{5,7},{6,4},{7,5},{8,10},{9,11},{10,... | collective-permute-start | bytes 589832 | tf_op jit(solution)/shard_map/ppermute | solution.py:192
  128.1 5.4 %collective-permute-start.4 = (bf16[128,768]{1,0:T(8,128)(2,1)S(1)}, bf16[128,768]{1,0:T(8,128)(2,1)S(1)}, u32[]{:S(2)}, u32[]{:S(2)}) collective-permute-start(bf16[128,768]{1,0:T(8,128)(2,1)S(1)} %shard_map.56.refs_0_), channel_id=1, source_target_pairs={{0,3},{1,2},{2,1},{3,0},{4,7},{5,6},{6,5},{7,4},{8,11},{9,10},{10,... | collective-permute-start | bytes 589832 | tf_op jit(solution)/shard_map/ppermute | solution.py:192
  133.5 0.3 collective-permute-done.2.refs_1_
  133.8 10.4 %collective-permute-done.3.refs_2_ = bf16[128,768]{1,0:T(8,128)(2,1)S(1)} collective-permute-done((bf16[128,768]{1,0:T(8,128)(2,1)S(1)}, bf16[128,768]{1,0:T(8,128)(2,1)S(1)}, u32[]{:S(2)}, u32[]{:S(2)}) %collective-permute-start.3) | collective-permute-done | bytes 196640 | tf_op jit(solution)/shard_map/ppermute | solution.py:192
  144.2 0.0 collective-permute-done.4.refs_3_
  144.2 0.0 all-gather.3.cloned.1.call-done
  144.2 4.3 %shard_map.58 = bf16[128,768]{1,0:T(8,128)(2,1)S(1)} custom-call(s32[4]{0:T(128)S(1)} %iota_xor_fusion.order_ref, bf16[128,768]{1,0:T(8,128)(2,1)S(1)} %shard_map.56.refs_0_, bf16[128,768]{1,0:T(8,128)(2,1)S(1)} %collective-permute-done.2.refs_1_, bf16[128,768]{1,0:T(8,128)(2,1)S(1)} %collective-permute-done.3.refs_2_, ...), custom_call_target="tpu_custom_call" | custom-call | flops 603979776 | bytes 5505024 | tf_op jit(solution)/shard_map/pallas_call | solution.py:50
  148.5 9.1 %collective-permute-start.6 = (bf16[128,768]{1,0:T(8,128)(2,1)S(1)}, bf16[128,768]{1,0:T(8,128)(2,1)S(1)}, u32[]{:S(2)}, u32[]{:S(2)}) collective-permute-start(bf16[128,768]{1,0:T(8,128)(2,1)S(1)} %shard_map.58), channel_id=1, source_target_pairs={{0,4},{4,0},{1,5},{5,1},{2,6},{6,2},{3,7},{7,3},{8,12},{12,8},{9,1... | collective-permute-start | bytes 589832 | tf_op jit(solution)/shard_map/ppermute | solution.py:196
  157.6 4.3 %shard_map.57 = f32[128,768]{1,0:T(8,128)S(1)} custom-call(s32[4]{0:T(128)S(1)} %iota_xor_fusion.order_ref, bf16[128,768]{1,0:T(8,128)(2,1)S(1)} %shard_map.56.refs_0_, bf16[128,768]{1,0:T(8,128)(2,1)S(1)} %collective-permute-done.2.refs_1_, bf16[128,768]{1,0:T(8,128)(2,1)S(1)} %collective-permute-done.3.refs_2_, ...), custom_call_target="tpu_custom_call" | custom-call | flops 603979776 | bytes 5505024 | tf_op jit(solution)/shard_map/pallas_call | solution.py:50
  161.9 12.8 %collective-permute-done.6 = bf16[128,768]{1,0:T(8,128)(2,1)S(1)} collective-permute-done((bf16[128,768]{1,0:T(8,128)(2,1)S(1)}, bf16[128,768]{1,0:T(8,128)(2,1)S(1)}, u32[]{:S(2)}, u32[]{:S(2)}) %collective-permute-start.6) | collective-permute-done | bytes 196640 | tf_op jit(solution)/shard_map/ppermute | solution.py:196
  174.7 0.7 add_convert_fusion
  (3 shorter events, 0.0 us)
Async XLA Ops:
  8.3 21.7 %all-to-all-start = ((bf16[32,16,384]{2,1,0:T(8,128)(2,1)}), bf16[32,16,384]{2,1,0:T(8,128)(2,1)S(1)}, u32[]{:S(2)}, u32[]{:S(2)}) async-start(bf16[32,16,384]{2,1,0:T(8,128)(2,1)} %bitcast), calls=%async_computation | async-start | bytes 786432 | tf_op jit(solution)/shard_map/all_to_all | solution.py:168
  17.9 126.3 %all-gather.3.cloned.1.call-start = ((), (), s32[]{:S(2)}) async-start(), calls=%async_computation.2 | async-start | bytes 9732096 | tf_op jit(solution)/shard_map/all_gather | solution.py:177
  18.0 12.1 %collective-permute-start = (bf16[96,768]{1,0:T(8,128)(2,1)}, bf16[96,768]{1,0:T(8,128)(2,1)S(1)}, u32[]{:S(2)}, u32[]{:S(2)}) collective-permute-start(bf16[96,768]{1,0:T(8,128)(2,1)} %bitcast.21), channel_id=1, source_target_pairs={{0,0},{1,64},{2,128},{3,192},{64,1},{65,65},{66,129},{67,193},{128... | collective-permute-start | bytes 442376 | tf_op jit(solution)/shard_map/ppermute | solution.py:160
  30.1 24.3 %collective-permute-start.5 = (bf16[96,768]{1,0:T(8,128)(2,1)S(1)}, bf16[96,768]{1,0:T(8,128)(2,1)S(1)}, u32[]{:S(2)}, u32[]{:S(2)}) collective-permute-start(bf16[96,768]{1,0:T(8,128)(2,1)S(1)} %collective-permute-done), channel_id=1, source_target_pairs={{0,256},{256,0},{1,257},{257,1},{2,258},{258,2},{3,259},{259,3},{4... | collective-permute-start | bytes 442376 | tf_op jit(solution)/shard_map/ppermute | solution.py:171
  55.1 26.5 %collective-permute-start.1 = (bf16[32,16,384]{2,1,0:T(8,128)(2,1)S(1)}, bf16[32,16,384]{2,1,0:T(8,128)(2,1)S(1)}, u32[]{:S(2)}, u32[]{:S(2)}) collective-permute-start(bf16[32,16,384]{2,1,0:T(8,128)(2,1)S(1)} %all-to-all-done), channel_id=1, source_target_pairs={{0,256},{256,0},{1,257},{257,1},{2,258},{258,2},{3,259},{259,3},{4... | collective-permute-start | bytes 1179656 | tf_op jit(solution)/shard_map/ppermute | solution.py:172
  123.3 10.5 %collective-permute-start.2 = (bf16[128,768]{1,0:T(8,128)(2,1)S(1)}, bf16[128,768]{1,0:T(8,128)(2,1)S(1)}, u32[]{:S(2)}, u32[]{:S(2)}) collective-permute-start(bf16[128,768]{1,0:T(8,128)(2,1)S(1)} %shard_map.56.refs_0_), channel_id=1, source_target_pairs={{0,1},{1,0},{2,3},{3,2},{4,5},{5,4},{6,7},{7,6},{8,9},{9,8},{10,11... | collective-permute-start | bytes 589832 | tf_op jit(solution)/shard_map/ppermute | solution.py:192
  125.3 19.0 %collective-permute-start.3 = (bf16[128,768]{1,0:T(8,128)(2,1)S(1)}, bf16[128,768]{1,0:T(8,128)(2,1)S(1)}, u32[]{:S(2)}, u32[]{:S(2)}) collective-permute-start(bf16[128,768]{1,0:T(8,128)(2,1)S(1)} %shard_map.56.refs_0_), channel_id=1, source_target_pairs={{0,2},{1,3},{2,0},{3,1},{4,6},{5,7},{6,4},{7,5},{8,10},{9,11},{10,... | collective-permute-start | bytes 589832 | tf_op jit(solution)/shard_map/ppermute | solution.py:192
  128.1 16.1 %collective-permute-start.4 = (bf16[128,768]{1,0:T(8,128)(2,1)S(1)}, bf16[128,768]{1,0:T(8,128)(2,1)S(1)}, u32[]{:S(2)}, u32[]{:S(2)}) collective-permute-start(bf16[128,768]{1,0:T(8,128)(2,1)S(1)} %shard_map.56.refs_0_), channel_id=1, source_target_pairs={{0,3},{1,2},{2,1},{3,0},{4,7},{5,6},{6,5},{7,4},{8,11},{9,10},{10,... | collective-permute-start | bytes 589832 | tf_op jit(solution)/shard_map/ppermute | solution.py:192
  148.5 26.2 %collective-permute-start.6 = (bf16[128,768]{1,0:T(8,128)(2,1)S(1)}, bf16[128,768]{1,0:T(8,128)(2,1)S(1)}, u32[]{:S(2)}, u32[]{:S(2)}) collective-permute-start(bf16[128,768]{1,0:T(8,128)(2,1)S(1)} %shard_map.58), channel_id=1, source_target_pairs={{0,4},{4,0},{1,5},{5,1},{2,6},{6,2},{3,7},{7,3},{8,12},{12,8},{9,1... | collective-permute-start | bytes 589832 | tf_op jit(solution)/shard_map/ppermute | solution.py:196
Sparse Core Ops, SparseCore 0:
  55.3 81.1 all-gather.2

commit v20 on v17

--- a/solution.py
+++ b/solution.py
@@ -110,25 +110,20 @@
             piece = routed_ref[kind * HALVES + at, :, turn, :, lane : lane + HEAD_DIM]
             return piece.reshape(tokens, HEAD_DIM)
 
-        query = own_ref[0, :, cols]
-        scores = [
-            lax.dot_general(
-                query, keys, (((1,), (1,)), ((), ())), preferred_element_type=jnp.float32
+        keys, values = [
+            jnp.concatenate(
+                [own_ref[1 + kind, :, cols]] + [rows(kind, turn) for turn in range(ROUNDS)]
             )
-            * (1.0 / HEAD_DIM**0.5)
-            for keys in [own_ref[1, :, cols]] + [rows(0, turn) for turn in range(ROUNDS)]
+            for kind in range(2)
         ]
-        peak = functools.reduce(jnp.maximum, scores)
-        peak = jnp.max(peak, axis=-1, keepdims=True)
-        exponents = [jnp.exp(score - peak) for score in scores]
-        row_total = jnp.sum(functools.reduce(jnp.add, exponents), axis=-1, keepdims=True)
-        summed = 0.0
-        for exponent, values in zip(
-            exponents, [own_ref[2, :, cols]] + [rows(1, turn) for turn in range(ROUNDS)]
-        ):
-            summed += jnp.dot(
-                exponent.astype(jnp.bfloat16), values, preferred_element_type=jnp.float32
-            )
+        scores = lax.dot_general(
+            own_ref[0, :, cols], keys, (((1,), (1,)), ((), ())), preferred_element_type=jnp.float32
+        ) * (1.0 / HEAD_DIM**0.5)
+        exponent = jnp.exp(scores - jnp.max(scores, axis=-1, keepdims=True))
+        row_total = jnp.sum(exponent, axis=-1, keepdims=True)
+        summed = jnp.dot(
+            exponent.astype(jnp.bfloat16), values, preferred_element_type=jnp.float32
+        )
         out_ref[:, cols] = (summed / row_total).astype(out_ref.dtype)
 
 

time: 184 us -> 184 us (level)
  no operation moved by 1% of the time
where the time goes in v20:
time: 184 us; the launch traced here: 182 us
  starting transfers between devices  59.9 us (33%)
  waiting for transfers between devices  53.3 us (29%)
  blocking collectives  39 us (21%)
  between operations  13.5 us (7%)
  Pallas kernels  11.9 us (6%)
  other arithmetic  3.54 us (2%)
    all_to_all x1, blocking collectives, body(): lax.all_to_all(chosen, PLANE, split_axis=0, concat_axis=0, tiled=True)  39 us
    ppermute x1, starting transfers between devices, body(): w_far = lax.ppermute(w_near, 'zh', SWAP)  13.8 us
    ppermute x1, starting transfers between devices, body(): far = lax.ppermute(spread, 'zh', SWAP)  13.1 us
    ppermute x1, waiting for transfers between devices, body(): arrived = lax.ppermute(sent, 'p', SWAP)  12.9 us
    ppermute x1, waiting for transfers between devices, body(): far = lax.ppermute(spread, 'zh', SWAP)  11.3 us
    ppermute x3, waiting for transfers between devices, body(): lax.ppermute(attended, 'q', [(i, i ^ k) for i in range(QUAD)])  10.7 us
    ppermute x1, waiting for transfers between devices, body(): w_far = lax.ppermute(w_near, 'zh', SWAP)  10.5 us
    ppermute x3, starting transfers between devices, body(): lax.ppermute(attended, 'q', [(i, i ^ k) for i in range(QUAD)])  10.1 us
  transfers between devices with their start and end apart: 9, of which 6 were waited for; matrix products, arithmetic and copies ran while one was open for 2% of the time, Pallas kernels for 3%

profile of v20, /device:TPU:6, one launch (start us, length us, event | category | flops | bytes accessed | tf_op | source)
XLA Modules:
  0.0 182.0 jit_solution(2033810522659534663)
XLA Ops:
  6.5 1.8 shard_map.55
  8.3 9.6 %all-to-all-start = ((bf16[32,16,384]{2,1,0:T(8,128)(2,1)}), bf16[32,16,384]{2,1,0:T(8,128)(2,1)S(1)}, u32[]{:S(2)}, u32[]{:S(2)}) async-start(bf16[32,16,384]{2,1,0:T(8,128)(2,1)} %bitcast), calls=%async_computation | async-start | bytes 786432 | tf_op jit(solution)/shard_map/all_to_all | solution.py:161
  17.9 0.0 all-gather.3.cloned.1.call-start
  18.0 4.2 %collective-permute-start = (bf16[96,768]{1,0:T(8,128)(2,1)}, bf16[96,768]{1,0:T(8,128)(2,1)S(1)}, u32[]{:S(2)}, u32[]{:S(2)}) collective-permute-start(bf16[96,768]{1,0:T(8,128)(2,1)} %bitcast.21), channel_id=1, source_target_pairs={{0,0},{1,64},{2,128},{3,192},{64,1},{65,65},{66,129},{67,193},{128... | collective-permute-start | bytes 442376 | tf_op jit(solution)/shard_map/ppermute | solution.py:153
  22.2 7.9 %collective-permute-done = bf16[96,768]{1,0:T(8,128)(2,1)S(1)} collective-permute-done((bf16[96,768]{1,0:T(8,128)(2,1)}, bf16[96,768]{1,0:T(8,128)(2,1)S(1)}, u32[]{:S(2)}, u32[]{:S(2)}) %collective-permute-start) | collective-permute-done | bytes 147488 | tf_op jit(solution)/shard_map/ppermute | solution.py:153
  30.1 0.0 all-to-all-done
  30.1 13.8 %collective-permute-start.5 = (bf16[96,768]{1,0:T(8,128)(2,1)S(1)}, bf16[96,768]{1,0:T(8,128)(2,1)S(1)}, u32[]{:S(2)}, u32[]{:S(2)}) collective-permute-start(bf16[96,768]{1,0:T(8,128)(2,1)S(1)} %collective-permute-done), channel_id=1, source_target_pairs={{0,256},{256,0},{1,257},{257,1},{2,258},{258,2},{3,259},{259,3},{4... | collective-permute-start | bytes 442376 | tf_op jit(solution)/shard_map/ppermute | solution.py:164
  43.9 10.5 %collective-permute-done.5 = bf16[96,768]{1,0:T(8,128)(2,1)S(1)} collective-permute-done((bf16[96,768]{1,0:T(8,128)(2,1)S(1)}, bf16[96,768]{1,0:T(8,128)(2,1)S(1)}, u32[]{:S(2)}, u32[]{:S(2)}) %collective-permute-start.5) | collective-permute-done | bytes 147488 | tf_op jit(solution)/shard_map/ppermute | solution.py:164
  54.4 0.7 pad_maximum_fusion.2
  55.1 0.0 all-gather.3.cloned.1.call-update
  55.1 13.1 %collective-permute-start.1 = (bf16[32,16,384]{2,1,0:T(8,128)(2,1)S(1)}, bf16[32,16,384]{2,1,0:T(8,128)(2,1)S(1)}, u32[]{:S(2)}, u32[]{:S(2)}) collective-permute-start(bf16[32,16,384]{2,1,0:T(8,128)(2,1)S(1)} %all-to-all-done), channel_id=1, source_target_pairs={{0,256},{256,0},{1,257},{257,1},{2,258},{258,2},{3,259},{259,3},{4... | collective-permute-start | bytes 1179656 | tf_op jit(solution)/shard_map/ppermute | solution.py:165
  68.3 0.8 compare_select_fusion
  69.0 0.1 copy.8
  69.1 0.1 reshape.14
  69.2 1.2 pad_maximum_fusion.1.own_ref
  70.4 11.3 %collective-permute-done.1 = bf16[32,16,384]{2,1,0:T(8,128)(2,1)S(1)} collective-permute-done((bf16[32,16,384]{2,1,0:T(8,128)(2,1)S(1)}, bf16[32,16,384]{2,1,0:T(8,128)(2,1)S(1)}, u32[]{:S(2)}, u32[]{:S(2)}) %collective-permute-start.1) | collective-permute-done | bytes 393248 | tf_op jit(solution)/shard_map/ppermute | solution.py:165
  81.7 0.1 pad_maximum_fusion
  81.8 0.7 gather_fusion
  82.5 39.0 %all_to_all.10 = bf16[32,2,16,384]{3,2,1,0:T(8,128)(2,1)S(1)} all-to-all(bf16[32,2,16,384]{3,2,1,0:T(8,128)(2,1)S(1)} %bitcast.17), channel_id=1, replica_groups=mesh['zh'=2,'x'=4,'y'=4,'c'=2,'p'=2,'q'=4] {'x','y','c'}, dimensions={0} | all-to-all | bytes 1572864 | tf_op jit(solution)/shard_map/all_to_all | solution.py:179
  121.5 1.7 shard_map.56.refs_0_
  123.2 1.9 %collective-permute-start.2 = (bf16[128,768]{1,0:T(8,128)(2,1)S(1)}, bf16[128,768]{1,0:T(8,128)(2,1)S(1)}, u32[]{:S(2)}, u32[]{:S(2)}) collective-permute-start(bf16[128,768]{1,0:T(8,128)(2,1)S(1)} %shard_map.56.refs_0_), channel_id=1, source_target_pairs={{0,1},{1,0},{2,3},{3,2},{4,5},{5,4},{6,7},{7,6},{8,9},{9,8},{10,11... | collective-permute-start | bytes 589832 | tf_op jit(solution)/shard_map/ppermute | solution.py:185
  125.1 2.8 %collective-permute-start.3 = (bf16[128,768]{1,0:T(8,128)(2,1)S(1)}, bf16[128,768]{1,0:T(8,128)(2,1)S(1)}, u32[]{:S(2)}, u32[]{:S(2)}) collective-permute-start(bf16[128,768]{1,0:T(8,128)(2,1)S(1)} %shard_map.56.refs_0_), channel_id=1, source_target_pairs={{0,2},{1,3},{2,0},{3,1},{4,6},{5,7},{6,4},{7,5},{8,10},{9,11},{10,... | collective-permute-start | bytes 589832 | tf_op jit(solution)/shard_map/ppermute | solution.py:185
  127.9 5.4 %collective-permute-start.4 = (bf16[128,768]{1,0:T(8,128)(2,1)S(1)}, bf16[128,768]{1,0:T(8,128)(2,1)S(1)}, u32[]{:S(2)}, u32[]{:S(2)}) collective-permute-start(bf16[128,768]{1,0:T(8,128)(2,1)S(1)} %shard_map.56.refs_0_), channel_id=1, source_target_pairs={{0,3},{1,2},{2,1},{3,0},{4,7},{5,6},{6,5},{7,4},{8,11},{9,10},{10,... | collective-permute-start | bytes 589832 | tf_op jit(solution)/shard_map/ppermute | solution.py:185
  133.3 0.3 collective-permute-done.2.refs_1_
  133.6 10.4 %collective-permute-done.3.refs_2_ = bf16[128,768]{1,0:T(8,128)(2,1)S(1)} collective-permute-done((bf16[128,768]{1,0:T(8,128)(2,1)S(1)}, bf16[128,768]{1,0:T(8,128)(2,1)S(1)}, u32[]{:S(2)}, u32[]{:S(2)}) %collective-permute-start.3) | collective-permute-done | bytes 196640 | tf_op jit(solution)/shard_map/ppermute | solution.py:185
  144.0 0.0 collective-permute-done.4.refs_3_
  144.0 0.0 all-gather.3.cloned.1.call-done
  144.0 4.2 %shard_map.58 = bf16[128,768]{1,0:T(8,128)(2,1)S(1)} custom-call(s32[4]{0:T(128)S(1)} %iota_xor_fusion.order_ref, bf16[128,768]{1,0:T(8,128)(2,1)S(1)} %shard_map.56.refs_0_, bf16[128,768]{1,0:T(8,128)(2,1)S(1)} %collective-permute-done.2.refs_1_, bf16[128,768]{1,0:T(8,128)(2,1)S(1)} %collective-permute-done.3.refs_2_, ...), custom_call_target="tpu_custom_call" | custom-call | flops 603979776 | bytes 5505024 | tf_op jit(solution)/shard_map/pallas_call | solution.py:48
  148.2 9.1 %collective-permute-start.6 = (bf16[128,768]{1,0:T(8,128)(2,1)S(1)}, bf16[128,768]{1,0:T(8,128)(2,1)S(1)}, u32[]{:S(2)}, u32[]{:S(2)}) collective-permute-start(bf16[128,768]{1,0:T(8,128)(2,1)S(1)} %shard_map.58), channel_id=1, source_target_pairs={{0,4},{4,0},{1,5},{5,1},{2,6},{6,2},{3,7},{7,3},{8,12},{12,8},{9,1... | collective-permute-start | bytes 589832 | tf_op jit(solution)/shard_map/ppermute | solution.py:189
  157.3 4.2 %shard_map.57 = f32[128,768]{1,0:T(8,128)S(1)} custom-call(s32[4]{0:T(128)S(1)} %iota_xor_fusion.order_ref, bf16[128,768]{1,0:T(8,128)(2,1)S(1)} %shard_map.56.refs_0_, bf16[128,768]{1,0:T(8,128)(2,1)S(1)} %collective-permute-done.2.refs_1_, bf16[128,768]{1,0:T(8,128)(2,1)S(1)} %collective-permute-done.3.refs_2_, ...), custom_call_target="tpu_custom_call" | custom-call | flops 603979776 | bytes 5505024 | tf_op jit(solution)/shard_map/pallas_call | solution.py:48
  161.5 12.9 %collective-permute-done.6 = bf16[128,768]{1,0:T(8,128)(2,1)S(1)} collective-permute-done((bf16[128,768]{1,0:T(8,128)(2,1)S(1)}, bf16[128,768]{1,0:T(8,128)(2,1)S(1)}, u32[]{:S(2)}, u32[]{:S(2)}) %collective-permute-start.6) | collective-permute-done | bytes 196640 | tf_op jit(solution)/shard_map/ppermute | solution.py:189
  174.4 0.7 add_convert_fusion
  (3 shorter events, 0.0 us)
Async XLA Ops:
  8.3 21.7 %all-to-all-start = ((bf16[32,16,384]{2,1,0:T(8,128)(2,1)}), bf16[32,16,384]{2,1,0:T(8,128)(2,1)S(1)}, u32[]{:S(2)}, u32[]{:S(2)}) async-start(bf16[32,16,384]{2,1,0:T(8,128)(2,1)} %bitcast), calls=%async_computation | async-start | bytes 786432 | tf_op jit(solution)/shard_map/all_to_all | solution.py:161
  17.9 126.1 %all-gather.3.cloned.1.call-start = ((), (), s32[]{:S(2)}) async-start(), calls=%async_computation.2 | async-start | bytes 9732096 | tf_op jit(solution)/shard_map/all_gather | solution.py:170
  18.0 12.1 %collective-permute-start = (bf16[96,768]{1,0:T(8,128)(2,1)}, bf16[96,768]{1,0:T(8,128)(2,1)S(1)}, u32[]{:S(2)}, u32[]{:S(2)}) collective-permute-start(bf16[96,768]{1,0:T(8,128)(2,1)} %bitcast.21), channel_id=1, source_target_pairs={{0,0},{1,64},{2,128},{3,192},{64,1},{65,65},{66,129},{67,193},{128... | collective-permute-start | bytes 442376 | tf_op jit(solution)/shard_map/ppermute | solution.py:153
  30.1 24.3 %collective-permute-start.5 = (bf16[96,768]{1,0:T(8,128)(2,1)S(1)}, bf16[96,768]{1,0:T(8,128)(2,1)S(1)}, u32[]{:S(2)}, u32[]{:S(2)}) collective-permute-start(bf16[96,768]{1,0:T(8,128)(2,1)S(1)} %collective-permute-done), channel_id=1, source_target_pairs={{0,256},{256,0},{1,257},{257,1},{2,258},{258,2},{3,259},{259,3},{4... | collective-permute-start | bytes 442376 | tf_op jit(solution)/shard_map/ppermute | solution.py:164
  55.1 26.5 %collective-permute-start.1 = (bf16[32,16,384]{2,1,0:T(8,128)(2,1)S(1)}, bf16[32,16,384]{2,1,0:T(8,128)(2,1)S(1)}, u32[]{:S(2)}, u32[]{:S(2)}) collective-permute-start(bf16[32,16,384]{2,1,0:T(8,128)(2,1)S(1)} %all-to-all-done), channel_id=1, source_target_pairs={{0,256},{256,0},{1,257},{257,1},{2,258},{258,2},{3,259},{259,3},{4... | collective-permute-start | bytes 1179656 | tf_op jit(solution)/shard_map/ppermute | solution.py:165
  123.2 10.5 %collective-permute-start.2 = (bf16[128,768]{1,0:T(8,128)(2,1)S(1)}, bf16[128,768]{1,0:T(8,128)(2,1)S(1)}, u32[]{:S(2)}, u32[]{:S(2)}) collective-permute-start(bf16[128,768]{1,0:T(8,128)(2,1)S(1)} %shard_map.56.refs_0_), channel_id=1, source_target_pairs={{0,1},{1,0},{2,3},{3,2},{4,5},{5,4},{6,7},{7,6},{8,9},{9,8},{10,11... | collective-permute-start | bytes 589832 | tf_op jit(solution)/shard_map/ppermute | solution.py:185
  125.1 19.0 %collective-permute-start.3 = (bf16[128,768]{1,0:T(8,128)(2,1)S(1)}, bf16[128,768]{1,0:T(8,128)(2,1)S(1)}, u32[]{:S(2)}, u32[]{:S(2)}) collective-permute-start(bf16[128,768]{1,0:T(8,128)(2,1)S(1)} %shard_map.56.refs_0_), channel_id=1, source_target_pairs={{0,2},{1,3},{2,0},{3,1},{4,6},{5,7},{6,4},{7,5},{8,10},{9,11},{10,... | collective-permute-start | bytes 589832 | tf_op jit(solution)/shard_map/ppermute | solution.py:185
  127.9 16.1 %collective-permute-start.4 = (bf16[128,768]{1,0:T(8,128)(2,1)S(1)}, bf16[128,768]{1,0:T(8,128)(2,1)S(1)}, u32[]{:S(2)}, u32[]{:S(2)}) collective-permute-start(bf16[128,768]{1,0:T(8,128)(2,1)S(1)} %shard_map.56.refs_0_), channel_id=1, source_target_pairs={{0,3},{1,2},{2,1},{3,0},{4,7},{5,6},{6,5},{7,4},{8,11},{9,10},{10,... | collective-permute-start | bytes 589832 | tf_op jit(solution)/shard_map/ppermute | solution.py:185
  148.2 26.2 %collective-permute-start.6 = (bf16[128,768]{1,0:T(8,128)(2,1)S(1)}, bf16[128,768]{1,0:T(8,128)(2,1)S(1)}, u32[]{:S(2)}, u32[]{:S(2)}) collective-permute-start(bf16[128,768]{1,0:T(8,128)(2,1)S(1)} %shard_map.58), channel_id=1, source_target_pairs={{0,4},{4,0},{1,5},{5,1},{2,6},{6,2},{3,7},{7,3},{8,12},{12,8},{9,1... | collective-permute-start | bytes 589832 | tf_op jit(solution)/shard_map/ppermute | solution.py:189
Sparse Core Ops, SparseCore 0:
  55.3 81.1 all-gather.2
